TPU v7x, 32 devices: a whole 2x2x4 slice. The times are simulated.
32 devices in a mesh: dp: 2 (over x), expert: 4 (over z), shard: 4 (over y, core).
Axes of the slice: x: 2, y: 2, z: 4, core: 2. Of those that a mesh axis runs over, the one named last changes fastest.
Arguments:
- tokens: bfloat16 [256, 6144], P(('dp', 'expert', 'shard')), may hold values from -6 to 6
- gate_up_weight: bfloat16 [4, 2, 8192, 6144], P(None, None, ('dp', 'expert', 'shard')), may hold values from -0.078125 to 0.078125
- down_weight: bfloat16 [4, 8192, 6144], P(None, ('dp', 'expert', 'shard')), may hold values from -0.0625 to 0.0625
- expert_ids: int32 [256, 2], P(('dp', 'expert', 'shard')), may hold values from 0 to 3, as said below
- slot_ids: int32 [256, 2], P(('dp', 'expert', 'shard')), may hold values from 0 to 7, as said below
- gate_values: float32 [256, 2], P(('dp', 'expert', 'shard')), may hold values from 0.1 to 1
- old_place: int32 [4], replicated, may hold values from 0 to 3, each once
- new_place: int32 [4], replicated, may hold values from 0 to 3, each once
Outputs:
- mixed_out: bfloat16 [256, 6144], P(('dp', 'expert', 'shard'))
Inputs may be any that keep to these rules, and one draw needn't show every extreme that they name: `expert_ids`: each token names 2 different experts; among the 8 tokens of one block no expert is named more than 8 times, and one expert is named exactly 8 times in every block. `slot_ids`: within one block, two choices that name the same expert have different slots. `old_place`: each expert number appears once. `new_place`: each expert number appears once.
All inputs are finite; a program needn't handle non-finite values.
Results may differ from a plain program's by a relative error of at most 0.02.
Values may be sent and summed in bfloat16 or wider, within the bound.
No kernel may reach another device: no remote copies, remote signals or barrier semaphores. Data moves between devices by JAX's collectives and lax.ppermute only.
A program may use at most 192 MiB of HBM per device.

v0:
```python
import jax
import jax.numpy as jnp
from jax import lax
from jax.sharding import PartitionSpec as P


def placement_order(old_place, new_place):
    slot_total = old_place.shape[0]
    matches = (new_place[:, None] == old_place[None, :]).astype(jnp.int32)
    return jnp.sum(matches * jnp.arange(slot_total, dtype=jnp.int32)[None, :], axis=1)


def local(
    tokens, gate_up_weight, down_weight, expert_ids, slot_ids, gate_values, old_place, new_place
):
    experts = gate_up_weight.shape[0]
    sliver = gate_up_weight.shape[2]
    model_width = tokens.shape[1]
    tok_rows = tokens.shape[0]
    choices_per_token = expert_ids.shape[1]
    capacity = 2 * tok_rows * choices_per_token // experts
    cell_count = experts * capacity
    data_ways = lax.axis_size("dp")
    half_cols = model_width // data_ways
    slot_order = placement_order(old_place, new_place)
    cell_ids = expert_ids * capacity + slot_ids
    cell_range = jnp.arange(cell_count, dtype=jnp.int32)
    cell_hits = (cell_ids[:, :, None] == cell_range[None, None, :]).astype(jnp.float32)
    token_picks = jnp.sum(cell_hits, axis=1)
    dispatched = jnp.dot(
        token_picks.T.astype(jnp.bfloat16), tokens, preferred_element_type=jnp.float32
    ).astype(jnp.bfloat16)
    received = lax.all_to_all(
        dispatched.reshape(experts, capacity, model_width),
        "expert",
        split_axis=0,
        concat_axis=0,
        tiled=True,
    )
    own_rows = received.reshape(cell_count, model_width)
    sectioned_in = gate_up_weight.reshape(experts, 2, sliver, data_ways, half_cols).transpose(
        0, 1, 3, 2, 4
    )
    sectioned_down = down_weight.reshape(experts, 1, sliver, data_ways, half_cols).transpose(
        0, 1, 3, 2, 4
    )
    sectioned_in = jnp.take(sectioned_in, slot_order, axis=0)
    sectioned_down = jnp.take(sectioned_down, slot_order, axis=0)
    relaid_in, relaid_down = (
        lax.all_to_all(
            lax.all_to_all(sectioned_in, "dp", split_axis=2, concat_axis=3, tiled=True),
            "expert",
            split_axis=0,
            concat_axis=3,
            tiled=True,
        ),
        lax.all_to_all(
            lax.all_to_all(sectioned_down, "dp", split_axis=2, concat_axis=3, tiled=True),
            "expert",
            split_axis=0,
            concat_axis=3,
            tiled=True,
        ),
    )
    half_in = relaid_in.reshape(2, -1, half_cols)
    half_down = relaid_down.reshape(-1, half_cols)
    split_rows = lax.all_to_all(own_rows, "dp", split_axis=1, concat_axis=0, tiled=True)
    group_half = lax.all_gather(split_rows, "shard", axis=0, tiled=True)
    pre_act = jnp.einsum("rd,gud->rgu", group_half, half_in, preferred_element_type=jnp.float32)
    pre_act = lax.psum(pre_act.astype(jnp.bfloat16), "dp").astype(jnp.float32)
    hidden = (jax.nn.silu(pre_act[:, 0]) * pre_act[:, 1]).astype(jnp.bfloat16)
    summed = lax.psum_scatter(
        jnp.dot(hidden, half_down, preferred_element_type=jnp.float32).astype(jnp.bfloat16),
        "shard",
        scatter_dimension=0,
        tiled=True,
    )
    expert_out = lax.all_to_all(summed, "dp", split_axis=0, concat_axis=1, tiled=True)
    returned = lax.all_to_all(
        expert_out.reshape(experts, capacity, model_width),
        "expert",
        split_axis=0,
        concat_axis=0,
        tiled=True,
    )
    combine_weights = jnp.sum(cell_hits * gate_values[:, :, None], axis=1)
    mixed_out = jnp.dot(
        combine_weights,
        returned.reshape(cell_count, model_width).astype(jnp.float32),
        precision=lax.Precision.HIGHEST,
    )
    return mixed_out.astype(jnp.bfloat16)


def solution(mesh):
    in_specs = (
        P(("dp", "expert", "shard"), None),
        P(None, None, ("dp", "expert", "shard"), None),
        P(None, ("dp", "expert", "shard"), None),
        P(("dp", "expert", "shard"), None),
        P(("dp", "expert", "shard"), None),
        P(("dp", "expert", "shard"), None),
        P(),
        P(),
    )
    out_specs = P(("dp", "expert", "shard"), None)
    return jax.shard_map(local, mesh=mesh, in_specs=in_specs, out_specs=out_specs, check_vma=False)
```

profile of v0, /device:TPU:0, one launch (start us, length us, event | category | flops | bytes accessed | tf_op | source)
XLA Modules:
  0.0 1496.4 jit_solution(681668470092873583)
XLA Ops:
  6.5 0.7 multiply_add_fusion
  7.3 1.3 convert_reduce_fusion
  8.6 1.0 fusion
  9.7 6.3 all-to-all-start
  16.0 32.7 %copy.69 = bf16[4,2,256,6144]{2,3,1,0:T(8,128)(2,1)} copy(bf16[4,2,256,6144]{3,2,1,0:T(8,128)(2,1)} %param.9) | data formatting | bytes 50331648 | tf_op args[1]
  48.7 32.7 %copy.70 = bf16[4,2,256,2,3072]{4,2,3,1,0:T(8,128)(2,1)} copy(bf16[4,2,256,2,3072]{2,4,3,1,0:T(8,128)(2,1)} %bitcast.48) | data formatting | bytes 50331648 | tf_op jit(solution)/shard_map/reshape | solution.py:41
  81.4 18.1 %fusion.9 = (bf16[4,2,2,256,768]{4,3,2,1,0:T(8,128)(2,1)}, bf16[4,2,2,256,768]{4,3,2,1,0:T(8,128)(2,1)}, bf16[4,2,2,256,768]{4,3,2,1,0:T(8,128)(2,1)}, bf16[4,2,2,256,768]{4,3,2,1,0:T(8,128)(2,1)}) fusion(bf16[4,2,2,256,3072]{4,3,2,1,0:T(8,128)(2,1)} %bitcast.47), kind=kLoop, calls=%fused_computation.32 | loop fusion | bytes 50331648 | tf_op jit(solution)/shard_map/jit(_take)/gather | solution.py:47
  99.7 6.4 gather_fusion
  106.1 6.4 gather_fusion.1
  112.5 6.4 gather_fusion.2
  118.8 6.4 gather_fusion.3
  125.3 0.3 all_to_all.69
  125.6 0.8 copy.68
  126.4 3.5 all-to-all-start.1
  129.9 17.4 %maximum_select_fusion = bf16[4,2,2,256,3072]{4,3,2,1,0:T(8,128)(2,1)} fusion(bf16[4,2,2,256,768]{4,3,2,1,0:T(8,128)(2,1)} %gather_fusion.3, bf16[4,2,2,256,768]{4,3,2,1,0:T(8,128)(2,1)} %gather_fusion.2, bf16[4,2,2,256,768]{4,3,2,1,0:T(8,128)(2,1)} %gather_fusion.1, bf16[4,2,2,256,768]{4,3,2,1,0:T(8,128)(2,1)} %gather_fusion, pred[4]{0:T(512)(128)(4,1)S(1)} %compare_and_fusion), kind=kLoop, calls=%fused_computation.6 | loop fusion | flops 113246208 | bytes 50331652 | tf_op jit(solution)/shard_map/jit(_take)/select_n | solution.py:47
  147.3 20.9 %copy.71 = bf16[4,2,2,256,3072]{4,3,1,0,2:T(8,128)(2,1)} copy(bf16[4,2,2,256,3072]{4,3,2,1,0:T(8,128)(2,1)} %maximum_select_fusion) | data formatting | bytes 50331648 | tf_op jit(solution)/shard_map/jit(_take)/select_n | solution.py:47
  168.2 0.7 copy-done.2
  169.0 11.8 all-to-all-start.2
  180.8 16.7 %copy.75 = bf16[4,256,6144]{1,2,0:T(8,128)(2,1)} copy(bf16[4,256,6144]{2,1,0:T(8,128)(2,1)} %param.10) | data formatting | bytes 25165824 | tf_op args[2]
  197.5 16.6 %copy.76 = bf16[4,1,256,2,3072]{4,2,3,0,1:T(8,128)(2,1)} copy(bf16[4,1,256,2,3072]{2,4,3,0,1:T(8,128)(2,1)} %bitcast.51) | data formatting | bytes 25165824 | tf_op jit(solution)/shard_map/reshape | solution.py:44
  214.1 10.4 slice_bitcast_fusion.1
  224.5 6.3 gather_fusion.4
  230.8 6.4 gather_fusion.5
  237.2 7.5 maximum_select_fusion.1
  244.7 5.5 copy.77
  250.1 202.7 %all-to-all-done.2 = bf16[4,2,2,256,3072]{4,3,1,0,2:T(8,128)(2,1)} async-done(((bf16[4,2,2,256,3072]{4,3,1,0,2:T(8,128)(2,1)}), bf16[4,2,2,256,3072]{4,3,1,0,2:T(8,128)(2,1)}, u32[]{:S(2)}, u32[]{:S(2)}) %all-to-all-start.2) | async-done | bytes 25165856 | tf_op jit(solution)/shard_map/all_to_all | solution.py:51
  452.9 8.3 all-to-all-start.4
  461.2 20.9 %copy.72 = bf16[4,2,2,256,3072]{4,3,2,1,0:T(8,128)(2,1)} copy(bf16[4,2,2,256,3072]{4,3,1,0,2:T(8,128)(2,1)} %all-to-all-done.2) | data formatting | bytes 50331648 | tf_op jit(solution)/shard_map/all_to_all | solution.py:51
  482.1 115.5 %all-to-all-done.4 = bf16[4,1,2,256,3072]{4,3,0,1,2:T(8,128)(2,1)} async-done(((bf16[4,1,2,256,3072]{4,3,0,1,2:T(8,128)(2,1)}), bf16[4,1,2,256,3072]{4,3,0,1,2:T(8,128)(2,1)}, u32[]{:S(2)}, u32[]{:S(2)}) %all-to-all-start.4) | async-done | bytes 12582944 | tf_op jit(solution)/shard_map/all_to_all | solution.py:58
  597.6 8.5 all-to-all-start.3
  606.1 10.6 copy.78
  616.7 530.2 %all-to-all-done.3 = bf16[4,2,1,512,3072]{4,3,1,2,0:T(8,128)(2,1)} async-done(((bf16[4,2,1,512,3072]{4,3,1,2,0:T(8,128)(2,1)}), bf16[4,2,1,512,3072]{4,3,1,2,0:T(8,128)(2,1)}, u32[]{:S(2)}, u32[]{:S(2)}) %all-to-all-start.3) | async-done | bytes 25165856 | tf_op jit(solution)/shard_map/all_to_all | solution.py:50
  1146.8 6.3 all-to-all-start.5
  1153.2 0.7 all-gather.2.cloned.1.call-update
  1153.9 0.2 all-reduce.2.cloned.1.call-start
  1154.1 21.0 %copy.74 = bf16[1,2,1,4,512,3072]{5,4,3,1,2,0:T(8,128)(2,1)} copy(bf16[1,2,1,4,512,3072]{5,4,1,3,2,0:T(8,128)(2,1)} %bitcast.11) | data formatting | bytes 50331648 | tf_op jit(solution)/shard_map/all_to_all | solution.py:50
  1175.1 0.6 all-gather.2.cloned.1.call-done
  1175.7 13.1 convolution_convert_fusion.3
  1188.9 63.0 %all-reduce.2.cloned.1.call-done = bf16[256,2,2048]{2,0,1:T(8,128)(2,1)} async-done(((bf16[256,2,2048]{2,0,1:T(8,128)(2,1)}), bf16[256,2,2048]{2,0,1:T(8,128)(2,1)}) %all-reduce.2.cloned.1.call-update) | async-done | bytes 2097168 | tf_op jit(solution)/shard_map/psum | solution.py:70
  1251.9 4.1 convert_element_type.34
  1256.0 169.6 %all-to-all-done.5 = bf16[4,1,1,512,3072]{4,3,2,1,0:T(8,128)(2,1)} async-done(((bf16[4,1,1,512,3072]{4,3,2,1,0:T(8,128)(2,1)}), bf16[4,1,1,512,3072]{4,3,2,1,0:T(8,128)(2,1)}, u32[]{:S(2)}, u32[]{:S(2)}) %all-to-all-start.5) | async-done | bytes 12582944 | tf_op jit(solution)/shard_map/all_to_all | solution.py:57
  1425.6 10.5 convolution_convert_fusion.2
  1436.2 26.5 %reduce-scatter.2.cloned.1.call-done = bf16[64,3072]{1,0:T(8,128)(2,1)} async-done(((bf16[256,3072]{1,0:T(8,128)(2,1)}), bf16[64,3072]{1,0:T(8,128)(2,1)}) %reduce-scatter.2.cloned.1.call-update) | async-done | bytes 393232 | tf_op jit(solution)/shard_map/reduce_scatter | solution.py:72
  1462.7 10.3 all_to_all.93
  1473.0 0.4 copy.80
  1473.4 0.3 reshape.77
  1473.7 15.2 %all_to_all.94 = bf16[4,8,6144]{2,1,0:T(8,128)(2,1)S(1)} all-to-all(bf16[4,8,6144]{2,1,0:T(8,128)(2,1)S(1)} %reshape.77), channel_id=1, replica_groups=mesh['dp'=2,'expert'=4,'shard'=4] {'expert'}, dimensions={0} | all-to-all | bytes 786432 | tf_op jit(solution)/shard_map/all_to_all | solution.py:79
  1488.9 0.9 convolution_convert_fusion.1
  (21 shorter events, 0.3 us)
Async XLA Ops:
  6.5 2.1 copy-start
  9.7 115.6 %all-to-all-start = ((bf16[4,8,6144]{2,1,0:T(8,128)(2,1)}), bf16[4,8,6144]{2,1,0:T(8,128)(2,1)S(1)}, u32[]{:S(2)}, u32[]{:S(2)}) async-start(bf16[4,8,6144]{2,1,0:T(8,128)(2,1)} %fusion), calls=%async_computation | async-start | bytes 786432 | tf_op jit(solution)/shard_map/all_to_all | solution.py:33
  81.4 18.1 %copy-start.4 = (s32[4]{0:T(128)S(1)}, s32[4]{0:T(128)}, u32[]{:S(2)}) copy-start(s32[4]{0:T(128)} %param.14) | copy-start | bytes 52
  81.4 18.1 %copy-start.5 = (s32[4]{0:T(128)S(1)}, s32[4]{0:T(128)}, u32[]{:S(2)}) copy-start(s32[4]{0:T(128)} %param.15) | copy-start | bytes 52
  126.4 41.8 %all-to-all-start.1 = ((bf16[32,2,3072]{2,0,1:T(8,128)(2,1)}), bf16[32,2,3072]{2,0,1:T(8,128)(2,1)S(1)}, u32[]{:S(2)}, u32[]{:S(2)}) async-start(bf16[32,2,3072]{2,0,1:T(8,128)(2,1)} %copy.68), calls=%async_computation.1 | async-start | bytes 786432 | tf_op jit(solution)/shard_map/all_to_all | solution.py:67
  168.2 0.7 copy-start.2
  169.0 283.9 %all-to-all-start.2 = ((bf16[4,2,2,256,3072]{4,3,1,0,2:T(8,128)(2,1)}), bf16[4,2,2,256,3072]{4,3,1,0,2:T(8,128)(2,1)}, u32[]{:S(2)}, u32[]{:S(2)}) async-start(bf16[4,2,2,256,3072]{4,3,1,0,2:T(8,128)(2,1)} %copy.71), calls=%async_computation.2 | async-start | bytes 50331648 | tf_op jit(solution)/shard_map/all_to_all | solution.py:51
  452.9 144.7 %all-to-all-start.4 = ((bf16[4,1,2,256,3072]{4,3,0,1,2:T(8,128)(2,1)}), bf16[4,1,2,256,3072]{4,3,0,1,2:T(8,128)(2,1)}, u32[]{:S(2)}, u32[]{:S(2)}) async-start(bf16[4,1,2,256,3072]{4,3,0,1,2:T(8,128)(2,1)} %copy.77), calls=%async_computation.4 | async-start | bytes 25165824 | tf_op jit(solution)/shard_map/all_to_all | solution.py:58
  597.6 549.3 %all-to-all-start.3 = ((bf16[4,2,1,512,3072]{4,3,1,2,0:T(8,128)(2,1)}), bf16[4,2,1,512,3072]{4,3,1,2,0:T(8,128)(2,1)}, u32[]{:S(2)}, u32[]{:S(2)}) async-start(bf16[4,2,1,512,3072]{4,3,1,2,0:T(8,128)(2,1)} %bitcast.46), calls=%async_computation.3 | async-start | bytes 50331648 | tf_op jit(solution)/shard_map/all_to_all | solution.py:50
  1146.8 278.8 %all-to-all-start.5 = ((bf16[4,1,1,512,3072]{4,3,2,1,0:T(8,128)(2,1)}), bf16[4,1,1,512,3072]{4,3,2,1,0:T(8,128)(2,1)}, u32[]{:S(2)}, u32[]{:S(2)}) async-start(bf16[4,1,1,512,3072]{4,3,2,1,0:T(8,128)(2,1)} %bitcast.49), calls=%async_computation.5 | async-start | bytes 25165824 | tf_op jit(solution)/shard_map/all_to_all | solution.py:57
  1153.2 22.6 %all-gather.2.cloned.1.call-start = ((), (), s32[]{:S(2)}) async-start(), calls=%async_computation.9 | async-start | bytes 1966080 | tf_op jit(solution)/shard_map/all_gather | solution.py:68
  1153.9 98.0 %all-reduce.2.cloned.1.call-start = ((), (), s32[]{:S(2)}) async-start(), calls=%async_computation.10 | async-start | bytes 4194304 | tf_op jit(solution)/shard_map/psum | solution.py:70
  1188.8 273.9 %reduce-scatter.2.cloned.1.call-start = ((), (), s32[]{:S(2)}) async-start(), calls=%async_computation.11 | async-start | bytes 1966080 | tf_op jit(solution)/shard_map/reduce_scatter | solution.py:72
  1425.6 63.3 %copy-start.3 = (f32[8,32]{1,0:T(8,128)S(1)}, f32[8,32]{1,0:T(8,128)}, u32[]{:S(2)}) copy-start(f32[8,32]{1,0:T(8,128)} %get-tuple-element.6) | copy-start | bytes 3076
  1425.6 64.2 %copy-start.1 = (bf16[8,6144]{1,0:T(8,128)(2,1)S(1)}, bf16[8,6144]{1,0:T(8,128)(2,1)}, u32[]{:S(2)}) copy-start(bf16[8,6144]{1,0:T(8,128)(2,1)} %param.8) | copy-start | bytes 294916
Sparse Core Ops, SparseCore 0:
  1155.5 20.1 all-gather.1
  1188.9 62.9 all-reduce.1
  1436.3 26.3 reduce-scatter.1
where the time goes:
time: 1500 us
  waiting for transfers between devices  1110 us (74%)
  local copies, waits for them, and re-layouts  247 us (16%)
  starting transfers between devices  45 us (3%)
  other arithmetic  31.3 us (2%)
  matrix products  25.6 us (2%)
  blocking collectives  25.5 us (2%)
    all_to_all x1, waiting for transfers between devices, local(): lax.all_to_all(lax.all_to_all(sectioned_in, 'dp', split_axis=2, concat_ax...  530 us
    all_to_all x1, waiting for transfers between devices, local(): lax.all_to_all(sectioned_in, 'dp', split_axis=2, concat_axis=3, tiled=True)  203 us
    all_to_all x1, waiting for transfers between devices, local(): lax.all_to_all(lax.all_to_all(sectioned_down, 'dp', split_axis=2, concat_...  170 us
    all_to_all x1, waiting for transfers between devices, local(): lax.all_to_all(sectioned_down, 'dp', split_axis=2, concat_axis=3, tiled=T...  115 us
    psum x1, waiting for transfers between devices, local(): pre_act = lax.psum(pre_act.astype(jnp.bfloat16), 'dp').astype(jnp.float32)  63 us
    unnamed x14, local copies, waits for them, and re-layouts  50.1 us
    gather x5, local copies, waits for them, and re-layouts, local(): sectioned_in = jnp.take(sectioned_in, slot_order, axis=0)  43.7 us
    reshape x1, local copies, waits for them, and re-layouts, local(): gate_up_weight.reshape(experts, 2, sliver, data_ways, half_cols)  32.7 us
  transfers between devices with their start and end apart: 9, of which 7 were waited for; matrix products, arithmetic and copies ran while one was open for 19% of the time, Pallas kernels for 0%

commit v1 on v0

v1 whole, which is shorter than its diff:
```python
import jax
import jax.numpy as jnp
from jax import lax
from jax.sharding import PartitionSpec as P

AXES = ("dp", "expert", "shard")


def slot_coefficients(expert_ids, gate_values, old_place, new_place):
    matches = (new_place[:, None] == old_place[None, :]).astype(jnp.float32)
    picks = (expert_ids[:, :, None] == jnp.arange(new_place.shape[0], dtype=jnp.int32)).astype(jnp.float32)
    by_expert = jnp.sum(picks * gate_values[:, :, None], axis=1)
    return jnp.sum(by_expert[:, :, None] * matches[None, :, :], axis=1)


def local(
    tokens, gate_up_weight, down_weight, expert_ids, slot_ids, gate_values, old_place, new_place
):
    experts, _, sliver, model_width = gate_up_weight.shape
    coefficients = slot_coefficients(expert_ids, gate_values, old_place, new_place)
    all_tokens = lax.all_gather(tokens, AXES, axis=0, tiled=True)
    all_coefficients = lax.all_gather(coefficients, AXES, axis=0, tiled=True)
    pre_act = jnp.einsum(
        "td,eghd->tegh", all_tokens, gate_up_weight, preferred_element_type=jnp.float32
    )
    hidden = jax.nn.silu(pre_act[:, :, 0]) * pre_act[:, :, 1]
    hidden = (hidden * all_coefficients[:, :, None]).astype(jnp.bfloat16)
    partial = jnp.dot(
        hidden.reshape(-1, experts * sliver),
        down_weight.reshape(experts * sliver, model_width),
        preferred_element_type=jnp.float32,
    ).astype(jnp.bfloat16)
    return lax.psum_scatter(partial, AXES, scatter_dimension=0, tiled=True)


def solution(mesh):
    in_specs = (
        P(AXES, None),
        P(None, None, AXES, None),
        P(None, AXES, None),
        P(AXES, None),
        P(AXES, None),
        P(AXES, None),
        P(),
        P(),
    )
    return jax.shard_map(
        local, mesh=mesh, in_specs=in_specs, out_specs=P(AXES, None), check_vma=False
    )
```

time: 1500 us -> 202 us (0.13)
  waiting for transfers between devices: 1110 us -> 121 us
  local copies, waits for them, and re-layouts: 247 us -> 0.11 us
  starting transfers between devices: 45 us -> 0.04 us
  other arithmetic: 31.3 us -> 1.54 us
  blocking collectives: 25.5 us -> 43.5 us
    all_to_all x6 -> x0, waiting for transfers between devices: 1020 us -> none  [the longest x1 530 us: local(): lax.all_to_all(lax.all_to_all(sectioned_in, 'dp', split_axis=2, concat_ax...]
    reduce_scatter x1, waiting for transfers between devices: 26.5 us -> 101 us  [local(): return lax.psum_scatter(partial, AXES, scatter_dimension=0, tiled=True)]
    gather x8 -> x0, local copies, waits for them, and re-layouts: 66.7 us -> none  [the longest x5 43.7 us: local(): sectioned_in = jnp.take(sectioned_in, slot_order, axis=0)]
    psum x1 -> x0, waiting for transfers between devices: 63 us -> none  [local(): pre_act = lax.psum(pre_act.astype(jnp.bfloat16), 'dp').astype(jnp.float32)]
    all_to_all x6 -> x0, local copies, waits for them, and re-layouts: 54 us -> none  [the longest x1 21 us: local(): lax.all_to_all(lax.all_to_all(sectioned_in, 'dp', split_axis=2, concat_ax...]
    unnamed x14 -> x1, local copies, waits for them, and re-layouts: 50.1 us -> 0.1 us
    reshape x3 -> x0, local copies, waits for them, and re-layouts: 49.7 us -> none  [the longest x1 32.7 us: local(): gate_up_weight.reshape(experts, 2, sliver, data_ways, half_cols)]
    all_to_all x6 -> x0, starting transfers between devices: 44.7 us -> none  [the longest x1 11.8 us: local(): lax.all_to_all(sectioned_in, 'dp', split_axis=2, concat_axis=3, tiled=True)]
  transfers between devices with their start and end apart: 9 -> 2, of which waited for: 7 -> 2; matrix products, arithmetic and copies ran while one was open for 19% -> 1% of each run, Pallas kernels for 0% -> 0%
where the time goes in v1:
time: 202 us
  waiting for transfers between devices  121 us (60%)
  blocking collectives  43.5 us (22%)
  matrix products  22.3 us (11%)
  between operations  13.4 us (7%)
    reduce_scatter x1, waiting for transfers between devices, local(): return lax.psum_scatter(partial, AXES, scatter_dimension=0, tiled=True)  101 us
    all_gather x1, blocking collectives, local(): all_coefficients = lax.all_gather(coefficients, AXES, axis=0, tiled=True)  43.5 us
    all_gather x1, waiting for transfers between devices, local(): all_tokens = lax.all_gather(tokens, AXES, axis=0, tiled=True)  19.6 us
    dot_general x1, matrix products, local(): jnp.einsum('td,eghd->tegh', all_tokens, gate_up_weight, preferred_element...  12.5 us
    dot_general x1, matrix products, local(): jnp.dot(hidden.reshape(-1, experts * sliver), down_weight.reshape(experts...  9.77 us
  transfers between devices with their start and end apart: 2, of which 2 were waited for; matrix products, arithmetic and copies ran while one was open for 1% of the time, Pallas kernels for 0%

profile of v1, /device:TPU:0, one launch (start us, length us, event | category | flops | bytes accessed | tf_op | source)
XLA Modules:
  0.0 201.7 jit_solution(3408422075803195679)
XLA Ops:
  6.5 0.0 all-gather.3.cloned.1.call-start
  6.5 0.7 all-gather.3.cloned.1.call-update
  7.3 0.0 reduce-scatter.2.cloned.1.call-start
  7.3 0.7 select_reduce_fusion
  8.0 0.7 compare_convert_fusion
  8.8 0.1 multiply_reduce_fusion
  8.8 43.5 %all-gather = f32[32,8,4]{1,2,0:T(4,128)S(1)} all-gather(f32[1,8,4]{1,2,0:T(4,128)S(1)} %bitcast.30), channel_id=1, replica_groups=mesh['dp'=2,'expert'=4,'shard'=4] {'dp','expert','shard'}, dimensions={0}, use_global_device_ids=true | all-gather | bytes 4224 | tf_op jit(solution)/shard_map/all_gather | solution.py:22
  52.3 0.1 reshape.35
  52.4 19.6 %all-gather.3.cloned.1.call-done = bf16[256,6144]{1,0:T(8,128)(2,1)} async-done(((bf16[8,6144]{1,0:T(8,128)(2,1)}), bf16[256,6144]{1,0:T(8,128)(2,1)}) %all-gather.3.cloned.1.call-update) | async-done | bytes 3145744 | tf_op jit(solution)/shard_map/all_gather | solution.py:21
  72.0 12.5 %fusion.1 = f32[256,4,2,256]{3,0,2,1:T(8,128)S(1)} fusion(bf16[4,2,256,6144]{3,2,1,0:T(8,128)(2,1)} %param.9, bf16[256,6144]{1,0:T(8,128)(2,1)} %all-gather.3.cloned.1.call-done), kind=kOutput, calls=%fused_computation.2 | convolution fusion | flops 6442450944 | bytes 30408704 | tf_op jit(solution)/shard_map/td,eghd->tegh/dot_general | solution.py:23
  84.5 9.8 %fusion = bf16[256,6144]{1,0:T(8,128)(2,1)} fusion(bf16[4,256,6144]{2,1,0:T(8,128)(2,1)} %param.10, f32[256,4,2,256]{3,0,2,1:T(8,128)S(1)} %fusion.1, f32[256,4]{0,1:T(4,128)S(1)} %reshape.35), kind=kOutput, calls=%fused_computation.1 | convolution fusion | flops 3224633344 | bytes 17829888 | tf_op jit(solution)/shard_map/dot_general | solution.py:28
  94.3 0.0 reduce-scatter.2.cloned.1.call-update
  94.3 100.5 %reduce-scatter.2.cloned.1.call-done = bf16[8,6144]{1,0:T(8,128)(2,1)} async-done(((bf16[256,6144]{1,0:T(8,128)(2,1)}), bf16[8,6144]{1,0:T(8,128)(2,1)}) %reduce-scatter.2.cloned.1.call-update) | async-done | bytes 98320 | tf_op jit(solution)/shard_map/reduce_scatter | solution.py:33
  (1 shorter events, 0.0 us)
Async XLA Ops:
  6.5 65.5 %all-gather.3.cloned.1.call-start = ((), (), s32[]{:S(2)}) async-start(), calls=%async_computation.1 | async-start | bytes 3244032 | tf_op jit(solution)/shard_map/all_gather | solution.py:21
  7.3 187.6 %reduce-scatter.2.cloned.1.call-start = ((), (), s32[]{:S(2)}) async-start(), calls=%async_computation.2 | async-start | bytes 3244032 | tf_op jit(solution)/shard_map/reduce_scatter | solution.py:33
Sparse Core Ops, SparseCore 0:
  10.2 61.7 all-gather.2
  94.4 100.3 reduce-scatter.1

commit v2 on v1

v2 whole, which is shorter than its diff:
```python
import jax
import jax.numpy as jnp
from jax import lax
from jax.sharding import PartitionSpec as P

AXES = ("dp", "expert", "shard")
LANES = 128


def slot_coefficients(expert_ids, gate_values, old_place, new_place):
    matches = (new_place[:, None] == old_place[None, :]).astype(jnp.float32)
    picks = (expert_ids[:, :, None] == jnp.arange(new_place.shape[0], dtype=jnp.int32)).astype(jnp.float32)
    by_expert = jnp.sum(picks * gate_values[:, :, None], axis=1)
    return jnp.sum(by_expert[:, :, None] * matches[None, :, :], axis=1)


def split_exact(value):
    pieces = []
    for _ in range(3):
        piece = lax.reduce_precision(value, exponent_bits=8, mantissa_bits=7)
        pieces.append(piece.astype(jnp.bfloat16))
        value = value - piece
    return pieces


class Line:
    def __init__(self, name, ways, stride, size):
        self.name, self.ways, self.stride, self.size = name, ways, stride, size

    def shift(self, value, step):
        pairs = []
        for index in range(self.ways):
            digit = index // self.stride % self.size
            target = (digit + step) % self.size
            pairs.append((index, index + (target - digit) * self.stride))
        return lax.ppermute(value, self.name, pairs)

    def gather(self, block, dim):
        return jnp.stack([block] + [self.shift(block, s) for s in range(1, self.size)], axis=dim)

    def reduce(self, slots, dim):
        own = lax.index_in_dim(slots, 0, dim, keepdims=False).astype(jnp.float32)
        for s in range(1, self.size):
            sent = lax.index_in_dim(slots, s, dim, keepdims=False)
            own = own + self.shift(sent, self.size - s).astype(jnp.float32)
        return own.astype(jnp.bfloat16)


def local(
    tokens, gate_up_weight, down_weight, expert_ids, slot_ids, gate_values, old_place, new_place
):
    experts, _, sliver, model_width = gate_up_weight.shape
    rows = tokens.shape[0]
    half = model_width // 2
    ways = {name: lax.axis_size(name) for name in AXES}
    cores = 2 if ways["shard"] % 2 == 0 else 1
    x_line = Line("dp", ways["dp"], 1, ways["dp"])
    z_line = Line("expert", ways["expert"], 1, ways["expert"])
    y_line = Line("shard", ways["shard"], cores, ways["shard"] // cores)
    core_line = Line("shard", ways["shard"], 1, cores)

    coefficients = slot_coefficients(expert_ids, gate_values, old_place, new_place)
    extra = jnp.concatenate(split_exact(coefficients), axis=1)
    extra = jnp.pad(extra, ((0, 0), (0, -extra.shape[1] % LANES)))
    parts = [
        jnp.concatenate([tokens[:, :half], extra], axis=1),
        tokens[:, half:],
    ]
    gathered = []
    for number, part in enumerate(parts):
        block = z_line.gather(part, 0)
        if number == 0:
            block = x_line.gather(y_line.gather(block, 0), 0)
        else:
            block = y_line.gather(x_line.gather(block, 0), 1)
        block = core_line.gather(block, 0)
        gathered.append(block.reshape(-1, part.shape[1]))
    weigh = gathered[0][:, half : half + 3 * experts].astype(jnp.float32)
    weigh = weigh.reshape(-1, 3, experts).sum(axis=1)
    flat_in = gate_up_weight.reshape(-1, model_width)
    pre_act = sum(
        lax.dot_general(
            rows_of[:, :half],
            flat_in[:, number * half : (number + 1) * half],
            (((1,), (1,)), ((), ())),
            preferred_element_type=jnp.float32,
        )
        for number, rows_of in enumerate(gathered)
    ).reshape(-1, experts, 2, sliver)
    hidden = jax.nn.silu(pre_act[:, :, 0]) * pre_act[:, :, 1]
    hidden = (hidden * weigh[:, :, None]).astype(jnp.bfloat16).reshape(-1, experts * sliver)
    flat_down = down_weight.reshape(-1, model_width)
    results = []
    for number in range(2):
        block = jnp.dot(
            hidden,
            flat_down[:, number * half : (number + 1) * half],
            preferred_element_type=jnp.float32,
        ).astype(jnp.bfloat16)
        block = block.reshape(
            core_line.size, x_line.size, y_line.size, z_line.size, rows, half
        )
        block = core_line.reduce(block, 0)
        if number == 0:
            block = y_line.reduce(x_line.reduce(block, 0), 0)
        else:
            block = x_line.reduce(y_line.reduce(block, 1), 0)
        results.append(z_line.reduce(block, 0))
    return jnp.concatenate(results, axis=1)


def solution(mesh):
    in_specs = (
        P(AXES, None),
        P(None, None, AXES, None),
        P(None, AXES, None),
        P(AXES, None),
        P(AXES, None),
        P(AXES, None),
        P(),
        P(),
    )
    return jax.shard_map(
        local, mesh=mesh, in_specs=in_specs, out_specs=P(AXES, None), check_vma=False
    )
```

time: 202 us -> 103 us (0.51)
  waiting for transfers between devices: 121 us -> 29.5 us
  blocking collectives: 43.5 us -> 0 us
  starting transfers between devices: 0.04 us -> 34.4 us
  between operations: 13.4 us -> 0.33 us
  local copies, waits for them, and re-layouts: 0.11 us -> 12.3 us
  other arithmetic: 1.54 us -> 4.04 us
    reduce_scatter x1 -> x0, waiting for transfers between devices: 101 us -> none  [local(): return lax.psum_scatter(partial, AXES, scatter_dimension=0, tiled=True)]
    all_gather x1 -> x0, blocking collectives: 43.5 us -> none  [local(): all_coefficients = lax.all_gather(coefficients, AXES, axis=0, tiled=True)]
    ppermute x0 -> x24, starting transfers between devices: none -> 34.4 us  [shift(): return lax.ppermute(value, self.name, pairs)]
    ppermute x0 -> x24, waiting for transfers between devices: none -> 29.5 us  [shift(): return lax.ppermute(value, self.name, pairs)]
    all_gather x1 -> x0, waiting for transfers between devices: 19.6 us -> none  [local(): all_tokens = lax.all_gather(tokens, AXES, axis=0, tiled=True)]
    slice x0 -> x4, local copies, waits for them, and re-layouts: none -> 6.52 us  [the longest x1 6.31 us: local(): hidden = jax.nn.silu(pre_act[:, :, 0]) * pre_act[:, :, 1]]
    reshape x0 -> x2, local copies, waits for them, and re-layouts: none -> 3.05 us  [the longest x1 3.03 us: local(): pre_act = sum((lax.dot_general(rows_of[:, :half], flat_in[:, number * hal...]
    dot_general x2 -> x4, matrix products: 22.3 us -> 22.6 us  [the longest x2 15.9 us: local(): lax.dot_general(rows_of[:, :half], flat_in[:, number * half:(number + 1)...]
  transfers between devices with their start and end apart: 2 -> 24, of which waited for: 2 -> 14; matrix products, arithmetic and copies ran while one was open for 1% -> 5% of each run, Pallas kernels for 0% -> 0%
where the time goes in v2:
time: 103 us
  starting transfers between devices  34.4 us (33%)
  waiting for transfers between devices  29.5 us (29%)
  matrix products  22.6 us (22%)
  local copies, waits for them, and re-layouts  12.3 us (12%)
  other arithmetic  4.04 us (4%)
    ppermute x24, starting transfers between devices, shift(): return lax.ppermute(value, self.name, pairs)  34.4 us
    ppermute x24, waiting for transfers between devices, shift(): return lax.ppermute(value, self.name, pairs)  29.5 us
    dot_general x2, matrix products, local(): lax.dot_general(rows_of[:, :half], flat_in[:, number * half:(number + 1)...  15.9 us
    dot_general x2, matrix products, local(): jnp.dot(hidden, flat_down[:, number * half:(number + 1) * half], preferre...  6.71 us
    slice x1, local copies, waits for them, and re-layouts, local(): hidden = jax.nn.silu(pre_act[:, :, 0]) * pre_act[:, :, 1]  6.31 us
    reshape x1, local copies, waits for them, and re-layouts, local(): pre_act = sum((lax.dot_general(rows_of[:, :half], flat_in[:, number * hal...  3.03 us
  transfers between devices with their start and end apart: 24, of which 14 were waited for; matrix products, arithmetic and copies ran while one was open for 5% of the time, Pallas kernels for 0%

profile of v2, /device:TPU:0, one launch (start us, length us, event | category | flops | bytes accessed | tf_op | source)
XLA Modules:
  0.0 103.1 jit_solution(12369176708388328096)
XLA Ops:
  0.0 0.8 slice_bitcast_fusion.16
  0.8 4.1 %collective-permute-start.7 = (bf16[8,3072]{1,0:T(8,128)(2,1)S(1)}, bf16[8,3072]{1,0:T(8,128)(2,1)S(1)}, u32[]{:S(2)}, u32[]{:S(2)}) collective-permute-start(bf16[8,3072]{1,0:T(8,128)(2,1)S(1)} %get-tuple-element.30), channel_id=1, source_target_pairs={{0,8},{4,12},{8,0},{12,4},{1,9},{5,13},{9,1},{13,5},{2,10},{6,14},... | collective-permute-start | bytes 147464 | tf_op jit(solution)/shard_map/ppermute | solution.py:36
  4.9 1.6 %collective-permute-start.6 = (bf16[8,3072]{1,0:T(8,128)(2,1)S(1)}, bf16[8,3072]{1,0:T(8,128)(2,1)S(1)}, u32[]{:S(2)}, u32[]{:S(2)}) collective-permute-start(bf16[8,3072]{1,0:T(8,128)(2,1)S(1)} %get-tuple-element.30), channel_id=1, source_target_pairs={{0,4},{4,8},{8,12},{12,0},{1,5},{5,9},{9,13},{13,1},{2,6},{6,10},{... | collective-permute-start | bytes 147464 | tf_op jit(solution)/shard_map/ppermute | solution.py:36
  6.5 2.2 %collective-permute-start.8 = (bf16[8,3072]{1,0:T(8,128)(2,1)S(1)}, bf16[8,3072]{1,0:T(8,128)(2,1)S(1)}, u32[]{:S(2)}, u32[]{:S(2)}) collective-permute-start(bf16[8,3072]{1,0:T(8,128)(2,1)S(1)} %get-tuple-element.30), channel_id=1, source_target_pairs={{0,12},{4,0},{8,4},{12,8},{1,13},{5,1},{9,5},{13,9},{2,14},{6,2},{... | collective-permute-start | bytes 147464 | tf_op jit(solution)/shard_map/ppermute | solution.py:36
  8.8 0.7 select_reduce_fusion
  9.5 0.7 compare_convert_fusion
  10.5 0.6 collective-permute-start
  11.1 3.3 %collective-permute-start.2 = (bf16[8,3200]{1,0:T(8,128)(2,1)S(1)}, bf16[8,3200]{1,0:T(8,128)(2,1)S(1)}, u32[]{:S(2)}, u32[]{:S(2)}) collective-permute-start(bf16[8,3200]{1,0:T(8,128)(2,1)S(1)} %get-tuple-element.33), channel_id=1, source_target_pairs={{0,12},{4,0},{8,4},{12,8},{1,13},{5,1},{9,5},{13,9},{2,14},{6,2},{... | collective-permute-start | bytes 153608 | tf_op jit(solution)/shard_map/ppermute | solution.py:36
  14.4 1.6 %collective-permute-start.9 = (bf16[4,8,3072]{2,1,0:T(8,128)(2,1)S(1)}, bf16[4,8,3072]{2,1,0:T(8,128)(2,1)S(1)}, u32[]{:S(2)}, u32[]{:S(2)}) collective-permute-start(bf16[4,8,3072]{2,1,0:T(8,128)(2,1)S(1)} %get-tuple-element.28), channel_id=1, source_target_pairs={{0,16},{16,0},{1,17},{17,1},{2,18},{18,2},{3,19},{19,3},{4,20},{20... | collective-permute-start | bytes 589832 | tf_op jit(solution)/shard_map/ppermute | solution.py:36
  16.0 0.7 collective-permute-done.1
  16.7 0.2 collective-permute-done.2
  17.0 1.6 %collective-permute-start.3 = (bf16[4,8,3200]{2,1,0:T(8,128)(2,1)S(1)}, bf16[4,8,3200]{2,1,0:T(8,128)(2,1)S(1)}, u32[]{:S(2)}, u32[]{:S(2)}) collective-permute-start(bf16[4,8,3200]{2,1,0:T(8,128)(2,1)S(1)} %get-tuple-element.20), channel_id=1, source_target_pairs={{0,2},{1,3},{2,0},{3,1},{4,6},{5,7},{6,4},{7,5},{8,10},{9,11},{10,... | collective-permute-start | bytes 614408 | tf_op jit(solution)/shard_map/ppermute | solution.py:36
  18.6 1.6 %collective-permute-done.9 = bf16[4,8,3072]{2,1,0:T(8,128)(2,1)S(1)} collective-permute-done((bf16[4,8,3072]{2,1,0:T(8,128)(2,1)S(1)}, bf16[4,8,3072]{2,1,0:T(8,128)(2,1)S(1)}, u32[]{:S(2)}, u32[]{:S(2)}) %collective-permute-start.9) | collective-permute-done | bytes 196640 | tf_op jit(solution)/shard_map/ppermute | solution.py:36
  20.2 1.6 %collective-permute-start.10 = (bf16[2,4,8,3072]{3,2,1,0:T(8,128)(2,1)S(1)}, bf16[2,4,8,3072]{3,2,1,0:T(8,128)(2,1)S(1)}, u32[]{:S(2)}, u32[]{:S(2)}) collective-permute-start(bf16[2,4,8,3072]{3,2,1,0:T(8,128)(2,1)S(1)} %get-tuple-element.18), channel_id=1, source_target_pairs={{0,2},{1,3},{2,0},{3,1},{4,6},{5,7},{6,4},{7,5},{8,10},{9,11},{10,... | collective-permute-start | bytes 1179656 | tf_op jit(solution)/shard_map/ppermute | solution.py:36
  21.8 3.1 %collective-permute-done.3 = bf16[4,8,3200]{2,1,0:T(8,128)(2,1)S(1)} collective-permute-done((bf16[4,8,3200]{2,1,0:T(8,128)(2,1)S(1)}, bf16[4,8,3200]{2,1,0:T(8,128)(2,1)S(1)}, u32[]{:S(2)}, u32[]{:S(2)}) %collective-permute-start.3) | collective-permute-done | bytes 204832 | tf_op jit(solution)/shard_map/ppermute | solution.py:36
  25.0 1.6 %collective-permute-start.4 = (bf16[2,4,8,3200]{3,2,1,0:T(8,128)(2,1)S(1)}, bf16[2,4,8,3200]{3,2,1,0:T(8,128)(2,1)S(1)}, u32[]{:S(2)}, u32[]{:S(2)}) collective-permute-start(bf16[2,4,8,3200]{3,2,1,0:T(8,128)(2,1)S(1)} %get-tuple-element.16), channel_id=1, source_target_pairs={{0,16},{16,0},{1,17},{17,1},{2,18},{18,2},{3,19},{19,3},{4,20},{20... | collective-permute-start | bytes 1228808 | tf_op jit(solution)/shard_map/ppermute | solution.py:36
  26.6 4.2 %collective-permute-done.10 = bf16[2,4,8,3072]{3,2,1,0:T(8,128)(2,1)S(1)} collective-permute-done((bf16[2,4,8,3072]{3,2,1,0:T(8,128)(2,1)S(1)}, bf16[2,4,8,3072]{3,2,1,0:T(8,128)(2,1)S(1)}, u32[]{:S(2)}, u32[]{:S(2)}) %collective-permute-start.10) | collective-permute-done | bytes 393248 | tf_op jit(solution)/shard_map/ppermute | solution.py:36
  31.0 2.1 %collective-permute-done.4 = bf16[2,4,8,3200]{3,2,1,0:T(8,128)(2,1)S(1)} collective-permute-done((bf16[2,4,8,3200]{3,2,1,0:T(8,128)(2,1)S(1)}, bf16[2,4,8,3200]{3,2,1,0:T(8,128)(2,1)S(1)}, u32[]{:S(2)}, u32[]{:S(2)}) %collective-permute-start.4) | collective-permute-done | bytes 409632 | tf_op jit(solution)/shard_map/ppermute | solution.py:36
  33.4 2.1 %collective-permute-done.5 = bf16[2,2,4,8,3200]{4,3,2,1,0:T(8,128)(2,1)S(1)} collective-permute-done((bf16[2,2,4,8,3200]{4,3,2,1,0:T(8,128)(2,1)S(1)}, bf16[2,2,4,8,3200]{4,3,2,1,0:T(8,128)(2,1)S(1)}, u32[]{:S(2)}, u32[]{:S(2)}) %collective-permute-start.5) | collective-permute-done | bytes 819232 | tf_op jit(solution)/shard_map/ppermute | solution.py:36
  36.0 6.5 %fusion.2 = f32[256,2048]{1,0:T(8,128)S(1)} fusion(bf16[2048,6144]{1,0:T(8,128)(2,1)} %bitcast.126, bf16[256,3200]{1,0:T(8,128)(2,1)S(1)} %bitcast.111), kind=kOutput, calls=%fused_computation.2 | convolution fusion | flops 3221225472 | bytes 16252928 | tf_op jit(solution)/shard_map/dot_general | solution.py:82
  42.5 9.4 %fusion.14 = f32[256,2048]{1,0:T(8,128)} fusion(f32[256,2048]{1,0:T(8,128)S(1)} %fusion.2, bf16[256,3072]{1,0:T(8,128)(2,1)S(1)} %bitcast.112, bf16[2048,6144]{1,0:T(8,128)(2,1)} %bitcast.127), kind=kOutput, calls=%fused_computation.10 | convolution fusion | flops 3221749760 | bytes 18350080 | tf_op jit(solution)/shard_map/dot_general | solution.py:82
  51.9 3.0 %reshape.86 = f32[256,4,2,256]{3,2,1,0:T(2,128)S(1)} reshape(f32[256,2048]{1,0:T(8,128)} %fusion.14) | data formatting | bytes 4194304 | tf_op jit(solution)/shard_map/reshape | solution.py:89
  54.9 6.3 %slice_reduce_fusion.1 = (f32[256,4,256]{2,1,0:T(4,128)S(1)}, f32[256,4,256]{2,1,0:T(4,128)S(1)}) fusion(f32[256,4,2,256]{3,2,1,0:T(2,128)S(1)} %reshape.86), kind=kLoop, calls=%fused_computation.19 | loop fusion | bytes 4194304 | tf_op jit(solution)/shard_map/slice | solution.py:90
  61.2 0.2 copy.33
  61.4 0.2 copy.34
  61.7 0.3 mul.48
  62.0 0.2 copy.35
  62.2 0.4 multiply_convert_fusion
  62.6 4.9 %fusion.11 = bf16[256,3072]{1,0:T(8,128)(2,1)S(1)} fusion(bf16[256,1024]{1,0:T(8,128)(2,1)S(1)} %multiply_convert_fusion, bf16[1024,6144]{1,0:T(8,128)(2,1)} %bitcast.128), kind=kOutput, calls=%fused_computation.9 | convolution fusion | flops 1611399168 | bytes 8388608 | tf_op jit(solution)/shard_map/dot_general | solution.py:95
  67.9 0.5 slice-done.2
  68.4 1.8 %fusion.8 = bf16[256,3072]{1,0:T(8,128)(2,1)S(1)} fusion(bf16[256,1024]{1,0:T(8,128)(2,1)S(1)} %multiply_convert_fusion, bf16[1024,6144]{1,0:T(8,128)(2,1)S(1)} %bitcast.131), kind=kOutput, calls=%fused_computation.8 | convolution fusion | flops 1611399168 | bytes 8388608 | tf_op jit(solution)/shard_map/dot_general | solution.py:95
  70.7 1.6 %collective-permute-start.19 = (bf16[2,4,8,3072]{3,2,1,0:T(8,128)(2,1)S(1)}, bf16[2,4,8,3072]{3,2,1,0:T(8,128)(2,1)S(1)}, u32[]{:S(2)}, u32[]{:S(2)}) collective-permute-start(bf16[2,4,8,3072]{3,2,1,0:T(8,128)(2,1)S(1)} %slice_bitcast_fusion), channel_id=1, source_target_pairs={{0,2},{1,3},{2,0},{3,1},{4,6},{5,7},{6,4},{7,5},{8,10},{9,11},{10,... | collective-permute-start | bytes 1179656 | tf_op jit(solution)/shard_map/ppermute | solution.py:36
  72.3 0.3 collective-permute-done.12
  72.6 0.2 fusion.18
  72.9 1.5 %collective-permute-start.13 = (bf16[2,4,8,3072]{3,2,1,0:T(8,128)(2,1)S(1)}, bf16[2,4,8,3072]{3,2,1,0:T(8,128)(2,1)S(1)}, u32[]{:S(2)}, u32[]{:S(2)}) collective-permute-start(bf16[2,4,8,3072]{3,2,1,0:T(8,128)(2,1)S(1)} %slice_bitcast_fusion.2), channel_id=1, source_target_pairs={{0,16},{16,0},{1,17},{17,1},{2,18},{18,2},{3,19},{19,3},{4,20},{20... | collective-permute-start | bytes 1179656 | tf_op jit(solution)/shard_map/ppermute | solution.py:36
  74.4 7.8 %collective-permute-done.19 = bf16[2,4,8,3072]{3,2,1,0:T(8,128)(2,1)S(1)} collective-permute-done((bf16[2,4,8,3072]{3,2,1,0:T(8,128)(2,1)S(1)}, bf16[2,4,8,3072]{3,2,1,0:T(8,128)(2,1)S(1)}, u32[]{:S(2)}, u32[]{:S(2)}) %collective-permute-start.19) | collective-permute-done | bytes 393248 | tf_op jit(solution)/shard_map/ppermute | solution.py:36
  82.3 1.5 %collective-permute-start.20 = (bf16[4,8,3072]{2,1,0:T(8,128)(2,1)S(1)}, bf16[4,8,3072]{2,1,0:T(8,128)(2,1)S(1)}, u32[]{:S(2)}, u32[]{:S(2)}) collective-permute-start(bf16[4,8,3072]{2,1,0:T(8,128)(2,1)S(1)} %slice_bitcast_fusion.4), channel_id=1, source_target_pairs={{0,16},{16,0},{1,17},{17,1},{2,18},{18,2},{3,19},{19,3},{4,20},{20... | collective-permute-start | bytes 589832 | tf_op jit(solution)/shard_map/ppermute | solution.py:36
  83.8 0.2 collective-permute-done.13
  84.2 1.6 %collective-permute-start.14 = (bf16[4,8,3072]{2,1,0:T(8,128)(2,1)S(1)}, bf16[4,8,3072]{2,1,0:T(8,128)(2,1)S(1)}, u32[]{:S(2)}, u32[]{:S(2)}) collective-permute-start(bf16[4,8,3072]{2,1,0:T(8,128)(2,1)S(1)} %slice_bitcast_fusion.6), channel_id=1, source_target_pairs={{0,2},{1,3},{2,0},{3,1},{4,6},{5,7},{6,4},{7,5},{8,10},{9,11},{10,... | collective-permute-start | bytes 589832 | tf_op jit(solution)/shard_map/ppermute | solution.py:36
  85.8 2.9 %collective-permute-done.20 = bf16[4,8,3072]{2,1,0:T(8,128)(2,1)S(1)} collective-permute-done((bf16[4,8,3072]{2,1,0:T(8,128)(2,1)S(1)}, bf16[4,8,3072]{2,1,0:T(8,128)(2,1)S(1)}, u32[]{:S(2)}, u32[]{:S(2)}) %collective-permute-start.20) | collective-permute-done | bytes 196640 | tf_op jit(solution)/shard_map/ppermute | solution.py:36
  88.8 3.5 %collective-permute-start.21 = (bf16[8,3072]{1,0:T(8,128)(2,1)S(1)}, bf16[8,3072]{1,0:T(8,128)(2,1)S(1)}, u32[]{:S(2)}, u32[]{:S(2)}) collective-permute-start(bf16[8,3072]{1,0:T(8,128)(2,1)S(1)} %get-tuple-element.24), channel_id=1, source_target_pairs={{0,12},{4,0},{8,4},{12,8},{1,13},{5,1},{9,5},{13,9},{2,14},{6,2},{... | collective-permute-start | bytes 147464 | tf_op jit(solution)/shard_map/ppermute | solution.py:36
  92.3 0.6 collective-permute-start.22
  93.0 3.2 %collective-permute-start.15 = (bf16[8,3072]{1,0:T(8,128)(2,1)S(1)}, bf16[8,3072]{1,0:T(8,128)(2,1)S(1)}, u32[]{:S(2)}, u32[]{:S(2)}) collective-permute-start(bf16[8,3072]{1,0:T(8,128)(2,1)S(1)} %get-tuple-element.21), channel_id=1, source_target_pairs={{0,12},{4,0},{8,4},{12,8},{1,13},{5,1},{9,5},{13,9},{2,14},{6,2},{... | collective-permute-start | bytes 147464 | tf_op jit(solution)/shard_map/ppermute | solution.py:36
  96.2 0.6 collective-permute-start.17
  96.9 1.4 %collective-permute-start.16 = (bf16[8,3072]{1,0:T(8,128)(2,1)S(1)}, bf16[8,3072]{1,0:T(8,128)(2,1)S(1)}, u32[]{:S(2)}, u32[]{:S(2)}) collective-permute-start(bf16[8,3072]{1,0:T(8,128)(2,1)S(1)} %get-tuple-element.23), channel_id=1, source_target_pairs={{0,8},{4,12},{8,0},{12,4},{1,9},{5,13},{9,1},{13,5},{2,10},{6,14},... | collective-permute-start | bytes 147464 | tf_op jit(solution)/shard_map/ppermute | solution.py:36
  98.3 1.3 %collective-permute-done.15 = bf16[8,3072]{1,0:T(8,128)(2,1)S(1)} collective-permute-done((bf16[8,3072]{1,0:T(8,128)(2,1)S(1)}, bf16[8,3072]{1,0:T(8,128)(2,1)S(1)}, u32[]{:S(2)}, u32[]{:S(2)}) %collective-permute-start.15) | collective-permute-done | bytes 49184 | tf_op jit(solution)/shard_map/ppermute | solution.py:36
  99.6 2.6 %collective-permute-done.17 = bf16[8,3072]{1,0:T(8,128)(2,1)S(1)} collective-permute-done((bf16[8,3072]{1,0:T(8,128)(2,1)S(1)}, bf16[8,3072]{1,0:T(8,128)(2,1)S(1)}, u32[]{:S(2)}, u32[]{:S(2)}) %collective-permute-start.17) | collective-permute-done | bytes 49184 | tf_op jit(solution)/shard_map/ppermute | solution.py:36
  102.4 0.6 pad_maximum_fusion.8
  (57 shorter events, 2.9 us)
Async XLA Ops:
  0.8 10.2 %collective-permute-start.7 = (bf16[8,3072]{1,0:T(8,128)(2,1)S(1)}, bf16[8,3072]{1,0:T(8,128)(2,1)S(1)}, u32[]{:S(2)}, u32[]{:S(2)}) collective-permute-start(bf16[8,3072]{1,0:T(8,128)(2,1)S(1)} %get-tuple-element.30), channel_id=1, source_target_pairs={{0,8},{4,12},{8,0},{12,4},{1,9},{5,13},{9,1},{13,5},{2,10},{6,14},... | collective-permute-start | bytes 147464 | tf_op jit(solution)/shard_map/ppermute | solution.py:36
  4.9 9.5 %collective-permute-start.6 = (bf16[8,3072]{1,0:T(8,128)(2,1)S(1)}, bf16[8,3072]{1,0:T(8,128)(2,1)S(1)}, u32[]{:S(2)}, u32[]{:S(2)}) collective-permute-start(bf16[8,3072]{1,0:T(8,128)(2,1)S(1)} %get-tuple-element.30), channel_id=1, source_target_pairs={{0,4},{4,8},{8,12},{12,0},{1,5},{5,9},{9,13},{13,1},{2,6},{6,10},{... | collective-permute-start | bytes 147464 | tf_op jit(solution)/shard_map/ppermute | solution.py:36
  6.5 7.9 %collective-permute-start.8 = (bf16[8,3072]{1,0:T(8,128)(2,1)S(1)}, bf16[8,3072]{1,0:T(8,128)(2,1)S(1)}, u32[]{:S(2)}, u32[]{:S(2)}) collective-permute-start(bf16[8,3072]{1,0:T(8,128)(2,1)S(1)} %get-tuple-element.30), channel_id=1, source_target_pairs={{0,12},{4,0},{8,4},{12,8},{1,13},{5,1},{9,5},{13,9},{2,14},{6,2},{... | collective-permute-start | bytes 147464 | tf_op jit(solution)/shard_map/ppermute | solution.py:36
  10.4 6.3 %collective-permute-start.1 = (bf16[8,3200]{1,0:T(8,128)(2,1)S(1)}, bf16[8,3200]{1,0:T(8,128)(2,1)S(1)}, u32[]{:S(2)}, u32[]{:S(2)}) collective-permute-start(bf16[8,3200]{1,0:T(8,128)(2,1)S(1)} %get-tuple-element.33), channel_id=1, source_target_pairs={{0,8},{4,12},{8,0},{12,4},{1,9},{5,13},{9,1},{13,5},{2,10},{6,14},... | collective-permute-start | bytes 153608 | tf_op jit(solution)/shard_map/ppermute | solution.py:36
  10.5 6.2 %collective-permute-start = (bf16[8,3200]{1,0:T(8,128)(2,1)S(1)}, bf16[8,3200]{1,0:T(8,128)(2,1)S(1)}, u32[]{:S(2)}, u32[]{:S(2)}) collective-permute-start(bf16[8,3200]{1,0:T(8,128)(2,1)S(1)} %get-tuple-element.33), channel_id=1, source_target_pairs={{0,4},{4,8},{8,12},{12,0},{1,5},{5,9},{9,13},{13,1},{2,6},{6,10},{... | collective-permute-start | bytes 153608 | tf_op jit(solution)/shard_map/ppermute | solution.py:36
  11.1 5.9 %collective-permute-start.2 = (bf16[8,3200]{1,0:T(8,128)(2,1)S(1)}, bf16[8,3200]{1,0:T(8,128)(2,1)S(1)}, u32[]{:S(2)}, u32[]{:S(2)}) collective-permute-start(bf16[8,3200]{1,0:T(8,128)(2,1)S(1)} %get-tuple-element.33), channel_id=1, source_target_pairs={{0,12},{4,0},{8,4},{12,8},{1,13},{5,1},{9,5},{13,9},{2,14},{6,2},{... | collective-permute-start | bytes 153608 | tf_op jit(solution)/shard_map/ppermute | solution.py:36
  14.4 5.7 %collective-permute-start.9 = (bf16[4,8,3072]{2,1,0:T(8,128)(2,1)S(1)}, bf16[4,8,3072]{2,1,0:T(8,128)(2,1)S(1)}, u32[]{:S(2)}, u32[]{:S(2)}) collective-permute-start(bf16[4,8,3072]{2,1,0:T(8,128)(2,1)S(1)} %get-tuple-element.28), channel_id=1, source_target_pairs={{0,16},{16,0},{1,17},{17,1},{2,18},{18,2},{3,19},{19,3},{4,20},{20... | collective-permute-start | bytes 589832 | tf_op jit(solution)/shard_map/ppermute | solution.py:36
  17.0 7.9 %collective-permute-start.3 = (bf16[4,8,3200]{2,1,0:T(8,128)(2,1)S(1)}, bf16[4,8,3200]{2,1,0:T(8,128)(2,1)S(1)}, u32[]{:S(2)}, u32[]{:S(2)}) collective-permute-start(bf16[4,8,3200]{2,1,0:T(8,128)(2,1)S(1)} %get-tuple-element.20), channel_id=1, source_target_pairs={{0,2},{1,3},{2,0},{3,1},{4,6},{5,7},{6,4},{7,5},{8,10},{9,11},{10,... | collective-permute-start | bytes 614408 | tf_op jit(solution)/shard_map/ppermute | solution.py:36
  20.2 10.6 %collective-permute-start.10 = (bf16[2,4,8,3072]{3,2,1,0:T(8,128)(2,1)S(1)}, bf16[2,4,8,3072]{3,2,1,0:T(8,128)(2,1)S(1)}, u32[]{:S(2)}, u32[]{:S(2)}) collective-permute-start(bf16[2,4,8,3072]{3,2,1,0:T(8,128)(2,1)S(1)} %get-tuple-element.18), channel_id=1, source_target_pairs={{0,2},{1,3},{2,0},{3,1},{4,6},{5,7},{6,4},{7,5},{8,10},{9,11},{10,... | collective-permute-start | bytes 1179656 | tf_op jit(solution)/shard_map/ppermute | solution.py:36
  25.0 8.0 %collective-permute-start.4 = (bf16[2,4,8,3200]{3,2,1,0:T(8,128)(2,1)S(1)}, bf16[2,4,8,3200]{3,2,1,0:T(8,128)(2,1)S(1)}, u32[]{:S(2)}, u32[]{:S(2)}) collective-permute-start(bf16[2,4,8,3200]{3,2,1,0:T(8,128)(2,1)S(1)} %get-tuple-element.16), channel_id=1, source_target_pairs={{0,16},{16,0},{1,17},{17,1},{2,18},{18,2},{3,19},{19,3},{4,20},{20... | collective-permute-start | bytes 1228808 | tf_op jit(solution)/shard_map/ppermute | solution.py:36
  30.9 2.4 %collective-permute-start.11 = (bf16[2,2,4,8,3072]{4,3,2,1,0:T(8,128)(2,1)S(1)}, bf16[2,2,4,8,3072]{4,3,2,1,0:T(8,128)(2,1)S(1)}, u32[]{:S(2)}, u32[]{:S(2)}) collective-permute-start(bf16[2,2,4,8,3072]{4,3,2,1,0:T(8,128)(2,1)S(1)} %get-tuple-element.14), channel_id=1, source_target_pairs={{0,1},{1,0},{2,3},{3,2},{4,5},{5,4},{6,7},{7,6},{8,9},{9,8},{10,11... | collective-permute-start | bytes 2359304 | tf_op jit(solution)/shard_map/ppermute | solution.py:36
  33.1 2.4 %collective-permute-start.5 = (bf16[2,2,4,8,3200]{4,3,2,1,0:T(8,128)(2,1)S(1)}, bf16[2,2,4,8,3200]{4,3,2,1,0:T(8,128)(2,1)S(1)}, u32[]{:S(2)}, u32[]{:S(2)}) collective-permute-start(bf16[2,2,4,8,3200]{4,3,2,1,0:T(8,128)(2,1)S(1)} %get-tuple-element.12), channel_id=1, source_target_pairs={{0,1},{1,0},{2,3},{3,2},{4,5},{5,4},{6,7},{7,6},{8,9},{9,8},{10,11... | collective-permute-start | bytes 2457608 | tf_op jit(solution)/shard_map/ppermute | solution.py:36
  61.6 6.3 %slice-start = ((s8[12582912]{0:T(1024)(128)(4,1)}), s8[4194304]{0:T(1024)(128)(4,1)S(1)}, s32[]{:S(2)}) async-start(s8[12582912]{0:T(1024)(128)(4,1)} %bitcast.129), calls=%async_computation | async-start | bytes 8388608
  62.6 5.3 %slice-start.1 = ((s8[12582912]{0:T(1024)(128)(4,1)}), s8[4194304]{0:T(1024)(128)(4,1)S(1)}, s32[]{:S(2)}) async-start(s8[12582912]{0:T(1024)(128)(4,1)} %bitcast.129), calls=%async_computation.1 | async-start | bytes 8388608
  62.6 5.8 %slice-start.2 = ((s8[12582912]{0:T(1024)(128)(4,1)}), s8[4194304]{0:T(1024)(128)(4,1)S(1)}, s32[]{:S(2)}) async-start(s8[12582912]{0:T(1024)(128)(4,1)} %bitcast.129), calls=%async_computation.2 | async-start | bytes 8388608
  67.7 2.8 %collective-permute-start.18 = (bf16[2,2,4,8,3072]{4,3,2,0,1:T(8,128)(2,1)S(1)}, bf16[2,2,4,8,3072]{4,3,2,0,1:T(8,128)(2,1)S(1)}, u32[]{:S(2)}, u32[]{:S(2)}) collective-permute-start(bf16[2,2,4,8,3072]{4,3,2,0,1:T(8,128)(2,1)S(1)} %copy.29), channel_id=1, source_target_pairs={{0,1},{1,0},{2,3},{3,2},{4,5},{5,4},{6,7},{7,6},{8,9},{9,8},{10,11... | collective-permute-start | bytes 2359304 | tf_op jit(solution)/shard_map/ppermute | solution.py:36
  70.3 2.4 %collective-permute-start.12 = (bf16[2,2,4,8,3072]{4,3,2,1,0:T(8,128)(2,1)S(1)}, bf16[2,2,4,8,3072]{4,3,2,1,0:T(8,128)(2,1)S(1)}, u32[]{:S(2)}, u32[]{:S(2)}) collective-permute-start(bf16[2,2,4,8,3072]{4,3,2,1,0:T(8,128)(2,1)S(1)} %bitcast.115), channel_id=1, source_target_pairs={{0,1},{1,0},{2,3},{3,2},{4,5},{5,4},{6,7},{7,6},{8,9},{9,8},{10,11... | collective-permute-start | bytes 2359304 | tf_op jit(solution)/shard_map/ppermute | solution.py:36
  70.7 11.5 %collective-permute-start.19 = (bf16[2,4,8,3072]{3,2,1,0:T(8,128)(2,1)S(1)}, bf16[2,4,8,3072]{3,2,1,0:T(8,128)(2,1)S(1)}, u32[]{:S(2)}, u32[]{:S(2)}) collective-permute-start(bf16[2,4,8,3072]{3,2,1,0:T(8,128)(2,1)S(1)} %slice_bitcast_fusion), channel_id=1, source_target_pairs={{0,2},{1,3},{2,0},{3,1},{4,6},{5,7},{6,4},{7,5},{8,10},{9,11},{10,... | collective-permute-start | bytes 1179656 | tf_op jit(solution)/shard_map/ppermute | solution.py:36
  72.9 11.2 %collective-permute-start.13 = (bf16[2,4,8,3072]{3,2,1,0:T(8,128)(2,1)S(1)}, bf16[2,4,8,3072]{3,2,1,0:T(8,128)(2,1)S(1)}, u32[]{:S(2)}, u32[]{:S(2)}) collective-permute-start(bf16[2,4,8,3072]{3,2,1,0:T(8,128)(2,1)S(1)} %slice_bitcast_fusion.2), channel_id=1, source_target_pairs={{0,16},{16,0},{1,17},{17,1},{2,18},{18,2},{3,19},{19,3},{4,20},{20... | collective-permute-start | bytes 1179656 | tf_op jit(solution)/shard_map/ppermute | solution.py:36
  82.3 6.4 %collective-permute-start.20 = (bf16[4,8,3072]{2,1,0:T(8,128)(2,1)S(1)}, bf16[4,8,3072]{2,1,0:T(8,128)(2,1)S(1)}, u32[]{:S(2)}, u32[]{:S(2)}) collective-permute-start(bf16[4,8,3072]{2,1,0:T(8,128)(2,1)S(1)} %slice_bitcast_fusion.4), channel_id=1, source_target_pairs={{0,16},{16,0},{1,17},{17,1},{2,18},{18,2},{3,19},{19,3},{4,20},{20... | collective-permute-start | bytes 589832 | tf_op jit(solution)/shard_map/ppermute | solution.py:36
  84.2 8.7 %collective-permute-start.14 = (bf16[4,8,3072]{2,1,0:T(8,128)(2,1)S(1)}, bf16[4,8,3072]{2,1,0:T(8,128)(2,1)S(1)}, u32[]{:S(2)}, u32[]{:S(2)}) collective-permute-start(bf16[4,8,3072]{2,1,0:T(8,128)(2,1)S(1)} %slice_bitcast_fusion.6), channel_id=1, source_target_pairs={{0,2},{1,3},{2,0},{3,1},{4,6},{5,7},{6,4},{7,5},{8,10},{9,11},{10,... | collective-permute-start | bytes 589832 | tf_op jit(solution)/shard_map/ppermute | solution.py:36
  88.8 8.1 %collective-permute-start.21 = (bf16[8,3072]{1,0:T(8,128)(2,1)S(1)}, bf16[8,3072]{1,0:T(8,128)(2,1)S(1)}, u32[]{:S(2)}, u32[]{:S(2)}) collective-permute-start(bf16[8,3072]{1,0:T(8,128)(2,1)S(1)} %get-tuple-element.24), channel_id=1, source_target_pairs={{0,12},{4,0},{8,4},{12,8},{1,13},{5,1},{9,5},{13,9},{2,14},{6,2},{... | collective-permute-start | bytes 147464 | tf_op jit(solution)/shard_map/ppermute | solution.py:36
  92.3 6.0 %collective-permute-start.23 = (bf16[8,3072]{1,0:T(8,128)(2,1)S(1)}, bf16[8,3072]{1,0:T(8,128)(2,1)S(1)}, u32[]{:S(2)}, u32[]{:S(2)}) collective-permute-start(bf16[8,3072]{1,0:T(8,128)(2,1)S(1)} %get-tuple-element.25), channel_id=1, source_target_pairs={{0,4},{4,8},{8,12},{12,0},{1,5},{5,9},{9,13},{13,1},{2,6},{6,10},{... | collective-permute-start | bytes 147464 | tf_op jit(solution)/shard_map/ppermute | solution.py:36
  92.3 6.0 %collective-permute-start.22 = (bf16[8,3072]{1,0:T(8,128)(2,1)S(1)}, bf16[8,3072]{1,0:T(8,128)(2,1)S(1)}, u32[]{:S(2)}, u32[]{:S(2)}) collective-permute-start(bf16[8,3072]{1,0:T(8,128)(2,1)S(1)} %get-tuple-element.26), channel_id=1, source_target_pairs={{0,8},{4,12},{8,0},{12,4},{1,9},{5,13},{9,1},{13,5},{2,10},{6,14},... | collective-permute-start | bytes 147464 | tf_op jit(solution)/shard_map/ppermute | solution.py:36
  93.0 6.6 %collective-permute-start.15 = (bf16[8,3072]{1,0:T(8,128)(2,1)S(1)}, bf16[8,3072]{1,0:T(8,128)(2,1)S(1)}, u32[]{:S(2)}, u32[]{:S(2)}) collective-permute-start(bf16[8,3072]{1,0:T(8,128)(2,1)S(1)} %get-tuple-element.21), channel_id=1, source_target_pairs={{0,12},{4,0},{8,4},{12,8},{1,13},{5,1},{9,5},{13,9},{2,14},{6,2},{... | collective-permute-start | bytes 147464 | tf_op jit(solution)/shard_map/ppermute | solution.py:36
  96.2 6.0 %collective-permute-start.17 = (bf16[8,3072]{1,0:T(8,128)(2,1)S(1)}, bf16[8,3072]{1,0:T(8,128)(2,1)S(1)}, u32[]{:S(2)}, u32[]{:S(2)}) collective-permute-start(bf16[8,3072]{1,0:T(8,128)(2,1)S(1)} %get-tuple-element.22), channel_id=1, source_target_pairs={{0,4},{4,8},{8,12},{12,0},{1,5},{5,9},{9,13},{13,1},{2,6},{6,10},{... | collective-permute-start | bytes 147464 | tf_op jit(solution)/shard_map/ppermute | solution.py:36
  96.9 5.5 %collective-permute-start.16 = (bf16[8,3072]{1,0:T(8,128)(2,1)S(1)}, bf16[8,3072]{1,0:T(8,128)(2,1)S(1)}, u32[]{:S(2)}, u32[]{:S(2)}) collective-permute-start(bf16[8,3072]{1,0:T(8,128)(2,1)S(1)} %get-tuple-element.23), channel_id=1, source_target_pairs={{0,8},{4,12},{8,0},{12,4},{1,9},{5,13},{9,1},{13,5},{2,10},{6,14},... | collective-permute-start | bytes 147464 | tf_op jit(solution)/shard_map/ppermute | solution.py:36

commit v3 on v2

v3 whole, which is shorter than its diff:
```python
import jax
import jax.numpy as jnp
from jax import lax
from jax.experimental import pallas as pl
from jax.experimental.pallas import tpu as pltpu
from jax.sharding import PartitionSpec as P

AXES = ("dp", "expert", "shard")
LANES = 128
ROW_BLOCK = 256
VMEM_LIMIT = 28 * 2**20


def slot_coefficients(expert_ids, gate_values, old_place, new_place):
    matches = (new_place[:, None] == old_place[None, :]).astype(jnp.float32)
    picks = (expert_ids[:, :, None] == jnp.arange(new_place.shape[0], dtype=jnp.int32)).astype(jnp.float32)
    by_expert = jnp.sum(picks * gate_values[:, :, None], axis=1)
    return jnp.sum(by_expert[:, :, None] * matches[None, :, :], axis=1)


def split_exact(value):
    pieces = []
    for _ in range(3):
        piece = lax.reduce_precision(value, exponent_bits=8, mantissa_bits=7)
        pieces.append(piece.astype(jnp.bfloat16))
        value = value - piece
    return pieces


class Digit:
    def __init__(self, name, ways, stride, size):
        self.name, self.ways, self.stride, self.size = name, ways, stride, size

    def shift(self, value, step):
        pairs = []
        for index in range(self.ways):
            digit = index // self.stride % self.size
            target = (digit + step) % self.size
            pairs.append((index, index + (target - digit) * self.stride))
        return lax.ppermute(value, self.name, pairs)

    def gather(self, block, dim):
        return jnp.stack([block] + [self.shift(block, s) for s in range(1, self.size)], axis=dim)

    def reduce(self, slots, dim):
        own = lax.index_in_dim(slots, 0, dim, keepdims=False).astype(jnp.float32)
        for s in range(1, self.size):
            sent = lax.index_in_dim(slots, s, dim, keepdims=False)
            own = own + self.shift(sent, self.size - s).astype(jnp.float32)
        return own.astype(jnp.bfloat16)


def digits_of(name, ways, low=1):
    digits, stride = [], low
    while stride < ways:
        left = ways // stride
        size = 2 if left % 2 == 0 else left
        digits.append(Digit(name, ways, stride, size))
        stride *= size
    return digits[::-1]


def hidden_kernel(experts, steps, first_ref, second_ref, extra_ref, w_ref, hidden_ref):
    half = second_ref.shape[1]
    units = w_ref.shape[2]
    weights = w_ref[0].reshape(2 * units, w_ref.shape[3])
    contract = (((1,), (1,)), ((), ()))
    pre = lax.dot_general(
        first_ref[...], weights[:, :half], contract, preferred_element_type=jnp.float32
    )
    pre += lax.dot_general(
        second_ref[...], weights[:, half:], contract, preferred_element_type=jnp.float32
    )
    slot = pl.program_id(1) // steps
    extra = extra_ref[...].astype(jnp.float32)
    lane = lax.broadcasted_iota(jnp.int32, extra.shape, 1)
    mine = (lane == slot) | (lane == slot + experts) | (lane == slot + 2 * experts)
    weigh = jnp.sum(jnp.where(mine, extra, 0.0), axis=1, keepdims=True)
    gate, up = pre[:, :units], pre[:, units:]
    hidden_ref[...] = (gate / (1.0 + jnp.exp(-gate)) * up * weigh).astype(hidden_ref.dtype)


def hidden_of(first, second, gate_up_weight):
    experts, _, sliver, model_width = gate_up_weight.shape
    rows, half = second.shape
    row_block = min(ROW_BLOCK, rows)
    units = min(LANES, sliver)
    steps = sliver // units
    if units % LANES:
        return hidden_plain(first, second, gate_up_weight)

    def kernel(*refs):
        hidden_kernel(experts, steps, *refs)

    return pl.pallas_call(
        kernel,
        grid=(rows // row_block, experts * steps),
        in_specs=[
            pl.BlockSpec((row_block, half), lambda r, i: (r, 0)),
            pl.BlockSpec((row_block, half), lambda r, i: (r, 0)),
            pl.BlockSpec((row_block, LANES), lambda r, i: (r, half // LANES)),
            pl.BlockSpec((1, 2, units, model_width), lambda r, i: (i // steps, 0, i % steps, 0)),
        ],
        out_specs=pl.BlockSpec((row_block, units), lambda r, i: (r, i)),
        out_shape=jax.ShapeDtypeStruct((rows, experts * sliver), jnp.bfloat16),
        compiler_params=pltpu.CompilerParams(vmem_limit_bytes=VMEM_LIMIT),
        cost_estimate=pl.CostEstimate(
            flops=4 * rows * experts * sliver * model_width,
            bytes_accessed=2 * (gate_up_weight.size + rows * model_width),
            transcendentals=rows * experts * sliver,
        ),
    )(first, second, first, gate_up_weight)


def hidden_plain(first, second, gate_up_weight):
    experts, _, sliver, model_width = gate_up_weight.shape
    half = second.shape[1]
    weigh = first[:, half : half + 3 * experts].astype(jnp.float32)
    weigh = weigh.reshape(-1, 3, experts).sum(axis=1)
    tokens = jnp.concatenate([first[:, :half], second], axis=1)
    hidden = []
    for slot in range(experts):
        gate, up = (
            lax.dot_general(
                tokens,
                gate_up_weight[slot, side],
                (((1,), (1,)), ((), ())),
                preferred_element_type=jnp.float32,
            )
            for side in range(2)
        )
        hidden.append((jax.nn.silu(gate) * up * weigh[:, slot : slot + 1]).astype(jnp.bfloat16))
    return jnp.concatenate(hidden, axis=1)


def down_kernel(hidden_ref, w_ref, out_ref):
    out_ref[...] = jnp.dot(
        hidden_ref[...], w_ref[...], preferred_element_type=jnp.float32
    ).astype(out_ref.dtype)


def down_of(hidden, flat_down, part, columns):
    rows, depth = hidden.shape
    row_block = min(ROW_BLOCK, rows)
    block = columns
    for candidate in (512, 384, 256, 128):
        if columns % candidate == 0:
            block = candidate
            break
    steps = columns // block
    return pl.pallas_call(
        down_kernel,
        grid=(rows // row_block, steps),
        in_specs=[
            pl.BlockSpec((row_block, depth), lambda r, j: (r, 0)),
            pl.BlockSpec((depth, block), lambda r, j: (0, part * steps + j)),
        ],
        out_specs=pl.BlockSpec((row_block, block), lambda r, j: (r, j)),
        out_shape=jax.ShapeDtypeStruct((rows, columns), jnp.bfloat16),
        compiler_params=pltpu.CompilerParams(vmem_limit_bytes=VMEM_LIMIT),
        cost_estimate=pl.CostEstimate(
            flops=2 * rows * depth * columns,
            bytes_accessed=2 * (depth * columns + rows * depth + rows * columns),
            transcendentals=0,
        ),
    )(hidden, flat_down)


def local(
    tokens, gate_up_weight, down_weight, expert_ids, slot_ids, gate_values, old_place, new_place
):
    model_width = tokens.shape[1]
    rows = tokens.shape[0]
    half = model_width // 2
    ways = {name: lax.axis_size(name) for name in AXES}
    cores = 2 if ways["shard"] % 2 == 0 else 1
    x_digits = digits_of("dp", ways["dp"])
    z_digits = digits_of("expert", ways["expert"])
    y_digits = digits_of("shard", ways["shard"], cores)
    core_digits = [Digit("shard", ways["shard"], 1, cores)]
    dim_order = core_digits + x_digits[::-1] + y_digits[::-1] + z_digits[::-1]
    routes = [z_digits + y_digits + x_digits, z_digits + x_digits + y_digits]

    coefficients = slot_coefficients(expert_ids, gate_values, old_place, new_place)
    extra = jnp.concatenate(split_exact(coefficients), axis=1)
    extra = jnp.pad(extra, ((0, 0), (0, -extra.shape[1] % LANES)))
    parts = [
        jnp.concatenate([tokens[:, :half], extra], axis=1),
        tokens[:, half:],
    ]
    gathered = []
    for part, route in zip(parts, routes):
        block, held = part, []
        for digit in route + core_digits:
            dim = sum(dim_order.index(other) < dim_order.index(digit) for other in held)
            block = digit.gather(block, dim)
            held.append(digit)
        gathered.append(block.reshape(-1, part.shape[1]))
    hidden = hidden_of(gathered[0], gathered[1], gate_up_weight)
    flat_down = down_weight.reshape(-1, model_width)
    results = []
    for number, route in enumerate(routes):
        block = down_of(hidden, flat_down, number, half)
        block = block.reshape([digit.size for digit in dim_order] + [rows, half])
        held = list(dim_order)
        for digit in core_digits + route[::-1]:
            block = digit.reduce(block, held.index(digit))
            held.remove(digit)
        results.append(block)
    return jnp.concatenate(results, axis=1)


def solution(mesh):
    in_specs = (
        P(AXES, None),
        P(None, None, AXES, None),
        P(None, AXES, None),
        P(AXES, None),
        P(AXES, None),
        P(AXES, None),
        P(),
        P(),
    )
    return jax.shard_map(
        local, mesh=mesh, in_specs=in_specs, out_specs=P(AXES, None), check_vma=False
    )
```

time: 103 us -> 88.9 us (0.86)
  matrix products: 22.6 us -> 0 us
  Pallas kernels: 0 us -> 20.9 us
  local copies, waits for them, and re-layouts: 12.3 us -> 1.45 us
  starting transfers between devices: 34.4 us -> 27.2 us
  waiting for transfers between devices: 29.5 us -> 35.1 us
    dot_general x4 -> x0, matrix products: 22.6 us -> none  [the longest x2 15.9 us: local(): lax.dot_general(rows_of[:, :half], flat_in[:, number * half:(number + 1)...]
    pallas_call x0 -> x3, Pallas kernels: none -> 20.9 us  [the longest x1 14.4 us: hidden_of(): pl.pallas_call(kernel, grid=(rows // row_block, experts * steps), in_spec...]
    ppermute x24 -> x20, starting transfers between devices: 34.4 us -> 27.2 us  [shift(): return lax.ppermute(value, self.name, pairs)]
    slice x2 -> x0, local copies, waits for them, and re-layouts: 6.32 us -> none  [the longest x1 6.31 us: local(): hidden = jax.nn.silu(pre_act[:, :, 0]) * pre_act[:, :, 1]]
    ppermute x24 -> x20, waiting for transfers between devices: 29.5 us -> 35.1 us  [shift(): return lax.ppermute(value, self.name, pairs)]
    reshape x2 -> x0, local copies, waits for them, and re-layouts: 3.05 us -> none  [the longest x1 3.03 us: local(): pre_act = sum((lax.dot_general(rows_of[:, :half], flat_in[:, number * hal...]
    unnamed x11 -> x7, local copies, waits for them, and re-layouts: 1.25 us -> 0.11 us
  transfers between devices with their start and end apart: 24 -> 20, of which waited for: 14 -> 16; matrix products, arithmetic and copies ran while one was open for 5% -> 4% of each run, Pallas kernels for 0% -> 4%
where the time goes in v3:
time: 88.9 us; the launch traced here: 88.7 us
  waiting for transfers between devices  35.1 us (39%)
  starting transfers between devices  27.2 us (31%)
  Pallas kernels  20.9 us (24%)
  other arithmetic  3.69 us (4%)
  local copies, waits for them, and re-layouts  1.45 us (2%)
    ppermute x20, waiting for transfers between devices, shift(): return lax.ppermute(value, self.name, pairs)  35.1 us
    ppermute x20, starting transfers between devices, shift(): return lax.ppermute(value, self.name, pairs)  27.2 us
    pallas_call x1, Pallas kernels, hidden_of(): pl.pallas_call(kernel, grid=(rows // row_block, experts * steps), in_spec...  14.4 us
    pallas_call x2, Pallas kernels, down_of(): pl.pallas_call(down_kernel, grid=(rows // row_block, steps), in_specs=[pl...  6.47 us
  transfers between devices with their start and end apart: 20, of which 16 were waited for; matrix products, arithmetic and copies ran while one was open for 4% of the time, Pallas kernels for 4%

profile of v3, /device:TPU:0, one launch (start us, length us, event | category | flops | bytes accessed | tf_op | source)
XLA Modules:
  0.0 88.7 jit_solution(8881722976899607950)
XLA Ops:
  0.0 0.8 slice_bitcast_fusion.16
  0.8 4.1 %collective-permute-start.5 = (bf16[8,3072]{1,0:T(8,128)(2,1)S(1)}, bf16[8,3072]{1,0:T(8,128)(2,1)S(1)}, u32[]{:S(2)}, u32[]{:S(2)}) collective-permute-start(bf16[8,3072]{1,0:T(8,128)(2,1)S(1)} %get-tuple-element.26), channel_id=1, source_target_pairs={{0,8},{4,12},{8,0},{12,4},{1,9},{5,13},{9,1},{13,5},{2,10},{6,14},... | collective-permute-start | bytes 147464 | tf_op jit(solution)/shard_map/ppermute | solution.py:40
  4.9 0.7 compare_convert_fusion
  5.7 0.7 select_reduce_fusion
  6.7 0.8 collective-permute-done.5
  7.6 2.0 %collective-permute-start.6 = (bf16[2,8,3072]{2,1,0:T(8,128)(2,1)S(1)}, bf16[2,8,3072]{2,1,0:T(8,128)(2,1)S(1)}, u32[]{:S(2)}, u32[]{:S(2)}) collective-permute-start(bf16[2,8,3072]{2,1,0:T(8,128)(2,1)S(1)} %get-tuple-element.24), channel_id=1, source_target_pairs={{0,4},{4,0},{8,12},{12,8},{1,5},{5,1},{9,13},{13,9},{2,6},{6,2},{1... | collective-permute-start | bytes 294920 | tf_op jit(solution)/shard_map/ppermute | solution.py:40
  9.5 2.4 %collective-permute-done = bf16[8,3200]{1,0:T(8,128)(2,1)S(1)} collective-permute-done((bf16[8,3200]{1,0:T(8,128)(2,1)S(1)}, bf16[8,3200]{1,0:T(8,128)(2,1)S(1)}, u32[]{:S(2)}, u32[]{:S(2)}) %collective-permute-start) | collective-permute-done | bytes 51232 | tf_op jit(solution)/shard_map/ppermute | solution.py:40
  12.0 1.6 %collective-permute-start.1 = (bf16[2,8,3200]{2,1,0:T(8,128)(2,1)S(1)}, bf16[2,8,3200]{2,1,0:T(8,128)(2,1)S(1)}, u32[]{:S(2)}, u32[]{:S(2)}) collective-permute-start(bf16[2,8,3200]{2,1,0:T(8,128)(2,1)S(1)} %get-tuple-element.22), channel_id=1, source_target_pairs={{0,4},{4,0},{8,12},{12,8},{1,5},{5,1},{9,13},{13,9},{2,6},{6,2},{1... | collective-permute-start | bytes 307208 | tf_op jit(solution)/shard_map/ppermute | solution.py:40
  13.6 1.6 %collective-permute-start.7 = (bf16[2,2,8,3072]{3,2,1,0:T(8,128)(2,1)S(1)}, bf16[2,2,8,3072]{3,2,1,0:T(8,128)(2,1)S(1)}, u32[]{:S(2)}, u32[]{:S(2)}) collective-permute-start(bf16[2,2,8,3072]{3,2,1,0:T(8,128)(2,1)S(1)} %get-tuple-element.20), channel_id=1, source_target_pairs={{0,16},{16,0},{1,17},{17,1},{2,18},{18,2},{3,19},{19,3},{4,20},{20... | collective-permute-start | bytes 589832 | tf_op jit(solution)/shard_map/ppermute | solution.py:40
  15.1 1.6 %collective-permute-done.1 = bf16[2,8,3200]{2,1,0:T(8,128)(2,1)S(1)} collective-permute-done((bf16[2,8,3200]{2,1,0:T(8,128)(2,1)S(1)}, bf16[2,8,3200]{2,1,0:T(8,128)(2,1)S(1)}, u32[]{:S(2)}, u32[]{:S(2)}) %collective-permute-start.1) | collective-permute-done | bytes 102432 | tf_op jit(solution)/shard_map/ppermute | solution.py:40
  16.7 1.5 %collective-permute-start.2 = (bf16[2,2,8,3200]{3,2,1,0:T(8,128)(2,1)S(1)}, bf16[2,2,8,3200]{3,2,1,0:T(8,128)(2,1)S(1)}, u32[]{:S(2)}, u32[]{:S(2)}) collective-permute-start(bf16[2,2,8,3200]{3,2,1,0:T(8,128)(2,1)S(1)} %get-tuple-element.18), channel_id=1, source_target_pairs={{0,2},{1,3},{2,0},{3,1},{4,6},{5,7},{6,4},{7,5},{8,10},{9,11},{10,... | collective-permute-start | bytes 614408 | tf_op jit(solution)/shard_map/ppermute | solution.py:40
  18.2 1.1 %collective-permute-done.7 = bf16[2,2,8,3072]{3,2,1,0:T(8,128)(2,1)S(1)} collective-permute-done((bf16[2,2,8,3072]{3,2,1,0:T(8,128)(2,1)S(1)}, bf16[2,2,8,3072]{3,2,1,0:T(8,128)(2,1)S(1)}, u32[]{:S(2)}, u32[]{:S(2)}) %collective-permute-start.7) | collective-permute-done | bytes 196640 | tf_op jit(solution)/shard_map/ppermute | solution.py:40
  19.4 1.6 %collective-permute-start.8 = (bf16[2,2,2,8,3072]{4,3,2,1,0:T(8,128)(2,1)S(1)}, bf16[2,2,2,8,3072]{4,3,2,1,0:T(8,128)(2,1)S(1)}, u32[]{:S(2)}, u32[]{:S(2)}) collective-permute-start(bf16[2,2,2,8,3072]{4,3,2,1,0:T(8,128)(2,1)S(1)} %get-tuple-element.16), channel_id=1, source_target_pairs={{0,2},{1,3},{2,0},{3,1},{4,6},{5,7},{6,4},{7,5},{8,10},{9,11},{10,... | collective-permute-start | bytes 1179656 | tf_op jit(solution)/shard_map/ppermute | solution.py:40
  20.9 3.8 %collective-permute-done.2 = bf16[2,2,8,3200]{3,2,1,0:T(8,128)(2,1)S(1)} collective-permute-done((bf16[2,2,8,3200]{3,2,1,0:T(8,128)(2,1)S(1)}, bf16[2,2,8,3200]{3,2,1,0:T(8,128)(2,1)S(1)}, u32[]{:S(2)}, u32[]{:S(2)}) %collective-permute-start.2) | collective-permute-done | bytes 204832 | tf_op jit(solution)/shard_map/ppermute | solution.py:40
  24.8 1.5 %collective-permute-start.3 = (bf16[2,2,2,8,3200]{4,3,2,1,0:T(8,128)(2,1)S(1)}, bf16[2,2,2,8,3200]{4,3,2,1,0:T(8,128)(2,1)S(1)}, u32[]{:S(2)}, u32[]{:S(2)}) collective-permute-start(bf16[2,2,2,8,3200]{4,3,2,1,0:T(8,128)(2,1)S(1)} %get-tuple-element.14), channel_id=1, source_target_pairs={{0,16},{16,0},{1,17},{17,1},{2,18},{18,2},{3,19},{19,3},{4,20},{20... | collective-permute-start | bytes 1228808 | tf_op jit(solution)/shard_map/ppermute | solution.py:40
  26.3 3.4 %collective-permute-done.8 = bf16[2,2,2,8,3072]{4,3,2,1,0:T(8,128)(2,1)S(1)} collective-permute-done((bf16[2,2,2,8,3072]{4,3,2,1,0:T(8,128)(2,1)S(1)}, bf16[2,2,2,8,3072]{4,3,2,1,0:T(8,128)(2,1)S(1)}, u32[]{:S(2)}, u32[]{:S(2)}) %collective-permute-start.8) | collective-permute-done | bytes 393248 | tf_op jit(solution)/shard_map/ppermute | solution.py:40
  29.9 2.9 %collective-permute-done.3 = bf16[2,2,2,8,3200]{4,3,2,1,0:T(8,128)(2,1)S(1)} collective-permute-done((bf16[2,2,2,8,3200]{4,3,2,1,0:T(8,128)(2,1)S(1)}, bf16[2,2,2,8,3200]{4,3,2,1,0:T(8,128)(2,1)S(1)}, u32[]{:S(2)}, u32[]{:S(2)}) %collective-permute-start.3) | collective-permute-done | bytes 409632 | tf_op jit(solution)/shard_map/ppermute | solution.py:40
  32.8 0.1 fusion.22
  33.0 0.1 pad_maximum_fusion.1
  33.2 0.1 copy.14
  33.3 2.0 %collective-permute-done.4 = bf16[2,2,2,2,8,3200]{5,4,3,2,1,0:T(8,128)(2,1)S(1)} collective-permute-done((bf16[2,2,2,2,8,3200]{5,4,3,2,1,0:T(8,128)(2,1)S(1)}, bf16[2,2,2,2,8,3200]{5,4,3,2,1,0:T(8,128)(2,1)S(1)}, u32[]{:S(2)}, u32[]{:S(2)}) %collective-permute-start.4) | collective-permute-done | bytes 819232 | tf_op jit(solution)/shard_map/ppermute | solution.py:40
  35.4 0.2 pad_maximum_fusion
  35.6 14.4 %shard_map.73.hidden_ref = bf16[256,1024]{1,0:T(8,128)(2,1)S(1)} custom-call(bf16[256,3200]{1,0:T(8,128)(2,1)S(1)} %bitcast.99, bf16[256,3072]{1,0:T(8,128)(2,1)S(1)} %bitcast.101, bf16[256,3200]{1,0:T(8,128)(2,1)S(1)} %bitcast.100, bf16[4,2,256,6144]{3,2,1,0:T(8,128)(2,1)} %refs_3_.1), custom_call_target="tpu_custom_call" | custom-call | flops 6442450944 | bytes 28311552 | tf_op jit(solution)/shard_map/pallas_call | solution.py:95
  50.0 3.2 %shard_map.74 = bf16[256,3072]{1,0:T(8,128)(2,1)S(1)} custom-call(bf16[256,1024]{1,0:T(8,128)(2,1)S(1)} %shard_map.73.hidden_ref, bf16[1024,6144]{1,0:T(8,128)(2,1)S(1)} %bitcast.97), custom_call_target="tpu_custom_call" | custom-call | flops 1610612736 | bytes 8388608 | tf_op jit(solution)/shard_map/pallas_call | solution.py:151
  53.3 0.1 fusion.23
  53.4 0.2 collective-permute-start.10
  53.6 3.2 %shard_map.75 = bf16[256,3072]{1,0:T(8,128)(2,1)S(1)} custom-call(bf16[256,1024]{1,0:T(8,128)(2,1)S(1)} %shard_map.73.hidden_ref, bf16[1024,6144]{1,0:T(8,128)(2,1)S(1)} %bitcast.98), custom_call_target="tpu_custom_call" | custom-call | flops 1610612736 | bytes 8388608 | tf_op jit(solution)/shard_map/pallas_call | solution.py:151
  56.8 0.1 fusion.24
  57.0 0.4 collective-permute-start.15
  57.5 0.2 fusion
  57.7 1.5 %collective-permute-start.11 = (bf16[2,2,2,8,3072]{4,3,2,1,0:T(8,128)(2,1)S(1)}, bf16[2,2,2,8,3072]{4,3,2,1,0:T(8,128)(2,1)S(1)}, u32[]{:S(2)}, u32[]{:S(2)}) collective-permute-start(bf16[2,2,2,8,3072]{4,3,2,1,0:T(8,128)(2,1)S(1)} %slice_bitcast_fusion.2), channel_id=1, source_target_pairs={{0,16},{16,0},{1,17},{17,1},{2,18},{18,2},{3,19},{19,3},{4,20},{20... | collective-permute-start | bytes 1179656 | tf_op jit(solution)/shard_map/ppermute | solution.py:40
  59.2 0.2 collective-permute-done.15
  59.4 0.2 fusion.1
  59.6 1.5 %collective-permute-start.16 = (bf16[2,2,2,8,3072]{4,3,2,1,0:T(8,128)(2,1)S(1)}, bf16[2,2,2,8,3072]{4,3,2,1,0:T(8,128)(2,1)S(1)}, u32[]{:S(2)}, u32[]{:S(2)}) collective-permute-start(bf16[2,2,2,8,3072]{4,3,2,1,0:T(8,128)(2,1)S(1)} %slice_bitcast_fusion), channel_id=1, source_target_pairs={{0,2},{1,3},{2,0},{3,1},{4,6},{5,7},{6,4},{7,5},{8,10},{9,11},{10,... | collective-permute-start | bytes 1179656 | tf_op jit(solution)/shard_map/ppermute | solution.py:40
  61.1 7.8 %collective-permute-done.11 = bf16[2,2,2,8,3072]{4,3,2,1,0:T(8,128)(2,1)S(1)} collective-permute-done((bf16[2,2,2,8,3072]{4,3,2,1,0:T(8,128)(2,1)S(1)}, bf16[2,2,2,8,3072]{4,3,2,1,0:T(8,128)(2,1)S(1)}, u32[]{:S(2)}, u32[]{:S(2)}) %collective-permute-start.11) | collective-permute-done | bytes 393248 | tf_op jit(solution)/shard_map/ppermute | solution.py:40
  69.0 1.5 %collective-permute-start.12 = (bf16[2,2,8,3072]{3,2,1,0:T(8,128)(2,1)S(1)}, bf16[2,2,8,3072]{3,2,1,0:T(8,128)(2,1)S(1)}, u32[]{:S(2)}, u32[]{:S(2)}) collective-permute-start(bf16[2,2,8,3072]{3,2,1,0:T(8,128)(2,1)S(1)} %slice_bitcast_fusion.6), channel_id=1, source_target_pairs={{0,2},{1,3},{2,0},{3,1},{4,6},{5,7},{6,4},{7,5},{8,10},{9,11},{10,... | collective-permute-start | bytes 589832 | tf_op jit(solution)/shard_map/ppermute | solution.py:40
  70.5 0.5 collective-permute-done.16
  71.2 1.5 %collective-permute-start.17 = (bf16[2,2,8,3072]{3,2,1,0:T(8,128)(2,1)S(1)}, bf16[2,2,8,3072]{3,2,1,0:T(8,128)(2,1)S(1)}, u32[]{:S(2)}, u32[]{:S(2)}) collective-permute-start(bf16[2,2,8,3072]{3,2,1,0:T(8,128)(2,1)S(1)} %slice_bitcast_fusion.4), channel_id=1, source_target_pairs={{0,16},{16,0},{1,17},{17,1},{2,18},{18,2},{3,19},{19,3},{4,20},{20... | collective-permute-start | bytes 589832 | tf_op jit(solution)/shard_map/ppermute | solution.py:40
  72.7 2.6 %collective-permute-done.12 = bf16[2,2,8,3072]{3,2,1,0:T(8,128)(2,1)S(1)} collective-permute-done((bf16[2,2,8,3072]{3,2,1,0:T(8,128)(2,1)S(1)}, bf16[2,2,8,3072]{3,2,1,0:T(8,128)(2,1)S(1)}, u32[]{:S(2)}, u32[]{:S(2)}) %collective-permute-start.12) | collective-permute-done | bytes 196640 | tf_op jit(solution)/shard_map/ppermute | solution.py:40
  75.3 1.6 %collective-permute-start.13 = (bf16[2,8,3072]{2,1,0:T(8,128)(2,1)S(1)}, bf16[2,8,3072]{2,1,0:T(8,128)(2,1)S(1)}, u32[]{:S(2)}, u32[]{:S(2)}) collective-permute-start(bf16[2,8,3072]{2,1,0:T(8,128)(2,1)S(1)} %slice_bitcast_fusion.10), channel_id=1, source_target_pairs={{0,4},{4,0},{8,12},{12,8},{1,5},{5,1},{9,13},{13,9},{2,6},{6,2},{1... | collective-permute-start | bytes 294920 | tf_op jit(solution)/shard_map/ppermute | solution.py:40
  77.0 0.7 collective-permute-done.17
  77.7 1.6 %collective-permute-start.18 = (bf16[2,8,3072]{2,1,0:T(8,128)(2,1)S(1)}, bf16[2,8,3072]{2,1,0:T(8,128)(2,1)S(1)}, u32[]{:S(2)}, u32[]{:S(2)}) collective-permute-start(bf16[2,8,3072]{2,1,0:T(8,128)(2,1)S(1)} %slice_bitcast_fusion.8), channel_id=1, source_target_pairs={{0,4},{4,0},{8,12},{12,8},{1,5},{5,1},{9,13},{13,9},{2,6},{6,2},{1... | collective-permute-start | bytes 294920 | tf_op jit(solution)/shard_map/ppermute | solution.py:40
  79.3 1.8 %collective-permute-done.13 = bf16[2,8,3072]{2,1,0:T(8,128)(2,1)S(1)} collective-permute-done((bf16[2,8,3072]{2,1,0:T(8,128)(2,1)S(1)}, bf16[2,8,3072]{2,1,0:T(8,128)(2,1)S(1)}, u32[]{:S(2)}, u32[]{:S(2)}) %collective-permute-start.13) | collective-permute-done | bytes 98336 | tf_op jit(solution)/shard_map/ppermute | solution.py:40
  81.1 1.8 %collective-permute-start.14 = (bf16[8,3072]{1,0:T(8,128)(2,1)S(1)}, bf16[8,3072]{1,0:T(8,128)(2,1)S(1)}, u32[]{:S(2)}, u32[]{:S(2)}) collective-permute-start(bf16[8,3072]{1,0:T(8,128)(2,1)S(1)} %slice_bitcast_fusion.14), channel_id=1, source_target_pairs={{0,8},{4,12},{8,0},{12,4},{1,9},{5,13},{9,1},{13,5},{2,10},{6,14},... | collective-permute-start | bytes 147464 | tf_op jit(solution)/shard_map/ppermute | solution.py:40
  83.0 1.5 %collective-permute-start.19 = (bf16[8,3072]{1,0:T(8,128)(2,1)S(1)}, bf16[8,3072]{1,0:T(8,128)(2,1)S(1)}, u32[]{:S(2)}, u32[]{:S(2)}) collective-permute-start(bf16[8,3072]{1,0:T(8,128)(2,1)S(1)} %slice_bitcast_fusion.12), channel_id=1, source_target_pairs={{0,8},{4,12},{8,0},{12,4},{1,9},{5,13},{9,1},{13,5},{2,10},{6,14},... | collective-permute-start | bytes 147464 | tf_op jit(solution)/shard_map/ppermute | solution.py:40
  84.5 2.7 %collective-permute-done.14 = bf16[8,3072]{1,0:T(8,128)(2,1)S(1)} collective-permute-done((bf16[8,3072]{1,0:T(8,128)(2,1)S(1)}, bf16[8,3072]{1,0:T(8,128)(2,1)S(1)}, u32[]{:S(2)}, u32[]{:S(2)}) %collective-permute-start.14) | collective-permute-done | bytes 49184 | tf_op jit(solution)/shard_map/ppermute | solution.py:40
  87.2 0.8 collective-permute-done.19
  88.0 0.6 pad_maximum_fusion.10
  (43 shorter events, 1.3 us)
Async XLA Ops:
  0.8 6.7 %collective-permute-start.5 = (bf16[8,3072]{1,0:T(8,128)(2,1)S(1)}, bf16[8,3072]{1,0:T(8,128)(2,1)S(1)}, u32[]{:S(2)}, u32[]{:S(2)}) collective-permute-start(bf16[8,3072]{1,0:T(8,128)(2,1)S(1)} %get-tuple-element.26), channel_id=1, source_target_pairs={{0,8},{4,12},{8,0},{12,4},{1,9},{5,13},{9,1},{13,5},{2,10},{6,14},... | collective-permute-start | bytes 147464 | tf_op jit(solution)/shard_map/ppermute | solution.py:40
  6.6 5.3 %collective-permute-start = (bf16[8,3200]{1,0:T(8,128)(2,1)S(1)}, bf16[8,3200]{1,0:T(8,128)(2,1)S(1)}, u32[]{:S(2)}, u32[]{:S(2)}) collective-permute-start(bf16[8,3200]{1,0:T(8,128)(2,1)S(1)} %get-tuple-element.29), channel_id=1, source_target_pairs={{0,8},{4,12},{8,0},{12,4},{1,9},{5,13},{9,1},{13,5},{2,10},{6,14},... | collective-permute-start | bytes 153608 | tf_op jit(solution)/shard_map/ppermute | solution.py:40
  7.6 6.0 %collective-permute-start.6 = (bf16[2,8,3072]{2,1,0:T(8,128)(2,1)S(1)}, bf16[2,8,3072]{2,1,0:T(8,128)(2,1)S(1)}, u32[]{:S(2)}, u32[]{:S(2)}) collective-permute-start(bf16[2,8,3072]{2,1,0:T(8,128)(2,1)S(1)} %get-tuple-element.24), channel_id=1, source_target_pairs={{0,4},{4,0},{8,12},{12,8},{1,5},{5,1},{9,13},{13,9},{2,6},{6,2},{1... | collective-permute-start | bytes 294920 | tf_op jit(solution)/shard_map/ppermute | solution.py:40
  12.0 4.7 %collective-permute-start.1 = (bf16[2,8,3200]{2,1,0:T(8,128)(2,1)S(1)}, bf16[2,8,3200]{2,1,0:T(8,128)(2,1)S(1)}, u32[]{:S(2)}, u32[]{:S(2)}) collective-permute-start(bf16[2,8,3200]{2,1,0:T(8,128)(2,1)S(1)} %get-tuple-element.22), channel_id=1, source_target_pairs={{0,4},{4,0},{8,12},{12,8},{1,5},{5,1},{9,13},{13,9},{2,6},{6,2},{1... | collective-permute-start | bytes 307208 | tf_op jit(solution)/shard_map/ppermute | solution.py:40
  13.6 5.7 %collective-permute-start.7 = (bf16[2,2,8,3072]{3,2,1,0:T(8,128)(2,1)S(1)}, bf16[2,2,8,3072]{3,2,1,0:T(8,128)(2,1)S(1)}, u32[]{:S(2)}, u32[]{:S(2)}) collective-permute-start(bf16[2,2,8,3072]{3,2,1,0:T(8,128)(2,1)S(1)} %get-tuple-element.20), channel_id=1, source_target_pairs={{0,16},{16,0},{1,17},{17,1},{2,18},{18,2},{3,19},{19,3},{4,20},{20... | collective-permute-start | bytes 589832 | tf_op jit(solution)/shard_map/ppermute | solution.py:40
  16.7 8.0 %collective-permute-start.2 = (bf16[2,2,8,3200]{3,2,1,0:T(8,128)(2,1)S(1)}, bf16[2,2,8,3200]{3,2,1,0:T(8,128)(2,1)S(1)}, u32[]{:S(2)}, u32[]{:S(2)}) collective-permute-start(bf16[2,2,8,3200]{3,2,1,0:T(8,128)(2,1)S(1)} %get-tuple-element.18), channel_id=1, source_target_pairs={{0,2},{1,3},{2,0},{3,1},{4,6},{5,7},{6,4},{7,5},{8,10},{9,11},{10,... | collective-permute-start | bytes 614408 | tf_op jit(solution)/shard_map/ppermute | solution.py:40
  19.4 10.4 %collective-permute-start.8 = (bf16[2,2,2,8,3072]{4,3,2,1,0:T(8,128)(2,1)S(1)}, bf16[2,2,2,8,3072]{4,3,2,1,0:T(8,128)(2,1)S(1)}, u32[]{:S(2)}, u32[]{:S(2)}) collective-permute-start(bf16[2,2,2,8,3072]{4,3,2,1,0:T(8,128)(2,1)S(1)} %get-tuple-element.16), channel_id=1, source_target_pairs={{0,2},{1,3},{2,0},{3,1},{4,6},{5,7},{6,4},{7,5},{8,10},{9,11},{10,... | collective-permute-start | bytes 1179656 | tf_op jit(solution)/shard_map/ppermute | solution.py:40
  24.8 8.0 %collective-permute-start.3 = (bf16[2,2,2,8,3200]{4,3,2,1,0:T(8,128)(2,1)S(1)}, bf16[2,2,2,8,3200]{4,3,2,1,0:T(8,128)(2,1)S(1)}, u32[]{:S(2)}, u32[]{:S(2)}) collective-permute-start(bf16[2,2,2,8,3200]{4,3,2,1,0:T(8,128)(2,1)S(1)} %get-tuple-element.14), channel_id=1, source_target_pairs={{0,16},{16,0},{1,17},{17,1},{2,18},{18,2},{3,19},{19,3},{4,20},{20... | collective-permute-start | bytes 1228808 | tf_op jit(solution)/shard_map/ppermute | solution.py:40
  29.8 3.2 %collective-permute-start.9 = (bf16[2,2,2,2,8,3072]{5,4,3,2,0,1:T(8,128)(2,1)S(1)}, bf16[2,2,2,2,8,3072]{5,4,3,2,0,1:T(8,128)(2,1)S(1)}, u32[]{:S(2)}, u32[]{:S(2)}) collective-permute-start(bf16[2,2,2,2,8,3072]{5,4,3,2,0,1:T(8,128)(2,1)S(1)} %get-tuple-element.12), channel_id=1, source_target_pairs={{0,1},{1,0},{2,3},{3,2},{4,5},{5,4},{6,7},{7,6},{8,9},{9,8},{10,11... | collective-permute-start | bytes 2359304 | tf_op jit(solution)/shard_map/ppermute | solution.py:40
  33.0 2.4 %collective-permute-start.4 = (bf16[2,2,2,2,8,3200]{5,4,3,2,1,0:T(8,128)(2,1)S(1)}, bf16[2,2,2,2,8,3200]{5,4,3,2,1,0:T(8,128)(2,1)S(1)}, u32[]{:S(2)}, u32[]{:S(2)}) collective-permute-start(bf16[2,2,2,2,8,3200]{5,4,3,2,1,0:T(8,128)(2,1)S(1)} %get-tuple-element.10), channel_id=1, source_target_pairs={{0,1},{1,0},{2,3},{3,2},{4,5},{5,4},{6,7},{7,6},{8,9},{9,8},{10,11... | collective-permute-start | bytes 2457608 | tf_op jit(solution)/shard_map/ppermute | solution.py:40
  35.4 14.6 %slice-start = ((s8[12582912]{0:T(1024)(128)(4,1)}), s8[4194304]{0:T(1024)(128)(4,1)S(1)}, s32[]{:S(2)}) async-start(s8[12582912]{0:T(1024)(128)(4,1)} %bitcast.95), calls=%async_computation | async-start | bytes 8388608
  35.5 14.5 %slice-start.1 = ((s8[12582912]{0:T(1024)(128)(4,1)}), s8[4194304]{0:T(1024)(128)(4,1)S(1)}, s32[]{:S(2)}) async-start(s8[12582912]{0:T(1024)(128)(4,1)} %bitcast.95), calls=%async_computation.1 | async-start | bytes 8388608
  35.5 14.5 %slice-start.2 = ((s8[12582912]{0:T(1024)(128)(4,1)}), s8[4194304]{0:T(1024)(128)(4,1)S(1)}, s32[]{:S(2)}) async-start(s8[12582912]{0:T(1024)(128)(4,1)} %bitcast.95), calls=%async_computation.2 | async-start | bytes 8388608
  53.4 4.1 %collective-permute-start.10 = (bf16[2,2,2,2,8,3072]{5,4,3,2,1,0:T(8,128)(2,1)S(1)}, bf16[2,2,2,2,8,3072]{5,4,3,2,1,0:T(8,128)(2,1)S(1)}, u32[]{:S(2)}, u32[]{:S(2)}) collective-permute-start(bf16[2,2,2,2,8,3072]{5,4,3,2,1,0:T(8,128)(2,1)S(1)} %bitcast.107), channel_id=1, source_target_pairs={{0,1},{1,0},{2,3},{3,2},{4,5},{5,4},{6,7},{7,6},{8,9},{9,8},{10,11... | collective-permute-start | bytes 2359304 | tf_op jit(solution)/shard_map/ppermute | solution.py:40
  57.0 2.4 %collective-permute-start.15 = (bf16[2,2,2,2,8,3072]{5,4,3,2,0,1:T(8,128)(2,1)S(1)}, bf16[2,2,2,2,8,3072]{5,4,3,2,0,1:T(8,128)(2,1)S(1)}, u32[]{:S(2)}, u32[]{:S(2)}) collective-permute-start(bf16[2,2,2,2,8,3072]{5,4,3,2,0,1:T(8,128)(2,1)S(1)} %copy.15), channel_id=1, source_target_pairs={{0,1},{1,0},{2,3},{3,2},{4,5},{5,4},{6,7},{7,6},{8,9},{9,8},{10,11... | collective-permute-start | bytes 2359304 | tf_op jit(solution)/shard_map/ppermute | solution.py:40
  57.7 11.2 %collective-permute-start.11 = (bf16[2,2,2,8,3072]{4,3,2,1,0:T(8,128)(2,1)S(1)}, bf16[2,2,2,8,3072]{4,3,2,1,0:T(8,128)(2,1)S(1)}, u32[]{:S(2)}, u32[]{:S(2)}) collective-permute-start(bf16[2,2,2,8,3072]{4,3,2,1,0:T(8,128)(2,1)S(1)} %slice_bitcast_fusion.2), channel_id=1, source_target_pairs={{0,16},{16,0},{1,17},{17,1},{2,18},{18,2},{3,19},{19,3},{4,20},{20... | collective-permute-start | bytes 1179656 | tf_op jit(solution)/shard_map/ppermute | solution.py:40
  59.6 11.5 %collective-permute-start.16 = (bf16[2,2,2,8,3072]{4,3,2,1,0:T(8,128)(2,1)S(1)}, bf16[2,2,2,8,3072]{4,3,2,1,0:T(8,128)(2,1)S(1)}, u32[]{:S(2)}, u32[]{:S(2)}) collective-permute-start(bf16[2,2,2,8,3072]{4,3,2,1,0:T(8,128)(2,1)S(1)} %slice_bitcast_fusion), channel_id=1, source_target_pairs={{0,2},{1,3},{2,0},{3,1},{4,6},{5,7},{6,4},{7,5},{8,10},{9,11},{10,... | collective-permute-start | bytes 1179656 | tf_op jit(solution)/shard_map/ppermute | solution.py:40
  69.0 6.2 %collective-permute-start.12 = (bf16[2,2,8,3072]{3,2,1,0:T(8,128)(2,1)S(1)}, bf16[2,2,8,3072]{3,2,1,0:T(8,128)(2,1)S(1)}, u32[]{:S(2)}, u32[]{:S(2)}) collective-permute-start(bf16[2,2,8,3072]{3,2,1,0:T(8,128)(2,1)S(1)} %slice_bitcast_fusion.6), channel_id=1, source_target_pairs={{0,2},{1,3},{2,0},{3,1},{4,6},{5,7},{6,4},{7,5},{8,10},{9,11},{10,... | collective-permute-start | bytes 589832 | tf_op jit(solution)/shard_map/ppermute | solution.py:40
  71.2 6.4 %collective-permute-start.17 = (bf16[2,2,8,3072]{3,2,1,0:T(8,128)(2,1)S(1)}, bf16[2,2,8,3072]{3,2,1,0:T(8,128)(2,1)S(1)}, u32[]{:S(2)}, u32[]{:S(2)}) collective-permute-start(bf16[2,2,8,3072]{3,2,1,0:T(8,128)(2,1)S(1)} %slice_bitcast_fusion.4), channel_id=1, source_target_pairs={{0,16},{16,0},{1,17},{17,1},{2,18},{18,2},{3,19},{19,3},{4,20},{20... | collective-permute-start | bytes 589832 | tf_op jit(solution)/shard_map/ppermute | solution.py:40
  75.3 5.7 %collective-permute-start.13 = (bf16[2,8,3072]{2,1,0:T(8,128)(2,1)S(1)}, bf16[2,8,3072]{2,1,0:T(8,128)(2,1)S(1)}, u32[]{:S(2)}, u32[]{:S(2)}) collective-permute-start(bf16[2,8,3072]{2,1,0:T(8,128)(2,1)S(1)} %slice_bitcast_fusion.10), channel_id=1, source_target_pairs={{0,4},{4,0},{8,12},{12,8},{1,5},{5,1},{9,13},{13,9},{2,6},{6,2},{1... | collective-permute-start | bytes 294920 | tf_op jit(solution)/shard_map/ppermute | solution.py:40
  77.7 5.2 %collective-permute-start.18 = (bf16[2,8,3072]{2,1,0:T(8,128)(2,1)S(1)}, bf16[2,8,3072]{2,1,0:T(8,128)(2,1)S(1)}, u32[]{:S(2)}, u32[]{:S(2)}) collective-permute-start(bf16[2,8,3072]{2,1,0:T(8,128)(2,1)S(1)} %slice_bitcast_fusion.8), channel_id=1, source_target_pairs={{0,4},{4,0},{8,12},{12,8},{1,5},{5,1},{9,13},{13,9},{2,6},{6,2},{1... | collective-permute-start | bytes 294920 | tf_op jit(solution)/shard_map/ppermute | solution.py:40
  81.1 6.1 %collective-permute-start.14 = (bf16[8,3072]{1,0:T(8,128)(2,1)S(1)}, bf16[8,3072]{1,0:T(8,128)(2,1)S(1)}, u32[]{:S(2)}, u32[]{:S(2)}) collective-permute-start(bf16[8,3072]{1,0:T(8,128)(2,1)S(1)} %slice_bitcast_fusion.14), channel_id=1, source_target_pairs={{0,8},{4,12},{8,0},{12,4},{1,9},{5,13},{9,1},{13,5},{2,10},{6,14},... | collective-permute-start | bytes 147464 | tf_op jit(solution)/shard_map/ppermute | solution.py:40
  83.0 5.1 %collective-permute-start.19 = (bf16[8,3072]{1,0:T(8,128)(2,1)S(1)}, bf16[8,3072]{1,0:T(8,128)(2,1)S(1)}, u32[]{:S(2)}, u32[]{:S(2)}) collective-permute-start(bf16[8,3072]{1,0:T(8,128)(2,1)S(1)} %slice_bitcast_fusion.12), channel_id=1, source_target_pairs={{0,8},{4,12},{8,0},{12,4},{1,9},{5,13},{9,1},{13,5},{2,10},{6,14},... | collective-permute-start | bytes 147464 | tf_op jit(solution)/shard_map/ppermute | solution.py:40

commit v4 on v3

v4 whole, which is shorter than its diff:
```python
import jax
import jax.numpy as jnp
from jax import lax
from jax.experimental import pallas as pl
from jax.experimental.pallas import tpu as pltpu
from jax.sharding import PartitionSpec as P

AXES = ("dp", "expert", "shard")
LANES = 128
ROW_BLOCK = 256
PIECES = 4
FETCH_LIMIT = 1 * 2**20
HIDDEN_LIMIT = 32 * 2**20
DOWN_LIMIT = 8 * 2**20


def slot_coefficients(expert_ids, gate_values, old_place, new_place):
    matches = (new_place[:, None] == old_place[None, :]).astype(jnp.float32)
    picks = (expert_ids[:, :, None] == jnp.arange(new_place.shape[0], dtype=jnp.int32)).astype(jnp.float32)
    by_expert = jnp.sum(picks * gate_values[:, :, None], axis=1)
    return jnp.sum(by_expert[:, :, None] * matches[None, :, :], axis=1)


def split_exact(value):
    pieces = []
    for _ in range(3):
        piece = lax.reduce_precision(value, exponent_bits=8, mantissa_bits=7)
        pieces.append(piece.astype(jnp.bfloat16))
        value = value - piece
    return pieces


class Digit:
    def __init__(self, name, ways, stride, size):
        self.name, self.ways, self.stride, self.size = name, ways, stride, size

    def shift(self, value, step):
        pairs = []
        for index in range(self.ways):
            digit = index // self.stride % self.size
            target = (digit + step) % self.size
            pairs.append((index, index + (target - digit) * self.stride))
        return lax.ppermute(value, self.name, pairs)

    def gather(self, block, dim):
        return jnp.stack([block] + [self.shift(block, s) for s in range(1, self.size)], axis=dim)

    def reduce(self, slots, dim):
        own = lax.index_in_dim(slots, 0, dim, keepdims=False).astype(jnp.float32)
        for s in range(1, self.size):
            sent = lax.index_in_dim(slots, s, dim, keepdims=False)
            own = own + self.shift(sent, self.size - s).astype(jnp.float32)
        return own.astype(jnp.bfloat16)


def digits_of(name, ways, low=1):
    digits, stride = [], low
    while stride < ways:
        left = ways // stride
        size = 2 if left % 2 == 0 else left
        digits.append(Digit(name, ways, stride, size))
        stride *= size
    return digits[::-1]


def resident(value):
    return pltpu.with_memory_space_constraint(value, pltpu.VMEM)


def in_hbm(value):
    return pltpu.with_memory_space_constraint(value, pltpu.HBM)


def fetch_kernel(w_ref, after_ref, out_ref, sem):
    del after_ref
    copy = pltpu.make_async_copy(w_ref, out_ref, sem)
    copy.start()
    copy.wait()


def fetched(weight, after):
    return pl.pallas_call(
        fetch_kernel,
        in_specs=[pl.BlockSpec(memory_space=pl.ANY)] * 2,
        out_specs=pl.BlockSpec(memory_space=pltpu.VMEM),
        out_shape=pltpu.VMEM(weight.shape, weight.dtype),
        scratch_shapes=[pltpu.SemaphoreType.DMA],
        compiler_params=pltpu.CompilerParams(vmem_limit_bytes=FETCH_LIMIT),
        cost_estimate=pl.CostEstimate(
            flops=0, bytes_accessed=2 * weight.size, transcendentals=0
        ),
    )(in_hbm(weight), after)


def hidden_kernel(first_ref, second_ref, w_hbm, hidden_ref, w_ref, sems):
    experts, _, sliver, model_width = w_hbm.shape
    half = model_width // 2
    depth = model_width // PIECES

    def copy(slot, piece):
        columns = pl.ds(piece * depth, depth)
        return pltpu.make_async_copy(
            w_hbm.at[slot, :, :, columns], w_ref.at[slot, :, :, columns], sems.at[slot, piece]
        )

    @pl.when(pl.program_id(0) == 0)
    def start():
        for slot in range(experts):
            for piece in range(PIECES):
                copy(slot, piece).start()

    extra = first_ref[:, half:].astype(jnp.float32)
    lane = lax.broadcasted_iota(jnp.int32, extra.shape, 1)
    for slot in range(experts):
        pre = None
        for piece in range(PIECES):
            pl.when(pl.program_id(0) == 0)(copy(slot, piece).wait)
            at = piece * depth
            weights = w_ref[slot, :, :, at : at + depth].reshape(2 * sliver, depth)
            if at < half:
                rows = first_ref[:, at : at + depth]
            else:
                rows = second_ref[:, at - half : at - half + depth]
            product = lax.dot_general(
                weights, rows, (((1,), (1,)), ((), ())), preferred_element_type=jnp.float32
            )
            pre = product if pre is None else pre + product
        gate, up = pre[:sliver], pre[sliver:]
        hidden = (gate / (1.0 + jnp.exp(-gate)) * up).T
        mine = (lane == slot) | (lane == slot + experts) | (lane == slot + 2 * experts)
        weigh = jnp.sum(jnp.where(mine, extra, 0.0), axis=1, keepdims=True)
        hidden_ref[slot] = (hidden * weigh).astype(hidden_ref.dtype)


def hidden_of(first, second, gate_up_weight):
    experts, _, sliver, model_width = gate_up_weight.shape
    rows, half = second.shape
    row_block = min(ROW_BLOCK, rows)
    if rows == row_block:
        first, second = resident(first), resident(second)
        row_specs = [pl.BlockSpec(memory_space=pltpu.VMEM)] * 2
    else:
        row_specs = [
            pl.BlockSpec((row_block, first.shape[1]), lambda r: (r, 0)),
            pl.BlockSpec((row_block, half), lambda r: (r, 0)),
        ]
    return pl.pallas_call(
        hidden_kernel,
        grid=(rows // row_block,),
        in_specs=row_specs + [pl.BlockSpec(memory_space=pl.ANY)],
        out_specs=pl.BlockSpec((experts, row_block, sliver), lambda r: (0, r, 0)),
        out_shape=jax.ShapeDtypeStruct((experts, rows, sliver), jnp.bfloat16),
        scratch_shapes=[
            pltpu.VMEM(gate_up_weight.shape, gate_up_weight.dtype),
            pltpu.SemaphoreType.DMA((experts, PIECES)),
        ],
        compiler_params=pltpu.CompilerParams(vmem_limit_bytes=HIDDEN_LIMIT),
        cost_estimate=pl.CostEstimate(
            flops=4 * rows * experts * sliver * model_width,
            bytes_accessed=2 * (gate_up_weight.size + rows * model_width),
            transcendentals=rows * experts * sliver,
        ),
    )(first, second, in_hbm(gate_up_weight))


def down_kernel(part, hidden_ref, w_ref, out_ref):
    experts, _, sliver = hidden_ref.shape
    columns = out_ref.shape[1]
    block = next(size for size in (512, 384, 256, 128, columns) if columns % size == 0)

    def one_block(step, carry):
        at = pl.multiple_of(step * block, block)
        taken = pl.ds(pl.multiple_of(part * columns + step * block, block), block)
        hidden = jnp.concatenate([hidden_ref[slot] for slot in range(experts)], axis=1)
        weights = w_ref[:, :, taken].reshape(experts * sliver, block)
        out_ref[:, pl.ds(at, block)] = jnp.dot(
            hidden, weights, preferred_element_type=jnp.float32
        ).astype(out_ref.dtype)
        return carry

    lax.fori_loop(0, columns // block, one_block, 0)


def down_of(hidden, down_weight, part, columns):
    experts, rows, sliver = hidden.shape
    row_block = min(ROW_BLOCK, rows)

    def kernel(*refs):
        down_kernel(part, *refs)

    return pl.pallas_call(
        kernel,
        grid=(rows // row_block,),
        in_specs=[
            pl.BlockSpec((experts, row_block, sliver), lambda r: (0, r, 0)),
            pl.BlockSpec(memory_space=pltpu.VMEM),
        ],
        out_specs=pl.BlockSpec((row_block, columns), lambda r: (r, 0)),
        out_shape=jax.ShapeDtypeStruct((rows, columns), jnp.bfloat16),
        compiler_params=pltpu.CompilerParams(vmem_limit_bytes=DOWN_LIMIT),
        cost_estimate=pl.CostEstimate(
            flops=2 * rows * experts * sliver * columns,
            bytes_accessed=2 * (experts * sliver * columns + rows * experts * sliver + rows * columns),
            transcendentals=0,
        ),
    )(hidden, down_weight)


def local(
    tokens, gate_up_weight, down_weight, expert_ids, slot_ids, gate_values, old_place, new_place
):
    model_width = tokens.shape[1]
    rows = tokens.shape[0]
    half = model_width // 2
    ways = {name: lax.axis_size(name) for name in AXES}
    cores = 2 if ways["shard"] % 2 == 0 else 1
    x_digits = digits_of("dp", ways["dp"])
    z_digits = digits_of("expert", ways["expert"])
    y_digits = digits_of("shard", ways["shard"], cores)
    core_digits = [Digit("shard", ways["shard"], 1, cores)]
    dim_order = core_digits + x_digits[::-1] + y_digits[::-1] + z_digits[::-1]
    routes = [z_digits + y_digits + x_digits, z_digits + x_digits + y_digits]

    coefficients = slot_coefficients(expert_ids, gate_values, old_place, new_place)
    extra = jnp.concatenate(split_exact(coefficients), axis=1)
    extra = jnp.pad(extra, ((0, 0), (0, -extra.shape[1] % LANES)))
    parts = [
        jnp.concatenate([tokens[:, :half], extra], axis=1),
        tokens[:, half:],
    ]
    blocks, held = list(parts), [[], []]
    last = len(routes[0]) - 1
    for step in range(last + 2):
        if step == last:
            before_last = blocks[0]
        if step == last + 1:
            blocks[1], down_weight = lax.optimization_barrier(
                (blocks[1], fetched(down_weight, before_last))
            )
        for number in (1, 0):
            digit = (routes[number] + core_digits)[step]
            dim = sum(dim_order.index(other) < dim_order.index(digit) for other in held[number])
            blocks[number] = digit.gather(blocks[number], dim)
            held[number].append(digit)
    gathered = [block.reshape(-1, part.shape[1]) for block, part in zip(blocks, parts)]
    hidden = hidden_of(gathered[0], gathered[1], gate_up_weight)
    down_weight = resident(down_weight)
    results = []
    for number, route in enumerate(routes):
        block = down_of(hidden, down_weight, number, half)
        block = block.reshape([digit.size for digit in dim_order] + [rows, half])
        held = list(dim_order)
        for digit in core_digits + route[::-1]:
            block = digit.reduce(block, held.index(digit))
            held.remove(digit)
        results.append(block)
    return jnp.concatenate(results, axis=1)


def solution(mesh):
    in_specs = (
        P(AXES, None),
        P(None, None, AXES, None),
        P(None, AXES, None),
        P(AXES, None),
        P(AXES, None),
        P(AXES, None),
        P(),
        P(),
    )
    return jax.shard_map(
        local, mesh=mesh, in_specs=in_specs, out_specs=P(AXES, None), check_vma=False
    )
```

time: 88.9 us -> 90.4 us (1.017)
  Pallas kernels: 20.9 us -> 27 us
  waiting for transfers between devices: 35.1 us -> 30.8 us
    pallas_call x3 -> x4, Pallas kernels: 20.9 us -> 27 us  [the longest x1 17.1 us: hidden_of(): pl.pallas_call(hidden_kernel, grid=(rows // row_block,), in_specs=row_spe...]
    ppermute x20, waiting for transfers between devices: 35.1 us -> 30.8 us  [shift(): return lax.ppermute(value, self.name, pairs)]
  transfers between devices with their start and end apart: 20 -> 20, of which waited for: 16 -> 17; matrix products, arithmetic and copies ran while one was open for 4% -> 4% of each run, Pallas kernels for 4% -> 8%
where the time goes in v4:
time: 90.4 us; the launch traced here: 90.1 us
  waiting for transfers between devices  30.8 us (34%)
  Pallas kernels  27 us (30%)
  starting transfers between devices  26.9 us (30%)
  other arithmetic  3.74 us (4%)
  local copies, waits for them, and re-layouts  1.41 us (2%)
    ppermute x20, waiting for transfers between devices, shift(): return lax.ppermute(value, self.name, pairs)  30.8 us
    ppermute x20, starting transfers between devices, shift(): return lax.ppermute(value, self.name, pairs)  26.9 us
    pallas_call x1, Pallas kernels, hidden_of(): pl.pallas_call(hidden_kernel, grid=(rows // row_block,), in_specs=row_spe...  17.1 us
    pallas_call x2, Pallas kernels, down_of(): pl.pallas_call(kernel, grid=(rows // row_block,), in_specs=[pl.BlockSpec(...  5.32 us
    pallas_call x1, Pallas kernels, fetched(): pl.pallas_call(fetch_kernel, in_specs=[pl.BlockSpec(memory_space=pl.ANY)]...  4.58 us
  transfers between devices with their start and end apart: 20, of which 17 were waited for; matrix products, arithmetic and copies ran while one was open for 4% of the time, Pallas kernels for 8%

profile of v4, /device:TPU:0, one launch (start us, length us, event | category | flops | bytes accessed | tf_op | source)
XLA Modules:
  0.0 90.1 jit_solution(6403330237734572305)
XLA Ops:
  0.0 0.8 slice_bitcast_fusion.16
  0.8 4.1 %collective-permute-start.5 = (bf16[8,3072]{1,0:T(8,128)(2,1)S(1)}, bf16[8,3072]{1,0:T(8,128)(2,1)S(1)}, u32[]{:S(2)}, u32[]{:S(2)}) collective-permute-start(bf16[8,3072]{1,0:T(8,128)(2,1)S(1)} %get-tuple-element.28), channel_id=1, source_target_pairs={{0,8},{4,12},{8,0},{12,4},{1,9},{5,13},{9,1},{13,5},{2,10},{6,14},... | collective-permute-start | bytes 147464 | tf_op jit(solution)/shard_map/ppermute | solution.py:43
  4.9 0.7 select_reduce_fusion
  5.6 0.7 compare_convert_fusion
  6.7 0.8 collective-permute-done.5
  7.6 1.9 %collective-permute-start.6 = (bf16[2,8,3072]{2,1,0:T(8,128)(2,1)S(1)}, bf16[2,8,3072]{2,1,0:T(8,128)(2,1)S(1)}, u32[]{:S(2)}, u32[]{:S(2)}) collective-permute-start(bf16[2,8,3072]{2,1,0:T(8,128)(2,1)S(1)} %get-tuple-element.26), channel_id=1, source_target_pairs={{0,4},{4,0},{8,12},{12,8},{1,5},{5,1},{9,13},{13,9},{2,6},{6,2},{1... | collective-permute-start | bytes 294920 | tf_op jit(solution)/shard_map/ppermute | solution.py:43
  9.4 2.6 %collective-permute-done = bf16[8,3200]{1,0:T(8,128)(2,1)S(1)} collective-permute-done((bf16[8,3200]{1,0:T(8,128)(2,1)S(1)}, bf16[8,3200]{1,0:T(8,128)(2,1)S(1)}, u32[]{:S(2)}, u32[]{:S(2)}) %collective-permute-start) | collective-permute-done | bytes 51232 | tf_op jit(solution)/shard_map/ppermute | solution.py:43
  12.0 1.6 %collective-permute-start.1 = (bf16[2,8,3200]{2,1,0:T(8,128)(2,1)S(1)}, bf16[2,8,3200]{2,1,0:T(8,128)(2,1)S(1)}, u32[]{:S(2)}, u32[]{:S(2)}) collective-permute-start(bf16[2,8,3200]{2,1,0:T(8,128)(2,1)S(1)} %get-tuple-element.24), channel_id=1, source_target_pairs={{0,4},{4,0},{8,12},{12,8},{1,5},{5,1},{9,13},{13,9},{2,6},{6,2},{1... | collective-permute-start | bytes 307208 | tf_op jit(solution)/shard_map/ppermute | solution.py:43
  13.6 1.6 %collective-permute-start.7 = (bf16[2,2,8,3072]{3,2,1,0:T(8,128)(2,1)S(1)}, bf16[2,2,8,3072]{3,2,1,0:T(8,128)(2,1)S(1)}, u32[]{:S(2)}, u32[]{:S(2)}) collective-permute-start(bf16[2,2,8,3072]{3,2,1,0:T(8,128)(2,1)S(1)} %get-tuple-element.22), channel_id=1, source_target_pairs={{0,16},{16,0},{1,17},{17,1},{2,18},{18,2},{3,19},{19,3},{4,20},{20... | collective-permute-start | bytes 589832 | tf_op jit(solution)/shard_map/ppermute | solution.py:43
  15.2 1.6 %collective-permute-done.1 = bf16[2,8,3200]{2,1,0:T(8,128)(2,1)S(1)} collective-permute-done((bf16[2,8,3200]{2,1,0:T(8,128)(2,1)S(1)}, bf16[2,8,3200]{2,1,0:T(8,128)(2,1)S(1)}, u32[]{:S(2)}, u32[]{:S(2)}) %collective-permute-start.1) | collective-permute-done | bytes 102432 | tf_op jit(solution)/shard_map/ppermute | solution.py:43
  16.8 1.5 %collective-permute-start.2 = (bf16[2,2,8,3200]{3,2,1,0:T(8,128)(2,1)S(1)}, bf16[2,2,8,3200]{3,2,1,0:T(8,128)(2,1)S(1)}, u32[]{:S(2)}, u32[]{:S(2)}) collective-permute-start(bf16[2,2,8,3200]{3,2,1,0:T(8,128)(2,1)S(1)} %get-tuple-element.20), channel_id=1, source_target_pairs={{0,2},{1,3},{2,0},{3,1},{4,6},{5,7},{6,4},{7,5},{8,10},{9,11},{10,... | collective-permute-start | bytes 614408 | tf_op jit(solution)/shard_map/ppermute | solution.py:43
  18.3 1.1 %collective-permute-done.7 = bf16[2,2,8,3072]{3,2,1,0:T(8,128)(2,1)S(1)} collective-permute-done((bf16[2,2,8,3072]{3,2,1,0:T(8,128)(2,1)S(1)}, bf16[2,2,8,3072]{3,2,1,0:T(8,128)(2,1)S(1)}, u32[]{:S(2)}, u32[]{:S(2)}) %collective-permute-start.7) | collective-permute-done | bytes 196640 | tf_op jit(solution)/shard_map/ppermute | solution.py:43
  19.4 1.6 %collective-permute-start.8 = (bf16[2,2,2,8,3072]{4,3,2,1,0:T(8,128)(2,1)S(1)}, bf16[2,2,2,8,3072]{4,3,2,1,0:T(8,128)(2,1)S(1)}, u32[]{:S(2)}, u32[]{:S(2)}) collective-permute-start(bf16[2,2,2,8,3072]{4,3,2,1,0:T(8,128)(2,1)S(1)} %get-tuple-element.18), channel_id=1, source_target_pairs={{0,2},{1,3},{2,0},{3,1},{4,6},{5,7},{6,4},{7,5},{8,10},{9,11},{10,... | collective-permute-start | bytes 1179656 | tf_op jit(solution)/shard_map/ppermute | solution.py:43
  21.0 3.8 %collective-permute-done.2 = bf16[2,2,8,3200]{3,2,1,0:T(8,128)(2,1)S(1)} collective-permute-done((bf16[2,2,8,3200]{3,2,1,0:T(8,128)(2,1)S(1)}, bf16[2,2,8,3200]{3,2,1,0:T(8,128)(2,1)S(1)}, u32[]{:S(2)}, u32[]{:S(2)}) %collective-permute-start.2) | collective-permute-done | bytes 204832 | tf_op jit(solution)/shard_map/ppermute | solution.py:43
  24.9 1.5 %collective-permute-start.3 = (bf16[2,2,2,8,3200]{4,3,2,1,0:T(8,128)(2,1)S(1)}, bf16[2,2,2,8,3200]{4,3,2,1,0:T(8,128)(2,1)S(1)}, u32[]{:S(2)}, u32[]{:S(2)}) collective-permute-start(bf16[2,2,2,8,3200]{4,3,2,1,0:T(8,128)(2,1)S(1)} %get-tuple-element.16.after_ref), channel_id=1, source_target_pairs={{0,16},{16,0},{1,17},{17,1},{2,18},{18,2},{3,19},{19,3},{4,20},{20... | collective-permute-start | bytes 1228808 | tf_op jit(solution)/shard_map/ppermute | solution.py:43
  26.4 4.6 %shard_map.73.refs_1_ = bf16[4,256,6144]{2,1,0:T(8,128)(2,1)S(1)} custom-call(bf16[4,256,6144]{2,1,0:T(8,128)(2,1)} %w_ref.1, bf16[2,2,2,8,3200]{4,3,2,1,0:T(8,128)(2,1)S(1)} %get-tuple-element.16.after_ref), custom_call_target="tpu_custom_call" | custom-call | bytes 12582912 | tf_op jit(solution)/shard_map/pallas_call | solution.py:82
  31.1 1.8 %collective-permute-done.3 = bf16[2,2,2,8,3200]{4,3,2,1,0:T(8,128)(2,1)S(1)} collective-permute-done((bf16[2,2,2,8,3200]{4,3,2,1,0:T(8,128)(2,1)S(1)}, bf16[2,2,2,8,3200]{4,3,2,1,0:T(8,128)(2,1)S(1)}, u32[]{:S(2)}, u32[]{:S(2)}) %collective-permute-start.3) | collective-permute-done | bytes 409632 | tf_op jit(solution)/shard_map/ppermute | solution.py:43
  32.9 0.1 fusion.24
  33.1 0.3 collective-permute-done.9
  33.4 0.1 pad_maximum_fusion.1
  33.6 0.1 copy.15
  33.7 1.7 %collective-permute-done.4 = bf16[2,2,2,2,8,3200]{5,4,3,2,1,0:T(8,128)(2,1)S(1)} collective-permute-done((bf16[2,2,2,2,8,3200]{5,4,3,2,1,0:T(8,128)(2,1)S(1)}, bf16[2,2,2,2,8,3200]{5,4,3,2,1,0:T(8,128)(2,1)S(1)}, u32[]{:S(2)}, u32[]{:S(2)}) %collective-permute-start.4) | collective-permute-done | bytes 819232 | tf_op jit(solution)/shard_map/ppermute | solution.py:43
  35.4 0.2 pad_maximum_fusion
  35.6 17.1 %shard_map.74.refs_0_ = bf16[4,256,256]{2,1,0:T(8,128)(2,1)S(1)} custom-call(bf16[256,3200]{1,0:T(8,128)(2,1)S(1)} %bitcast.93, bf16[256,3072]{1,0:T(8,128)(2,1)S(1)} %bitcast.94, bf16[4,2,256,6144]{3,2,1,0:T(8,128)(2,1)} %w_hbm.1), custom_call_target="tpu_custom_call" | custom-call | flops 6442450944 | bytes 28311552 | tf_op jit(solution)/shard_map/pallas_call | solution.py:147
  52.7 2.7 %shard_map.76 = bf16[256,3072]{1,0:T(8,128)(2,1)S(1)} custom-call(bf16[4,256,256]{2,1,0:T(8,128)(2,1)S(1)} %shard_map.74.refs_0_, bf16[4,256,6144]{2,1,0:T(8,128)(2,1)S(1)} %shard_map.73.refs_1_), custom_call_target="tpu_custom_call" | custom-call | flops 1610612736 | bytes 8388608 | tf_op jit(solution)/shard_map/pallas_call | solution.py:191
  55.6 0.2 collective-permute-start.15
  55.8 2.7 %shard_map.75 = bf16[256,3072]{1,0:T(8,128)(2,1)S(1)} custom-call(bf16[4,256,256]{2,1,0:T(8,128)(2,1)S(1)} %shard_map.74.refs_0_, bf16[4,256,6144]{2,1,0:T(8,128)(2,1)S(1)} %shard_map.73.refs_1_), custom_call_target="tpu_custom_call" | custom-call | flops 1610612736 | bytes 8388608 | tf_op jit(solution)/shard_map/pallas_call | solution.py:191
  58.5 0.5 collective-permute-start.10
  59.0 0.2 fusion.1
  59.2 1.5 %collective-permute-start.16 = (bf16[2,2,2,8,3072]{4,3,2,1,0:T(8,128)(2,1)S(1)}, bf16[2,2,2,8,3072]{4,3,2,1,0:T(8,128)(2,1)S(1)}, u32[]{:S(2)}, u32[]{:S(2)}) collective-permute-start(bf16[2,2,2,8,3072]{4,3,2,1,0:T(8,128)(2,1)S(1)} %slice_bitcast_fusion), channel_id=1, source_target_pairs={{0,2},{1,3},{2,0},{3,1},{4,6},{5,7},{6,4},{7,5},{8,10},{9,11},{10,... | collective-permute-start | bytes 1179656 | tf_op jit(solution)/shard_map/ppermute | solution.py:43
  60.8 0.2 collective-permute-done.10
  60.9 0.2 fusion
  61.2 1.5 %collective-permute-start.11 = (bf16[2,2,2,8,3072]{4,3,2,1,0:T(8,128)(2,1)S(1)}, bf16[2,2,2,8,3072]{4,3,2,1,0:T(8,128)(2,1)S(1)}, u32[]{:S(2)}, u32[]{:S(2)}) collective-permute-start(bf16[2,2,2,8,3072]{4,3,2,1,0:T(8,128)(2,1)S(1)} %slice_bitcast_fusion.2), channel_id=1, source_target_pairs={{0,16},{16,0},{1,17},{17,1},{2,18},{18,2},{3,19},{19,3},{4,20},{20... | collective-permute-start | bytes 1179656 | tf_op jit(solution)/shard_map/ppermute | solution.py:43
  62.7 7.8 %collective-permute-done.16 = bf16[2,2,2,8,3072]{4,3,2,1,0:T(8,128)(2,1)S(1)} collective-permute-done((bf16[2,2,2,8,3072]{4,3,2,1,0:T(8,128)(2,1)S(1)}, bf16[2,2,2,8,3072]{4,3,2,1,0:T(8,128)(2,1)S(1)}, u32[]{:S(2)}, u32[]{:S(2)}) %collective-permute-start.16) | collective-permute-done | bytes 393248 | tf_op jit(solution)/shard_map/ppermute | solution.py:43
  70.6 1.5 %collective-permute-start.17 = (bf16[2,2,8,3072]{3,2,1,0:T(8,128)(2,1)S(1)}, bf16[2,2,8,3072]{3,2,1,0:T(8,128)(2,1)S(1)}, u32[]{:S(2)}, u32[]{:S(2)}) collective-permute-start(bf16[2,2,8,3072]{3,2,1,0:T(8,128)(2,1)S(1)} %slice_bitcast_fusion.4), channel_id=1, source_target_pairs={{0,16},{16,0},{1,17},{17,1},{2,18},{18,2},{3,19},{19,3},{4,20},{20... | collective-permute-start | bytes 589832 | tf_op jit(solution)/shard_map/ppermute | solution.py:43
  72.1 0.6 collective-permute-done.11
  72.8 1.5 %collective-permute-start.12 = (bf16[2,2,8,3072]{3,2,1,0:T(8,128)(2,1)S(1)}, bf16[2,2,8,3072]{3,2,1,0:T(8,128)(2,1)S(1)}, u32[]{:S(2)}, u32[]{:S(2)}) collective-permute-start(bf16[2,2,8,3072]{3,2,1,0:T(8,128)(2,1)S(1)} %slice_bitcast_fusion.6), channel_id=1, source_target_pairs={{0,2},{1,3},{2,0},{3,1},{4,6},{5,7},{6,4},{7,5},{8,10},{9,11},{10,... | collective-permute-start | bytes 589832 | tf_op jit(solution)/shard_map/ppermute | solution.py:43
  74.3 2.6 %collective-permute-done.17 = bf16[2,2,8,3072]{3,2,1,0:T(8,128)(2,1)S(1)} collective-permute-done((bf16[2,2,8,3072]{3,2,1,0:T(8,128)(2,1)S(1)}, bf16[2,2,8,3072]{3,2,1,0:T(8,128)(2,1)S(1)}, u32[]{:S(2)}, u32[]{:S(2)}) %collective-permute-start.17) | collective-permute-done | bytes 196640 | tf_op jit(solution)/shard_map/ppermute | solution.py:43
  76.9 1.6 %collective-permute-start.18 = (bf16[2,8,3072]{2,1,0:T(8,128)(2,1)S(1)}, bf16[2,8,3072]{2,1,0:T(8,128)(2,1)S(1)}, u32[]{:S(2)}, u32[]{:S(2)}) collective-permute-start(bf16[2,8,3072]{2,1,0:T(8,128)(2,1)S(1)} %slice_bitcast_fusion.8), channel_id=1, source_target_pairs={{0,4},{4,0},{8,12},{12,8},{1,5},{5,1},{9,13},{13,9},{2,6},{6,2},{1... | collective-permute-start | bytes 294920 | tf_op jit(solution)/shard_map/ppermute | solution.py:43
  78.5 0.7 collective-permute-done.12
  79.2 1.6 %collective-permute-start.13 = (bf16[2,8,3072]{2,1,0:T(8,128)(2,1)S(1)}, bf16[2,8,3072]{2,1,0:T(8,128)(2,1)S(1)}, u32[]{:S(2)}, u32[]{:S(2)}) collective-permute-start(bf16[2,8,3072]{2,1,0:T(8,128)(2,1)S(1)} %slice_bitcast_fusion.10), channel_id=1, source_target_pairs={{0,4},{4,0},{8,12},{12,8},{1,5},{5,1},{9,13},{13,9},{2,6},{6,2},{1... | collective-permute-start | bytes 294920 | tf_op jit(solution)/shard_map/ppermute | solution.py:43
  80.8 1.8 %collective-permute-done.18 = bf16[2,8,3072]{2,1,0:T(8,128)(2,1)S(1)} collective-permute-done((bf16[2,8,3072]{2,1,0:T(8,128)(2,1)S(1)}, bf16[2,8,3072]{2,1,0:T(8,128)(2,1)S(1)}, u32[]{:S(2)}, u32[]{:S(2)}) %collective-permute-start.18) | collective-permute-done | bytes 98336 | tf_op jit(solution)/shard_map/ppermute | solution.py:43
  82.6 1.5 %collective-permute-start.19 = (bf16[8,3072]{1,0:T(8,128)(2,1)S(1)}, bf16[8,3072]{1,0:T(8,128)(2,1)S(1)}, u32[]{:S(2)}, u32[]{:S(2)}) collective-permute-start(bf16[8,3072]{1,0:T(8,128)(2,1)S(1)} %slice_bitcast_fusion.12), channel_id=1, source_target_pairs={{0,8},{4,12},{8,0},{12,4},{1,9},{5,13},{9,1},{13,5},{2,10},{6,14},... | collective-permute-start | bytes 147464 | tf_op jit(solution)/shard_map/ppermute | solution.py:43
  84.2 0.2 collective-permute-done.13
  84.4 1.6 %collective-permute-start.14 = (bf16[8,3072]{1,0:T(8,128)(2,1)S(1)}, bf16[8,3072]{1,0:T(8,128)(2,1)S(1)}, u32[]{:S(2)}, u32[]{:S(2)}) collective-permute-start(bf16[8,3072]{1,0:T(8,128)(2,1)S(1)} %slice_bitcast_fusion.14), channel_id=1, source_target_pairs={{0,8},{4,12},{8,0},{12,4},{1,9},{5,13},{9,1},{13,5},{2,10},{6,14},... | collective-permute-start | bytes 147464 | tf_op jit(solution)/shard_map/ppermute | solution.py:43
  86.0 2.8 %collective-permute-done.19 = bf16[8,3072]{1,0:T(8,128)(2,1)S(1)} collective-permute-done((bf16[8,3072]{1,0:T(8,128)(2,1)S(1)}, bf16[8,3072]{1,0:T(8,128)(2,1)S(1)}, u32[]{:S(2)}, u32[]{:S(2)}) %collective-permute-start.19) | collective-permute-done | bytes 49184 | tf_op jit(solution)/shard_map/ppermute | solution.py:43
  88.8 0.7 collective-permute-done.14
  89.5 0.6 pad_maximum_fusion.10
  (37 shorter events, 1.5 us)
Async XLA Ops:
  0.8 6.7 %collective-permute-start.5 = (bf16[8,3072]{1,0:T(8,128)(2,1)S(1)}, bf16[8,3072]{1,0:T(8,128)(2,1)S(1)}, u32[]{:S(2)}, u32[]{:S(2)}) collective-permute-start(bf16[8,3072]{1,0:T(8,128)(2,1)S(1)} %get-tuple-element.28), channel_id=1, source_target_pairs={{0,8},{4,12},{8,0},{12,4},{1,9},{5,13},{9,1},{13,5},{2,10},{6,14},... | collective-permute-start | bytes 147464 | tf_op jit(solution)/shard_map/ppermute | solution.py:43
  6.7 5.3 %collective-permute-start = (bf16[8,3200]{1,0:T(8,128)(2,1)S(1)}, bf16[8,3200]{1,0:T(8,128)(2,1)S(1)}, u32[]{:S(2)}, u32[]{:S(2)}) collective-permute-start(bf16[8,3200]{1,0:T(8,128)(2,1)S(1)} %get-tuple-element.31), channel_id=1, source_target_pairs={{0,8},{4,12},{8,0},{12,4},{1,9},{5,13},{9,1},{13,5},{2,10},{6,14},... | collective-permute-start | bytes 153608 | tf_op jit(solution)/shard_map/ppermute | solution.py:43
  7.6 6.0 %collective-permute-start.6 = (bf16[2,8,3072]{2,1,0:T(8,128)(2,1)S(1)}, bf16[2,8,3072]{2,1,0:T(8,128)(2,1)S(1)}, u32[]{:S(2)}, u32[]{:S(2)}) collective-permute-start(bf16[2,8,3072]{2,1,0:T(8,128)(2,1)S(1)} %get-tuple-element.26), channel_id=1, source_target_pairs={{0,4},{4,0},{8,12},{12,8},{1,5},{5,1},{9,13},{13,9},{2,6},{6,2},{1... | collective-permute-start | bytes 294920 | tf_op jit(solution)/shard_map/ppermute | solution.py:43
  12.0 4.7 %collective-permute-start.1 = (bf16[2,8,3200]{2,1,0:T(8,128)(2,1)S(1)}, bf16[2,8,3200]{2,1,0:T(8,128)(2,1)S(1)}, u32[]{:S(2)}, u32[]{:S(2)}) collective-permute-start(bf16[2,8,3200]{2,1,0:T(8,128)(2,1)S(1)} %get-tuple-element.24), channel_id=1, source_target_pairs={{0,4},{4,0},{8,12},{12,8},{1,5},{5,1},{9,13},{13,9},{2,6},{6,2},{1... | collective-permute-start | bytes 307208 | tf_op jit(solution)/shard_map/ppermute | solution.py:43
  13.6 5.7 %collective-permute-start.7 = (bf16[2,2,8,3072]{3,2,1,0:T(8,128)(2,1)S(1)}, bf16[2,2,8,3072]{3,2,1,0:T(8,128)(2,1)S(1)}, u32[]{:S(2)}, u32[]{:S(2)}) collective-permute-start(bf16[2,2,8,3072]{3,2,1,0:T(8,128)(2,1)S(1)} %get-tuple-element.22), channel_id=1, source_target_pairs={{0,16},{16,0},{1,17},{17,1},{2,18},{18,2},{3,19},{19,3},{4,20},{20... | collective-permute-start | bytes 589832 | tf_op jit(solution)/shard_map/ppermute | solution.py:43
  16.8 8.0 %collective-permute-start.2 = (bf16[2,2,8,3200]{3,2,1,0:T(8,128)(2,1)S(1)}, bf16[2,2,8,3200]{3,2,1,0:T(8,128)(2,1)S(1)}, u32[]{:S(2)}, u32[]{:S(2)}) collective-permute-start(bf16[2,2,8,3200]{3,2,1,0:T(8,128)(2,1)S(1)} %get-tuple-element.20), channel_id=1, source_target_pairs={{0,2},{1,3},{2,0},{3,1},{4,6},{5,7},{6,4},{7,5},{8,10},{9,11},{10,... | collective-permute-start | bytes 614408 | tf_op jit(solution)/shard_map/ppermute | solution.py:43
  19.4 11.6 %collective-permute-start.8 = (bf16[2,2,2,8,3072]{4,3,2,1,0:T(8,128)(2,1)S(1)}, bf16[2,2,2,8,3072]{4,3,2,1,0:T(8,128)(2,1)S(1)}, u32[]{:S(2)}, u32[]{:S(2)}) collective-permute-start(bf16[2,2,2,8,3072]{4,3,2,1,0:T(8,128)(2,1)S(1)} %get-tuple-element.18), channel_id=1, source_target_pairs={{0,2},{1,3},{2,0},{3,1},{4,6},{5,7},{6,4},{7,5},{8,10},{9,11},{10,... | collective-permute-start | bytes 1179656 | tf_op jit(solution)/shard_map/ppermute | solution.py:43
  24.9 8.0 %collective-permute-start.3 = (bf16[2,2,2,8,3200]{4,3,2,1,0:T(8,128)(2,1)S(1)}, bf16[2,2,2,8,3200]{4,3,2,1,0:T(8,128)(2,1)S(1)}, u32[]{:S(2)}, u32[]{:S(2)}) collective-permute-start(bf16[2,2,2,8,3200]{4,3,2,1,0:T(8,128)(2,1)S(1)} %get-tuple-element.16.after_ref), channel_id=1, source_target_pairs={{0,16},{16,0},{1,17},{17,1},{2,18},{18,2},{3,19},{19,3},{4,20},{20... | collective-permute-start | bytes 1228808 | tf_op jit(solution)/shard_map/ppermute | solution.py:43
  31.1 2.4 %collective-permute-start.9 = (bf16[2,2,2,2,8,3072]{5,4,3,2,0,1:T(8,128)(2,1)S(1)}, bf16[2,2,2,2,8,3072]{5,4,3,2,0,1:T(8,128)(2,1)S(1)}, u32[]{:S(2)}, u32[]{:S(2)}) collective-permute-start(bf16[2,2,2,2,8,3072]{5,4,3,2,0,1:T(8,128)(2,1)S(1)} %pad_maximum_fusion.3), channel_id=1, source_target_pairs={{0,1},{1,0},{2,3},{3,2},{4,5},{5,4},{6,7},{7,6},{8,9},{9,8},{10,11... | collective-permute-start | bytes 2359304 | tf_op jit(solution)/shard_map/ppermute | solution.py:43
  33.0 2.4 %collective-permute-start.4 = (bf16[2,2,2,2,8,3200]{5,4,3,2,1,0:T(8,128)(2,1)S(1)}, bf16[2,2,2,2,8,3200]{5,4,3,2,1,0:T(8,128)(2,1)S(1)}, u32[]{:S(2)}, u32[]{:S(2)}) collective-permute-start(bf16[2,2,2,2,8,3200]{5,4,3,2,1,0:T(8,128)(2,1)S(1)} %get-tuple-element.14), channel_id=1, source_target_pairs={{0,1},{1,0},{2,3},{3,2},{4,5},{5,4},{6,7},{7,6},{8,9},{9,8},{10,11... | collective-permute-start | bytes 2457608 | tf_op jit(solution)/shard_map/ppermute | solution.py:43
  55.6 3.4 %collective-permute-start.15 = (bf16[2,2,2,2,8,3072]{5,4,3,2,0,1:T(8,128)(2,1)S(1)}, bf16[2,2,2,2,8,3072]{5,4,3,2,0,1:T(8,128)(2,1)S(1)}, u32[]{:S(2)}, u32[]{:S(2)}) collective-permute-start(bf16[2,2,2,2,8,3072]{5,4,3,2,0,1:T(8,128)(2,1)S(1)} %copy.16), channel_id=1, source_target_pairs={{0,1},{1,0},{2,3},{3,2},{4,5},{5,4},{6,7},{7,6},{8,9},{9,8},{10,11... | collective-permute-start | bytes 2359304 | tf_op jit(solution)/shard_map/ppermute | solution.py:43
  58.5 2.4 %collective-permute-start.10 = (bf16[2,2,2,2,8,3072]{5,4,3,2,1,0:T(8,128)(2,1)S(1)}, bf16[2,2,2,2,8,3072]{5,4,3,2,1,0:T(8,128)(2,1)S(1)}, u32[]{:S(2)}, u32[]{:S(2)}) collective-permute-start(bf16[2,2,2,2,8,3072]{5,4,3,2,1,0:T(8,128)(2,1)S(1)} %bitcast.100), channel_id=1, source_target_pairs={{0,1},{1,0},{2,3},{3,2},{4,5},{5,4},{6,7},{7,6},{8,9},{9,8},{10,11... | collective-permute-start | bytes 2359304 | tf_op jit(solution)/shard_map/ppermute | solution.py:43
  59.2 11.2 %collective-permute-start.16 = (bf16[2,2,2,8,3072]{4,3,2,1,0:T(8,128)(2,1)S(1)}, bf16[2,2,2,8,3072]{4,3,2,1,0:T(8,128)(2,1)S(1)}, u32[]{:S(2)}, u32[]{:S(2)}) collective-permute-start(bf16[2,2,2,8,3072]{4,3,2,1,0:T(8,128)(2,1)S(1)} %slice_bitcast_fusion), channel_id=1, source_target_pairs={{0,2},{1,3},{2,0},{3,1},{4,6},{5,7},{6,4},{7,5},{8,10},{9,11},{10,... | collective-permute-start | bytes 1179656 | tf_op jit(solution)/shard_map/ppermute | solution.py:43
  61.2 11.5 %collective-permute-start.11 = (bf16[2,2,2,8,3072]{4,3,2,1,0:T(8,128)(2,1)S(1)}, bf16[2,2,2,8,3072]{4,3,2,1,0:T(8,128)(2,1)S(1)}, u32[]{:S(2)}, u32[]{:S(2)}) collective-permute-start(bf16[2,2,2,8,3072]{4,3,2,1,0:T(8,128)(2,1)S(1)} %slice_bitcast_fusion.2), channel_id=1, source_target_pairs={{0,16},{16,0},{1,17},{17,1},{2,18},{18,2},{3,19},{19,3},{4,20},{20... | collective-permute-start | bytes 1179656 | tf_op jit(solution)/shard_map/ppermute | solution.py:43
  70.6 6.3 %collective-permute-start.17 = (bf16[2,2,8,3072]{3,2,1,0:T(8,128)(2,1)S(1)}, bf16[2,2,8,3072]{3,2,1,0:T(8,128)(2,1)S(1)}, u32[]{:S(2)}, u32[]{:S(2)}) collective-permute-start(bf16[2,2,8,3072]{3,2,1,0:T(8,128)(2,1)S(1)} %slice_bitcast_fusion.4), channel_id=1, source_target_pairs={{0,16},{16,0},{1,17},{17,1},{2,18},{18,2},{3,19},{19,3},{4,20},{20... | collective-permute-start | bytes 589832 | tf_op jit(solution)/shard_map/ppermute | solution.py:43
  72.8 6.4 %collective-permute-start.12 = (bf16[2,2,8,3072]{3,2,1,0:T(8,128)(2,1)S(1)}, bf16[2,2,8,3072]{3,2,1,0:T(8,128)(2,1)S(1)}, u32[]{:S(2)}, u32[]{:S(2)}) collective-permute-start(bf16[2,2,8,3072]{3,2,1,0:T(8,128)(2,1)S(1)} %slice_bitcast_fusion.6), channel_id=1, source_target_pairs={{0,2},{1,3},{2,0},{3,1},{4,6},{5,7},{6,4},{7,5},{8,10},{9,11},{10,... | collective-permute-start | bytes 589832 | tf_op jit(solution)/shard_map/ppermute | solution.py:43
  76.9 5.7 %collective-permute-start.18 = (bf16[2,8,3072]{2,1,0:T(8,128)(2,1)S(1)}, bf16[2,8,3072]{2,1,0:T(8,128)(2,1)S(1)}, u32[]{:S(2)}, u32[]{:S(2)}) collective-permute-start(bf16[2,8,3072]{2,1,0:T(8,128)(2,1)S(1)} %slice_bitcast_fusion.8), channel_id=1, source_target_pairs={{0,4},{4,0},{8,12},{12,8},{1,5},{5,1},{9,13},{13,9},{2,6},{6,2},{1... | collective-permute-start | bytes 294920 | tf_op jit(solution)/shard_map/ppermute | solution.py:43
  79.2 5.1 %collective-permute-start.13 = (bf16[2,8,3072]{2,1,0:T(8,128)(2,1)S(1)}, bf16[2,8,3072]{2,1,0:T(8,128)(2,1)S(1)}, u32[]{:S(2)}, u32[]{:S(2)}) collective-permute-start(bf16[2,8,3072]{2,1,0:T(8,128)(2,1)S(1)} %slice_bitcast_fusion.10), channel_id=1, source_target_pairs={{0,4},{4,0},{8,12},{12,8},{1,5},{5,1},{9,13},{13,9},{2,6},{6,2},{1... | collective-permute-start | bytes 294920 | tf_op jit(solution)/shard_map/ppermute | solution.py:43
  82.6 6.1 %collective-permute-start.19 = (bf16[8,3072]{1,0:T(8,128)(2,1)S(1)}, bf16[8,3072]{1,0:T(8,128)(2,1)S(1)}, u32[]{:S(2)}, u32[]{:S(2)}) collective-permute-start(bf16[8,3072]{1,0:T(8,128)(2,1)S(1)} %slice_bitcast_fusion.12), channel_id=1, source_target_pairs={{0,8},{4,12},{8,0},{12,4},{1,9},{5,13},{9,1},{13,5},{2,10},{6,14},... | collective-permute-start | bytes 147464 | tf_op jit(solution)/shard_map/ppermute | solution.py:43
  84.4 5.1 %collective-permute-start.14 = (bf16[8,3072]{1,0:T(8,128)(2,1)S(1)}, bf16[8,3072]{1,0:T(8,128)(2,1)S(1)}, u32[]{:S(2)}, u32[]{:S(2)}) collective-permute-start(bf16[8,3072]{1,0:T(8,128)(2,1)S(1)} %slice_bitcast_fusion.14), channel_id=1, source_target_pairs={{0,8},{4,12},{8,0},{12,4},{1,9},{5,13},{9,1},{13,5},{2,10},{6,14},... | collective-permute-start | bytes 147464 | tf_op jit(solution)/shard_map/ppermute | solution.py:43

commit v5 on v4

--- a/solution.py
+++ b/solution.py
@@ -8,9 +8,9 @@
 AXES = ("dp", "expert", "shard")
 LANES = 128
 ROW_BLOCK = 256
-PIECES = 4
+PIECES = 2
 FETCH_LIMIT = 1 * 2**20
-HIDDEN_LIMIT = 32 * 2**20
+GATE_UP_LIMIT = 24 * 2**20
 DOWN_LIMIT = 8 * 2**20
 
 
@@ -92,15 +92,20 @@
     )(in_hbm(weight), after)
 
 
-def hidden_kernel(first_ref, second_ref, w_hbm, hidden_ref, w_ref, sems):
-    experts, _, sliver, model_width = w_hbm.shape
-    half = model_width // 2
-    depth = model_width // PIECES
+def gate_up_kernel(part, rows_ref, *refs):
+    last = part == 0
+    if last:
+        sum_ref, w_hbm, out_ref, w_ref, turned_ref, sems = refs
+    else:
+        w_hbm, out_ref, w_ref, turned_ref, sems = refs
+    experts, _, sliver, half = w_ref.shape
+    depth = half // PIECES
 
     def copy(slot, piece):
-        columns = pl.ds(piece * depth, depth)
         return pltpu.make_async_copy(
-            w_hbm.at[slot, :, :, columns], w_ref.at[slot, :, :, columns], sems.at[slot, piece]
+            w_hbm.at[slot, :, :, pl.ds(part * half + piece * depth, depth)],
+            w_ref.at[slot, :, :, pl.ds(piece * depth, depth)],
+            sems.at[slot, piece],
         )
 
     @pl.when(pl.program_id(0) == 0)
@@ -109,64 +114,85 @@
             for piece in range(PIECES):
                 copy(slot, piece).start()
 
-    extra = first_ref[:, half:].astype(jnp.float32)
-    lane = lax.broadcasted_iota(jnp.int32, extra.shape, 1)
+    for piece in range(PIECES):
+        at = piece * depth
+        turned_ref[at : at + depth] = rows_ref[:, at : at + depth].T
+    if last:
+        extra = rows_ref[:, half:].astype(jnp.float32)
+        lane = lax.broadcasted_iota(jnp.int32, extra.shape, 1)
     for slot in range(experts):
-        pre = None
+        pre = sum_ref[slot] if last else None
         for piece in range(PIECES):
             pl.when(pl.program_id(0) == 0)(copy(slot, piece).wait)
             at = piece * depth
-            weights = w_ref[slot, :, :, at : at + depth].reshape(2 * sliver, depth)
-            if at < half:
-                rows = first_ref[:, at : at + depth]
-            else:
-                rows = second_ref[:, at - half : at - half + depth]
-            product = lax.dot_general(
-                weights, rows, (((1,), (1,)), ((), ())), preferred_element_type=jnp.float32
+            product = jnp.dot(
+                w_ref[slot, :, :, at : at + depth].reshape(2 * sliver, depth),
+                turned_ref[at : at + depth],
+                preferred_element_type=jnp.float32,
             )
             pre = product if pre is None else pre + product
+        if not last:
+            out_ref[slot] = pre
+            continue
         gate, up = pre[:sliver], pre[sliver:]
         hidden = (gate / (1.0 + jnp.exp(-gate)) * up).T
         mine = (lane == slot) | (lane == slot + experts) | (lane == slot + 2 * experts)
         weigh = jnp.sum(jnp.where(mine, extra, 0.0), axis=1, keepdims=True)
-        hidden_ref[slot] = (hidden * weigh).astype(hidden_ref.dtype)
-
-
-def hidden_of(first, second, gate_up_weight):
+        out_ref[slot] = (hidden * weigh).astype(out_ref.dtype)
+
+
+def gate_up_of(part, rows_of_part, sums, gate_up_weight):
     experts, _, sliver, model_width = gate_up_weight.shape
-    rows, half = second.shape
+    half = model_width // 2
+    rows, width = rows_of_part.shape
     row_block = min(ROW_BLOCK, rows)
-    if rows == row_block:
-        first, second = resident(first), resident(second)
-        row_specs = [pl.BlockSpec(memory_space=pltpu.VMEM)] * 2
+    whole = rows == row_block
+    operands = [rows_of_part] if sums is None else [rows_of_part, sums]
+    if whole:
+        operands = [resident(operand) for operand in operands]
+        specs = [pl.BlockSpec(memory_space=pltpu.VMEM)] * len(operands)
     else:
-        row_specs = [
-            pl.BlockSpec((row_block, first.shape[1]), lambda r: (r, 0)),
-            pl.BlockSpec((row_block, half), lambda r: (r, 0)),
-        ]
+        specs = [
+            pl.BlockSpec((row_block, width), lambda r: (r, 0)),
+            pl.BlockSpec((experts, 2 * sliver, row_block), lambda r: (0, 0, r)),
+        ][: len(operands)]
+    if sums is None:
+        out_spec = pl.BlockSpec((experts, 2 * sliver, row_block), lambda r: (0, 0, r))
+        out_shape = jax.ShapeDtypeStruct((experts, 2 * sliver, rows), jnp.float32)
+    else:
+        out_spec = pl.BlockSpec((experts, row_block, sliver), lambda r: (0, r, 0))
+        out_shape = jax.ShapeDtypeStruct((experts, rows, sliver), jnp.bfloat16)
+    if whole:
+        out_spec = pl.BlockSpec(memory_space=pltpu.VMEM)
+        out_shape = pltpu.VMEM(out_shape.shape, out_shape.dtype)
+
+    def kernel(*refs):
+        gate_up_kernel(part, *refs)
+
     return pl.pallas_call(
-        hidden_kernel,
+        kernel,
         grid=(rows // row_block,),
-        in_specs=row_specs + [pl.BlockSpec(memory_space=pl.ANY)],
-        out_specs=pl.BlockSpec((experts, row_block, sliver), lambda r: (0, r, 0)),
-        out_shape=jax.ShapeDtypeStruct((experts, rows, sliver), jnp.bfloat16),
+        in_specs=specs + [pl.BlockSpec(memory_space=pl.ANY)],
+        out_specs=out_spec,
+        out_shape=out_shape,
         scratch_shapes=[
-            pltpu.VMEM(gate_up_weight.shape, gate_up_weight.dtype),
+            pltpu.VMEM((experts, 2, sliver, half), gate_up_weight.dtype),
+            pltpu.VMEM((half, row_block), rows_of_part.dtype),
             pltpu.SemaphoreType.DMA((experts, PIECES)),
         ],
-        compiler_params=pltpu.CompilerParams(vmem_limit_bytes=HIDDEN_LIMIT),
+        compiler_params=pltpu.CompilerParams(vmem_limit_bytes=GATE_UP_LIMIT),
         cost_estimate=pl.CostEstimate(
-            flops=4 * rows * experts * sliver * model_width,
-            bytes_accessed=2 * (gate_up_weight.size + rows * model_width),
+            flops=2 * rows * experts * sliver * model_width,
+            bytes_accessed=gate_up_weight.size + rows * model_width,
             transcendentals=rows * experts * sliver,
         ),
-    )(first, second, in_hbm(gate_up_weight))
+    )(*operands, in_hbm(gate_up_weight))
 
 
 def down_kernel(part, hidden_ref, w_ref, out_ref):
     experts, _, sliver = hidden_ref.shape
     columns = out_ref.shape[1]
-    block = next(size for size in (512, 384, 256, 128, columns) if columns % size == 0)
+    block = next(size for size in (1024, 512, 384, 256, 128, columns) if columns % size == 0)
 
     def one_block(step, carry):
         at = pl.multiple_of(step * block, block)
@@ -243,7 +269,8 @@
             blocks[number] = digit.gather(blocks[number], dim)
             held[number].append(digit)
     gathered = [block.reshape(-1, part.shape[1]) for block, part in zip(blocks, parts)]
-    hidden = hidden_of(gathered[0], gathered[1], gate_up_weight)
+    sums = gate_up_of(1, gathered[1], None, gate_up_weight)
+    hidden = gate_up_of(0, gathered[0], sums, gate_up_weight)
     down_weight = resident(down_weight)
     results = []
     for number, route in enumerate(routes):

time: 90.4 us -> 89.2 us (0.987)
  waiting for transfers between devices: 30.8 us -> 28.9 us
    ppermute x20, waiting for transfers between devices: 30.8 us -> 28.9 us  [shift(): return lax.ppermute(value, self.name, pairs)]
    pallas_call x1 -> x2, Pallas kernels: 17.1 us -> 18.5 us  [gate_up_of(): pl.pallas_call(kernel, grid=(rows // row_block,), in_specs=specs + [pl.Bl...]
  transfers between devices with their start and end apart: 20 -> 20, of which waited for: 17 -> 16; matrix products, arithmetic and copies ran while one was open for 4% -> 4% of each run, Pallas kernels for 8% -> 18%
where the time goes in v5:
time: 89.2 us; the launch traced here: 89 us
  waiting for transfers between devices  28.9 us (32%)
  Pallas kernels  27.6 us (31%)
  starting transfers between devices  27.1 us (30%)
  other arithmetic  3.73 us (4%)
  local copies, waits for them, and re-layouts  1.42 us (2%)
    ppermute x20, waiting for transfers between devices, shift(): return lax.ppermute(value, self.name, pairs)  28.9 us
    ppermute x20, starting transfers between devices, shift(): return lax.ppermute(value, self.name, pairs)  27.1 us
    pallas_call x2, Pallas kernels, gate_up_of(): pl.pallas_call(kernel, grid=(rows // row_block,), in_specs=specs + [pl.Bl...  18.5 us
    pallas_call x1, Pallas kernels, fetched(): pl.pallas_call(fetch_kernel, in_specs=[pl.BlockSpec(memory_space=pl.ANY)]...  4.58 us
    pallas_call x2, Pallas kernels, down_of(): pl.pallas_call(kernel, grid=(rows // row_block,), in_specs=[pl.BlockSpec(...  4.44 us
  transfers between devices with their start and end apart: 20, of which 16 were waited for; matrix products, arithmetic and copies ran while one was open for 4% of the time, Pallas kernels for 18%

profile of v5, /device:TPU:0, one launch (start us, length us, event | category | flops | bytes accessed | tf_op | source)
XLA Modules:
  0.0 89.0 jit_solution(8811658247458460633)
XLA Ops:
  0.0 0.8 slice_bitcast_fusion.16
  0.8 4.1 %collective-permute-start.5 = (bf16[8,3072]{1,0:T(8,128)(2,1)S(1)}, bf16[8,3072]{1,0:T(8,128)(2,1)S(1)}, u32[]{:S(2)}, u32[]{:S(2)}) collective-permute-start(bf16[8,3072]{1,0:T(8,128)(2,1)S(1)} %get-tuple-element.28), channel_id=1, source_target_pairs={{0,8},{4,12},{8,0},{12,4},{1,9},{5,13},{9,1},{13,5},{2,10},{6,14},... | collective-permute-start | bytes 147464 | tf_op jit(solution)/shard_map/ppermute | solution.py:43
  4.9 0.7 select_reduce_fusion
  5.6 0.7 compare_convert_fusion
  6.7 0.8 collective-permute-done.5
  7.6 1.9 %collective-permute-start.6 = (bf16[2,8,3072]{2,1,0:T(8,128)(2,1)S(1)}, bf16[2,8,3072]{2,1,0:T(8,128)(2,1)S(1)}, u32[]{:S(2)}, u32[]{:S(2)}) collective-permute-start(bf16[2,8,3072]{2,1,0:T(8,128)(2,1)S(1)} %get-tuple-element.26), channel_id=1, source_target_pairs={{0,4},{4,0},{8,12},{12,8},{1,5},{5,1},{9,13},{13,9},{2,6},{6,2},{1... | collective-permute-start | bytes 294920 | tf_op jit(solution)/shard_map/ppermute | solution.py:43
  9.4 2.6 %collective-permute-done = bf16[8,3200]{1,0:T(8,128)(2,1)S(1)} collective-permute-done((bf16[8,3200]{1,0:T(8,128)(2,1)S(1)}, bf16[8,3200]{1,0:T(8,128)(2,1)S(1)}, u32[]{:S(2)}, u32[]{:S(2)}) %collective-permute-start) | collective-permute-done | bytes 51232 | tf_op jit(solution)/shard_map/ppermute | solution.py:43
  12.0 1.6 %collective-permute-start.1 = (bf16[2,8,3200]{2,1,0:T(8,128)(2,1)S(1)}, bf16[2,8,3200]{2,1,0:T(8,128)(2,1)S(1)}, u32[]{:S(2)}, u32[]{:S(2)}) collective-permute-start(bf16[2,8,3200]{2,1,0:T(8,128)(2,1)S(1)} %get-tuple-element.24), channel_id=1, source_target_pairs={{0,4},{4,0},{8,12},{12,8},{1,5},{5,1},{9,13},{13,9},{2,6},{6,2},{1... | collective-permute-start | bytes 307208 | tf_op jit(solution)/shard_map/ppermute | solution.py:43
  13.6 1.6 %collective-permute-start.7 = (bf16[2,2,8,3072]{3,2,1,0:T(8,128)(2,1)S(1)}, bf16[2,2,8,3072]{3,2,1,0:T(8,128)(2,1)S(1)}, u32[]{:S(2)}, u32[]{:S(2)}) collective-permute-start(bf16[2,2,8,3072]{3,2,1,0:T(8,128)(2,1)S(1)} %get-tuple-element.22), channel_id=1, source_target_pairs={{0,16},{16,0},{1,17},{17,1},{2,18},{18,2},{3,19},{19,3},{4,20},{20... | collective-permute-start | bytes 589832 | tf_op jit(solution)/shard_map/ppermute | solution.py:43
  15.2 1.6 %collective-permute-done.1 = bf16[2,8,3200]{2,1,0:T(8,128)(2,1)S(1)} collective-permute-done((bf16[2,8,3200]{2,1,0:T(8,128)(2,1)S(1)}, bf16[2,8,3200]{2,1,0:T(8,128)(2,1)S(1)}, u32[]{:S(2)}, u32[]{:S(2)}) %collective-permute-start.1) | collective-permute-done | bytes 102432 | tf_op jit(solution)/shard_map/ppermute | solution.py:43
  16.8 1.5 %collective-permute-start.2 = (bf16[2,2,8,3200]{3,2,1,0:T(8,128)(2,1)S(1)}, bf16[2,2,8,3200]{3,2,1,0:T(8,128)(2,1)S(1)}, u32[]{:S(2)}, u32[]{:S(2)}) collective-permute-start(bf16[2,2,8,3200]{3,2,1,0:T(8,128)(2,1)S(1)} %get-tuple-element.20), channel_id=1, source_target_pairs={{0,2},{1,3},{2,0},{3,1},{4,6},{5,7},{6,4},{7,5},{8,10},{9,11},{10,... | collective-permute-start | bytes 614408 | tf_op jit(solution)/shard_map/ppermute | solution.py:43
  18.3 1.1 %collective-permute-done.7 = bf16[2,2,8,3072]{3,2,1,0:T(8,128)(2,1)S(1)} collective-permute-done((bf16[2,2,8,3072]{3,2,1,0:T(8,128)(2,1)S(1)}, bf16[2,2,8,3072]{3,2,1,0:T(8,128)(2,1)S(1)}, u32[]{:S(2)}, u32[]{:S(2)}) %collective-permute-start.7) | collective-permute-done | bytes 196640 | tf_op jit(solution)/shard_map/ppermute | solution.py:43
  19.4 1.6 %collective-permute-start.8 = (bf16[2,2,2,8,3072]{4,3,2,1,0:T(8,128)(2,1)S(1)}, bf16[2,2,2,8,3072]{4,3,2,1,0:T(8,128)(2,1)S(1)}, u32[]{:S(2)}, u32[]{:S(2)}) collective-permute-start(bf16[2,2,2,8,3072]{4,3,2,1,0:T(8,128)(2,1)S(1)} %get-tuple-element.18), channel_id=1, source_target_pairs={{0,2},{1,3},{2,0},{3,1},{4,6},{5,7},{6,4},{7,5},{8,10},{9,11},{10,... | collective-permute-start | bytes 1179656 | tf_op jit(solution)/shard_map/ppermute | solution.py:43
  21.0 3.8 %collective-permute-done.2 = bf16[2,2,8,3200]{3,2,1,0:T(8,128)(2,1)S(1)} collective-permute-done((bf16[2,2,8,3200]{3,2,1,0:T(8,128)(2,1)S(1)}, bf16[2,2,8,3200]{3,2,1,0:T(8,128)(2,1)S(1)}, u32[]{:S(2)}, u32[]{:S(2)}) %collective-permute-start.2) | collective-permute-done | bytes 204832 | tf_op jit(solution)/shard_map/ppermute | solution.py:43
  24.9 1.5 %collective-permute-start.3 = (bf16[2,2,2,8,3200]{4,3,2,1,0:T(8,128)(2,1)S(1)}, bf16[2,2,2,8,3200]{4,3,2,1,0:T(8,128)(2,1)S(1)}, u32[]{:S(2)}, u32[]{:S(2)}) collective-permute-start(bf16[2,2,2,8,3200]{4,3,2,1,0:T(8,128)(2,1)S(1)} %get-tuple-element.16.after_ref), channel_id=1, source_target_pairs={{0,16},{16,0},{1,17},{17,1},{2,18},{18,2},{3,19},{19,3},{4,20},{20... | collective-permute-start | bytes 1228808 | tf_op jit(solution)/shard_map/ppermute | solution.py:43
  26.4 4.6 %shard_map.73.refs_1_ = bf16[4,256,6144]{2,1,0:T(8,128)(2,1)S(1)} custom-call(bf16[4,256,6144]{2,1,0:T(8,128)(2,1)} %w_ref.1, bf16[2,2,2,8,3200]{4,3,2,1,0:T(8,128)(2,1)S(1)} %get-tuple-element.16.after_ref), custom_call_target="tpu_custom_call" | custom-call | bytes 12582912 | tf_op jit(solution)/shard_map/pallas_call | solution.py:82
  31.1 1.8 %collective-permute-done.3 = bf16[2,2,2,8,3200]{4,3,2,1,0:T(8,128)(2,1)S(1)} collective-permute-done((bf16[2,2,2,8,3200]{4,3,2,1,0:T(8,128)(2,1)S(1)}, bf16[2,2,2,8,3200]{4,3,2,1,0:T(8,128)(2,1)S(1)}, u32[]{:S(2)}, u32[]{:S(2)}) %collective-permute-start.3) | collective-permute-done | bytes 409632 | tf_op jit(solution)/shard_map/ppermute | solution.py:43
  32.9 0.1 fusion.24
  33.1 0.3 collective-permute-done.9
  33.4 0.1 pad_maximum_fusion.1
  33.6 0.1 copy.15
  33.7 9.4 %shard_map.74.refs_1_ = f32[4,512,256]{2,1,0:T(8,128)S(1)} custom-call(bf16[256,3072]{1,0:T(8,128)(2,1)S(1)} %bitcast.94, bf16[4,2,256,6144]{3,2,1,0:T(8,128)(2,1)} %refs_2_.1), custom_call_target="tpu_custom_call" | custom-call | flops 3221225472 | bytes 14155776 | tf_op jit(solution)/shard_map/pallas_call | solution.py:172
  43.1 0.2 pad_maximum_fusion
  43.3 9.1 %shard_map.75.refs_0_ = bf16[4,256,256]{2,1,0:T(8,128)(2,1)S(1)} custom-call(bf16[256,3200]{1,0:T(8,128)(2,1)S(1)} %bitcast.93, f32[4,512,256]{2,1,0:T(8,128)S(1)} %shard_map.74.refs_1_, bf16[4,2,256,6144]{3,2,1,0:T(8,128)(2,1)} %refs_2_.1), custom_call_target="tpu_custom_call" | custom-call | flops 3221225472 | bytes 14155776 | tf_op jit(solution)/shard_map/pallas_call | solution.py:172
  52.4 2.3 %shard_map.77 = bf16[256,3072]{1,0:T(8,128)(2,1)S(1)} custom-call(bf16[4,256,256]{2,1,0:T(8,128)(2,1)S(1)} %shard_map.75.refs_0_, bf16[4,256,6144]{2,1,0:T(8,128)(2,1)S(1)} %shard_map.73.refs_1_), custom_call_target="tpu_custom_call" | custom-call | flops 1610612736 | bytes 8388608 | tf_op jit(solution)/shard_map/pallas_call | solution.py:217
  54.9 0.2 collective-permute-start.15
  55.2 2.1 %shard_map.76 = bf16[256,3072]{1,0:T(8,128)(2,1)S(1)} custom-call(bf16[4,256,256]{2,1,0:T(8,128)(2,1)S(1)} %shard_map.75.refs_0_, bf16[4,256,6144]{2,1,0:T(8,128)(2,1)S(1)} %shard_map.73.refs_1_), custom_call_target="tpu_custom_call" | custom-call | flops 1610612736 | bytes 8388608 | tf_op jit(solution)/shard_map/pallas_call | solution.py:217
  57.4 0.4 collective-permute-start.10
  57.8 0.2 fusion.1
  58.1 1.6 %collective-permute-start.16 = (bf16[2,2,2,8,3072]{4,3,2,1,0:T(8,128)(2,1)S(1)}, bf16[2,2,2,8,3072]{4,3,2,1,0:T(8,128)(2,1)S(1)}, u32[]{:S(2)}, u32[]{:S(2)}) collective-permute-start(bf16[2,2,2,8,3072]{4,3,2,1,0:T(8,128)(2,1)S(1)} %slice_bitcast_fusion), channel_id=1, source_target_pairs={{0,2},{1,3},{2,0},{3,1},{4,6},{5,7},{6,4},{7,5},{8,10},{9,11},{10,... | collective-permute-start | bytes 1179656 | tf_op jit(solution)/shard_map/ppermute | solution.py:43
  59.6 0.1 collective-permute-done.10
  59.8 0.2 fusion
  60.0 1.5 %collective-permute-start.11 = (bf16[2,2,2,8,3072]{4,3,2,1,0:T(8,128)(2,1)S(1)}, bf16[2,2,2,8,3072]{4,3,2,1,0:T(8,128)(2,1)S(1)}, u32[]{:S(2)}, u32[]{:S(2)}) collective-permute-start(bf16[2,2,2,8,3072]{4,3,2,1,0:T(8,128)(2,1)S(1)} %slice_bitcast_fusion.2), channel_id=1, source_target_pairs={{0,16},{16,0},{1,17},{17,1},{2,18},{18,2},{3,19},{19,3},{4,20},{20... | collective-permute-start | bytes 1179656 | tf_op jit(solution)/shard_map/ppermute | solution.py:43
  61.5 7.8 %collective-permute-done.16 = bf16[2,2,2,8,3072]{4,3,2,1,0:T(8,128)(2,1)S(1)} collective-permute-done((bf16[2,2,2,8,3072]{4,3,2,1,0:T(8,128)(2,1)S(1)}, bf16[2,2,2,8,3072]{4,3,2,1,0:T(8,128)(2,1)S(1)}, u32[]{:S(2)}, u32[]{:S(2)}) %collective-permute-start.16) | collective-permute-done | bytes 393248 | tf_op jit(solution)/shard_map/ppermute | solution.py:43
  69.4 1.5 %collective-permute-start.17 = (bf16[2,2,8,3072]{3,2,1,0:T(8,128)(2,1)S(1)}, bf16[2,2,8,3072]{3,2,1,0:T(8,128)(2,1)S(1)}, u32[]{:S(2)}, u32[]{:S(2)}) collective-permute-start(bf16[2,2,8,3072]{3,2,1,0:T(8,128)(2,1)S(1)} %slice_bitcast_fusion.4), channel_id=1, source_target_pairs={{0,16},{16,0},{1,17},{17,1},{2,18},{18,2},{3,19},{19,3},{4,20},{20... | collective-permute-start | bytes 589832 | tf_op jit(solution)/shard_map/ppermute | solution.py:43
  70.9 0.5 collective-permute-done.11
  71.6 1.6 %collective-permute-start.12 = (bf16[2,2,8,3072]{3,2,1,0:T(8,128)(2,1)S(1)}, bf16[2,2,8,3072]{3,2,1,0:T(8,128)(2,1)S(1)}, u32[]{:S(2)}, u32[]{:S(2)}) collective-permute-start(bf16[2,2,8,3072]{3,2,1,0:T(8,128)(2,1)S(1)} %slice_bitcast_fusion.6), channel_id=1, source_target_pairs={{0,2},{1,3},{2,0},{3,1},{4,6},{5,7},{6,4},{7,5},{8,10},{9,11},{10,... | collective-permute-start | bytes 589832 | tf_op jit(solution)/shard_map/ppermute | solution.py:43
  73.1 2.6 %collective-permute-done.17 = bf16[2,2,8,3072]{3,2,1,0:T(8,128)(2,1)S(1)} collective-permute-done((bf16[2,2,8,3072]{3,2,1,0:T(8,128)(2,1)S(1)}, bf16[2,2,8,3072]{3,2,1,0:T(8,128)(2,1)S(1)}, u32[]{:S(2)}, u32[]{:S(2)}) %collective-permute-start.17) | collective-permute-done | bytes 196640 | tf_op jit(solution)/shard_map/ppermute | solution.py:43
  75.8 1.7 %collective-permute-start.18 = (bf16[2,8,3072]{2,1,0:T(8,128)(2,1)S(1)}, bf16[2,8,3072]{2,1,0:T(8,128)(2,1)S(1)}, u32[]{:S(2)}, u32[]{:S(2)}) collective-permute-start(bf16[2,8,3072]{2,1,0:T(8,128)(2,1)S(1)} %slice_bitcast_fusion.8), channel_id=1, source_target_pairs={{0,4},{4,0},{8,12},{12,8},{1,5},{5,1},{9,13},{13,9},{2,6},{6,2},{1... | collective-permute-start | bytes 294920 | tf_op jit(solution)/shard_map/ppermute | solution.py:43
  77.5 0.5 collective-permute-done.12
  78.0 1.7 %collective-permute-start.13 = (bf16[2,8,3072]{2,1,0:T(8,128)(2,1)S(1)}, bf16[2,8,3072]{2,1,0:T(8,128)(2,1)S(1)}, u32[]{:S(2)}, u32[]{:S(2)}) collective-permute-start(bf16[2,8,3072]{2,1,0:T(8,128)(2,1)S(1)} %slice_bitcast_fusion.10), channel_id=1, source_target_pairs={{0,4},{4,0},{8,12},{12,8},{1,5},{5,1},{9,13},{13,9},{2,6},{6,2},{1... | collective-permute-start | bytes 294920 | tf_op jit(solution)/shard_map/ppermute | solution.py:43
  79.7 1.7 %collective-permute-done.18 = bf16[2,8,3072]{2,1,0:T(8,128)(2,1)S(1)} collective-permute-done((bf16[2,8,3072]{2,1,0:T(8,128)(2,1)S(1)}, bf16[2,8,3072]{2,1,0:T(8,128)(2,1)S(1)}, u32[]{:S(2)}, u32[]{:S(2)}) %collective-permute-start.18) | collective-permute-done | bytes 98336 | tf_op jit(solution)/shard_map/ppermute | solution.py:43
  81.4 1.5 %collective-permute-start.19 = (bf16[8,3072]{1,0:T(8,128)(2,1)S(1)}, bf16[8,3072]{1,0:T(8,128)(2,1)S(1)}, u32[]{:S(2)}, u32[]{:S(2)}) collective-permute-start(bf16[8,3072]{1,0:T(8,128)(2,1)S(1)} %slice_bitcast_fusion.12), channel_id=1, source_target_pairs={{0,8},{4,12},{8,0},{12,4},{1,9},{5,13},{9,1},{13,5},{2,10},{6,14},... | collective-permute-start | bytes 147464 | tf_op jit(solution)/shard_map/ppermute | solution.py:43
  82.9 0.3 collective-permute-done.13
  83.3 1.5 %collective-permute-start.14 = (bf16[8,3072]{1,0:T(8,128)(2,1)S(1)}, bf16[8,3072]{1,0:T(8,128)(2,1)S(1)}, u32[]{:S(2)}, u32[]{:S(2)}) collective-permute-start(bf16[8,3072]{1,0:T(8,128)(2,1)S(1)} %slice_bitcast_fusion.14), channel_id=1, source_target_pairs={{0,8},{4,12},{8,0},{12,4},{1,9},{5,13},{9,1},{13,5},{2,10},{6,14},... | collective-permute-start | bytes 147464 | tf_op jit(solution)/shard_map/ppermute | solution.py:43
  84.8 2.2 %collective-permute-done.19 = bf16[8,3072]{1,0:T(8,128)(2,1)S(1)} collective-permute-done((bf16[8,3072]{1,0:T(8,128)(2,1)S(1)}, bf16[8,3072]{1,0:T(8,128)(2,1)S(1)}, u32[]{:S(2)}, u32[]{:S(2)}) %collective-permute-start.19) | collective-permute-done | bytes 49184 | tf_op jit(solution)/shard_map/ppermute | solution.py:43
  87.0 1.3 %collective-permute-done.14 = bf16[8,3072]{1,0:T(8,128)(2,1)S(1)} collective-permute-done((bf16[8,3072]{1,0:T(8,128)(2,1)S(1)}, bf16[8,3072]{1,0:T(8,128)(2,1)S(1)}, u32[]{:S(2)}, u32[]{:S(2)}) %collective-permute-start.14) | collective-permute-done | bytes 49184 | tf_op jit(solution)/shard_map/ppermute | solution.py:43
  88.3 0.6 pad_maximum_fusion.10
  (38 shorter events, 1.5 us)
Async XLA Ops:
  0.8 6.7 %collective-permute-start.5 = (bf16[8,3072]{1,0:T(8,128)(2,1)S(1)}, bf16[8,3072]{1,0:T(8,128)(2,1)S(1)}, u32[]{:S(2)}, u32[]{:S(2)}) collective-permute-start(bf16[8,3072]{1,0:T(8,128)(2,1)S(1)} %get-tuple-element.28), channel_id=1, source_target_pairs={{0,8},{4,12},{8,0},{12,4},{1,9},{5,13},{9,1},{13,5},{2,10},{6,14},... | collective-permute-start | bytes 147464 | tf_op jit(solution)/shard_map/ppermute | solution.py:43
  6.7 5.3 %collective-permute-start = (bf16[8,3200]{1,0:T(8,128)(2,1)S(1)}, bf16[8,3200]{1,0:T(8,128)(2,1)S(1)}, u32[]{:S(2)}, u32[]{:S(2)}) collective-permute-start(bf16[8,3200]{1,0:T(8,128)(2,1)S(1)} %get-tuple-element.31), channel_id=1, source_target_pairs={{0,8},{4,12},{8,0},{12,4},{1,9},{5,13},{9,1},{13,5},{2,10},{6,14},... | collective-permute-start | bytes 153608 | tf_op jit(solution)/shard_map/ppermute | solution.py:43
  7.6 6.0 %collective-permute-start.6 = (bf16[2,8,3072]{2,1,0:T(8,128)(2,1)S(1)}, bf16[2,8,3072]{2,1,0:T(8,128)(2,1)S(1)}, u32[]{:S(2)}, u32[]{:S(2)}) collective-permute-start(bf16[2,8,3072]{2,1,0:T(8,128)(2,1)S(1)} %get-tuple-element.26), channel_id=1, source_target_pairs={{0,4},{4,0},{8,12},{12,8},{1,5},{5,1},{9,13},{13,9},{2,6},{6,2},{1... | collective-permute-start | bytes 294920 | tf_op jit(solution)/shard_map/ppermute | solution.py:43
  12.0 4.7 %collective-permute-start.1 = (bf16[2,8,3200]{2,1,0:T(8,128)(2,1)S(1)}, bf16[2,8,3200]{2,1,0:T(8,128)(2,1)S(1)}, u32[]{:S(2)}, u32[]{:S(2)}) collective-permute-start(bf16[2,8,3200]{2,1,0:T(8,128)(2,1)S(1)} %get-tuple-element.24), channel_id=1, source_target_pairs={{0,4},{4,0},{8,12},{12,8},{1,5},{5,1},{9,13},{13,9},{2,6},{6,2},{1... | collective-permute-start | bytes 307208 | tf_op jit(solution)/shard_map/ppermute | solution.py:43
  13.6 5.7 %collective-permute-start.7 = (bf16[2,2,8,3072]{3,2,1,0:T(8,128)(2,1)S(1)}, bf16[2,2,8,3072]{3,2,1,0:T(8,128)(2,1)S(1)}, u32[]{:S(2)}, u32[]{:S(2)}) collective-permute-start(bf16[2,2,8,3072]{3,2,1,0:T(8,128)(2,1)S(1)} %get-tuple-element.22), channel_id=1, source_target_pairs={{0,16},{16,0},{1,17},{17,1},{2,18},{18,2},{3,19},{19,3},{4,20},{20... | collective-permute-start | bytes 589832 | tf_op jit(solution)/shard_map/ppermute | solution.py:43
  16.8 8.0 %collective-permute-start.2 = (bf16[2,2,8,3200]{3,2,1,0:T(8,128)(2,1)S(1)}, bf16[2,2,8,3200]{3,2,1,0:T(8,128)(2,1)S(1)}, u32[]{:S(2)}, u32[]{:S(2)}) collective-permute-start(bf16[2,2,8,3200]{3,2,1,0:T(8,128)(2,1)S(1)} %get-tuple-element.20), channel_id=1, source_target_pairs={{0,2},{1,3},{2,0},{3,1},{4,6},{5,7},{6,4},{7,5},{8,10},{9,11},{10,... | collective-permute-start | bytes 614408 | tf_op jit(solution)/shard_map/ppermute | solution.py:43
  19.4 11.6 %collective-permute-start.8 = (bf16[2,2,2,8,3072]{4,3,2,1,0:T(8,128)(2,1)S(1)}, bf16[2,2,2,8,3072]{4,3,2,1,0:T(8,128)(2,1)S(1)}, u32[]{:S(2)}, u32[]{:S(2)}) collective-permute-start(bf16[2,2,2,8,3072]{4,3,2,1,0:T(8,128)(2,1)S(1)} %get-tuple-element.18), channel_id=1, source_target_pairs={{0,2},{1,3},{2,0},{3,1},{4,6},{5,7},{6,4},{7,5},{8,10},{9,11},{10,... | collective-permute-start | bytes 1179656 | tf_op jit(solution)/shard_map/ppermute | solution.py:43
  24.9 8.0 %collective-permute-start.3 = (bf16[2,2,2,8,3200]{4,3,2,1,0:T(8,128)(2,1)S(1)}, bf16[2,2,2,8,3200]{4,3,2,1,0:T(8,128)(2,1)S(1)}, u32[]{:S(2)}, u32[]{:S(2)}) collective-permute-start(bf16[2,2,2,8,3200]{4,3,2,1,0:T(8,128)(2,1)S(1)} %get-tuple-element.16.after_ref), channel_id=1, source_target_pairs={{0,16},{16,0},{1,17},{17,1},{2,18},{18,2},{3,19},{19,3},{4,20},{20... | collective-permute-start | bytes 1228808 | tf_op jit(solution)/shard_map/ppermute | solution.py:43
  31.1 2.4 %collective-permute-start.9 = (bf16[2,2,2,2,8,3072]{5,4,3,2,0,1:T(8,128)(2,1)S(1)}, bf16[2,2,2,2,8,3072]{5,4,3,2,0,1:T(8,128)(2,1)S(1)}, u32[]{:S(2)}, u32[]{:S(2)}) collective-permute-start(bf16[2,2,2,2,8,3072]{5,4,3,2,0,1:T(8,128)(2,1)S(1)} %pad_maximum_fusion.3), channel_id=1, source_target_pairs={{0,1},{1,0},{2,3},{3,2},{4,5},{5,4},{6,7},{7,6},{8,9},{9,8},{10,11... | collective-permute-start | bytes 2359304 | tf_op jit(solution)/shard_map/ppermute | solution.py:43
  33.0 10.1 %collective-permute-start.4 = (bf16[2,2,2,2,8,3200]{5,4,3,2,1,0:T(8,128)(2,1)S(1)}, bf16[2,2,2,2,8,3200]{5,4,3,2,1,0:T(8,128)(2,1)S(1)}, u32[]{:S(2)}, u32[]{:S(2)}) collective-permute-start(bf16[2,2,2,2,8,3200]{5,4,3,2,1,0:T(8,128)(2,1)S(1)} %get-tuple-element.14), channel_id=1, source_target_pairs={{0,1},{1,0},{2,3},{3,2},{4,5},{5,4},{6,7},{7,6},{8,9},{9,8},{10,11... | collective-permute-start | bytes 2457608 | tf_op jit(solution)/shard_map/ppermute | solution.py:43
  54.9 2.9 %collective-permute-start.15 = (bf16[2,2,2,2,8,3072]{5,4,3,2,0,1:T(8,128)(2,1)S(1)}, bf16[2,2,2,2,8,3072]{5,4,3,2,0,1:T(8,128)(2,1)S(1)}, u32[]{:S(2)}, u32[]{:S(2)}) collective-permute-start(bf16[2,2,2,2,8,3072]{5,4,3,2,0,1:T(8,128)(2,1)S(1)} %copy.16), channel_id=1, source_target_pairs={{0,1},{1,0},{2,3},{3,2},{4,5},{5,4},{6,7},{7,6},{8,9},{9,8},{10,11... | collective-permute-start | bytes 2359304 | tf_op jit(solution)/shard_map/ppermute | solution.py:43
  57.4 2.4 %collective-permute-start.10 = (bf16[2,2,2,2,8,3072]{5,4,3,2,1,0:T(8,128)(2,1)S(1)}, bf16[2,2,2,2,8,3072]{5,4,3,2,1,0:T(8,128)(2,1)S(1)}, u32[]{:S(2)}, u32[]{:S(2)}) collective-permute-start(bf16[2,2,2,2,8,3072]{5,4,3,2,1,0:T(8,128)(2,1)S(1)} %bitcast.100), channel_id=1, source_target_pairs={{0,1},{1,0},{2,3},{3,2},{4,5},{5,4},{6,7},{7,6},{8,9},{9,8},{10,11... | collective-permute-start | bytes 2359304 | tf_op jit(solution)/shard_map/ppermute | solution.py:43
  58.1 11.3 %collective-permute-start.16 = (bf16[2,2,2,8,3072]{4,3,2,1,0:T(8,128)(2,1)S(1)}, bf16[2,2,2,8,3072]{4,3,2,1,0:T(8,128)(2,1)S(1)}, u32[]{:S(2)}, u32[]{:S(2)}) collective-permute-start(bf16[2,2,2,8,3072]{4,3,2,1,0:T(8,128)(2,1)S(1)} %slice_bitcast_fusion), channel_id=1, source_target_pairs={{0,2},{1,3},{2,0},{3,1},{4,6},{5,7},{6,4},{7,5},{8,10},{9,11},{10,... | collective-permute-start | bytes 1179656 | tf_op jit(solution)/shard_map/ppermute | solution.py:43
  60.0 11.4 %collective-permute-start.11 = (bf16[2,2,2,8,3072]{4,3,2,1,0:T(8,128)(2,1)S(1)}, bf16[2,2,2,8,3072]{4,3,2,1,0:T(8,128)(2,1)S(1)}, u32[]{:S(2)}, u32[]{:S(2)}) collective-permute-start(bf16[2,2,2,8,3072]{4,3,2,1,0:T(8,128)(2,1)S(1)} %slice_bitcast_fusion.2), channel_id=1, source_target_pairs={{0,16},{16,0},{1,17},{17,1},{2,18},{18,2},{3,19},{19,3},{4,20},{20... | collective-permute-start | bytes 1179656 | tf_op jit(solution)/shard_map/ppermute | solution.py:43
  69.4 6.3 %collective-permute-start.17 = (bf16[2,2,8,3072]{3,2,1,0:T(8,128)(2,1)S(1)}, bf16[2,2,8,3072]{3,2,1,0:T(8,128)(2,1)S(1)}, u32[]{:S(2)}, u32[]{:S(2)}) collective-permute-start(bf16[2,2,8,3072]{3,2,1,0:T(8,128)(2,1)S(1)} %slice_bitcast_fusion.4), channel_id=1, source_target_pairs={{0,16},{16,0},{1,17},{17,1},{2,18},{18,2},{3,19},{19,3},{4,20},{20... | collective-permute-start | bytes 589832 | tf_op jit(solution)/shard_map/ppermute | solution.py:43
  71.6 6.4 %collective-permute-start.12 = (bf16[2,2,8,3072]{3,2,1,0:T(8,128)(2,1)S(1)}, bf16[2,2,8,3072]{3,2,1,0:T(8,128)(2,1)S(1)}, u32[]{:S(2)}, u32[]{:S(2)}) collective-permute-start(bf16[2,2,8,3072]{3,2,1,0:T(8,128)(2,1)S(1)} %slice_bitcast_fusion.6), channel_id=1, source_target_pairs={{0,2},{1,3},{2,0},{3,1},{4,6},{5,7},{6,4},{7,5},{8,10},{9,11},{10,... | collective-permute-start | bytes 589832 | tf_op jit(solution)/shard_map/ppermute | solution.py:43
  75.8 5.6 %collective-permute-start.18 = (bf16[2,8,3072]{2,1,0:T(8,128)(2,1)S(1)}, bf16[2,8,3072]{2,1,0:T(8,128)(2,1)S(1)}, u32[]{:S(2)}, u32[]{:S(2)}) collective-permute-start(bf16[2,8,3072]{2,1,0:T(8,128)(2,1)S(1)} %slice_bitcast_fusion.8), channel_id=1, source_target_pairs={{0,4},{4,0},{8,12},{12,8},{1,5},{5,1},{9,13},{13,9},{2,6},{6,2},{1... | collective-permute-start | bytes 294920 | tf_op jit(solution)/shard_map/ppermute | solution.py:43
  78.0 5.2 %collective-permute-start.13 = (bf16[2,8,3072]{2,1,0:T(8,128)(2,1)S(1)}, bf16[2,8,3072]{2,1,0:T(8,128)(2,1)S(1)}, u32[]{:S(2)}, u32[]{:S(2)}) collective-permute-start(bf16[2,8,3072]{2,1,0:T(8,128)(2,1)S(1)} %slice_bitcast_fusion.10), channel_id=1, source_target_pairs={{0,4},{4,0},{8,12},{12,8},{1,5},{5,1},{9,13},{13,9},{2,6},{6,2},{1... | collective-permute-start | bytes 294920 | tf_op jit(solution)/shard_map/ppermute | solution.py:43
  81.4 5.6 %collective-permute-start.19 = (bf16[8,3072]{1,0:T(8,128)(2,1)S(1)}, bf16[8,3072]{1,0:T(8,128)(2,1)S(1)}, u32[]{:S(2)}, u32[]{:S(2)}) collective-permute-start(bf16[8,3072]{1,0:T(8,128)(2,1)S(1)} %slice_bitcast_fusion.12), channel_id=1, source_target_pairs={{0,8},{4,12},{8,0},{12,4},{1,9},{5,13},{9,1},{13,5},{2,10},{6,14},... | collective-permute-start | bytes 147464 | tf_op jit(solution)/shard_map/ppermute | solution.py:43
  83.3 5.1 %collective-permute-start.14 = (bf16[8,3072]{1,0:T(8,128)(2,1)S(1)}, bf16[8,3072]{1,0:T(8,128)(2,1)S(1)}, u32[]{:S(2)}, u32[]{:S(2)}) collective-permute-start(bf16[8,3072]{1,0:T(8,128)(2,1)S(1)} %slice_bitcast_fusion.14), channel_id=1, source_target_pairs={{0,8},{4,12},{8,0},{12,4},{1,9},{5,13},{9,1},{13,5},{2,10},{6,14},... | collective-permute-start | bytes 147464 | tf_op jit(solution)/shard_map/ppermute | solution.py:43

commit v6 on v5

--- a/solution.py
+++ b/solution.py
@@ -95,50 +95,53 @@
 def gate_up_kernel(part, rows_ref, *refs):
     last = part == 0
     if last:
-        sum_ref, w_hbm, out_ref, w_ref, turned_ref, sems = refs
+        sum_ref, w_hbm, out_ref, w_ref, sems = refs
     else:
-        w_hbm, out_ref, w_ref, turned_ref, sems = refs
+        w_hbm, out_ref, w_ref, sems = refs
     experts, _, sliver, half = w_ref.shape
     depth = half // PIECES
+    group = 2 if experts % 2 == 0 else 1
+    units = 2 * sliver
 
     def copy(slot, piece):
         return pltpu.make_async_copy(
-            w_hbm.at[slot, :, :, pl.ds(part * half + piece * depth, depth)],
-            w_ref.at[slot, :, :, pl.ds(piece * depth, depth)],
-            sems.at[slot, piece],
+            w_hbm.at[pl.ds(slot, group), :, :, pl.ds(part * half + piece * depth, depth)],
+            w_ref.at[pl.ds(slot, group), :, :, pl.ds(piece * depth, depth)],
+            sems.at[slot // group, piece],
         )
 
     @pl.when(pl.program_id(0) == 0)
     def start():
-        for slot in range(experts):
+        for slot in range(0, experts, group):
             for piece in range(PIECES):
                 copy(slot, piece).start()
 
-    for piece in range(PIECES):
-        at = piece * depth
-        turned_ref[at : at + depth] = rows_ref[:, at : at + depth].T
     if last:
         extra = rows_ref[:, half:].astype(jnp.float32)
         lane = lax.broadcasted_iota(jnp.int32, extra.shape, 1)
-    for slot in range(experts):
-        pre = sum_ref[slot] if last else None
+    for first in range(0, experts, group):
+        columns = slice(first * units, (first + group) * units)
+        pre = sum_ref[:, columns] if last else None
         for piece in range(PIECES):
-            pl.when(pl.program_id(0) == 0)(copy(slot, piece).wait)
+            pl.when(pl.program_id(0) == 0)(copy(first, piece).wait)
             at = piece * depth
-            product = jnp.dot(
-                w_ref[slot, :, :, at : at + depth].reshape(2 * sliver, depth),
-                turned_ref[at : at + depth],
+            product = lax.dot_general(
+                rows_ref[:, at : at + depth],
+                w_ref[first : first + group, :, :, at : at + depth].reshape(group * units, depth),
+                (((1,), (1,)), ((), ())),
                 preferred_element_type=jnp.float32,
             )
             pre = product if pre is None else pre + product
         if not last:
-            out_ref[slot] = pre
+            out_ref[:, columns] = pre
             continue
-        gate, up = pre[:sliver], pre[sliver:]
-        hidden = (gate / (1.0 + jnp.exp(-gate)) * up).T
-        mine = (lane == slot) | (lane == slot + experts) | (lane == slot + 2 * experts)
-        weigh = jnp.sum(jnp.where(mine, extra, 0.0), axis=1, keepdims=True)
-        out_ref[slot] = (hidden * weigh).astype(out_ref.dtype)
+        for slot in range(first, first + group):
+            at = (slot - first) * units
+            gate, up = pre[:, at : at + sliver], pre[:, at + sliver : at + units]
+            mine = (lane == slot) | (lane == slot + experts) | (lane == slot + 2 * experts)
+            weigh = jnp.sum(jnp.where(mine, extra, 0.0), axis=1, keepdims=True)
+            hidden = gate / (1.0 + jnp.exp(-gate)) * up * weigh
+            out_ref[slot] = hidden.astype(out_ref.dtype)
 
 
 def gate_up_of(part, rows_of_part, sums, gate_up_weight):
@@ -147,6 +150,7 @@
     rows, width = rows_of_part.shape
     row_block = min(ROW_BLOCK, rows)
     whole = rows == row_block
+    units = experts * 2 * sliver
     operands = [rows_of_part] if sums is None else [rows_of_part, sums]
     if whole:
         operands = [resident(operand) for operand in operands]
@@ -154,11 +158,11 @@
     else:
         specs = [
             pl.BlockSpec((row_block, width), lambda r: (r, 0)),
-            pl.BlockSpec((experts, 2 * sliver, row_block), lambda r: (0, 0, r)),
+            pl.BlockSpec((row_block, units), lambda r: (r, 0)),
         ][: len(operands)]
     if sums is None:
-        out_spec = pl.BlockSpec((experts, 2 * sliver, row_block), lambda r: (0, 0, r))
-        out_shape = jax.ShapeDtypeStruct((experts, 2 * sliver, rows), jnp.float32)
+        out_spec = pl.BlockSpec((row_block, units), lambda r: (r, 0))
+        out_shape = jax.ShapeDtypeStruct((rows, units), jnp.float32)
     else:
         out_spec = pl.BlockSpec((experts, row_block, sliver), lambda r: (0, r, 0))
         out_shape = jax.ShapeDtypeStruct((experts, rows, sliver), jnp.bfloat16)
@@ -177,7 +181,6 @@
         out_shape=out_shape,
         scratch_shapes=[
             pltpu.VMEM((experts, 2, sliver, half), gate_up_weight.dtype),
-            pltpu.VMEM((half, row_block), rows_of_part.dtype),
             pltpu.SemaphoreType.DMA((experts, PIECES)),
         ],
         compiler_params=pltpu.CompilerParams(vmem_limit_bytes=GATE_UP_LIMIT),

time: 89.2 us -> 83.4 us (0.935)
  Pallas kernels: 27.6 us -> 21.8 us
    pallas_call x2, Pallas kernels: 18.5 us -> 12.9 us  [gate_up_of(): pl.pallas_call(kernel, grid=(rows // row_block,), in_specs=specs + [pl.Bl...]
  transfers between devices with their start and end apart: 20 -> 20, of which waited for: 16 -> 16; matrix products, arithmetic and copies ran while one was open for 4% -> 4% of each run, Pallas kernels for 18% -> 16%
where the time goes in v6:
time: 83.4 us; the launch traced here: 83.2 us
  waiting for transfers between devices  28.8 us (35%)
  starting transfers between devices  27.2 us (33%)
  Pallas kernels  21.8 us (26%)
  other arithmetic  3.73 us (4%)
  local copies, waits for them, and re-layouts  1.42 us (2%)
    ppermute x20, waiting for transfers between devices, shift(): return lax.ppermute(value, self.name, pairs)  28.8 us
    ppermute x20, starting transfers between devices, shift(): return lax.ppermute(value, self.name, pairs)  27.2 us
    pallas_call x2, Pallas kernels, gate_up_of(): pl.pallas_call(kernel, grid=(rows // row_block,), in_specs=specs + [pl.Bl...  12.9 us
    pallas_call x1, Pallas kernels, fetched(): pl.pallas_call(fetch_kernel, in_specs=[pl.BlockSpec(memory_space=pl.ANY)]...  4.58 us
    pallas_call x2, Pallas kernels, down_of(): pl.pallas_call(kernel, grid=(rows // row_block,), in_specs=[pl.BlockSpec(...  4.26 us
  transfers between devices with their start and end apart: 20, of which 16 were waited for; matrix products, arithmetic and copies ran while one was open for 4% of the time, Pallas kernels for 16%

profile of v6, /device:TPU:0, one launch (start us, length us, event | category | flops | bytes accessed | tf_op | source)
XLA Modules:
  0.0 83.2 jit_solution(8336308292929384349)
XLA Ops:
  0.0 0.8 %slice_bitcast_fusion.16 = (bf16[1,8,3072]{2,1,0:T(8,128)(2,1)S(1)}, bf16[8,3072]{1,0:T(8,128)(2,1)S(1)}, bf16[8,3072]{1,0:T(8,128)(2,1)S(1)}) fusion(bf16[8,6144]{1,0:T(8,128)(2,1)} %param.8), kind=kLoop, calls=%fused_computation.64 | loop fusion | bytes 245760 | tf_op jit(solution)/shard_map/stack | solution.py:46
  0.8 4.1 %collective-permute-start.5 = (bf16[8,3072]{1,0:T(8,128)(2,1)S(1)}, bf16[8,3072]{1,0:T(8,128)(2,1)S(1)}, u32[]{:S(2)}, u32[]{:S(2)}) collective-permute-start(bf16[8,3072]{1,0:T(8,128)(2,1)S(1)} %get-tuple-element.28), channel_id=1, source_target_pairs={{0,8},{4,12},{8,0},{12,4},{1,9},{5,13},{9,1},{13,5},{2,10},{6,14},... | collective-permute-start | bytes 147464 | tf_op jit(solution)/shard_map/ppermute | solution.py:43
  4.9 0.7 select_reduce_fusion
  5.6 0.7 compare_convert_fusion
  6.7 0.8 collective-permute-done.5
  7.6 1.9 %collective-permute-start.6 = (bf16[2,8,3072]{2,1,0:T(8,128)(2,1)S(1)}, bf16[2,8,3072]{2,1,0:T(8,128)(2,1)S(1)}, u32[]{:S(2)}, u32[]{:S(2)}) collective-permute-start(bf16[2,8,3072]{2,1,0:T(8,128)(2,1)S(1)} %get-tuple-element.26), channel_id=1, source_target_pairs={{0,4},{4,0},{8,12},{12,8},{1,5},{5,1},{9,13},{13,9},{2,6},{6,2},{1... | collective-permute-start | bytes 294920 | tf_op jit(solution)/shard_map/ppermute | solution.py:43
  9.4 2.6 %collective-permute-done = bf16[8,3200]{1,0:T(8,128)(2,1)S(1)} collective-permute-done((bf16[8,3200]{1,0:T(8,128)(2,1)S(1)}, bf16[8,3200]{1,0:T(8,128)(2,1)S(1)}, u32[]{:S(2)}, u32[]{:S(2)}) %collective-permute-start) | collective-permute-done | bytes 51232 | tf_op jit(solution)/shard_map/ppermute | solution.py:43
  12.0 1.6 %collective-permute-start.1 = (bf16[2,8,3200]{2,1,0:T(8,128)(2,1)S(1)}, bf16[2,8,3200]{2,1,0:T(8,128)(2,1)S(1)}, u32[]{:S(2)}, u32[]{:S(2)}) collective-permute-start(bf16[2,8,3200]{2,1,0:T(8,128)(2,1)S(1)} %get-tuple-element.24), channel_id=1, source_target_pairs={{0,4},{4,0},{8,12},{12,8},{1,5},{5,1},{9,13},{13,9},{2,6},{6,2},{1... | collective-permute-start | bytes 307208 | tf_op jit(solution)/shard_map/ppermute | solution.py:43
  13.6 1.6 %collective-permute-start.7 = (bf16[2,2,8,3072]{3,2,1,0:T(8,128)(2,1)S(1)}, bf16[2,2,8,3072]{3,2,1,0:T(8,128)(2,1)S(1)}, u32[]{:S(2)}, u32[]{:S(2)}) collective-permute-start(bf16[2,2,8,3072]{3,2,1,0:T(8,128)(2,1)S(1)} %get-tuple-element.22), channel_id=1, source_target_pairs={{0,16},{16,0},{1,17},{17,1},{2,18},{18,2},{3,19},{19,3},{4,20},{20... | collective-permute-start | bytes 589832 | tf_op jit(solution)/shard_map/ppermute | solution.py:43
  15.2 1.6 %collective-permute-done.1 = bf16[2,8,3200]{2,1,0:T(8,128)(2,1)S(1)} collective-permute-done((bf16[2,8,3200]{2,1,0:T(8,128)(2,1)S(1)}, bf16[2,8,3200]{2,1,0:T(8,128)(2,1)S(1)}, u32[]{:S(2)}, u32[]{:S(2)}) %collective-permute-start.1) | collective-permute-done | bytes 102432 | tf_op jit(solution)/shard_map/ppermute | solution.py:43
  16.8 1.5 %collective-permute-start.2 = (bf16[2,2,8,3200]{3,2,1,0:T(8,128)(2,1)S(1)}, bf16[2,2,8,3200]{3,2,1,0:T(8,128)(2,1)S(1)}, u32[]{:S(2)}, u32[]{:S(2)}) collective-permute-start(bf16[2,2,8,3200]{3,2,1,0:T(8,128)(2,1)S(1)} %get-tuple-element.20), channel_id=1, source_target_pairs={{0,2},{1,3},{2,0},{3,1},{4,6},{5,7},{6,4},{7,5},{8,10},{9,11},{10,... | collective-permute-start | bytes 614408 | tf_op jit(solution)/shard_map/ppermute | solution.py:43
  18.3 1.1 %collective-permute-done.7 = bf16[2,2,8,3072]{3,2,1,0:T(8,128)(2,1)S(1)} collective-permute-done((bf16[2,2,8,3072]{3,2,1,0:T(8,128)(2,1)S(1)}, bf16[2,2,8,3072]{3,2,1,0:T(8,128)(2,1)S(1)}, u32[]{:S(2)}, u32[]{:S(2)}) %collective-permute-start.7) | collective-permute-done | bytes 196640 | tf_op jit(solution)/shard_map/ppermute | solution.py:43
  19.4 1.6 %collective-permute-start.8 = (bf16[2,2,2,8,3072]{4,3,2,1,0:T(8,128)(2,1)S(1)}, bf16[2,2,2,8,3072]{4,3,2,1,0:T(8,128)(2,1)S(1)}, u32[]{:S(2)}, u32[]{:S(2)}) collective-permute-start(bf16[2,2,2,8,3072]{4,3,2,1,0:T(8,128)(2,1)S(1)} %get-tuple-element.18), channel_id=1, source_target_pairs={{0,2},{1,3},{2,0},{3,1},{4,6},{5,7},{6,4},{7,5},{8,10},{9,11},{10,... | collective-permute-start | bytes 1179656 | tf_op jit(solution)/shard_map/ppermute | solution.py:43
  21.0 3.8 %collective-permute-done.2 = bf16[2,2,8,3200]{3,2,1,0:T(8,128)(2,1)S(1)} collective-permute-done((bf16[2,2,8,3200]{3,2,1,0:T(8,128)(2,1)S(1)}, bf16[2,2,8,3200]{3,2,1,0:T(8,128)(2,1)S(1)}, u32[]{:S(2)}, u32[]{:S(2)}) %collective-permute-start.2) | collective-permute-done | bytes 204832 | tf_op jit(solution)/shard_map/ppermute | solution.py:43
  24.9 1.5 %collective-permute-start.3 = (bf16[2,2,2,8,3200]{4,3,2,1,0:T(8,128)(2,1)S(1)}, bf16[2,2,2,8,3200]{4,3,2,1,0:T(8,128)(2,1)S(1)}, u32[]{:S(2)}, u32[]{:S(2)}) collective-permute-start(bf16[2,2,2,8,3200]{4,3,2,1,0:T(8,128)(2,1)S(1)} %get-tuple-element.16.after_ref), channel_id=1, source_target_pairs={{0,16},{16,0},{1,17},{17,1},{2,18},{18,2},{3,19},{19,3},{4,20},{20... | collective-permute-start | bytes 1228808 | tf_op jit(solution)/shard_map/ppermute | solution.py:43
  26.4 4.6 %shard_map.73.refs_1_ = bf16[4,256,6144]{2,1,0:T(8,128)(2,1)S(1)} custom-call(bf16[4,256,6144]{2,1,0:T(8,128)(2,1)} %w_ref.1, bf16[2,2,2,8,3200]{4,3,2,1,0:T(8,128)(2,1)S(1)} %get-tuple-element.16.after_ref), custom_call_target="tpu_custom_call" | custom-call | bytes 12582912 | tf_op jit(solution)/shard_map/pallas_call | solution.py:82
  31.1 1.8 %collective-permute-done.3 = bf16[2,2,2,8,3200]{4,3,2,1,0:T(8,128)(2,1)S(1)} collective-permute-done((bf16[2,2,2,8,3200]{4,3,2,1,0:T(8,128)(2,1)S(1)}, bf16[2,2,2,8,3200]{4,3,2,1,0:T(8,128)(2,1)S(1)}, u32[]{:S(2)}, u32[]{:S(2)}) %collective-permute-start.3) | collective-permute-done | bytes 409632 | tf_op jit(solution)/shard_map/ppermute | solution.py:43
  32.9 0.1 fusion.24
  33.1 0.3 collective-permute-done.9
  33.4 0.1 pad_maximum_fusion.1
  33.6 0.1 copy.15
  33.7 6.8 %shard_map.74.refs_1_ = f32[256,2048]{1,0:T(8,128)S(1)} custom-call(bf16[256,3072]{1,0:T(8,128)(2,1)S(1)} %bitcast.94, bf16[4,2,256,6144]{3,2,1,0:T(8,128)(2,1)} %refs_2_.1), custom_call_target="tpu_custom_call" | custom-call | flops 3221225472 | bytes 14155776 | tf_op jit(solution)/shard_map/pallas_call | solution.py:176
  40.5 0.2 pad_maximum_fusion
  40.7 6.1 %shard_map.75.refs_0_ = bf16[4,256,256]{2,1,0:T(8,128)(2,1)S(1)} custom-call(bf16[256,3200]{1,0:T(8,128)(2,1)S(1)} %bitcast.93, f32[256,2048]{1,0:T(8,128)S(1)} %shard_map.74.refs_1_, bf16[4,2,256,6144]{3,2,1,0:T(8,128)(2,1)} %refs_2_.1), custom_call_target="tpu_custom_call" | custom-call | flops 3221225472 | bytes 14155776 | tf_op jit(solution)/shard_map/pallas_call | solution.py:176
  46.8 2.1 %shard_map.77 = bf16[256,3072]{1,0:T(8,128)(2,1)S(1)} custom-call(bf16[4,256,256]{2,1,0:T(8,128)(2,1)S(1)} %shard_map.75.refs_0_, bf16[4,256,6144]{2,1,0:T(8,128)(2,1)S(1)} %shard_map.73.refs_1_), custom_call_target="tpu_custom_call" | custom-call | flops 1610612736 | bytes 8388608 | tf_op jit(solution)/shard_map/pallas_call | solution.py:220
  49.1 0.3 collective-permute-start.15
  49.4 2.1 %shard_map.76 = bf16[256,3072]{1,0:T(8,128)(2,1)S(1)} custom-call(bf16[4,256,256]{2,1,0:T(8,128)(2,1)S(1)} %shard_map.75.refs_0_, bf16[4,256,6144]{2,1,0:T(8,128)(2,1)S(1)} %shard_map.73.refs_1_), custom_call_target="tpu_custom_call" | custom-call | flops 1610612736 | bytes 8388608 | tf_op jit(solution)/shard_map/pallas_call | solution.py:220
  51.6 0.4 collective-permute-start.10
  52.0 0.2 fusion.1
  52.2 1.6 %collective-permute-start.16 = (bf16[2,2,2,8,3072]{4,3,2,1,0:T(8,128)(2,1)S(1)}, bf16[2,2,2,8,3072]{4,3,2,1,0:T(8,128)(2,1)S(1)}, u32[]{:S(2)}, u32[]{:S(2)}) collective-permute-start(bf16[2,2,2,8,3072]{4,3,2,1,0:T(8,128)(2,1)S(1)} %slice_bitcast_fusion), channel_id=1, source_target_pairs={{0,2},{1,3},{2,0},{3,1},{4,6},{5,7},{6,4},{7,5},{8,10},{9,11},{10,... | collective-permute-start | bytes 1179656 | tf_op jit(solution)/shard_map/ppermute | solution.py:43
  53.8 0.1 collective-permute-done.10
  54.0 0.2 fusion
  54.2 1.5 %collective-permute-start.11 = (bf16[2,2,2,8,3072]{4,3,2,1,0:T(8,128)(2,1)S(1)}, bf16[2,2,2,8,3072]{4,3,2,1,0:T(8,128)(2,1)S(1)}, u32[]{:S(2)}, u32[]{:S(2)}) collective-permute-start(bf16[2,2,2,8,3072]{4,3,2,1,0:T(8,128)(2,1)S(1)} %slice_bitcast_fusion.2), channel_id=1, source_target_pairs={{0,16},{16,0},{1,17},{17,1},{2,18},{18,2},{3,19},{19,3},{4,20},{20... | collective-permute-start | bytes 1179656 | tf_op jit(solution)/shard_map/ppermute | solution.py:43
  55.7 7.8 %collective-permute-done.16 = bf16[2,2,2,8,3072]{4,3,2,1,0:T(8,128)(2,1)S(1)} collective-permute-done((bf16[2,2,2,8,3072]{4,3,2,1,0:T(8,128)(2,1)S(1)}, bf16[2,2,2,8,3072]{4,3,2,1,0:T(8,128)(2,1)S(1)}, u32[]{:S(2)}, u32[]{:S(2)}) %collective-permute-start.16) | collective-permute-done | bytes 393248 | tf_op jit(solution)/shard_map/ppermute | solution.py:43
  63.6 1.5 %collective-permute-start.17 = (bf16[2,2,8,3072]{3,2,1,0:T(8,128)(2,1)S(1)}, bf16[2,2,8,3072]{3,2,1,0:T(8,128)(2,1)S(1)}, u32[]{:S(2)}, u32[]{:S(2)}) collective-permute-start(bf16[2,2,8,3072]{3,2,1,0:T(8,128)(2,1)S(1)} %slice_bitcast_fusion.4), channel_id=1, source_target_pairs={{0,16},{16,0},{1,17},{17,1},{2,18},{18,2},{3,19},{19,3},{4,20},{20... | collective-permute-start | bytes 589832 | tf_op jit(solution)/shard_map/ppermute | solution.py:43
  65.1 0.5 collective-permute-done.11
  65.7 1.6 %collective-permute-start.12 = (bf16[2,2,8,3072]{3,2,1,0:T(8,128)(2,1)S(1)}, bf16[2,2,8,3072]{3,2,1,0:T(8,128)(2,1)S(1)}, u32[]{:S(2)}, u32[]{:S(2)}) collective-permute-start(bf16[2,2,8,3072]{3,2,1,0:T(8,128)(2,1)S(1)} %slice_bitcast_fusion.6), channel_id=1, source_target_pairs={{0,2},{1,3},{2,0},{3,1},{4,6},{5,7},{6,4},{7,5},{8,10},{9,11},{10,... | collective-permute-start | bytes 589832 | tf_op jit(solution)/shard_map/ppermute | solution.py:43
  67.3 2.6 %collective-permute-done.17 = bf16[2,2,8,3072]{3,2,1,0:T(8,128)(2,1)S(1)} collective-permute-done((bf16[2,2,8,3072]{3,2,1,0:T(8,128)(2,1)S(1)}, bf16[2,2,8,3072]{3,2,1,0:T(8,128)(2,1)S(1)}, u32[]{:S(2)}, u32[]{:S(2)}) %collective-permute-start.17) | collective-permute-done | bytes 196640 | tf_op jit(solution)/shard_map/ppermute | solution.py:43
  70.0 1.7 %collective-permute-start.18 = (bf16[2,8,3072]{2,1,0:T(8,128)(2,1)S(1)}, bf16[2,8,3072]{2,1,0:T(8,128)(2,1)S(1)}, u32[]{:S(2)}, u32[]{:S(2)}) collective-permute-start(bf16[2,8,3072]{2,1,0:T(8,128)(2,1)S(1)} %slice_bitcast_fusion.8), channel_id=1, source_target_pairs={{0,4},{4,0},{8,12},{12,8},{1,5},{5,1},{9,13},{13,9},{2,6},{6,2},{1... | collective-permute-start | bytes 294920 | tf_op jit(solution)/shard_map/ppermute | solution.py:43
  71.6 0.5 collective-permute-done.12
  72.2 1.7 %collective-permute-start.13 = (bf16[2,8,3072]{2,1,0:T(8,128)(2,1)S(1)}, bf16[2,8,3072]{2,1,0:T(8,128)(2,1)S(1)}, u32[]{:S(2)}, u32[]{:S(2)}) collective-permute-start(bf16[2,8,3072]{2,1,0:T(8,128)(2,1)S(1)} %slice_bitcast_fusion.10), channel_id=1, source_target_pairs={{0,4},{4,0},{8,12},{12,8},{1,5},{5,1},{9,13},{13,9},{2,6},{6,2},{1... | collective-permute-start | bytes 294920 | tf_op jit(solution)/shard_map/ppermute | solution.py:43
  73.9 1.7 %collective-permute-done.18 = bf16[2,8,3072]{2,1,0:T(8,128)(2,1)S(1)} collective-permute-done((bf16[2,8,3072]{2,1,0:T(8,128)(2,1)S(1)}, bf16[2,8,3072]{2,1,0:T(8,128)(2,1)S(1)}, u32[]{:S(2)}, u32[]{:S(2)}) %collective-permute-start.18) | collective-permute-done | bytes 98336 | tf_op jit(solution)/shard_map/ppermute | solution.py:43
  75.6 1.5 %collective-permute-start.19 = (bf16[8,3072]{1,0:T(8,128)(2,1)S(1)}, bf16[8,3072]{1,0:T(8,128)(2,1)S(1)}, u32[]{:S(2)}, u32[]{:S(2)}) collective-permute-start(bf16[8,3072]{1,0:T(8,128)(2,1)S(1)} %slice_bitcast_fusion.12), channel_id=1, source_target_pairs={{0,8},{4,12},{8,0},{12,4},{1,9},{5,13},{9,1},{13,5},{2,10},{6,14},... | collective-permute-start | bytes 147464 | tf_op jit(solution)/shard_map/ppermute | solution.py:43
  77.2 0.3 collective-permute-done.13
  77.5 1.5 %collective-permute-start.14 = (bf16[8,3072]{1,0:T(8,128)(2,1)S(1)}, bf16[8,3072]{1,0:T(8,128)(2,1)S(1)}, u32[]{:S(2)}, u32[]{:S(2)}) collective-permute-start(bf16[8,3072]{1,0:T(8,128)(2,1)S(1)} %slice_bitcast_fusion.14), channel_id=1, source_target_pairs={{0,8},{4,12},{8,0},{12,4},{1,9},{5,13},{9,1},{13,5},{2,10},{6,14},... | collective-permute-start | bytes 147464 | tf_op jit(solution)/shard_map/ppermute | solution.py:43
  79.0 2.2 %collective-permute-done.19 = bf16[8,3072]{1,0:T(8,128)(2,1)S(1)} collective-permute-done((bf16[8,3072]{1,0:T(8,128)(2,1)S(1)}, bf16[8,3072]{1,0:T(8,128)(2,1)S(1)}, u32[]{:S(2)}, u32[]{:S(2)}) %collective-permute-start.19) | collective-permute-done | bytes 49184 | tf_op jit(solution)/shard_map/ppermute | solution.py:43
  81.2 1.3 %collective-permute-done.14 = bf16[8,3072]{1,0:T(8,128)(2,1)S(1)} collective-permute-done((bf16[8,3072]{1,0:T(8,128)(2,1)S(1)}, bf16[8,3072]{1,0:T(8,128)(2,1)S(1)}, u32[]{:S(2)}, u32[]{:S(2)}) %collective-permute-start.14) | collective-permute-done | bytes 49184 | tf_op jit(solution)/shard_map/ppermute | solution.py:43
  82.5 0.6 pad_maximum_fusion.10
  (38 shorter events, 1.5 us)
Async XLA Ops:
  0.8 6.7 %collective-permute-start.5 = (bf16[8,3072]{1,0:T(8,128)(2,1)S(1)}, bf16[8,3072]{1,0:T(8,128)(2,1)S(1)}, u32[]{:S(2)}, u32[]{:S(2)}) collective-permute-start(bf16[8,3072]{1,0:T(8,128)(2,1)S(1)} %get-tuple-element.28), channel_id=1, source_target_pairs={{0,8},{4,12},{8,0},{12,4},{1,9},{5,13},{9,1},{13,5},{2,10},{6,14},... | collective-permute-start | bytes 147464 | tf_op jit(solution)/shard_map/ppermute | solution.py:43
  6.7 5.3 %collective-permute-start = (bf16[8,3200]{1,0:T(8,128)(2,1)S(1)}, bf16[8,3200]{1,0:T(8,128)(2,1)S(1)}, u32[]{:S(2)}, u32[]{:S(2)}) collective-permute-start(bf16[8,3200]{1,0:T(8,128)(2,1)S(1)} %get-tuple-element.31), channel_id=1, source_target_pairs={{0,8},{4,12},{8,0},{12,4},{1,9},{5,13},{9,1},{13,5},{2,10},{6,14},... | collective-permute-start | bytes 153608 | tf_op jit(solution)/shard_map/ppermute | solution.py:43
  7.6 6.0 %collective-permute-start.6 = (bf16[2,8,3072]{2,1,0:T(8,128)(2,1)S(1)}, bf16[2,8,3072]{2,1,0:T(8,128)(2,1)S(1)}, u32[]{:S(2)}, u32[]{:S(2)}) collective-permute-start(bf16[2,8,3072]{2,1,0:T(8,128)(2,1)S(1)} %get-tuple-element.26), channel_id=1, source_target_pairs={{0,4},{4,0},{8,12},{12,8},{1,5},{5,1},{9,13},{13,9},{2,6},{6,2},{1... | collective-permute-start | bytes 294920 | tf_op jit(solution)/shard_map/ppermute | solution.py:43
  12.0 4.7 %collective-permute-start.1 = (bf16[2,8,3200]{2,1,0:T(8,128)(2,1)S(1)}, bf16[2,8,3200]{2,1,0:T(8,128)(2,1)S(1)}, u32[]{:S(2)}, u32[]{:S(2)}) collective-permute-start(bf16[2,8,3200]{2,1,0:T(8,128)(2,1)S(1)} %get-tuple-element.24), channel_id=1, source_target_pairs={{0,4},{4,0},{8,12},{12,8},{1,5},{5,1},{9,13},{13,9},{2,6},{6,2},{1... | collective-permute-start | bytes 307208 | tf_op jit(solution)/shard_map/ppermute | solution.py:43
  13.6 5.7 %collective-permute-start.7 = (bf16[2,2,8,3072]{3,2,1,0:T(8,128)(2,1)S(1)}, bf16[2,2,8,3072]{3,2,1,0:T(8,128)(2,1)S(1)}, u32[]{:S(2)}, u32[]{:S(2)}) collective-permute-start(bf16[2,2,8,3072]{3,2,1,0:T(8,128)(2,1)S(1)} %get-tuple-element.22), channel_id=1, source_target_pairs={{0,16},{16,0},{1,17},{17,1},{2,18},{18,2},{3,19},{19,3},{4,20},{20... | collective-permute-start | bytes 589832 | tf_op jit(solution)/shard_map/ppermute | solution.py:43
  16.8 8.0 %collective-permute-start.2 = (bf16[2,2,8,3200]{3,2,1,0:T(8,128)(2,1)S(1)}, bf16[2,2,8,3200]{3,2,1,0:T(8,128)(2,1)S(1)}, u32[]{:S(2)}, u32[]{:S(2)}) collective-permute-start(bf16[2,2,8,3200]{3,2,1,0:T(8,128)(2,1)S(1)} %get-tuple-element.20), channel_id=1, source_target_pairs={{0,2},{1,3},{2,0},{3,1},{4,6},{5,7},{6,4},{7,5},{8,10},{9,11},{10,... | collective-permute-start | bytes 614408 | tf_op jit(solution)/shard_map/ppermute | solution.py:43
  19.4 11.6 %collective-permute-start.8 = (bf16[2,2,2,8,3072]{4,3,2,1,0:T(8,128)(2,1)S(1)}, bf16[2,2,2,8,3072]{4,3,2,1,0:T(8,128)(2,1)S(1)}, u32[]{:S(2)}, u32[]{:S(2)}) collective-permute-start(bf16[2,2,2,8,3072]{4,3,2,1,0:T(8,128)(2,1)S(1)} %get-tuple-element.18), channel_id=1, source_target_pairs={{0,2},{1,3},{2,0},{3,1},{4,6},{5,7},{6,4},{7,5},{8,10},{9,11},{10,... | collective-permute-start | bytes 1179656 | tf_op jit(solution)/shard_map/ppermute | solution.py:43
  24.9 8.0 %collective-permute-start.3 = (bf16[2,2,2,8,3200]{4,3,2,1,0:T(8,128)(2,1)S(1)}, bf16[2,2,2,8,3200]{4,3,2,1,0:T(8,128)(2,1)S(1)}, u32[]{:S(2)}, u32[]{:S(2)}) collective-permute-start(bf16[2,2,2,8,3200]{4,3,2,1,0:T(8,128)(2,1)S(1)} %get-tuple-element.16.after_ref), channel_id=1, source_target_pairs={{0,16},{16,0},{1,17},{17,1},{2,18},{18,2},{3,19},{19,3},{4,20},{20... | collective-permute-start | bytes 1228808 | tf_op jit(solution)/shard_map/ppermute | solution.py:43
  31.1 2.4 %collective-permute-start.9 = (bf16[2,2,2,2,8,3072]{5,4,3,2,0,1:T(8,128)(2,1)S(1)}, bf16[2,2,2,2,8,3072]{5,4,3,2,0,1:T(8,128)(2,1)S(1)}, u32[]{:S(2)}, u32[]{:S(2)}) collective-permute-start(bf16[2,2,2,2,8,3072]{5,4,3,2,0,1:T(8,128)(2,1)S(1)} %pad_maximum_fusion.3), channel_id=1, source_target_pairs={{0,1},{1,0},{2,3},{3,2},{4,5},{5,4},{6,7},{7,6},{8,9},{9,8},{10,11... | collective-permute-start | bytes 2359304 | tf_op jit(solution)/shard_map/ppermute | solution.py:43
  33.0 7.5 %collective-permute-start.4 = (bf16[2,2,2,2,8,3200]{5,4,3,2,1,0:T(8,128)(2,1)S(1)}, bf16[2,2,2,2,8,3200]{5,4,3,2,1,0:T(8,128)(2,1)S(1)}, u32[]{:S(2)}, u32[]{:S(2)}) collective-permute-start(bf16[2,2,2,2,8,3200]{5,4,3,2,1,0:T(8,128)(2,1)S(1)} %get-tuple-element.14), channel_id=1, source_target_pairs={{0,1},{1,0},{2,3},{3,2},{4,5},{5,4},{6,7},{7,6},{8,9},{9,8},{10,11... | collective-permute-start | bytes 2457608 | tf_op jit(solution)/shard_map/ppermute | solution.py:43
  49.1 2.9 %collective-permute-start.15 = (bf16[2,2,2,2,8,3072]{5,4,3,2,0,1:T(8,128)(2,1)S(1)}, bf16[2,2,2,2,8,3072]{5,4,3,2,0,1:T(8,128)(2,1)S(1)}, u32[]{:S(2)}, u32[]{:S(2)}) collective-permute-start(bf16[2,2,2,2,8,3072]{5,4,3,2,0,1:T(8,128)(2,1)S(1)} %copy.16), channel_id=1, source_target_pairs={{0,1},{1,0},{2,3},{3,2},{4,5},{5,4},{6,7},{7,6},{8,9},{9,8},{10,11... | collective-permute-start | bytes 2359304 | tf_op jit(solution)/shard_map/ppermute | solution.py:43
  51.6 2.4 %collective-permute-start.10 = (bf16[2,2,2,2,8,3072]{5,4,3,2,1,0:T(8,128)(2,1)S(1)}, bf16[2,2,2,2,8,3072]{5,4,3,2,1,0:T(8,128)(2,1)S(1)}, u32[]{:S(2)}, u32[]{:S(2)}) collective-permute-start(bf16[2,2,2,2,8,3072]{5,4,3,2,1,0:T(8,128)(2,1)S(1)} %bitcast.100), channel_id=1, source_target_pairs={{0,1},{1,0},{2,3},{3,2},{4,5},{5,4},{6,7},{7,6},{8,9},{9,8},{10,11... | collective-permute-start | bytes 2359304 | tf_op jit(solution)/shard_map/ppermute | solution.py:43
  52.2 11.3 %collective-permute-start.16 = (bf16[2,2,2,8,3072]{4,3,2,1,0:T(8,128)(2,1)S(1)}, bf16[2,2,2,8,3072]{4,3,2,1,0:T(8,128)(2,1)S(1)}, u32[]{:S(2)}, u32[]{:S(2)}) collective-permute-start(bf16[2,2,2,8,3072]{4,3,2,1,0:T(8,128)(2,1)S(1)} %slice_bitcast_fusion), channel_id=1, source_target_pairs={{0,2},{1,3},{2,0},{3,1},{4,6},{5,7},{6,4},{7,5},{8,10},{9,11},{10,... | collective-permute-start | bytes 1179656 | tf_op jit(solution)/shard_map/ppermute | solution.py:43
  54.2 11.4 %collective-permute-start.11 = (bf16[2,2,2,8,3072]{4,3,2,1,0:T(8,128)(2,1)S(1)}, bf16[2,2,2,8,3072]{4,3,2,1,0:T(8,128)(2,1)S(1)}, u32[]{:S(2)}, u32[]{:S(2)}) collective-permute-start(bf16[2,2,2,8,3072]{4,3,2,1,0:T(8,128)(2,1)S(1)} %slice_bitcast_fusion.2), channel_id=1, source_target_pairs={{0,16},{16,0},{1,17},{17,1},{2,18},{18,2},{3,19},{19,3},{4,20},{20... | collective-permute-start | bytes 1179656 | tf_op jit(solution)/shard_map/ppermute | solution.py:43
  63.6 6.3 %collective-permute-start.17 = (bf16[2,2,8,3072]{3,2,1,0:T(8,128)(2,1)S(1)}, bf16[2,2,8,3072]{3,2,1,0:T(8,128)(2,1)S(1)}, u32[]{:S(2)}, u32[]{:S(2)}) collective-permute-start(bf16[2,2,8,3072]{3,2,1,0:T(8,128)(2,1)S(1)} %slice_bitcast_fusion.4), channel_id=1, source_target_pairs={{0,16},{16,0},{1,17},{17,1},{2,18},{18,2},{3,19},{19,3},{4,20},{20... | collective-permute-start | bytes 589832 | tf_op jit(solution)/shard_map/ppermute | solution.py:43
  65.7 6.4 %collective-permute-start.12 = (bf16[2,2,8,3072]{3,2,1,0:T(8,128)(2,1)S(1)}, bf16[2,2,8,3072]{3,2,1,0:T(8,128)(2,1)S(1)}, u32[]{:S(2)}, u32[]{:S(2)}) collective-permute-start(bf16[2,2,8,3072]{3,2,1,0:T(8,128)(2,1)S(1)} %slice_bitcast_fusion.6), channel_id=1, source_target_pairs={{0,2},{1,3},{2,0},{3,1},{4,6},{5,7},{6,4},{7,5},{8,10},{9,11},{10,... | collective-permute-start | bytes 589832 | tf_op jit(solution)/shard_map/ppermute | solution.py:43
  70.0 5.6 %collective-permute-start.18 = (bf16[2,8,3072]{2,1,0:T(8,128)(2,1)S(1)}, bf16[2,8,3072]{2,1,0:T(8,128)(2,1)S(1)}, u32[]{:S(2)}, u32[]{:S(2)}) collective-permute-start(bf16[2,8,3072]{2,1,0:T(8,128)(2,1)S(1)} %slice_bitcast_fusion.8), channel_id=1, source_target_pairs={{0,4},{4,0},{8,12},{12,8},{1,5},{5,1},{9,13},{13,9},{2,6},{6,2},{1... | collective-permute-start | bytes 294920 | tf_op jit(solution)/shard_map/ppermute | solution.py:43
  72.2 5.2 %collective-permute-start.13 = (bf16[2,8,3072]{2,1,0:T(8,128)(2,1)S(1)}, bf16[2,8,3072]{2,1,0:T(8,128)(2,1)S(1)}, u32[]{:S(2)}, u32[]{:S(2)}) collective-permute-start(bf16[2,8,3072]{2,1,0:T(8,128)(2,1)S(1)} %slice_bitcast_fusion.10), channel_id=1, source_target_pairs={{0,4},{4,0},{8,12},{12,8},{1,5},{5,1},{9,13},{13,9},{2,6},{6,2},{1... | collective-permute-start | bytes 294920 | tf_op jit(solution)/shard_map/ppermute | solution.py:43
  75.6 5.6 %collective-permute-start.19 = (bf16[8,3072]{1,0:T(8,128)(2,1)S(1)}, bf16[8,3072]{1,0:T(8,128)(2,1)S(1)}, u32[]{:S(2)}, u32[]{:S(2)}) collective-permute-start(bf16[8,3072]{1,0:T(8,128)(2,1)S(1)} %slice_bitcast_fusion.12), channel_id=1, source_target_pairs={{0,8},{4,12},{8,0},{12,4},{1,9},{5,13},{9,1},{13,5},{2,10},{6,14},... | collective-permute-start | bytes 147464 | tf_op jit(solution)/shard_map/ppermute | solution.py:43
  77.5 5.1 %collective-permute-start.14 = (bf16[8,3072]{1,0:T(8,128)(2,1)S(1)}, bf16[8,3072]{1,0:T(8,128)(2,1)S(1)}, u32[]{:S(2)}, u32[]{:S(2)}) collective-permute-start(bf16[8,3072]{1,0:T(8,128)(2,1)S(1)} %slice_bitcast_fusion.14), channel_id=1, source_target_pairs={{0,8},{4,12},{8,0},{12,4},{1,9},{5,13},{9,1},{13,5},{2,10},{6,14},... | collective-permute-start | bytes 147464 | tf_op jit(solution)/shard_map/ppermute | solution.py:43

commit v7 on v6

--- a/solution.py
+++ b/solution.py
@@ -1,3 +1,5 @@
+import math
+
 import jax
 import jax.numpy as jnp
 from jax import lax
@@ -8,9 +10,8 @@
 AXES = ("dp", "expert", "shard")
 LANES = 128
 ROW_BLOCK = 256
-PIECES = 2
 FETCH_LIMIT = 1 * 2**20
-GATE_UP_LIMIT = 24 * 2**20
+GATE_UP_LIMIT = 8 * 2**20
 DOWN_LIMIT = 8 * 2**20
 
 
@@ -71,70 +72,55 @@
     return pltpu.with_memory_space_constraint(value, pltpu.HBM)
 
 
-def fetch_kernel(w_ref, after_ref, out_ref, sem):
+def fetch_kernel(take, w_ref, after_ref, out_ref, sem):
     del after_ref
-    copy = pltpu.make_async_copy(w_ref, out_ref, sem)
+    copy = pltpu.make_async_copy(take(w_ref), out_ref, sem)
     copy.start()
     copy.wait()
 
 
-def fetched(weight, after):
+def fetched(weight, take, shape, after):
+    def kernel(*refs):
+        fetch_kernel(take, *refs)
+
     return pl.pallas_call(
-        fetch_kernel,
+        kernel,
         in_specs=[pl.BlockSpec(memory_space=pl.ANY)] * 2,
         out_specs=pl.BlockSpec(memory_space=pltpu.VMEM),
-        out_shape=pltpu.VMEM(weight.shape, weight.dtype),
+        out_shape=pltpu.VMEM(shape, weight.dtype),
         scratch_shapes=[pltpu.SemaphoreType.DMA],
         compiler_params=pltpu.CompilerParams(vmem_limit_bytes=FETCH_LIMIT),
         cost_estimate=pl.CostEstimate(
-            flops=0, bytes_accessed=2 * weight.size, transcendentals=0
+            flops=0, bytes_accessed=4 * math.prod(shape), transcendentals=0
         ),
     )(in_hbm(weight), after)
 
 
-def gate_up_kernel(part, rows_ref, *refs):
-    last = part == 0
+def gate_up_kernel(last, take, rows_ref, *refs):
     if last:
-        sum_ref, w_hbm, out_ref, w_ref, sems = refs
+        sum_ref, w_ref, next_hbm, out_ref, next_ref, sem = refs
     else:
-        w_hbm, out_ref, w_ref, sems = refs
+        w_ref, next_hbm, out_ref, next_ref, sem = refs
     experts, _, sliver, half = w_ref.shape
-    depth = half // PIECES
     group = 2 if experts % 2 == 0 else 1
     units = 2 * sliver
-
-    def copy(slot, piece):
-        return pltpu.make_async_copy(
-            w_hbm.at[pl.ds(slot, group), :, :, pl.ds(part * half + piece * depth, depth)],
-            w_ref.at[pl.ds(slot, group), :, :, pl.ds(piece * depth, depth)],
-            sems.at[slot // group, piece],
-        )
-
-    @pl.when(pl.program_id(0) == 0)
-    def start():
-        for slot in range(0, experts, group):
-            for piece in range(PIECES):
-                copy(slot, piece).start()
-
+    copy = pltpu.make_async_copy(take(next_hbm), next_ref, sem)
+    pl.when(pl.program_id(0) == 0)(copy.start)
     if last:
         extra = rows_ref[:, half:].astype(jnp.float32)
         lane = lax.broadcasted_iota(jnp.int32, extra.shape, 1)
     for first in range(0, experts, group):
         columns = slice(first * units, (first + group) * units)
-        pre = sum_ref[:, columns] if last else None
-        for piece in range(PIECES):
-            pl.when(pl.program_id(0) == 0)(copy(first, piece).wait)
-            at = piece * depth
-            product = lax.dot_general(
-                rows_ref[:, at : at + depth],
-                w_ref[first : first + group, :, :, at : at + depth].reshape(group * units, depth),
-                (((1,), (1,)), ((), ())),
-                preferred_element_type=jnp.float32,
-            )
-            pre = product if pre is None else pre + product
+        pre = lax.dot_general(
+            rows_ref[:, :half],
+            w_ref[first : first + group].reshape(group * units, half),
+            (((1,), (1,)), ((), ())),
+            preferred_element_type=jnp.float32,
+        )
         if not last:
             out_ref[:, columns] = pre
             continue
+        pre += sum_ref[:, columns]
         for slot in range(first, first + group):
             at = (slot - first) * units
             gate, up = pre[:, at : at + sliver], pre[:, at + sliver : at + units]
@@ -142,16 +128,17 @@
             weigh = jnp.sum(jnp.where(mine, extra, 0.0), axis=1, keepdims=True)
             hidden = gate / (1.0 + jnp.exp(-gate)) * up * weigh
             out_ref[slot] = hidden.astype(out_ref.dtype)
-
-
-def gate_up_of(part, rows_of_part, sums, gate_up_weight):
-    experts, _, sliver, model_width = gate_up_weight.shape
-    half = model_width // 2
+    pl.when(pl.program_id(0) == 0)(copy.wait)
+
+
+def gate_up_of(rows_of_part, sums, weights, next_weight, take, next_shape):
+    experts, _, sliver, half = weights.shape
     rows, width = rows_of_part.shape
     row_block = min(ROW_BLOCK, rows)
     whole = rows == row_block
+    last = sums is not None
     units = experts * 2 * sliver
-    operands = [rows_of_part] if sums is None else [rows_of_part, sums]
+    operands = [rows_of_part, sums] if last else [rows_of_part]
     if whole:
         operands = [resident(operand) for operand in operands]
         specs = [pl.BlockSpec(memory_space=pltpu.VMEM)] * len(operands)
@@ -160,36 +147,34 @@
             pl.BlockSpec((row_block, width), lambda r: (r, 0)),
             pl.BlockSpec((row_block, units), lambda r: (r, 0)),
         ][: len(operands)]
-    if sums is None:
+    if last:
+        out_spec = pl.BlockSpec((experts, row_block, sliver), lambda r: (0, r, 0))
+        out_shape = jax.ShapeDtypeStruct((experts, rows, sliver), jnp.bfloat16)
+    else:
         out_spec = pl.BlockSpec((row_block, units), lambda r: (r, 0))
         out_shape = jax.ShapeDtypeStruct((rows, units), jnp.float32)
-    else:
-        out_spec = pl.BlockSpec((experts, row_block, sliver), lambda r: (0, r, 0))
-        out_shape = jax.ShapeDtypeStruct((experts, rows, sliver), jnp.bfloat16)
     if whole:
         out_spec = pl.BlockSpec(memory_space=pltpu.VMEM)
         out_shape = pltpu.VMEM(out_shape.shape, out_shape.dtype)
 
     def kernel(*refs):
-        gate_up_kernel(part, *refs)
+        gate_up_kernel(last, take, *refs)
 
     return pl.pallas_call(
         kernel,
         grid=(rows // row_block,),
-        in_specs=specs + [pl.BlockSpec(memory_space=pl.ANY)],
-        out_specs=out_spec,
-        out_shape=out_shape,
-        scratch_shapes=[
-            pltpu.VMEM((experts, 2, sliver, half), gate_up_weight.dtype),
-            pltpu.SemaphoreType.DMA((experts, PIECES)),
-        ],
+        in_specs=specs
+        + [pl.BlockSpec(memory_space=pltpu.VMEM), pl.BlockSpec(memory_space=pl.ANY)],
+        out_specs=[out_spec, pl.BlockSpec(memory_space=pltpu.VMEM)],
+        out_shape=[out_shape, pltpu.VMEM(next_shape, next_weight.dtype)],
+        scratch_shapes=[pltpu.SemaphoreType.DMA],
         compiler_params=pltpu.CompilerParams(vmem_limit_bytes=GATE_UP_LIMIT),
         cost_estimate=pl.CostEstimate(
-            flops=2 * rows * experts * sliver * model_width,
-            bytes_accessed=gate_up_weight.size + rows * model_width,
+            flops=4 * rows * experts * sliver * half,
+            bytes_accessed=2 * math.prod(next_shape) + 4 * rows * units,
             transcendentals=rows * experts * sliver,
         ),
-    )(*operands, in_hbm(gate_up_weight))
+    )(*operands, resident(weights), in_hbm(next_weight))
 
 
 def down_kernel(part, hidden_ref, w_ref, out_ref):
@@ -257,23 +242,34 @@
         jnp.concatenate([tokens[:, :half], extra], axis=1),
         tokens[:, half:],
     ]
+    half_shape = gate_up_weight.shape[:3] + (half,)
+
+    def take_first(ref):
+        return ref.at[:, :, :, pl.ds(0, half)]
+
+    def take_second(ref):
+        return ref.at[:, :, :, pl.ds(half, half)]
+
     blocks, held = list(parts), [[], []]
     last = len(routes[0]) - 1
     for step in range(last + 2):
         if step == last:
             before_last = blocks[0]
         if step == last + 1:
-            blocks[1], down_weight = lax.optimization_barrier(
-                (blocks[1], fetched(down_weight, before_last))
-            )
+            first_weights = fetched(gate_up_weight, take_second, half_shape, before_last)
+            blocks[1], first_weights = lax.optimization_barrier((blocks[1], first_weights))
         for number in (1, 0):
             digit = (routes[number] + core_digits)[step]
             dim = sum(dim_order.index(other) < dim_order.index(digit) for other in held[number])
             blocks[number] = digit.gather(blocks[number], dim)
             held[number].append(digit)
     gathered = [block.reshape(-1, part.shape[1]) for block, part in zip(blocks, parts)]
-    sums = gate_up_of(1, gathered[1], None, gate_up_weight)
-    hidden = gate_up_of(0, gathered[0], sums, gate_up_weight)
+    sums, weights = gate_up_of(
+        gathered[1], None, first_weights, gate_up_weight, take_first, half_shape
+    )
+    hidden, down_weight = gate_up_of(
+        gathered[0], sums, weights, down_weight, lambda ref: ref, down_weight.shape
+    )
     down_weight = resident(down_weight)
     results = []
     for number, route in enumerate(routes):

time: 83.4 us -> 83.4 us (level)
  transfers between devices with their start and end apart: 20 -> 20, of which waited for: 16 -> 16; matrix products, arithmetic and copies ran while one was open for 4% -> 4% of each run, Pallas kernels for 16% -> 14%
where the time goes in v7:
time: 83.4 us; the launch traced here: 83.1 us
  waiting for transfers between devices  29.3 us (35%)
  starting transfers between devices  26.7 us (32%)
  Pallas kernels  21.7 us (26%)
  other arithmetic  3.74 us (4%)
  local copies, waits for them, and re-layouts  1.43 us (2%)
    ppermute x20, waiting for transfers between devices, shift(): return lax.ppermute(value, self.name, pairs)  29.3 us
    ppermute x20, starting transfers between devices, shift(): return lax.ppermute(value, self.name, pairs)  26.7 us
    pallas_call x2, Pallas kernels, gate_up_of(): pl.pallas_call(kernel, grid=(rows // row_block,), in_specs=specs + [pl.Bl...  12.7 us
    pallas_call x1, Pallas kernels, fetched(): pl.pallas_call(kernel, in_specs=[pl.BlockSpec(memory_space=pl.ANY)] * 2,...  4.58 us
    pallas_call x2, Pallas kernels, down_of(): pl.pallas_call(kernel, grid=(rows // row_block,), in_specs=[pl.BlockSpec(...  4.36 us
  transfers between devices with their start and end apart: 20, of which 16 were waited for; matrix products, arithmetic and copies ran while one was open for 4% of the time, Pallas kernels for 14%

profile of v7, /device:TPU:0, one launch (start us, length us, event | category | flops | bytes accessed | tf_op | source)
XLA Modules:
  0.0 83.1 jit_solution(12428754756973011908)
XLA Ops:
  0.0 0.8 %slice_bitcast_fusion.16 = (bf16[1,8,3072]{2,1,0:T(8,128)(2,1)S(1)}, bf16[8,3072]{1,0:T(8,128)(2,1)S(1)}, bf16[8,3072]{1,0:T(8,128)(2,1)S(1)}) fusion(bf16[8,6144]{1,0:T(8,128)(2,1)} %param.8), kind=kLoop, calls=%fused_computation.64 | loop fusion | bytes 245760 | tf_op jit(solution)/shard_map/stack | solution.py:47
  0.8 4.1 %collective-permute-start.5 = (bf16[8,3072]{1,0:T(8,128)(2,1)S(1)}, bf16[8,3072]{1,0:T(8,128)(2,1)S(1)}, u32[]{:S(2)}, u32[]{:S(2)}) collective-permute-start(bf16[8,3072]{1,0:T(8,128)(2,1)S(1)} %get-tuple-element.36), channel_id=1, source_target_pairs={{0,8},{4,12},{8,0},{12,4},{1,9},{5,13},{9,1},{13,5},{2,10},{6,14},... | collective-permute-start | bytes 147464 | tf_op jit(solution)/shard_map/ppermute | solution.py:44
  4.9 0.7 compare_convert_fusion
  5.7 0.7 select_reduce_fusion
  6.7 0.8 collective-permute-done.5
  7.6 1.9 %collective-permute-start.6 = (bf16[2,8,3072]{2,1,0:T(8,128)(2,1)S(1)}, bf16[2,8,3072]{2,1,0:T(8,128)(2,1)S(1)}, u32[]{:S(2)}, u32[]{:S(2)}) collective-permute-start(bf16[2,8,3072]{2,1,0:T(8,128)(2,1)S(1)} %get-tuple-element.34), channel_id=1, source_target_pairs={{0,4},{4,0},{8,12},{12,8},{1,5},{5,1},{9,13},{13,9},{2,6},{6,2},{1... | collective-permute-start | bytes 294920 | tf_op jit(solution)/shard_map/ppermute | solution.py:44
  9.4 2.6 %collective-permute-done = bf16[8,3200]{1,0:T(8,128)(2,1)S(1)} collective-permute-done((bf16[8,3200]{1,0:T(8,128)(2,1)S(1)}, bf16[8,3200]{1,0:T(8,128)(2,1)S(1)}, u32[]{:S(2)}, u32[]{:S(2)}) %collective-permute-start) | collective-permute-done | bytes 51232 | tf_op jit(solution)/shard_map/ppermute | solution.py:44
  12.0 1.6 %collective-permute-start.1 = (bf16[2,8,3200]{2,1,0:T(8,128)(2,1)S(1)}, bf16[2,8,3200]{2,1,0:T(8,128)(2,1)S(1)}, u32[]{:S(2)}, u32[]{:S(2)}) collective-permute-start(bf16[2,8,3200]{2,1,0:T(8,128)(2,1)S(1)} %get-tuple-element.32), channel_id=1, source_target_pairs={{0,4},{4,0},{8,12},{12,8},{1,5},{5,1},{9,13},{13,9},{2,6},{6,2},{1... | collective-permute-start | bytes 307208 | tf_op jit(solution)/shard_map/ppermute | solution.py:44
  13.6 1.6 %collective-permute-start.7 = (bf16[2,2,8,3072]{3,2,1,0:T(8,128)(2,1)S(1)}, bf16[2,2,8,3072]{3,2,1,0:T(8,128)(2,1)S(1)}, u32[]{:S(2)}, u32[]{:S(2)}) collective-permute-start(bf16[2,2,8,3072]{3,2,1,0:T(8,128)(2,1)S(1)} %get-tuple-element.30), channel_id=1, source_target_pairs={{0,16},{16,0},{1,17},{17,1},{2,18},{18,2},{3,19},{19,3},{4,20},{20... | collective-permute-start | bytes 589832 | tf_op jit(solution)/shard_map/ppermute | solution.py:44
  15.2 1.6 %collective-permute-done.1 = bf16[2,8,3200]{2,1,0:T(8,128)(2,1)S(1)} collective-permute-done((bf16[2,8,3200]{2,1,0:T(8,128)(2,1)S(1)}, bf16[2,8,3200]{2,1,0:T(8,128)(2,1)S(1)}, u32[]{:S(2)}, u32[]{:S(2)}) %collective-permute-start.1) | collective-permute-done | bytes 102432 | tf_op jit(solution)/shard_map/ppermute | solution.py:44
  16.8 1.5 %collective-permute-start.2 = (bf16[2,2,8,3200]{3,2,1,0:T(8,128)(2,1)S(1)}, bf16[2,2,8,3200]{3,2,1,0:T(8,128)(2,1)S(1)}, u32[]{:S(2)}, u32[]{:S(2)}) collective-permute-start(bf16[2,2,8,3200]{3,2,1,0:T(8,128)(2,1)S(1)} %get-tuple-element.28), channel_id=1, source_target_pairs={{0,2},{1,3},{2,0},{3,1},{4,6},{5,7},{6,4},{7,5},{8,10},{9,11},{10,... | collective-permute-start | bytes 614408 | tf_op jit(solution)/shard_map/ppermute | solution.py:44
  18.3 1.1 %collective-permute-done.7 = bf16[2,2,8,3072]{3,2,1,0:T(8,128)(2,1)S(1)} collective-permute-done((bf16[2,2,8,3072]{3,2,1,0:T(8,128)(2,1)S(1)}, bf16[2,2,8,3072]{3,2,1,0:T(8,128)(2,1)S(1)}, u32[]{:S(2)}, u32[]{:S(2)}) %collective-permute-start.7) | collective-permute-done | bytes 196640 | tf_op jit(solution)/shard_map/ppermute | solution.py:44
  19.4 1.6 %collective-permute-start.8 = (bf16[2,2,2,8,3072]{4,3,2,1,0:T(8,128)(2,1)S(1)}, bf16[2,2,2,8,3072]{4,3,2,1,0:T(8,128)(2,1)S(1)}, u32[]{:S(2)}, u32[]{:S(2)}) collective-permute-start(bf16[2,2,2,8,3072]{4,3,2,1,0:T(8,128)(2,1)S(1)} %get-tuple-element.26), channel_id=1, source_target_pairs={{0,2},{1,3},{2,0},{3,1},{4,6},{5,7},{6,4},{7,5},{8,10},{9,11},{10,... | collective-permute-start | bytes 1179656 | tf_op jit(solution)/shard_map/ppermute | solution.py:44
  21.0 3.8 %collective-permute-done.2 = bf16[2,2,8,3200]{3,2,1,0:T(8,128)(2,1)S(1)} collective-permute-done((bf16[2,2,8,3200]{3,2,1,0:T(8,128)(2,1)S(1)}, bf16[2,2,8,3200]{3,2,1,0:T(8,128)(2,1)S(1)}, u32[]{:S(2)}, u32[]{:S(2)}) %collective-permute-start.2) | collective-permute-done | bytes 204832 | tf_op jit(solution)/shard_map/ppermute | solution.py:44
  24.9 1.5 %collective-permute-start.3 = (bf16[2,2,2,8,3200]{4,3,2,1,0:T(8,128)(2,1)S(1)}, bf16[2,2,2,8,3200]{4,3,2,1,0:T(8,128)(2,1)S(1)}, u32[]{:S(2)}, u32[]{:S(2)}) collective-permute-start(bf16[2,2,2,8,3200]{4,3,2,1,0:T(8,128)(2,1)S(1)} %get-tuple-element.24.refs_1_), channel_id=1, source_target_pairs={{0,16},{16,0},{1,17},{17,1},{2,18},{18,2},{3,19},{19,3},{4,20},{20... | collective-permute-start | bytes 1228808 | tf_op jit(solution)/shard_map/ppermute | solution.py:44
  26.4 4.6 %shard_map.73.refs_1_ = bf16[4,2,256,3072]{3,2,1,0:T(8,128)(2,1)S(1)} custom-call(bf16[4,2,256,6144]{3,2,1,0:T(8,128)(2,1)} %refs_2_.1, bf16[2,2,2,8,3200]{4,3,2,1,0:T(8,128)(2,1)S(1)} %get-tuple-element.24.refs_1_), custom_call_target="tpu_custom_call" | custom-call | bytes 25165824 | tf_op jit(solution)/shard_map/pallas_call | solution.py:86
  31.1 1.8 %collective-permute-done.3 = bf16[2,2,2,8,3200]{4,3,2,1,0:T(8,128)(2,1)S(1)} collective-permute-done((bf16[2,2,2,8,3200]{4,3,2,1,0:T(8,128)(2,1)S(1)}, bf16[2,2,2,8,3200]{4,3,2,1,0:T(8,128)(2,1)S(1)}, u32[]{:S(2)}, u32[]{:S(2)}) %collective-permute-start.3) | collective-permute-done | bytes 409632 | tf_op jit(solution)/shard_map/ppermute | solution.py:44
  32.9 0.1 fusion.24
  33.1 0.3 collective-permute-done.9
  33.4 0.1 pad_maximum_fusion.1
  33.6 0.1 copy.15
  33.7 4.7 %shard_map.74 = (f32[256,2048]{1,0:T(8,128)S(1)}, bf16[4,2,256,3072]{3,2,1,0:T(8,128)(2,1)S(1)}) custom-call(bf16[256,3072]{1,0:T(8,128)(2,1)S(1)} %bitcast.94, bf16[4,2,256,3072]{3,2,1,0:T(8,128)(2,1)S(1)} %shard_map.73.refs_1_, bf16[4,2,256,6144]{3,2,1,0:T(8,128)(2,1)} %refs_2_.1), custom_call_target="tpu_custom_call" | custom-call | flops 3221225472 | bytes 14680064 | tf_op jit(solution)/shard_map/pallas_call | solution.py:163
  38.4 0.2 pad_maximum_fusion
  38.6 8.0 %shard_map.75 = (bf16[4,256,256]{2,1,0:T(8,128)(2,1)S(1)}, bf16[4,256,6144]{2,1,0:T(8,128)(2,1)S(1)}) custom-call(bf16[256,3200]{1,0:T(8,128)(2,1)S(1)} %bitcast.93, f32[256,2048]{1,0:T(8,128)S(1)} %get-tuple-element.13.refs_1_, bf16[4,2,256,3072]{3,2,1,0:T(8,128)(2,1)S(1)} %get-tuple-element.14.refs_2_, bf16[4,256,6144]{2,1,0:T(8,128)(2,1)} %refs_3_.1), custom_call_target="tpu_custom_call" | custom-call | flops 3221225472 | bytes 14680064 | tf_op jit(solution)/shard_map/pallas_call | solution.py:163
  46.6 2.2 %shard_map.76 = bf16[256,3072]{1,0:T(8,128)(2,1)S(1)} custom-call(bf16[4,256,256]{2,1,0:T(8,128)(2,1)S(1)} %get-tuple-element.15.refs_0_, bf16[4,256,6144]{2,1,0:T(8,128)(2,1)S(1)} %get-tuple-element.16.refs_1_), custom_call_target="tpu_custom_call" | custom-call | flops 1610612736 | bytes 8388608 | tf_op jit(solution)/shard_map/pallas_call | solution.py:205
  48.9 0.2 collective-permute-start.10
  49.2 2.2 %shard_map.77 = bf16[256,3072]{1,0:T(8,128)(2,1)S(1)} custom-call(bf16[4,256,256]{2,1,0:T(8,128)(2,1)S(1)} %get-tuple-element.15.refs_0_, bf16[4,256,6144]{2,1,0:T(8,128)(2,1)S(1)} %get-tuple-element.16.refs_1_), custom_call_target="tpu_custom_call" | custom-call | flops 1610612736 | bytes 8388608 | tf_op jit(solution)/shard_map/pallas_call | solution.py:205
  51.5 0.4 collective-permute-start.15
  51.9 0.2 fusion
  52.2 1.2 %collective-permute-start.11 = (bf16[2,2,2,8,3072]{4,3,2,1,0:T(8,128)(2,1)S(1)}, bf16[2,2,2,8,3072]{4,3,2,1,0:T(8,128)(2,1)S(1)}, u32[]{:S(2)}, u32[]{:S(2)}) collective-permute-start(bf16[2,2,2,8,3072]{4,3,2,1,0:T(8,128)(2,1)S(1)} %slice_bitcast_fusion.2), channel_id=1, source_target_pairs={{0,16},{16,0},{1,17},{17,1},{2,18},{18,2},{3,19},{19,3},{4,20},{20... | collective-permute-start | bytes 1179656 | tf_op jit(solution)/shard_map/ppermute | solution.py:44
  53.4 0.5 collective-permute-done.15
  53.9 0.2 fusion.1
  54.1 1.6 %collective-permute-start.16 = (bf16[2,2,2,8,3072]{4,3,2,1,0:T(8,128)(2,1)S(1)}, bf16[2,2,2,8,3072]{4,3,2,1,0:T(8,128)(2,1)S(1)}, u32[]{:S(2)}, u32[]{:S(2)}) collective-permute-start(bf16[2,2,2,8,3072]{4,3,2,1,0:T(8,128)(2,1)S(1)} %slice_bitcast_fusion), channel_id=1, source_target_pairs={{0,2},{1,3},{2,0},{3,1},{4,6},{5,7},{6,4},{7,5},{8,10},{9,11},{10,... | collective-permute-start | bytes 1179656 | tf_op jit(solution)/shard_map/ppermute | solution.py:44
  55.7 7.8 %collective-permute-done.11 = bf16[2,2,2,8,3072]{4,3,2,1,0:T(8,128)(2,1)S(1)} collective-permute-done((bf16[2,2,2,8,3072]{4,3,2,1,0:T(8,128)(2,1)S(1)}, bf16[2,2,2,8,3072]{4,3,2,1,0:T(8,128)(2,1)S(1)}, u32[]{:S(2)}, u32[]{:S(2)}) %collective-permute-start.11) | collective-permute-done | bytes 393248 | tf_op jit(solution)/shard_map/ppermute | solution.py:44
  63.6 1.5 %collective-permute-start.12 = (bf16[2,2,8,3072]{3,2,1,0:T(8,128)(2,1)S(1)}, bf16[2,2,8,3072]{3,2,1,0:T(8,128)(2,1)S(1)}, u32[]{:S(2)}, u32[]{:S(2)}) collective-permute-start(bf16[2,2,8,3072]{3,2,1,0:T(8,128)(2,1)S(1)} %slice_bitcast_fusion.6), channel_id=1, source_target_pairs={{0,2},{1,3},{2,0},{3,1},{4,6},{5,7},{6,4},{7,5},{8,10},{9,11},{10,... | collective-permute-start | bytes 589832 | tf_op jit(solution)/shard_map/ppermute | solution.py:44
  65.1 0.4 collective-permute-done.16
  65.7 1.3 %collective-permute-start.17 = (bf16[2,2,8,3072]{3,2,1,0:T(8,128)(2,1)S(1)}, bf16[2,2,8,3072]{3,2,1,0:T(8,128)(2,1)S(1)}, u32[]{:S(2)}, u32[]{:S(2)}) collective-permute-start(bf16[2,2,8,3072]{3,2,1,0:T(8,128)(2,1)S(1)} %slice_bitcast_fusion.4), channel_id=1, source_target_pairs={{0,16},{16,0},{1,17},{17,1},{2,18},{18,2},{3,19},{19,3},{4,20},{20... | collective-permute-start | bytes 589832 | tf_op jit(solution)/shard_map/ppermute | solution.py:44
  67.0 2.8 %collective-permute-done.12 = bf16[2,2,8,3072]{3,2,1,0:T(8,128)(2,1)S(1)} collective-permute-done((bf16[2,2,8,3072]{3,2,1,0:T(8,128)(2,1)S(1)}, bf16[2,2,8,3072]{3,2,1,0:T(8,128)(2,1)S(1)}, u32[]{:S(2)}, u32[]{:S(2)}) %collective-permute-start.12) | collective-permute-done | bytes 196640 | tf_op jit(solution)/shard_map/ppermute | solution.py:44
  69.9 1.6 %collective-permute-start.13 = (bf16[2,8,3072]{2,1,0:T(8,128)(2,1)S(1)}, bf16[2,8,3072]{2,1,0:T(8,128)(2,1)S(1)}, u32[]{:S(2)}, u32[]{:S(2)}) collective-permute-start(bf16[2,8,3072]{2,1,0:T(8,128)(2,1)S(1)} %slice_bitcast_fusion.10), channel_id=1, source_target_pairs={{0,4},{4,0},{8,12},{12,8},{1,5},{5,1},{9,13},{13,9},{2,6},{6,2},{1... | collective-permute-start | bytes 294920 | tf_op jit(solution)/shard_map/ppermute | solution.py:44
  71.5 0.6 collective-permute-done.17
  72.1 1.7 %collective-permute-start.18 = (bf16[2,8,3072]{2,1,0:T(8,128)(2,1)S(1)}, bf16[2,8,3072]{2,1,0:T(8,128)(2,1)S(1)}, u32[]{:S(2)}, u32[]{:S(2)}) collective-permute-start(bf16[2,8,3072]{2,1,0:T(8,128)(2,1)S(1)} %slice_bitcast_fusion.8), channel_id=1, source_target_pairs={{0,4},{4,0},{8,12},{12,8},{1,5},{5,1},{9,13},{13,9},{2,6},{6,2},{1... | collective-permute-start | bytes 294920 | tf_op jit(solution)/shard_map/ppermute | solution.py:44
  73.8 1.7 %collective-permute-done.13 = bf16[2,8,3072]{2,1,0:T(8,128)(2,1)S(1)} collective-permute-done((bf16[2,8,3072]{2,1,0:T(8,128)(2,1)S(1)}, bf16[2,8,3072]{2,1,0:T(8,128)(2,1)S(1)}, u32[]{:S(2)}, u32[]{:S(2)}) %collective-permute-start.13) | collective-permute-done | bytes 98336 | tf_op jit(solution)/shard_map/ppermute | solution.py:44
  75.6 1.6 %collective-permute-start.14 = (bf16[8,3072]{1,0:T(8,128)(2,1)S(1)}, bf16[8,3072]{1,0:T(8,128)(2,1)S(1)}, u32[]{:S(2)}, u32[]{:S(2)}) collective-permute-start(bf16[8,3072]{1,0:T(8,128)(2,1)S(1)} %slice_bitcast_fusion.14), channel_id=1, source_target_pairs={{0,8},{4,12},{8,0},{12,4},{1,9},{5,13},{9,1},{13,5},{2,10},{6,14},... | collective-permute-start | bytes 147464 | tf_op jit(solution)/shard_map/ppermute | solution.py:44
  77.1 0.2 collective-permute-done.18
  77.4 1.6 %collective-permute-start.19 = (bf16[8,3072]{1,0:T(8,128)(2,1)S(1)}, bf16[8,3072]{1,0:T(8,128)(2,1)S(1)}, u32[]{:S(2)}, u32[]{:S(2)}) collective-permute-start(bf16[8,3072]{1,0:T(8,128)(2,1)S(1)} %slice_bitcast_fusion.12), channel_id=1, source_target_pairs={{0,8},{4,12},{8,0},{12,4},{1,9},{5,13},{9,1},{13,5},{2,10},{6,14},... | collective-permute-start | bytes 147464 | tf_op jit(solution)/shard_map/ppermute | solution.py:44
  78.9 2.2 %collective-permute-done.14 = bf16[8,3072]{1,0:T(8,128)(2,1)S(1)} collective-permute-done((bf16[8,3072]{1,0:T(8,128)(2,1)S(1)}, bf16[8,3072]{1,0:T(8,128)(2,1)S(1)}, u32[]{:S(2)}, u32[]{:S(2)}) %collective-permute-start.14) | collective-permute-done | bytes 49184 | tf_op jit(solution)/shard_map/ppermute | solution.py:44
  81.2 1.3 %collective-permute-done.19 = bf16[8,3072]{1,0:T(8,128)(2,1)S(1)} collective-permute-done((bf16[8,3072]{1,0:T(8,128)(2,1)S(1)}, bf16[8,3072]{1,0:T(8,128)(2,1)S(1)}, u32[]{:S(2)}, u32[]{:S(2)}) %collective-permute-start.19) | collective-permute-done | bytes 49184 | tf_op jit(solution)/shard_map/ppermute | solution.py:44
  82.5 0.6 pad_maximum_fusion.10
  (38 shorter events, 1.5 us)
Async XLA Ops:
  0.8 6.7 %collective-permute-start.5 = (bf16[8,3072]{1,0:T(8,128)(2,1)S(1)}, bf16[8,3072]{1,0:T(8,128)(2,1)S(1)}, u32[]{:S(2)}, u32[]{:S(2)}) collective-permute-start(bf16[8,3072]{1,0:T(8,128)(2,1)S(1)} %get-tuple-element.36), channel_id=1, source_target_pairs={{0,8},{4,12},{8,0},{12,4},{1,9},{5,13},{9,1},{13,5},{2,10},{6,14},... | collective-permute-start | bytes 147464 | tf_op jit(solution)/shard_map/ppermute | solution.py:44
  6.7 5.3 %collective-permute-start = (bf16[8,3200]{1,0:T(8,128)(2,1)S(1)}, bf16[8,3200]{1,0:T(8,128)(2,1)S(1)}, u32[]{:S(2)}, u32[]{:S(2)}) collective-permute-start(bf16[8,3200]{1,0:T(8,128)(2,1)S(1)} %get-tuple-element.39), channel_id=1, source_target_pairs={{0,8},{4,12},{8,0},{12,4},{1,9},{5,13},{9,1},{13,5},{2,10},{6,14},... | collective-permute-start | bytes 153608 | tf_op jit(solution)/shard_map/ppermute | solution.py:44
  7.6 6.0 %collective-permute-start.6 = (bf16[2,8,3072]{2,1,0:T(8,128)(2,1)S(1)}, bf16[2,8,3072]{2,1,0:T(8,128)(2,1)S(1)}, u32[]{:S(2)}, u32[]{:S(2)}) collective-permute-start(bf16[2,8,3072]{2,1,0:T(8,128)(2,1)S(1)} %get-tuple-element.34), channel_id=1, source_target_pairs={{0,4},{4,0},{8,12},{12,8},{1,5},{5,1},{9,13},{13,9},{2,6},{6,2},{1... | collective-permute-start | bytes 294920 | tf_op jit(solution)/shard_map/ppermute | solution.py:44
  12.0 4.7 %collective-permute-start.1 = (bf16[2,8,3200]{2,1,0:T(8,128)(2,1)S(1)}, bf16[2,8,3200]{2,1,0:T(8,128)(2,1)S(1)}, u32[]{:S(2)}, u32[]{:S(2)}) collective-permute-start(bf16[2,8,3200]{2,1,0:T(8,128)(2,1)S(1)} %get-tuple-element.32), channel_id=1, source_target_pairs={{0,4},{4,0},{8,12},{12,8},{1,5},{5,1},{9,13},{13,9},{2,6},{6,2},{1... | collective-permute-start | bytes 307208 | tf_op jit(solution)/shard_map/ppermute | solution.py:44
  13.6 5.7 %collective-permute-start.7 = (bf16[2,2,8,3072]{3,2,1,0:T(8,128)(2,1)S(1)}, bf16[2,2,8,3072]{3,2,1,0:T(8,128)(2,1)S(1)}, u32[]{:S(2)}, u32[]{:S(2)}) collective-permute-start(bf16[2,2,8,3072]{3,2,1,0:T(8,128)(2,1)S(1)} %get-tuple-element.30), channel_id=1, source_target_pairs={{0,16},{16,0},{1,17},{17,1},{2,18},{18,2},{3,19},{19,3},{4,20},{20... | collective-permute-start | bytes 589832 | tf_op jit(solution)/shard_map/ppermute | solution.py:44
  16.8 8.0 %collective-permute-start.2 = (bf16[2,2,8,3200]{3,2,1,0:T(8,128)(2,1)S(1)}, bf16[2,2,8,3200]{3,2,1,0:T(8,128)(2,1)S(1)}, u32[]{:S(2)}, u32[]{:S(2)}) collective-permute-start(bf16[2,2,8,3200]{3,2,1,0:T(8,128)(2,1)S(1)} %get-tuple-element.28), channel_id=1, source_target_pairs={{0,2},{1,3},{2,0},{3,1},{4,6},{5,7},{6,4},{7,5},{8,10},{9,11},{10,... | collective-permute-start | bytes 614408 | tf_op jit(solution)/shard_map/ppermute | solution.py:44
  19.4 11.6 %collective-permute-start.8 = (bf16[2,2,2,8,3072]{4,3,2,1,0:T(8,128)(2,1)S(1)}, bf16[2,2,2,8,3072]{4,3,2,1,0:T(8,128)(2,1)S(1)}, u32[]{:S(2)}, u32[]{:S(2)}) collective-permute-start(bf16[2,2,2,8,3072]{4,3,2,1,0:T(8,128)(2,1)S(1)} %get-tuple-element.26), channel_id=1, source_target_pairs={{0,2},{1,3},{2,0},{3,1},{4,6},{5,7},{6,4},{7,5},{8,10},{9,11},{10,... | collective-permute-start | bytes 1179656 | tf_op jit(solution)/shard_map/ppermute | solution.py:44
  24.9 8.0 %collective-permute-start.3 = (bf16[2,2,2,8,3200]{4,3,2,1,0:T(8,128)(2,1)S(1)}, bf16[2,2,2,8,3200]{4,3,2,1,0:T(8,128)(2,1)S(1)}, u32[]{:S(2)}, u32[]{:S(2)}) collective-permute-start(bf16[2,2,2,8,3200]{4,3,2,1,0:T(8,128)(2,1)S(1)} %get-tuple-element.24.refs_1_), channel_id=1, source_target_pairs={{0,16},{16,0},{1,17},{17,1},{2,18},{18,2},{3,19},{19,3},{4,20},{20... | collective-permute-start | bytes 1228808 | tf_op jit(solution)/shard_map/ppermute | solution.py:44
  31.1 2.4 %collective-permute-start.9 = (bf16[2,2,2,2,8,3072]{5,4,3,2,0,1:T(8,128)(2,1)S(1)}, bf16[2,2,2,2,8,3072]{5,4,3,2,0,1:T(8,128)(2,1)S(1)}, u32[]{:S(2)}, u32[]{:S(2)}) collective-permute-start(bf16[2,2,2,2,8,3072]{5,4,3,2,0,1:T(8,128)(2,1)S(1)} %pad_maximum_fusion.3), channel_id=1, source_target_pairs={{0,1},{1,0},{2,3},{3,2},{4,5},{5,4},{6,7},{7,6},{8,9},{9,8},{10,11... | collective-permute-start | bytes 2359304 | tf_op jit(solution)/shard_map/ppermute | solution.py:44
  33.0 5.4 %collective-permute-start.4 = (bf16[2,2,2,2,8,3200]{5,4,3,2,1,0:T(8,128)(2,1)S(1)}, bf16[2,2,2,2,8,3200]{5,4,3,2,1,0:T(8,128)(2,1)S(1)}, u32[]{:S(2)}, u32[]{:S(2)}) collective-permute-start(bf16[2,2,2,2,8,3200]{5,4,3,2,1,0:T(8,128)(2,1)S(1)} %get-tuple-element.22), channel_id=1, source_target_pairs={{0,1},{1,0},{2,3},{3,2},{4,5},{5,4},{6,7},{7,6},{8,9},{9,8},{10,11... | collective-permute-start | bytes 2457608 | tf_op jit(solution)/shard_map/ppermute | solution.py:44
  48.9 3.0 %collective-permute-start.10 = (bf16[2,2,2,2,8,3072]{5,4,3,2,1,0:T(8,128)(2,1)S(1)}, bf16[2,2,2,2,8,3072]{5,4,3,2,1,0:T(8,128)(2,1)S(1)}, u32[]{:S(2)}, u32[]{:S(2)}) collective-permute-start(bf16[2,2,2,2,8,3072]{5,4,3,2,1,0:T(8,128)(2,1)S(1)} %bitcast.100), channel_id=1, source_target_pairs={{0,1},{1,0},{2,3},{3,2},{4,5},{5,4},{6,7},{7,6},{8,9},{9,8},{10,11... | collective-permute-start | bytes 2359304 | tf_op jit(solution)/shard_map/ppermute | solution.py:44
  51.5 2.4 %collective-permute-start.15 = (bf16[2,2,2,2,8,3072]{5,4,3,2,0,1:T(8,128)(2,1)S(1)}, bf16[2,2,2,2,8,3072]{5,4,3,2,0,1:T(8,128)(2,1)S(1)}, u32[]{:S(2)}, u32[]{:S(2)}) collective-permute-start(bf16[2,2,2,2,8,3072]{5,4,3,2,0,1:T(8,128)(2,1)S(1)} %copy.16), channel_id=1, source_target_pairs={{0,1},{1,0},{2,3},{3,2},{4,5},{5,4},{6,7},{7,6},{8,9},{9,8},{10,11... | collective-permute-start | bytes 2359304 | tf_op jit(solution)/shard_map/ppermute | solution.py:44
  52.2 11.3 %collective-permute-start.11 = (bf16[2,2,2,8,3072]{4,3,2,1,0:T(8,128)(2,1)S(1)}, bf16[2,2,2,8,3072]{4,3,2,1,0:T(8,128)(2,1)S(1)}, u32[]{:S(2)}, u32[]{:S(2)}) collective-permute-start(bf16[2,2,2,8,3072]{4,3,2,1,0:T(8,128)(2,1)S(1)} %slice_bitcast_fusion.2), channel_id=1, source_target_pairs={{0,16},{16,0},{1,17},{17,1},{2,18},{18,2},{3,19},{19,3},{4,20},{20... | collective-permute-start | bytes 1179656 | tf_op jit(solution)/shard_map/ppermute | solution.py:44
  54.1 11.4 %collective-permute-start.16 = (bf16[2,2,2,8,3072]{4,3,2,1,0:T(8,128)(2,1)S(1)}, bf16[2,2,2,8,3072]{4,3,2,1,0:T(8,128)(2,1)S(1)}, u32[]{:S(2)}, u32[]{:S(2)}) collective-permute-start(bf16[2,2,2,8,3072]{4,3,2,1,0:T(8,128)(2,1)S(1)} %slice_bitcast_fusion), channel_id=1, source_target_pairs={{0,2},{1,3},{2,0},{3,1},{4,6},{5,7},{6,4},{7,5},{8,10},{9,11},{10,... | collective-permute-start | bytes 1179656 | tf_op jit(solution)/shard_map/ppermute | solution.py:44
  63.6 6.2 %collective-permute-start.12 = (bf16[2,2,8,3072]{3,2,1,0:T(8,128)(2,1)S(1)}, bf16[2,2,8,3072]{3,2,1,0:T(8,128)(2,1)S(1)}, u32[]{:S(2)}, u32[]{:S(2)}) collective-permute-start(bf16[2,2,8,3072]{3,2,1,0:T(8,128)(2,1)S(1)} %slice_bitcast_fusion.6), channel_id=1, source_target_pairs={{0,2},{1,3},{2,0},{3,1},{4,6},{5,7},{6,4},{7,5},{8,10},{9,11},{10,... | collective-permute-start | bytes 589832 | tf_op jit(solution)/shard_map/ppermute | solution.py:44
  65.7 6.4 %collective-permute-start.17 = (bf16[2,2,8,3072]{3,2,1,0:T(8,128)(2,1)S(1)}, bf16[2,2,8,3072]{3,2,1,0:T(8,128)(2,1)S(1)}, u32[]{:S(2)}, u32[]{:S(2)}) collective-permute-start(bf16[2,2,8,3072]{3,2,1,0:T(8,128)(2,1)S(1)} %slice_bitcast_fusion.4), channel_id=1, source_target_pairs={{0,16},{16,0},{1,17},{17,1},{2,18},{18,2},{3,19},{19,3},{4,20},{20... | collective-permute-start | bytes 589832 | tf_op jit(solution)/shard_map/ppermute | solution.py:44
  69.9 5.7 %collective-permute-start.13 = (bf16[2,8,3072]{2,1,0:T(8,128)(2,1)S(1)}, bf16[2,8,3072]{2,1,0:T(8,128)(2,1)S(1)}, u32[]{:S(2)}, u32[]{:S(2)}) collective-permute-start(bf16[2,8,3072]{2,1,0:T(8,128)(2,1)S(1)} %slice_bitcast_fusion.10), channel_id=1, source_target_pairs={{0,4},{4,0},{8,12},{12,8},{1,5},{5,1},{9,13},{13,9},{2,6},{6,2},{1... | collective-permute-start | bytes 294920 | tf_op jit(solution)/shard_map/ppermute | solution.py:44
  72.1 5.2 %collective-permute-start.18 = (bf16[2,8,3072]{2,1,0:T(8,128)(2,1)S(1)}, bf16[2,8,3072]{2,1,0:T(8,128)(2,1)S(1)}, u32[]{:S(2)}, u32[]{:S(2)}) collective-permute-start(bf16[2,8,3072]{2,1,0:T(8,128)(2,1)S(1)} %slice_bitcast_fusion.8), channel_id=1, source_target_pairs={{0,4},{4,0},{8,12},{12,8},{1,5},{5,1},{9,13},{13,9},{2,6},{6,2},{1... | collective-permute-start | bytes 294920 | tf_op jit(solution)/shard_map/ppermute | solution.py:44
  75.6 5.6 %collective-permute-start.14 = (bf16[8,3072]{1,0:T(8,128)(2,1)S(1)}, bf16[8,3072]{1,0:T(8,128)(2,1)S(1)}, u32[]{:S(2)}, u32[]{:S(2)}) collective-permute-start(bf16[8,3072]{1,0:T(8,128)(2,1)S(1)} %slice_bitcast_fusion.14), channel_id=1, source_target_pairs={{0,8},{4,12},{8,0},{12,4},{1,9},{5,13},{9,1},{13,5},{2,10},{6,14},... | collective-permute-start | bytes 147464 | tf_op jit(solution)/shard_map/ppermute | solution.py:44
  77.4 5.1 %collective-permute-start.19 = (bf16[8,3072]{1,0:T(8,128)(2,1)S(1)}, bf16[8,3072]{1,0:T(8,128)(2,1)S(1)}, u32[]{:S(2)}, u32[]{:S(2)}) collective-permute-start(bf16[8,3072]{1,0:T(8,128)(2,1)S(1)} %slice_bitcast_fusion.12), channel_id=1, source_target_pairs={{0,8},{4,12},{8,0},{12,4},{1,9},{5,13},{9,1},{13,5},{2,10},{6,14},... | collective-permute-start | bytes 147464 | tf_op jit(solution)/shard_map/ppermute | solution.py:44

commit v8 on v7

--- a/solution.py
+++ b/solution.py
@@ -96,57 +96,65 @@
     )(in_hbm(weight), after)
 
 
-def gate_up_kernel(last, take, rows_ref, *refs):
+def gate_up_kernel(last, take, pieces, *refs):
+    row_refs, refs = refs[:2], refs[2:]
     if last:
-        sum_ref, w_ref, next_hbm, out_ref, next_ref, sem = refs
-    else:
-        w_ref, next_hbm, out_ref, next_ref, sem = refs
-    experts, _, sliver, half = w_ref.shape
-    group = 2 if experts % 2 == 0 else 1
+        sum_ref, refs = refs[0], refs[1:]
+    w_refs, (next_hbm, out_ref, next_ref, sem) = refs[:pieces], refs[pieces:]
+    held, _, sliver, half = w_refs[0].shape
+    experts = held * pieces
+    group = experts // 2 if experts % 2 == 0 else experts
     units = 2 * sliver
+    depth = half // 2
     copy = pltpu.make_async_copy(take(next_hbm), next_ref, sem)
     pl.when(pl.program_id(0) == 0)(copy.start)
     if last:
-        extra = rows_ref[:, half:].astype(jnp.float32)
+        extra = row_refs[1][:, depth:].astype(jnp.float32)
         lane = lax.broadcasted_iota(jnp.int32, extra.shape, 1)
     for first in range(0, experts, group):
         columns = slice(first * units, (first + group) * units)
-        pre = lax.dot_general(
-            rows_ref[:, :half],
-            w_ref[first : first + group].reshape(group * units, half),
-            (((1,), (1,)), ((), ())),
-            preferred_element_type=jnp.float32,
-        )
+        w_ref, at_slot = w_refs[first // held], first % held
+        pre = sum_ref[:, columns] if last else None
+        for number, row_ref in enumerate(row_refs):
+            product = lax.dot_general(
+                row_ref[:, :depth],
+                w_ref[
+                    at_slot : at_slot + group, :, :, number * depth : (number + 1) * depth
+                ].reshape(group * units, depth),
+                (((1,), (1,)), ((), ())),
+                preferred_element_type=jnp.float32,
+            )
+            pre = product if pre is None else pre + product
         if not last:
             out_ref[:, columns] = pre
             continue
-        pre += sum_ref[:, columns]
         for slot in range(first, first + group):
             at = (slot - first) * units
             gate, up = pre[:, at : at + sliver], pre[:, at + sliver : at + units]
             mine = (lane == slot) | (lane == slot + experts) | (lane == slot + 2 * experts)
             weigh = jnp.sum(jnp.where(mine, extra, 0.0), axis=1, keepdims=True)
-            hidden = gate / (1.0 + jnp.exp(-gate)) * up * weigh
+            hidden = (0.5 * gate) * (1.0 + jnp.tanh(0.5 * gate)) * up * weigh
             out_ref[slot] = hidden.astype(out_ref.dtype)
     pl.when(pl.program_id(0) == 0)(copy.wait)
 
 
-def gate_up_of(rows_of_part, sums, weights, next_weight, take, next_shape):
-    experts, _, sliver, half = weights.shape
-    rows, width = rows_of_part.shape
+def gate_up_of(row_parts, sums, weights, next_weight, take, next_shape):
+    held, _, sliver, half = weights[0].shape
+    pieces = len(weights)
+    experts = held * pieces
+    rows = row_parts[0].shape[0]
     row_block = min(ROW_BLOCK, rows)
     whole = rows == row_block
     last = sums is not None
     units = experts * 2 * sliver
-    operands = [rows_of_part, sums] if last else [rows_of_part]
+    operands = list(row_parts) + ([sums] if last else [])
     if whole:
+        specs = [pl.BlockSpec(memory_space=pltpu.VMEM)] * len(operands)
         operands = [resident(operand) for operand in operands]
-        specs = [pl.BlockSpec(memory_space=pltpu.VMEM)] * len(operands)
     else:
         specs = [
-            pl.BlockSpec((row_block, width), lambda r: (r, 0)),
-            pl.BlockSpec((row_block, units), lambda r: (r, 0)),
-        ][: len(operands)]
+            pl.BlockSpec((row_block, operand.shape[1]), lambda r: (r, 0)) for operand in operands
+        ]
     if last:
         out_spec = pl.BlockSpec((experts, row_block, sliver), lambda r: (0, r, 0))
         out_shape = jax.ShapeDtypeStruct((experts, rows, sliver), jnp.bfloat16)
@@ -158,13 +166,14 @@
         out_shape = pltpu.VMEM(out_shape.shape, out_shape.dtype)
 
     def kernel(*refs):
-        gate_up_kernel(last, take, *refs)
+        gate_up_kernel(last, take, pieces, *refs)
 
     return pl.pallas_call(
         kernel,
         grid=(rows // row_block,),
         in_specs=specs
-        + [pl.BlockSpec(memory_space=pltpu.VMEM), pl.BlockSpec(memory_space=pl.ANY)],
+        + [pl.BlockSpec(memory_space=pltpu.VMEM)] * pieces
+        + [pl.BlockSpec(memory_space=pl.ANY)],
         out_specs=[out_spec, pl.BlockSpec(memory_space=pltpu.VMEM)],
         out_shape=[out_shape, pltpu.VMEM(next_shape, next_weight.dtype)],
         scratch_shapes=[pltpu.SemaphoreType.DMA],
@@ -174,13 +183,13 @@
             bytes_accessed=2 * math.prod(next_shape) + 4 * rows * units,
             transcendentals=rows * experts * sliver,
         ),
-    )(*operands, resident(weights), in_hbm(next_weight))
+    )(*operands, *(resident(weight) for weight in weights), in_hbm(next_weight))
 
 
 def down_kernel(part, hidden_ref, w_ref, out_ref):
     experts, _, sliver = hidden_ref.shape
     columns = out_ref.shape[1]
-    block = next(size for size in (1024, 512, 384, 256, 128, columns) if columns % size == 0)
+    block = next(size for size in (1536, 1024, 512, 384, 256, 128, columns) if columns % size == 0)
 
     def one_block(step, carry):
         at = pl.multiple_of(step * block, block)
@@ -233,54 +242,97 @@
     y_digits = digits_of("shard", ways["shard"], cores)
     core_digits = [Digit("shard", ways["shard"], 1, cores)]
     dim_order = core_digits + x_digits[::-1] + y_digits[::-1] + z_digits[::-1]
-    routes = [z_digits + y_digits + x_digits, z_digits + x_digits + y_digits]
+    routes = [y_digits + x_digits, x_digits + y_digits]
+    quarter = half // 2
+
+    def gather(block, digit, held):
+        dim = sum(dim_order.index(other) < dim_order.index(digit) for other in held)
+        return digit.gather(block, dim)
+
+    def reduce(block, digit, held):
+        return digit.reduce(block, sum(other in held for other in dim_order[: dim_order.index(digit)]))
 
     coefficients = slot_coefficients(expert_ids, gate_values, old_place, new_place)
     extra = jnp.concatenate(split_exact(coefficients), axis=1)
     extra = jnp.pad(extra, ((0, 0), (0, -extra.shape[1] % LANES)))
-    parts = [
-        jnp.concatenate([tokens[:, :half], extra], axis=1),
-        tokens[:, half:],
-    ]
+
+    experts = gate_up_weight.shape[0]
+    pieces = 2 if experts % 2 == 0 else 1
     half_shape = gate_up_weight.shape[:3] + (half,)
+    piece_shape = (experts // pieces,) + half_shape[1:]
+
+    def take_piece(number):
+        slots = pl.ds(number * (experts // pieces), experts // pieces)
+        return lambda ref: ref.at[slots, :, :, pl.ds(half, half)]
 
     def take_first(ref):
         return ref.at[:, :, :, pl.ds(0, half)]
 
-    def take_second(ref):
-        return ref.at[:, :, :, pl.ds(half, half)]
-
-    blocks, held = list(parts), [[], []]
-    last = len(routes[0]) - 1
-    for step in range(last + 2):
-        if step == last:
-            before_last = blocks[0]
-        if step == last + 1:
-            first_weights = fetched(gate_up_weight, take_second, half_shape, before_last)
-            blocks[1], first_weights = lax.optimization_barrier((blocks[1], first_weights))
+    halves = [jnp.concatenate([tokens[:, :half], extra], axis=1), tokens[:, half:]]
+    first_weights, held = [], []
+    for step, digit in enumerate(z_digits):
+        halves = [gather(block, digit, held) for block in halves]
+        held.append(digit)
+        if step == 0:
+            fresh = fetched(gate_up_weight, take_piece(0), piece_shape, halves[1])
+            halves[0], fresh = lax.optimization_barrier((halves[0], fresh))
+            first_weights.append(fresh)
+    quarters = [[block[..., :quarter], block[..., quarter:]] for block in halves]
+    for step in range(len(routes[0])):
         for number in (1, 0):
-            digit = (routes[number] + core_digits)[step]
-            dim = sum(dim_order.index(other) < dim_order.index(digit) for other in held[number])
-            blocks[number] = digit.gather(blocks[number], dim)
-            held[number].append(digit)
-    gathered = [block.reshape(-1, part.shape[1]) for block, part in zip(blocks, parts)]
+            for side in (0, 1):
+                done = held + routes[side][:step]
+                quarters[number][side] = gather(quarters[number][side], routes[side][step], done)
+    for piece in range(len(first_weights), pieces):
+        fresh = fetched(gate_up_weight, take_piece(piece), piece_shape, quarters[1][0])
+        quarters[0][0], fresh = lax.optimization_barrier((quarters[0][0], fresh))
+        first_weights.append(fresh)
+    for digit in core_digits:
+        quarters = [
+            [gather(block, digit, dim_order[len(core_digits) :]) for block in pair]
+            for pair in quarters
+        ]
+    gathered = [[block.reshape(-1, block.shape[-1]) for block in pair] for pair in quarters]
     sums, weights = gate_up_of(
         gathered[1], None, first_weights, gate_up_weight, take_first, half_shape
     )
     hidden, down_weight = gate_up_of(
-        gathered[0], sums, weights, down_weight, lambda ref: ref, down_weight.shape
+        gathered[0], sums, [weights], down_weight, lambda ref: ref, down_weight.shape
     )
     down_weight = resident(down_weight)
-    results = []
-    for number, route in enumerate(routes):
-        block = down_of(hidden, down_weight, number, half)
-        block = block.reshape([digit.size for digit in dim_order] + [rows, half])
-        held = list(dim_order)
-        for digit in core_digits + route[::-1]:
-            block = digit.reduce(block, held.index(digit))
-            held.remove(digit)
-        results.append(block)
-    return jnp.concatenate(results, axis=1)
+    order = [(1, 0), (1, 1), (0, 0), (0, 1)]
+    blocks, left = {}, list(dim_order)
+    for digit in core_digits:
+        left.remove(digit)
+    for place, (number, side) in enumerate(order):
+        if place >= 2:
+            before = order[place - 2]
+            hidden, blocks[before] = lax.optimization_barrier((hidden, blocks[before]))
+        block = down_of(hidden, down_weight, 2 * number + side, quarter)
+        block = block.reshape([digit.size for digit in dim_order] + [rows, quarter])
+        for digit in core_digits:
+            block = reduce(block, digit, dim_order)
+        blocks[number, side] = block
+    blocks = lax.optimization_barrier(blocks)
+    pairs = {number: [blocks[number, side] for side in (0, 1)] for number in (0, 1)}
+    helds = [list(left), list(left)]
+
+    def after(first, second):
+        return lax.optimization_barrier((first, second))[0]
+
+    for step in range(len(left)):
+        waiting = pairs[0]
+        for number in (1, 0):
+            if step == len(routes[0]):
+                pairs[number] = [jnp.concatenate(pairs[number], axis=-1)]
+            moved = []
+            for side, block in enumerate(pairs[number]):
+                digit = (routes[side][::-1] + z_digits[::-1])[step]
+                moved.append(reduce(block, digit, helds[side]))
+            pairs[number] = after(moved, waiting) if number else moved
+        for side in (0, 1):
+            helds[side].remove((routes[side][::-1] + z_digits[::-1])[step])
+    return jnp.concatenate([pairs[number][0] for number in (0, 1)], axis=1)
 
 
 def solution(mesh):

time: 83.4 us -> 86.7 us (1.040)
  starting transfers between devices: 26.7 us -> 36.3 us
  waiting for transfers between devices: 29.3 us -> 23.3 us
    ppermute x20 -> x32, starting transfers between devices: 26.7 us -> 36.3 us  [shift(): return lax.ppermute(value, self.name, pairs)]
    ppermute x20 -> x32, waiting for transfers between devices: 29.3 us -> 23.3 us  [shift(): return lax.ppermute(value, self.name, pairs)]
    pallas_call x1 -> x2, Pallas kernels: 4.58 us -> 5.59 us  [fetched(): pl.pallas_call(kernel, in_specs=[pl.BlockSpec(memory_space=pl.ANY)] * 2,...]
    pallas_call x2, Pallas kernels: 12.7 us -> 11.7 us  [gate_up_of(): pl.pallas_call(kernel, grid=(rows // row_block,), in_specs=specs + [pl.Bl...]
    pallas_call x2 -> x4, Pallas kernels: 4.36 us -> 3.9 us  [down_of(): pl.pallas_call(kernel, grid=(rows // row_block,), in_specs=[pl.BlockSpec(...]
  transfers between devices with their start and end apart: 20 -> 32, of which waited for: 16 -> 18; matrix products, arithmetic and copies ran while one was open for 4% -> 4% of each run, Pallas kernels for 14% -> 16%
where the time goes in v8:
time: 86.7 us; the launch traced here: 86.4 us
  starting transfers between devices  36.3 us (42%)
  waiting for transfers between devices  23.3 us (27%)
  Pallas kernels  21.2 us (24%)
  other arithmetic  3.7 us (4%)
  local copies, waits for them, and re-layouts  1.43 us (2%)
    ppermute x32, starting transfers between devices, shift(): return lax.ppermute(value, self.name, pairs)  36.3 us
    ppermute x32, waiting for transfers between devices, shift(): return lax.ppermute(value, self.name, pairs)  23.3 us
    pallas_call x2, Pallas kernels, gate_up_of(): pl.pallas_call(kernel, grid=(rows // row_block,), in_specs=specs + [pl.Bl...  11.7 us
    pallas_call x2, Pallas kernels, fetched(): pl.pallas_call(kernel, in_specs=[pl.BlockSpec(memory_space=pl.ANY)] * 2,...  5.59 us
    pallas_call x4, Pallas kernels, down_of(): pl.pallas_call(kernel, grid=(rows // row_block,), in_specs=[pl.BlockSpec(...  3.9 us
  transfers between devices with their start and end apart: 32, of which 18 were waited for; matrix products, arithmetic and copies ran while one was open for 4% of the time, Pallas kernels for 16%

profile of v8, /device:TPU:0, one launch (start us, length us, event | category | flops | bytes accessed | tf_op | source)
XLA Modules:
  0.0 86.4 jit_solution(14129449684108250684)
XLA Ops:
  0.0 0.8 slice_bitcast_fusion.15
  0.8 4.1 %collective-permute-start.1 = (bf16[8,3072]{1,0:T(8,128)(2,1)S(1)}, bf16[8,3072]{1,0:T(8,128)(2,1)S(1)}, u32[]{:S(2)}, u32[]{:S(2)}) collective-permute-start(bf16[8,3072]{1,0:T(8,128)(2,1)S(1)} %get-tuple-element.76), channel_id=1, source_target_pairs={{0,8},{4,12},{8,0},{12,4},{1,9},{5,13},{9,1},{13,5},{2,10},{6,14},... | collective-permute-start | bytes 147464 | tf_op jit(solution)/shard_map/ppermute | solution.py:44
  4.9 0.7 compare_convert_fusion
  5.7 0.7 select_reduce_fusion
  6.7 0.8 collective-permute-done.1
  7.6 2.0 %collective-permute-start.5 = (bf16[2,8,3072]{2,1,0:T(8,128)(2,1)S(1)}, bf16[2,8,3072]{2,1,0:T(8,128)(2,1)S(1)}, u32[]{:S(2)}, u32[]{:S(2)}) collective-permute-start(bf16[2,8,3072]{2,1,0:T(8,128)(2,1)S(1)} %get-tuple-element.74.refs_1_), channel_id=1, source_target_pairs={{0,4},{4,0},{8,12},{12,8},{1,5},{5,1},{9,13},{13,9},{2,6},{6,2},{1... | collective-permute-start | bytes 294920 | tf_op jit(solution)/shard_map/ppermute | solution.py:44
  9.5 2.8 %shard_map.73.refs_2_ = bf16[2,2,256,3072]{3,2,1,0:T(8,128)(2,1)S(1)} custom-call(bf16[4,2,256,6144]{3,2,1,0:T(8,128)(2,1)} %refs_4_.2, bf16[2,8,3072]{2,1,0:T(8,128)(2,1)S(1)} %get-tuple-element.74.refs_1_), custom_call_target="tpu_custom_call" | custom-call | bytes 12582912 | tf_op jit(solution)/shard_map/pallas_call | solution.py:86
  12.4 1.2 %collective-permute-start.2 = (bf16[2,8,3200]{2,1,0:T(8,128)(2,1)S(1)}, bf16[2,8,3200]{2,1,0:T(8,128)(2,1)S(1)}, u32[]{:S(2)}, u32[]{:S(2)}) collective-permute-start(bf16[2,8,3200]{2,1,0:T(8,128)(2,1)S(1)} %pad_maximum_fusion.13), channel_id=1, source_target_pairs={{0,4},{4,0},{8,12},{12,8},{1,5},{5,1},{9,13},{13,9},{2,6},{6,2},{1... | collective-permute-start | bytes 307208 | tf_op jit(solution)/shard_map/ppermute | solution.py:44
  13.6 1.6 %collective-permute-start.6 = (bf16[2,2,8,1536]{3,2,1,0:T(8,128)(2,1)S(1)}, bf16[2,2,8,1536]{3,2,1,0:T(8,128)(2,1)S(1)}, u32[]{:S(2)}, u32[]{:S(2)}) collective-permute-start(bf16[2,2,8,1536]{3,2,1,0:T(8,128)(2,1)S(1)} %get-tuple-element.68), channel_id=1, source_target_pairs={{0,2},{1,3},{2,0},{3,1},{4,6},{5,7},{6,4},{7,5},{8,10},{9,11},{10,... | collective-permute-start | bytes 294920 | tf_op jit(solution)/shard_map/ppermute | solution.py:44
  15.1 1.5 %collective-permute-start.13 = (bf16[2,2,8,1536]{3,2,1,0:T(8,128)(2,1)S(1)}, bf16[2,2,8,1536]{3,2,1,0:T(8,128)(2,1)S(1)}, u32[]{:S(2)}, u32[]{:S(2)}) collective-permute-start(bf16[2,2,8,1536]{3,2,1,0:T(8,128)(2,1)S(1)} %get-tuple-element.67), channel_id=1, source_target_pairs={{0,16},{16,0},{1,17},{17,1},{2,18},{18,2},{3,19},{19,3},{4,20},{20... | collective-permute-start | bytes 294920 | tf_op jit(solution)/shard_map/ppermute | solution.py:44
  17.1 1.5 %collective-permute-start.3 = (bf16[2,2,8,1536]{3,2,1,0:T(8,128)(2,1)S(1)}, bf16[2,2,8,1536]{3,2,1,0:T(8,128)(2,1)S(1)}, u32[]{:S(2)}, u32[]{:S(2)}) collective-permute-start(bf16[2,2,8,1536]{3,2,1,0:T(8,128)(2,1)S(1)} %pad_maximum_fusion.16), channel_id=1, source_target_pairs={{0,2},{1,3},{2,0},{3,1},{4,6},{5,7},{6,4},{7,5},{8,10},{9,11},{10,... | collective-permute-start | bytes 294920 | tf_op jit(solution)/shard_map/ppermute | solution.py:44
  18.6 1.5 %collective-permute-start.9 = (bf16[2,2,8,1664]{3,2,1,0:T(8,128)(2,1)S(1)}, bf16[2,2,8,1664]{3,2,1,0:T(8,128)(2,1)S(1)}, u32[]{:S(2)}, u32[]{:S(2)}) collective-permute-start(bf16[2,2,8,1664]{3,2,1,0:T(8,128)(2,1)S(1)} %pad_maximum_fusion.12), channel_id=1, source_target_pairs={{0,16},{16,0},{1,17},{17,1},{2,18},{18,2},{3,19},{19,3},{4,20},{20... | collective-permute-start | bytes 319496 | tf_op jit(solution)/shard_map/ppermute | solution.py:44
  20.2 0.6 collective-permute-start.7
  20.8 1.5 %collective-permute-start.14 = (bf16[2,2,2,8,1536]{4,3,2,1,0:T(8,128)(2,1)S(1)}, bf16[2,2,2,8,1536]{4,3,2,1,0:T(8,128)(2,1)S(1)}, u32[]{:S(2)}, u32[]{:S(2)}) collective-permute-start(bf16[2,2,2,8,1536]{4,3,2,1,0:T(8,128)(2,1)S(1)} %get-tuple-element.66), channel_id=1, source_target_pairs={{0,2},{1,3},{2,0},{3,1},{4,6},{5,7},{6,4},{7,5},{8,10},{9,11},{10,... | collective-permute-start | bytes 589832 | tf_op jit(solution)/shard_map/ppermute | solution.py:44
  22.3 0.6 collective-permute-done.3
  22.9 1.4 %collective-permute-start.4 = (bf16[2,2,2,8,1536]{4,3,2,1,0:T(8,128)(2,1)S(1)}, bf16[2,2,2,8,1536]{4,3,2,1,0:T(8,128)(2,1)S(1)}, u32[]{:S(2)}, u32[]{:S(2)}) collective-permute-start(bf16[2,2,2,8,1536]{4,3,2,1,0:T(8,128)(2,1)S(1)} %get-tuple-element.72), channel_id=1, source_target_pairs={{0,16},{16,0},{1,17},{17,1},{2,18},{18,2},{3,19},{19,3},{4,20},{20... | collective-permute-start | bytes 589832 | tf_op jit(solution)/shard_map/ppermute | solution.py:44
  24.6 1.0 %collective-permute-start.10 = (bf16[2,2,2,8,1664]{4,3,2,1,0:T(8,128)(2,1)S(1)}, bf16[2,2,2,8,1664]{4,3,2,1,0:T(8,128)(2,1)S(1)}, u32[]{:S(2)}, u32[]{:S(2)}) collective-permute-start(bf16[2,2,2,8,1664]{4,3,2,1,0:T(8,128)(2,1)S(1)} %get-tuple-element.64), channel_id=1, source_target_pairs={{0,2},{1,3},{2,0},{3,1},{4,6},{5,7},{6,4},{7,5},{8,10},{9,11},{10,... | collective-permute-start | bytes 638984 | tf_op jit(solution)/shard_map/ppermute | solution.py:44
  25.6 2.1 %collective-permute-done.7 = bf16[2,2,2,8,1536]{4,3,2,1,0:T(8,128)(2,1)S(1)} collective-permute-done((bf16[2,2,2,8,1536]{4,3,2,1,0:T(8,128)(2,1)S(1)}, bf16[2,2,2,8,1536]{4,3,2,1,0:T(8,128)(2,1)S(1)}, u32[]{:S(2)}, u32[]{:S(2)}) %collective-permute-start.7) | collective-permute-done | bytes 196640 | tf_op jit(solution)/shard_map/ppermute | solution.py:44
  27.8 2.8 %shard_map.74.refs_3_ = bf16[2,2,256,3072]{3,2,1,0:T(8,128)(2,1)S(1)} custom-call(bf16[4,2,256,6144]{3,2,1,0:T(8,128)(2,1)} %refs_4_.2, bf16[2,2,2,2,8,1536]{5,4,3,2,1,0:T(8,128)(2,1)S(1)} %get-tuple-element.62.refs_1_), custom_call_target="tpu_custom_call" | custom-call | bytes 12582912 | tf_op jit(solution)/shard_map/pallas_call | solution.py:86
  31.5 0.5 collective-permute-start.11
  33.0 7.1 %shard_map.75 = (f32[256,2048]{1,0:T(8,128)S(1)}, bf16[4,2,256,3072]{3,2,1,0:T(8,128)(2,1)S(1)}) custom-call(bf16[256,1536]{1,0:T(8,128)(2,1)S(1)} %bitcast.132, bf16[256,1536]{1,0:T(8,128)(2,1)S(1)} %bitcast.133, bf16[2,2,256,3072]{3,2,1,0:T(8,128)(2,1)S(1)} %shard_map.73.refs_2_, bf16[2,2,256,3072]{3,2,1,0:T(8,128)(2,1)S(1)} %shard_map.74.refs_3_, ...), custom_call_target="tpu_custom_call" | custom-call | flops 3221225472 | bytes 14680064 | tf_op jit(solution)/shard_map/pallas_call | solution.py:171
  40.5 4.6 %shard_map.76 = (bf16[4,256,256]{2,1,0:T(8,128)(2,1)S(1)}, bf16[4,256,6144]{2,1,0:T(8,128)(2,1)S(1)}) custom-call(bf16[256,1536]{1,0:T(8,128)(2,1)S(1)} %bitcast.131, bf16[256,1664]{1,0:T(8,128)(2,1)S(1)} %bitcast.130, f32[256,2048]{1,0:T(8,128)S(1)} %get-tuple-element.31.refs_2_, bf16[4,2,256,3072]{3,2,1,0:T(8,128)(2,1)S(1)} %get-tuple-element.32.refs_3_, ...), custom_call_target="tpu_custom_call" | custom-call | flops 3221225472 | bytes 14680064 | tf_op jit(solution)/shard_map/pallas_call | solution.py:171
  45.1 1.0 %shard_map.79 = bf16[256,1536]{1,0:T(8,128)(2,1)S(1)} custom-call(bf16[4,256,256]{2,1,0:T(8,128)(2,1)S(1)} %get-tuple-element.36.refs_0_, bf16[4,256,6144]{2,1,0:T(8,128)(2,1)S(1)} %get-tuple-element.34.refs_1_), custom_call_target="tpu_custom_call" | custom-call | flops 805306368 | bytes 4456448 | tf_op jit(solution)/shard_map/pallas_call | solution.py:214
  46.0 1.0 %shard_map.77 = bf16[256,1536]{1,0:T(8,128)(2,1)S(1)} custom-call(bf16[4,256,256]{2,1,0:T(8,128)(2,1)S(1)} %get-tuple-element.36.refs_0_, bf16[4,256,6144]{2,1,0:T(8,128)(2,1)S(1)} %get-tuple-element.34.refs_1_), custom_call_target="tpu_custom_call" | custom-call | flops 805306368 | bytes 4456448 | tf_op jit(solution)/shard_map/pallas_call | solution.py:214
  47.8 1.1 %collective-permute-done.16 = bf16[2,2,2,2,8,1536]{5,4,3,2,1,0:T(8,128)(2,1)S(1)} collective-permute-done((bf16[2,2,2,2,8,1536]{5,4,3,2,1,0:T(8,128)(2,1)S(1)}, bf16[2,2,2,2,8,1536]{5,4,3,2,1,0:T(8,128)(2,1)S(1)}, u32[]{:S(2)}, u32[]{:S(2)}) %collective-permute-start.16) | collective-permute-done | bytes 393248 | tf_op jit(solution)/shard_map/ppermute | solution.py:44
  49.0 1.0 %shard_map.78 = bf16[256,1536]{1,0:T(8,128)(2,1)S(1)} custom-call(bf16[4,256,256]{2,1,0:T(8,128)(2,1)S(1)} %get-tuple-element.36.refs_0_, bf16[4,256,6144]{2,1,0:T(8,128)(2,1)S(1)} %get-tuple-element.34.refs_1_), custom_call_target="tpu_custom_call" | custom-call | flops 805306368 | bytes 4456448 | tf_op jit(solution)/shard_map/pallas_call | solution.py:214
  50.1 1.0 %shard_map.80 = bf16[256,1536]{1,0:T(8,128)(2,1)S(1)} custom-call(bf16[4,256,256]{2,1,0:T(8,128)(2,1)S(1)} %get-tuple-element.36.refs_0_, bf16[4,256,6144]{2,1,0:T(8,128)(2,1)S(1)} %get-tuple-element.34.refs_1_), custom_call_target="tpu_custom_call" | custom-call | flops 805306368 | bytes 4456448 | tf_op jit(solution)/shard_map/pallas_call | solution.py:214
  51.8 1.1 %collective-permute-done.19 = bf16[2,2,2,2,8,1536]{5,4,3,2,0,1:T(8,128)(2,1)S(1)} collective-permute-done((bf16[2,2,2,2,8,1536]{5,4,3,2,0,1:T(8,128)(2,1)S(1)}, bf16[2,2,2,2,8,1536]{5,4,3,2,0,1:T(8,128)(2,1)S(1)}, u32[]{:S(2)}, u32[]{:S(2)}) %collective-permute-start.19) | collective-permute-done | bytes 393248 | tf_op jit(solution)/shard_map/ppermute | solution.py:44
  53.6 0.6 collective-permute-start.22
  54.2 1.6 %collective-permute-start.20 = (bf16[2,2,2,8,1536]{4,3,2,1,0:T(8,128)(2,1)S(1)}, bf16[2,2,2,8,1536]{4,3,2,1,0:T(8,128)(2,1)S(1)}, u32[]{:S(2)}, u32[]{:S(2)}) collective-permute-start(bf16[2,2,2,8,1536]{4,3,2,1,0:T(8,128)(2,1)S(1)} %slice_bitcast_fusion.3), channel_id=1, source_target_pairs={{0,16},{16,0},{1,17},{17,1},{2,18},{18,2},{3,19},{19,3},{4,20},{20... | collective-permute-start | bytes 589832 | tf_op jit(solution)/shard_map/ppermute | solution.py:44
  55.8 1.6 %collective-permute-start.27 = (bf16[2,2,2,8,1536]{4,3,2,1,0:T(8,128)(2,1)S(1)}, bf16[2,2,2,8,1536]{4,3,2,1,0:T(8,128)(2,1)S(1)}, u32[]{:S(2)}, u32[]{:S(2)}) collective-permute-start(bf16[2,2,2,8,1536]{4,3,2,1,0:T(8,128)(2,1)S(1)} %slice_bitcast_fusion), channel_id=1, source_target_pairs={{0,2},{1,3},{2,0},{3,1},{4,6},{5,7},{6,4},{7,5},{8,10},{9,11},{10,... | collective-permute-start | bytes 589832 | tf_op jit(solution)/shard_map/ppermute | solution.py:44
  57.4 0.6 collective-permute-start.26
  58.0 3.4 %collective-permute-done.22 = bf16[2,2,2,8,1536]{4,3,2,1,0:T(8,128)(2,1)S(1)} collective-permute-done((bf16[2,2,2,8,1536]{4,3,2,1,0:T(8,128)(2,1)S(1)}, bf16[2,2,2,8,1536]{4,3,2,1,0:T(8,128)(2,1)S(1)}, u32[]{:S(2)}, u32[]{:S(2)}) %collective-permute-start.22) | collective-permute-done | bytes 196640 | tf_op jit(solution)/shard_map/ppermute | solution.py:44
  61.5 1.6 %collective-permute-start.23 = (bf16[2,2,8,1536]{3,2,1,0:T(8,128)(2,1)S(1)}, bf16[2,2,8,1536]{3,2,1,0:T(8,128)(2,1)S(1)}, u32[]{:S(2)}, u32[]{:S(2)}) collective-permute-start(bf16[2,2,8,1536]{3,2,1,0:T(8,128)(2,1)S(1)} %slice_bitcast_fusion.6), channel_id=1, source_target_pairs={{0,16},{16,0},{1,17},{17,1},{2,18},{18,2},{3,19},{19,3},{4,20},{20... | collective-permute-start | bytes 294920 | tf_op jit(solution)/shard_map/ppermute | solution.py:44
  63.1 0.6 collective-permute-start.21
  63.7 1.9 %collective-permute-done.27 = bf16[2,2,2,8,1536]{4,3,2,1,0:T(8,128)(2,1)S(1)} collective-permute-done((bf16[2,2,2,8,1536]{4,3,2,1,0:T(8,128)(2,1)S(1)}, bf16[2,2,2,8,1536]{4,3,2,1,0:T(8,128)(2,1)S(1)}, u32[]{:S(2)}, u32[]{:S(2)}) %collective-permute-start.27) | collective-permute-done | bytes 196640 | tf_op jit(solution)/shard_map/ppermute | solution.py:44
  66.3 1.6 %collective-permute-start.29 = (bf16[2,2,8,1536]{3,2,1,0:T(8,128)(2,1)S(1)}, bf16[2,2,8,1536]{3,2,1,0:T(8,128)(2,1)S(1)}, u32[]{:S(2)}, u32[]{:S(2)}) collective-permute-start(bf16[2,2,8,1536]{3,2,1,0:T(8,128)(2,1)S(1)} %slice_bitcast_fusion.10), channel_id=1, source_target_pairs={{0,16},{16,0},{1,17},{17,1},{2,18},{18,2},{3,19},{19,3},{4,20},{20... | collective-permute-start | bytes 294920 | tf_op jit(solution)/shard_map/ppermute | solution.py:44
  67.8 1.6 %collective-permute-start.28 = (bf16[2,2,8,1536]{3,2,1,0:T(8,128)(2,1)S(1)}, bf16[2,2,8,1536]{3,2,1,0:T(8,128)(2,1)S(1)}, u32[]{:S(2)}, u32[]{:S(2)}) collective-permute-start(bf16[2,2,8,1536]{3,2,1,0:T(8,128)(2,1)S(1)} %slice_bitcast_fusion.11), channel_id=1, source_target_pairs={{0,2},{1,3},{2,0},{3,1},{4,6},{5,7},{6,4},{7,5},{8,10},{9,11},{10,... | collective-permute-start | bytes 294920 | tf_op jit(solution)/shard_map/ppermute | solution.py:44
  69.4 1.5 %collective-permute-done.29 = bf16[2,2,8,1536]{3,2,1,0:T(8,128)(2,1)S(1)} collective-permute-done((bf16[2,2,8,1536]{3,2,1,0:T(8,128)(2,1)S(1)}, bf16[2,2,8,1536]{3,2,1,0:T(8,128)(2,1)S(1)}, u32[]{:S(2)}, u32[]{:S(2)}) %collective-permute-start.29) | collective-permute-done | bytes 98336 | tf_op jit(solution)/shard_map/ppermute | solution.py:44
  71.0 1.5 %collective-permute-done.28 = bf16[2,2,8,1536]{3,2,1,0:T(8,128)(2,1)S(1)} collective-permute-done((bf16[2,2,8,1536]{3,2,1,0:T(8,128)(2,1)S(1)}, bf16[2,2,8,1536]{3,2,1,0:T(8,128)(2,1)S(1)}, u32[]{:S(2)}, u32[]{:S(2)}) %collective-permute-start.28) | collective-permute-done | bytes 98336 | tf_op jit(solution)/shard_map/ppermute | solution.py:44
  72.6 1.3 %collective-permute-start.30 = (bf16[2,8,3072]{2,1,0:T(8,128)(2,1)S(1)}, bf16[2,8,3072]{2,1,0:T(8,128)(2,1)S(1)}, u32[]{:S(2)}, u32[]{:S(2)}) collective-permute-start(bf16[2,8,3072]{2,1,0:T(8,128)(2,1)S(1)} %slice_bitcast_fusion.4), channel_id=1, source_target_pairs={{0,4},{4,0},{8,12},{12,8},{1,5},{5,1},{9,13},{13,9},{2,6},{6,2},{1... | collective-permute-start | bytes 294920 | tf_op jit(solution)/shard_map/ppermute | solution.py:44
  74.0 0.9 %collective-permute-start.24 = (bf16[2,8,3072]{2,1,0:T(8,128)(2,1)S(1)}, bf16[2,8,3072]{2,1,0:T(8,128)(2,1)S(1)}, u32[]{:S(2)}, u32[]{:S(2)}) collective-permute-start(bf16[2,8,3072]{2,1,0:T(8,128)(2,1)S(1)} %fusion.18), channel_id=1, source_target_pairs={{0,4},{4,0},{8,12},{12,8},{1,5},{5,1},{9,13},{13,9},{2,6},{6,2},{1... | collective-permute-start | bytes 294920 | tf_op jit(solution)/shard_map/ppermute | solution.py:44
  74.9 3.0 %collective-permute-done.30 = bf16[2,8,3072]{2,1,0:T(8,128)(2,1)S(1)} collective-permute-done((bf16[2,8,3072]{2,1,0:T(8,128)(2,1)S(1)}, bf16[2,8,3072]{2,1,0:T(8,128)(2,1)S(1)}, u32[]{:S(2)}, u32[]{:S(2)}) %collective-permute-start.30) | collective-permute-done | bytes 98336 | tf_op jit(solution)/shard_map/ppermute | solution.py:44
  77.8 2.8 %collective-permute-start.31 = (bf16[8,3072]{1,0:T(8,128)(2,1)S(1)}, bf16[8,3072]{1,0:T(8,128)(2,1)S(1)}, u32[]{:S(2)}, u32[]{:S(2)}) collective-permute-start(bf16[8,3072]{1,0:T(8,128)(2,1)S(1)} %slice_bitcast_fusion.14), channel_id=1, source_target_pairs={{0,8},{4,12},{8,0},{12,4},{1,9},{5,13},{9,1},{13,5},{2,10},{6,14},... | collective-permute-start | bytes 147464 | tf_op jit(solution)/shard_map/ppermute | solution.py:44
  80.7 1.4 %collective-permute-start.25 = (bf16[8,3072]{1,0:T(8,128)(2,1)S(1)}, bf16[8,3072]{1,0:T(8,128)(2,1)S(1)}, u32[]{:S(2)}, u32[]{:S(2)}) collective-permute-start(bf16[8,3072]{1,0:T(8,128)(2,1)S(1)} %slice_bitcast_fusion.12), channel_id=1, source_target_pairs={{0,8},{4,12},{8,0},{12,4},{1,9},{5,13},{9,1},{13,5},{2,10},{6,14},... | collective-permute-start | bytes 147464 | tf_op jit(solution)/shard_map/ppermute | solution.py:44
  82.1 0.8 collective-permute-done.31
  82.9 2.8 %collective-permute-done.25 = bf16[8,3072]{1,0:T(8,128)(2,1)S(1)} collective-permute-done((bf16[8,3072]{1,0:T(8,128)(2,1)S(1)}, bf16[8,3072]{1,0:T(8,128)(2,1)S(1)}, u32[]{:S(2)}, u32[]{:S(2)}) %collective-permute-start.25) | collective-permute-done | bytes 49184 | tf_op jit(solution)/shard_map/ppermute | solution.py:44
  85.7 0.6 pad_maximum_fusion.18
  (90 shorter events, 6.7 us)
Async XLA Ops:
  0.8 6.7 %collective-permute-start.1 = (bf16[8,3072]{1,0:T(8,128)(2,1)S(1)}, bf16[8,3072]{1,0:T(8,128)(2,1)S(1)}, u32[]{:S(2)}, u32[]{:S(2)}) collective-permute-start(bf16[8,3072]{1,0:T(8,128)(2,1)S(1)} %get-tuple-element.76), channel_id=1, source_target_pairs={{0,8},{4,12},{8,0},{12,4},{1,9},{5,13},{9,1},{13,5},{2,10},{6,14},... | collective-permute-start | bytes 147464 | tf_op jit(solution)/shard_map/ppermute | solution.py:44
  6.6 5.7 %collective-permute-start = (bf16[8,3200]{1,0:T(8,128)(2,1)S(1)}, bf16[8,3200]{1,0:T(8,128)(2,1)S(1)}, u32[]{:S(2)}, u32[]{:S(2)}) collective-permute-start(bf16[8,3200]{1,0:T(8,128)(2,1)S(1)} %get-tuple-element.79), channel_id=1, source_target_pairs={{0,8},{4,12},{8,0},{12,4},{1,9},{5,13},{9,1},{13,5},{2,10},{6,14},... | collective-permute-start | bytes 153608 | tf_op jit(solution)/shard_map/ppermute | solution.py:44
  7.6 6.0 %collective-permute-start.5 = (bf16[2,8,3072]{2,1,0:T(8,128)(2,1)S(1)}, bf16[2,8,3072]{2,1,0:T(8,128)(2,1)S(1)}, u32[]{:S(2)}, u32[]{:S(2)}) collective-permute-start(bf16[2,8,3072]{2,1,0:T(8,128)(2,1)S(1)} %get-tuple-element.74.refs_1_), channel_id=1, source_target_pairs={{0,4},{4,0},{8,12},{12,8},{1,5},{5,1},{9,13},{13,9},{2,6},{6,2},{1... | collective-permute-start | bytes 294920 | tf_op jit(solution)/shard_map/ppermute | solution.py:44
  12.4 4.7 %collective-permute-start.2 = (bf16[2,8,3200]{2,1,0:T(8,128)(2,1)S(1)}, bf16[2,8,3200]{2,1,0:T(8,128)(2,1)S(1)}, u32[]{:S(2)}, u32[]{:S(2)}) collective-permute-start(bf16[2,8,3200]{2,1,0:T(8,128)(2,1)S(1)} %pad_maximum_fusion.13), channel_id=1, source_target_pairs={{0,4},{4,0},{8,12},{12,8},{1,5},{5,1},{9,13},{13,9},{2,6},{6,2},{1... | collective-permute-start | bytes 307208 | tf_op jit(solution)/shard_map/ppermute | solution.py:44
  13.6 6.6 %collective-permute-start.6 = (bf16[2,2,8,1536]{3,2,1,0:T(8,128)(2,1)S(1)}, bf16[2,2,8,1536]{3,2,1,0:T(8,128)(2,1)S(1)}, u32[]{:S(2)}, u32[]{:S(2)}) collective-permute-start(bf16[2,2,8,1536]{3,2,1,0:T(8,128)(2,1)S(1)} %get-tuple-element.68), channel_id=1, source_target_pairs={{0,2},{1,3},{2,0},{3,1},{4,6},{5,7},{6,4},{7,5},{8,10},{9,11},{10,... | collective-permute-start | bytes 294920 | tf_op jit(solution)/shard_map/ppermute | solution.py:44
  15.1 5.6 %collective-permute-start.13 = (bf16[2,2,8,1536]{3,2,1,0:T(8,128)(2,1)S(1)}, bf16[2,2,8,1536]{3,2,1,0:T(8,128)(2,1)S(1)}, u32[]{:S(2)}, u32[]{:S(2)}) collective-permute-start(bf16[2,2,8,1536]{3,2,1,0:T(8,128)(2,1)S(1)} %get-tuple-element.67), channel_id=1, source_target_pairs={{0,16},{16,0},{1,17},{17,1},{2,18},{18,2},{3,19},{19,3},{4,20},{20... | collective-permute-start | bytes 294920 | tf_op jit(solution)/shard_map/ppermute | solution.py:44
  17.1 5.7 %collective-permute-start.3 = (bf16[2,2,8,1536]{3,2,1,0:T(8,128)(2,1)S(1)}, bf16[2,2,8,1536]{3,2,1,0:T(8,128)(2,1)S(1)}, u32[]{:S(2)}, u32[]{:S(2)}) collective-permute-start(bf16[2,2,8,1536]{3,2,1,0:T(8,128)(2,1)S(1)} %pad_maximum_fusion.16), channel_id=1, source_target_pairs={{0,2},{1,3},{2,0},{3,1},{4,6},{5,7},{6,4},{7,5},{8,10},{9,11},{10,... | collective-permute-start | bytes 294920 | tf_op jit(solution)/shard_map/ppermute | solution.py:44
  18.6 5.9 %collective-permute-start.9 = (bf16[2,2,8,1664]{3,2,1,0:T(8,128)(2,1)S(1)}, bf16[2,2,8,1664]{3,2,1,0:T(8,128)(2,1)S(1)}, u32[]{:S(2)}, u32[]{:S(2)}) collective-permute-start(bf16[2,2,8,1664]{3,2,1,0:T(8,128)(2,1)S(1)} %pad_maximum_fusion.12), channel_id=1, source_target_pairs={{0,16},{16,0},{1,17},{17,1},{2,18},{18,2},{3,19},{19,3},{4,20},{20... | collective-permute-start | bytes 319496 | tf_op jit(solution)/shard_map/ppermute | solution.py:44
  20.2 7.5 %collective-permute-start.7 = (bf16[2,2,2,8,1536]{4,3,2,1,0:T(8,128)(2,1)S(1)}, bf16[2,2,2,8,1536]{4,3,2,1,0:T(8,128)(2,1)S(1)}, u32[]{:S(2)}, u32[]{:S(2)}) collective-permute-start(bf16[2,2,2,8,1536]{4,3,2,1,0:T(8,128)(2,1)S(1)} %get-tuple-element.70), channel_id=1, source_target_pairs={{0,16},{16,0},{1,17},{17,1},{2,18},{18,2},{3,19},{19,3},{4,20},{20... | collective-permute-start | bytes 589832 | tf_op jit(solution)/shard_map/ppermute | solution.py:44
  20.8 9.8 %collective-permute-start.14 = (bf16[2,2,2,8,1536]{4,3,2,1,0:T(8,128)(2,1)S(1)}, bf16[2,2,2,8,1536]{4,3,2,1,0:T(8,128)(2,1)S(1)}, u32[]{:S(2)}, u32[]{:S(2)}) collective-permute-start(bf16[2,2,2,8,1536]{4,3,2,1,0:T(8,128)(2,1)S(1)} %get-tuple-element.66), channel_id=1, source_target_pairs={{0,2},{1,3},{2,0},{3,1},{4,6},{5,7},{6,4},{7,5},{8,10},{9,11},{10,... | collective-permute-start | bytes 589832 | tf_op jit(solution)/shard_map/ppermute | solution.py:44
  22.9 8.3 %collective-permute-start.4 = (bf16[2,2,2,8,1536]{4,3,2,1,0:T(8,128)(2,1)S(1)}, bf16[2,2,2,8,1536]{4,3,2,1,0:T(8,128)(2,1)S(1)}, u32[]{:S(2)}, u32[]{:S(2)}) collective-permute-start(bf16[2,2,2,8,1536]{4,3,2,1,0:T(8,128)(2,1)S(1)} %get-tuple-element.72), channel_id=1, source_target_pairs={{0,16},{16,0},{1,17},{17,1},{2,18},{18,2},{3,19},{19,3},{4,20},{20... | collective-permute-start | bytes 589832 | tf_op jit(solution)/shard_map/ppermute | solution.py:44
  24.6 6.8 %collective-permute-start.10 = (bf16[2,2,2,8,1664]{4,3,2,1,0:T(8,128)(2,1)S(1)}, bf16[2,2,2,8,1664]{4,3,2,1,0:T(8,128)(2,1)S(1)}, u32[]{:S(2)}, u32[]{:S(2)}) collective-permute-start(bf16[2,2,2,8,1664]{4,3,2,1,0:T(8,128)(2,1)S(1)} %get-tuple-element.64), channel_id=1, source_target_pairs={{0,2},{1,3},{2,0},{3,1},{4,6},{5,7},{6,4},{7,5},{8,10},{9,11},{10,... | collective-permute-start | bytes 638984 | tf_op jit(solution)/shard_map/ppermute | solution.py:44
  30.6 1.8 %collective-permute-start.12 = (bf16[2,2,2,2,8,1536]{5,4,3,2,1,0:T(8,128)(2,1)S(1)}, bf16[2,2,2,2,8,1536]{5,4,3,2,1,0:T(8,128)(2,1)S(1)}, u32[]{:S(2)}, u32[]{:S(2)}) collective-permute-start(bf16[2,2,2,2,8,1536]{5,4,3,2,1,0:T(8,128)(2,1)S(1)} %get-tuple-element.62.refs_1_), channel_id=1, source_target_pairs={{0,1},{1,0},{2,3},{3,2},{4,5},{5,4},{6,7},{7,6},{8,9},{9,8},{10,11... | collective-permute-start | bytes 1179656 | tf_op jit(solution)/shard_map/ppermute | solution.py:44
  30.7 2.2 %collective-permute-start.15 = (bf16[2,2,2,2,8,1536]{5,4,3,2,0,1:T(8,128)(2,1)S(1)}, bf16[2,2,2,2,8,1536]{5,4,3,2,0,1:T(8,128)(2,1)S(1)}, u32[]{:S(2)}, u32[]{:S(2)}) collective-permute-start(bf16[2,2,2,2,8,1536]{5,4,3,2,0,1:T(8,128)(2,1)S(1)} %get-tuple-element.60), channel_id=1, source_target_pairs={{0,1},{1,0},{2,3},{3,2},{4,5},{5,4},{6,7},{7,6},{8,9},{9,8},{10,11... | collective-permute-start | bytes 1179656 | tf_op jit(solution)/shard_map/ppermute | solution.py:44
  31.3 8.9 %collective-permute-start.8 = (bf16[2,2,2,2,8,1536]{5,4,3,2,1,0:T(8,128)(2,1)S(1)}, bf16[2,2,2,2,8,1536]{5,4,3,2,1,0:T(8,128)(2,1)S(1)}, u32[]{:S(2)}, u32[]{:S(2)}) collective-permute-start(bf16[2,2,2,2,8,1536]{5,4,3,2,1,0:T(8,128)(2,1)S(1)} %pad_maximum_fusion.5), channel_id=1, source_target_pairs={{0,1},{1,0},{2,3},{3,2},{4,5},{5,4},{6,7},{7,6},{8,9},{9,8},{10,11... | collective-permute-start | bytes 1179656 | tf_op jit(solution)/shard_map/ppermute | solution.py:44
  31.5 8.8 %collective-permute-start.11 = (bf16[2,2,2,2,8,1664]{5,4,3,2,0,1:T(8,128)(2,1)S(1)}, bf16[2,2,2,2,8,1664]{5,4,3,2,0,1:T(8,128)(2,1)S(1)}, u32[]{:S(2)}, u32[]{:S(2)}) collective-permute-start(bf16[2,2,2,2,8,1664]{5,4,3,2,0,1:T(8,128)(2,1)S(1)} %get-tuple-element.58), channel_id=1, source_target_pairs={{0,1},{1,0},{2,3},{3,2},{4,5},{5,4},{6,7},{7,6},{8,9},{9,8},{10,11... | collective-permute-start | bytes 1277960 | tf_op jit(solution)/shard_map/ppermute | solution.py:44
  47.1 1.8 %collective-permute-start.16 = (bf16[2,2,2,2,8,1536]{5,4,3,2,1,0:T(8,128)(2,1)S(1)}, bf16[2,2,2,2,8,1536]{5,4,3,2,1,0:T(8,128)(2,1)S(1)}, u32[]{:S(2)}, u32[]{:S(2)}) collective-permute-start(bf16[2,2,2,2,8,1536]{5,4,3,2,1,0:T(8,128)(2,1)S(1)} %bitcast.155), channel_id=1, source_target_pairs={{0,1},{1,0},{2,3},{3,2},{4,5},{5,4},{6,7},{7,6},{8,9},{9,8},{10,11... | collective-permute-start | bytes 1179656 | tf_op jit(solution)/shard_map/ppermute | solution.py:44
  47.4 2.6 %collective-permute-start.18 = (bf16[2,2,2,2,8,1536]{5,4,3,2,0,1:T(8,128)(2,1)S(1)}, bf16[2,2,2,2,8,1536]{5,4,3,2,0,1:T(8,128)(2,1)S(1)}, u32[]{:S(2)}, u32[]{:S(2)}) collective-permute-start(bf16[2,2,2,2,8,1536]{5,4,3,2,0,1:T(8,128)(2,1)S(1)} %copy.19), channel_id=1, source_target_pairs={{0,1},{1,0},{2,3},{3,2},{4,5},{5,4},{6,7},{7,6},{8,9},{9,8},{10,11... | collective-permute-start | bytes 1179656 | tf_op jit(solution)/shard_map/ppermute | solution.py:44
  51.1 1.8 %collective-permute-start.19 = (bf16[2,2,2,2,8,1536]{5,4,3,2,0,1:T(8,128)(2,1)S(1)}, bf16[2,2,2,2,8,1536]{5,4,3,2,0,1:T(8,128)(2,1)S(1)}, u32[]{:S(2)}, u32[]{:S(2)}) collective-permute-start(bf16[2,2,2,2,8,1536]{5,4,3,2,0,1:T(8,128)(2,1)S(1)} %copy.21), channel_id=1, source_target_pairs={{0,1},{1,0},{2,3},{3,2},{4,5},{5,4},{6,7},{7,6},{8,9},{9,8},{10,11... | collective-permute-start | bytes 1179656 | tf_op jit(solution)/shard_map/ppermute | solution.py:44
  51.4 2.1 %collective-permute-start.17 = (bf16[2,2,2,2,8,1536]{5,4,3,2,1,0:T(8,128)(2,1)S(1)}, bf16[2,2,2,2,8,1536]{5,4,3,2,1,0:T(8,128)(2,1)S(1)}, u32[]{:S(2)}, u32[]{:S(2)}) collective-permute-start(bf16[2,2,2,2,8,1536]{5,4,3,2,1,0:T(8,128)(2,1)S(1)} %bitcast.156), channel_id=1, source_target_pairs={{0,1},{1,0},{2,3},{3,2},{4,5},{5,4},{6,7},{7,6},{8,9},{9,8},{10,11... | collective-permute-start | bytes 1179656 | tf_op jit(solution)/shard_map/ppermute | solution.py:44
  53.6 7.8 %collective-permute-start.22 = (bf16[2,2,2,8,1536]{4,3,2,1,0:T(8,128)(2,1)S(1)}, bf16[2,2,2,8,1536]{4,3,2,1,0:T(8,128)(2,1)S(1)}, u32[]{:S(2)}, u32[]{:S(2)}) collective-permute-start(bf16[2,2,2,8,1536]{4,3,2,1,0:T(8,128)(2,1)S(1)} %slice_bitcast_fusion.2), channel_id=1, source_target_pairs={{0,2},{1,3},{2,0},{3,1},{4,6},{5,7},{6,4},{7,5},{8,10},{9,11},{10,... | collective-permute-start | bytes 589832 | tf_op jit(solution)/shard_map/ppermute | solution.py:44
  54.2 8.9 %collective-permute-start.20 = (bf16[2,2,2,8,1536]{4,3,2,1,0:T(8,128)(2,1)S(1)}, bf16[2,2,2,8,1536]{4,3,2,1,0:T(8,128)(2,1)S(1)}, u32[]{:S(2)}, u32[]{:S(2)}) collective-permute-start(bf16[2,2,2,8,1536]{4,3,2,1,0:T(8,128)(2,1)S(1)} %slice_bitcast_fusion.3), channel_id=1, source_target_pairs={{0,16},{16,0},{1,17},{17,1},{2,18},{18,2},{3,19},{19,3},{4,20},{20... | collective-permute-start | bytes 589832 | tf_op jit(solution)/shard_map/ppermute | solution.py:44
  55.8 9.9 %collective-permute-start.27 = (bf16[2,2,2,8,1536]{4,3,2,1,0:T(8,128)(2,1)S(1)}, bf16[2,2,2,8,1536]{4,3,2,1,0:T(8,128)(2,1)S(1)}, u32[]{:S(2)}, u32[]{:S(2)}) collective-permute-start(bf16[2,2,2,8,1536]{4,3,2,1,0:T(8,128)(2,1)S(1)} %slice_bitcast_fusion), channel_id=1, source_target_pairs={{0,2},{1,3},{2,0},{3,1},{4,6},{5,7},{6,4},{7,5},{8,10},{9,11},{10,... | collective-permute-start | bytes 589832 | tf_op jit(solution)/shard_map/ppermute | solution.py:44
  57.4 8.8 %collective-permute-start.26 = (bf16[2,2,2,8,1536]{4,3,2,1,0:T(8,128)(2,1)S(1)}, bf16[2,2,2,8,1536]{4,3,2,1,0:T(8,128)(2,1)S(1)}, u32[]{:S(2)}, u32[]{:S(2)}) collective-permute-start(bf16[2,2,2,8,1536]{4,3,2,1,0:T(8,128)(2,1)S(1)} %slice_bitcast_fusion.1), channel_id=1, source_target_pairs={{0,16},{16,0},{1,17},{17,1},{2,18},{18,2},{3,19},{19,3},{4,20},{20... | collective-permute-start | bytes 589832 | tf_op jit(solution)/shard_map/ppermute | solution.py:44
  61.5 12.4 %collective-permute-start.23 = (bf16[2,2,8,1536]{3,2,1,0:T(8,128)(2,1)S(1)}, bf16[2,2,8,1536]{3,2,1,0:T(8,128)(2,1)S(1)}, u32[]{:S(2)}, u32[]{:S(2)}) collective-permute-start(bf16[2,2,8,1536]{3,2,1,0:T(8,128)(2,1)S(1)} %slice_bitcast_fusion.6), channel_id=1, source_target_pairs={{0,16},{16,0},{1,17},{17,1},{2,18},{18,2},{3,19},{19,3},{4,20},{20... | collective-permute-start | bytes 294920 | tf_op jit(solution)/shard_map/ppermute | solution.py:44
  63.1 10.8 %collective-permute-start.21 = (bf16[2,2,8,1536]{3,2,1,0:T(8,128)(2,1)S(1)}, bf16[2,2,8,1536]{3,2,1,0:T(8,128)(2,1)S(1)}, u32[]{:S(2)}, u32[]{:S(2)}) collective-permute-start(bf16[2,2,8,1536]{3,2,1,0:T(8,128)(2,1)S(1)} %slice_bitcast_fusion.8), channel_id=1, source_target_pairs={{0,2},{1,3},{2,0},{3,1},{4,6},{5,7},{6,4},{7,5},{8,10},{9,11},{10,... | collective-permute-start | bytes 294920 | tf_op jit(solution)/shard_map/ppermute | solution.py:44
  66.3 4.7 %collective-permute-start.29 = (bf16[2,2,8,1536]{3,2,1,0:T(8,128)(2,1)S(1)}, bf16[2,2,8,1536]{3,2,1,0:T(8,128)(2,1)S(1)}, u32[]{:S(2)}, u32[]{:S(2)}) collective-permute-start(bf16[2,2,8,1536]{3,2,1,0:T(8,128)(2,1)S(1)} %slice_bitcast_fusion.10), channel_id=1, source_target_pairs={{0,16},{16,0},{1,17},{17,1},{2,18},{18,2},{3,19},{19,3},{4,20},{20... | collective-permute-start | bytes 294920 | tf_op jit(solution)/shard_map/ppermute | solution.py:44
  67.8 4.7 %collective-permute-start.28 = (bf16[2,2,8,1536]{3,2,1,0:T(8,128)(2,1)S(1)}, bf16[2,2,8,1536]{3,2,1,0:T(8,128)(2,1)S(1)}, u32[]{:S(2)}, u32[]{:S(2)}) collective-permute-start(bf16[2,2,8,1536]{3,2,1,0:T(8,128)(2,1)S(1)} %slice_bitcast_fusion.11), channel_id=1, source_target_pairs={{0,2},{1,3},{2,0},{3,1},{4,6},{5,7},{6,4},{7,5},{8,10},{9,11},{10,... | collective-permute-start | bytes 294920 | tf_op jit(solution)/shard_map/ppermute | solution.py:44
  72.6 5.2 %collective-permute-start.30 = (bf16[2,8,3072]{2,1,0:T(8,128)(2,1)S(1)}, bf16[2,8,3072]{2,1,0:T(8,128)(2,1)S(1)}, u32[]{:S(2)}, u32[]{:S(2)}) collective-permute-start(bf16[2,8,3072]{2,1,0:T(8,128)(2,1)S(1)} %slice_bitcast_fusion.4), channel_id=1, source_target_pairs={{0,4},{4,0},{8,12},{12,8},{1,5},{5,1},{9,13},{13,9},{2,6},{6,2},{1... | collective-permute-start | bytes 294920 | tf_op jit(solution)/shard_map/ppermute | solution.py:44
  74.0 6.7 %collective-permute-start.24 = (bf16[2,8,3072]{2,1,0:T(8,128)(2,1)S(1)}, bf16[2,8,3072]{2,1,0:T(8,128)(2,1)S(1)}, u32[]{:S(2)}, u32[]{:S(2)}) collective-permute-start(bf16[2,8,3072]{2,1,0:T(8,128)(2,1)S(1)} %fusion.18), channel_id=1, source_target_pairs={{0,4},{4,0},{8,12},{12,8},{1,5},{5,1},{9,13},{13,9},{2,6},{6,2},{1... | collective-permute-start | bytes 294920 | tf_op jit(solution)/shard_map/ppermute | solution.py:44
  77.8 5.1 %collective-permute-start.31 = (bf16[8,3072]{1,0:T(8,128)(2,1)S(1)}, bf16[8,3072]{1,0:T(8,128)(2,1)S(1)}, u32[]{:S(2)}, u32[]{:S(2)}) collective-permute-start(bf16[8,3072]{1,0:T(8,128)(2,1)S(1)} %slice_bitcast_fusion.14), channel_id=1, source_target_pairs={{0,8},{4,12},{8,0},{12,4},{1,9},{5,13},{9,1},{13,5},{2,10},{6,14},... | collective-permute-start | bytes 147464 | tf_op jit(solution)/shard_map/ppermute | solution.py:44
  80.7 5.1 %collective-permute-start.25 = (bf16[8,3072]{1,0:T(8,128)(2,1)S(1)}, bf16[8,3072]{1,0:T(8,128)(2,1)S(1)}, u32[]{:S(2)}, u32[]{:S(2)}) collective-permute-start(bf16[8,3072]{1,0:T(8,128)(2,1)S(1)} %slice_bitcast_fusion.12), channel_id=1, source_target_pairs={{0,8},{4,12},{8,0},{12,4},{1,9},{5,13},{9,1},{13,5},{2,10},{6,14},... | collective-permute-start | bytes 147464 | tf_op jit(solution)/shard_map/ppermute | solution.py:44

commit v9 on v7

--- a/solution.py
+++ b/solution.py
@@ -96,57 +96,65 @@
     )(in_hbm(weight), after)
 
 
-def gate_up_kernel(last, take, rows_ref, *refs):
+def gate_up_kernel(last, take, pieces, row_ref, *refs):
     if last:
-        sum_ref, w_ref, next_hbm, out_ref, next_ref, sem = refs
-    else:
-        w_ref, next_hbm, out_ref, next_ref, sem = refs
-    experts, _, sliver, half = w_ref.shape
-    group = 2 if experts % 2 == 0 else 1
+        sum_ref, refs = refs[0], refs[1:]
+    w_refs, (next_hbm, out_ref, next_ref, sem) = refs[:pieces], refs[pieces:]
+    held, _, sliver, half = w_refs[0].shape
+    experts = held * pieces
+    group = experts // 2 if experts % 2 == 0 else experts
     units = 2 * sliver
+    depths = 2 if last else 1
+    depth = half // depths
     copy = pltpu.make_async_copy(take(next_hbm), next_ref, sem)
     pl.when(pl.program_id(0) == 0)(copy.start)
     if last:
-        extra = rows_ref[:, half:].astype(jnp.float32)
+        extra = row_ref[:, half:].astype(jnp.float32)
         lane = lax.broadcasted_iota(jnp.int32, extra.shape, 1)
     for first in range(0, experts, group):
         columns = slice(first * units, (first + group) * units)
-        pre = lax.dot_general(
-            rows_ref[:, :half],
-            w_ref[first : first + group].reshape(group * units, half),
-            (((1,), (1,)), ((), ())),
-            preferred_element_type=jnp.float32,
-        )
+        w_ref, at_slot = w_refs[first // held], first % held
+        pre = sum_ref[:, columns] if last else None
+        for at in range(0, half, depth):
+            product = lax.dot_general(
+                row_ref[:, at : at + depth],
+                w_ref[at_slot : at_slot + group, :, :, at : at + depth].reshape(
+                    group * units, depth
+                ),
+                (((1,), (1,)), ((), ())),
+                preferred_element_type=jnp.float32,
+            )
+            pre = product if pre is None else pre + product
         if not last:
             out_ref[:, columns] = pre
             continue
-        pre += sum_ref[:, columns]
         for slot in range(first, first + group):
             at = (slot - first) * units
             gate, up = pre[:, at : at + sliver], pre[:, at + sliver : at + units]
             mine = (lane == slot) | (lane == slot + experts) | (lane == slot + 2 * experts)
             weigh = jnp.sum(jnp.where(mine, extra, 0.0), axis=1, keepdims=True)
-            hidden = gate / (1.0 + jnp.exp(-gate)) * up * weigh
+            hidden = (0.5 * gate) * (1.0 + jnp.tanh(0.5 * gate)) * up * weigh
             out_ref[slot] = hidden.astype(out_ref.dtype)
     pl.when(pl.program_id(0) == 0)(copy.wait)
 
 
-def gate_up_of(rows_of_part, sums, weights, next_weight, take, next_shape):
-    experts, _, sliver, half = weights.shape
-    rows, width = rows_of_part.shape
+def gate_up_of(row_part, sums, weights, next_weight, take, next_shape):
+    held, _, sliver, half = weights[0].shape
+    pieces = len(weights)
+    experts = held * pieces
+    rows = row_part.shape[0]
     row_block = min(ROW_BLOCK, rows)
     whole = rows == row_block
     last = sums is not None
     units = experts * 2 * sliver
-    operands = [rows_of_part, sums] if last else [rows_of_part]
+    operands = [row_part, sums] if last else [row_part]
     if whole:
+        specs = [pl.BlockSpec(memory_space=pltpu.VMEM)] * len(operands)
         operands = [resident(operand) for operand in operands]
-        specs = [pl.BlockSpec(memory_space=pltpu.VMEM)] * len(operands)
     else:
         specs = [
-            pl.BlockSpec((row_block, width), lambda r: (r, 0)),
-            pl.BlockSpec((row_block, units), lambda r: (r, 0)),
-        ][: len(operands)]
+            pl.BlockSpec((row_block, operand.shape[1]), lambda r: (r, 0)) for operand in operands
+        ]
     if last:
         out_spec = pl.BlockSpec((experts, row_block, sliver), lambda r: (0, r, 0))
         out_shape = jax.ShapeDtypeStruct((experts, rows, sliver), jnp.bfloat16)
@@ -158,13 +166,14 @@
         out_shape = pltpu.VMEM(out_shape.shape, out_shape.dtype)
 
     def kernel(*refs):
-        gate_up_kernel(last, take, *refs)
+        gate_up_kernel(last, take, pieces, *refs)
 
     return pl.pallas_call(
         kernel,
         grid=(rows // row_block,),
         in_specs=specs
-        + [pl.BlockSpec(memory_space=pltpu.VMEM), pl.BlockSpec(memory_space=pl.ANY)],
+        + [pl.BlockSpec(memory_space=pltpu.VMEM)] * pieces
+        + [pl.BlockSpec(memory_space=pl.ANY)],
         out_specs=[out_spec, pl.BlockSpec(memory_space=pltpu.VMEM)],
         out_shape=[out_shape, pltpu.VMEM(next_shape, next_weight.dtype)],
         scratch_shapes=[pltpu.SemaphoreType.DMA],
@@ -174,13 +183,13 @@
             bytes_accessed=2 * math.prod(next_shape) + 4 * rows * units,
             transcendentals=rows * experts * sliver,
         ),
-    )(*operands, resident(weights), in_hbm(next_weight))
+    )(*operands, *(resident(weight) for weight in weights), in_hbm(next_weight))
 
 
 def down_kernel(part, hidden_ref, w_ref, out_ref):
     experts, _, sliver = hidden_ref.shape
     columns = out_ref.shape[1]
-    block = next(size for size in (1024, 512, 384, 256, 128, columns) if columns % size == 0)
+    block = next(size for size in (1536, 1024, 512, 384, 256, 128, columns) if columns % size == 0)
 
     def one_block(step, carry):
         at = pl.multiple_of(step * block, block)
@@ -244,11 +253,11 @@
     ]
     half_shape = gate_up_weight.shape[:3] + (half,)
 
+    def take_second(ref):
+        return ref.at[:, :, :, pl.ds(half, half)]
+
     def take_first(ref):
         return ref.at[:, :, :, pl.ds(0, half)]
-
-    def take_second(ref):
-        return ref.at[:, :, :, pl.ds(half, half)]
 
     blocks, held = list(parts), [[], []]
     last = len(routes[0]) - 1
@@ -264,11 +273,11 @@
             blocks[number] = digit.gather(blocks[number], dim)
             held[number].append(digit)
     gathered = [block.reshape(-1, part.shape[1]) for block, part in zip(blocks, parts)]
-    sums, weights = gate_up_of(
-        gathered[1], None, first_weights, gate_up_weight, take_first, half_shape
+    sums, next_weights = gate_up_of(
+        gathered[1], None, [first_weights], gate_up_weight, take_first, half_shape
     )
     hidden, down_weight = gate_up_of(
-        gathered[0], sums, weights, down_weight, lambda ref: ref, down_weight.shape
+        gathered[0], sums, [next_weights], down_weight, lambda ref: ref, down_weight.shape
     )
     down_weight = resident(down_weight)
     results = []

time: 83.4 us -> 79.6 us (0.954)
  Pallas kernels: 21.7 us -> 17.8 us
    pallas_call x2, Pallas kernels: 12.7 us -> 9.27 us  [gate_up_of(): pl.pallas_call(kernel, grid=(rows // row_block,), in_specs=specs + [pl.Bl...]
where the time goes in v9:
time: 79.6 us; the launch traced here: 79.3 us
  waiting for transfers between devices  29.3 us (37%)
  starting transfers between devices  26.6 us (33%)
  Pallas kernels  17.8 us (22%)
  other arithmetic  3.74 us (5%)
  local copies, waits for them, and re-layouts  1.43 us (2%)
    ppermute x20, waiting for transfers between devices, shift(): return lax.ppermute(value, self.name, pairs)  29.3 us
    ppermute x20, starting transfers between devices, shift(): return lax.ppermute(value, self.name, pairs)  26.6 us
    pallas_call x2, Pallas kernels, gate_up_of(): pl.pallas_call(kernel, grid=(rows // row_block,), in_specs=specs + [pl.Bl...  9.27 us
    pallas_call x1, Pallas kernels, fetched(): pl.pallas_call(kernel, in_specs=[pl.BlockSpec(memory_space=pl.ANY)] * 2,...  4.58 us
    pallas_call x2, Pallas kernels, down_of(): pl.pallas_call(kernel, grid=(rows // row_block,), in_specs=[pl.BlockSpec(...  3.98 us
  transfers between devices with their start and end apart: 20, of which 16 were waited for; matrix products, arithmetic and copies ran while one was open for 4% of the time, Pallas kernels for 14%

profile of v9, /device:TPU:0, one launch (start us, length us, event | category | flops | bytes accessed | tf_op | source)
XLA Modules:
  0.0 79.3 jit_solution(7372524702884937002)
XLA Ops:
  0.0 0.8 %slice_bitcast_fusion.16 = (bf16[1,8,3072]{2,1,0:T(8,128)(2,1)S(1)}, bf16[8,3072]{1,0:T(8,128)(2,1)S(1)}, bf16[8,3072]{1,0:T(8,128)(2,1)S(1)}) fusion(bf16[8,6144]{1,0:T(8,128)(2,1)} %param.8), kind=kLoop, calls=%fused_computation.64 | loop fusion | bytes 245760 | tf_op jit(solution)/shard_map/stack | solution.py:47
  0.8 4.1 %collective-permute-start.5 = (bf16[8,3072]{1,0:T(8,128)(2,1)S(1)}, bf16[8,3072]{1,0:T(8,128)(2,1)S(1)}, u32[]{:S(2)}, u32[]{:S(2)}) collective-permute-start(bf16[8,3072]{1,0:T(8,128)(2,1)S(1)} %get-tuple-element.36), channel_id=1, source_target_pairs={{0,8},{4,12},{8,0},{12,4},{1,9},{5,13},{9,1},{13,5},{2,10},{6,14},... | collective-permute-start | bytes 147464 | tf_op jit(solution)/shard_map/ppermute | solution.py:44
  4.9 0.7 compare_convert_fusion
  5.7 0.7 select_reduce_fusion
  6.7 0.8 collective-permute-done.5
  7.6 1.9 %collective-permute-start.6 = (bf16[2,8,3072]{2,1,0:T(8,128)(2,1)S(1)}, bf16[2,8,3072]{2,1,0:T(8,128)(2,1)S(1)}, u32[]{:S(2)}, u32[]{:S(2)}) collective-permute-start(bf16[2,8,3072]{2,1,0:T(8,128)(2,1)S(1)} %get-tuple-element.34), channel_id=1, source_target_pairs={{0,4},{4,0},{8,12},{12,8},{1,5},{5,1},{9,13},{13,9},{2,6},{6,2},{1... | collective-permute-start | bytes 294920 | tf_op jit(solution)/shard_map/ppermute | solution.py:44
  9.4 2.6 %collective-permute-done = bf16[8,3200]{1,0:T(8,128)(2,1)S(1)} collective-permute-done((bf16[8,3200]{1,0:T(8,128)(2,1)S(1)}, bf16[8,3200]{1,0:T(8,128)(2,1)S(1)}, u32[]{:S(2)}, u32[]{:S(2)}) %collective-permute-start) | collective-permute-done | bytes 51232 | tf_op jit(solution)/shard_map/ppermute | solution.py:44
  12.0 1.6 %collective-permute-start.1 = (bf16[2,8,3200]{2,1,0:T(8,128)(2,1)S(1)}, bf16[2,8,3200]{2,1,0:T(8,128)(2,1)S(1)}, u32[]{:S(2)}, u32[]{:S(2)}) collective-permute-start(bf16[2,8,3200]{2,1,0:T(8,128)(2,1)S(1)} %get-tuple-element.32), channel_id=1, source_target_pairs={{0,4},{4,0},{8,12},{12,8},{1,5},{5,1},{9,13},{13,9},{2,6},{6,2},{1... | collective-permute-start | bytes 307208 | tf_op jit(solution)/shard_map/ppermute | solution.py:44
  13.6 1.6 %collective-permute-start.7 = (bf16[2,2,8,3072]{3,2,1,0:T(8,128)(2,1)S(1)}, bf16[2,2,8,3072]{3,2,1,0:T(8,128)(2,1)S(1)}, u32[]{:S(2)}, u32[]{:S(2)}) collective-permute-start(bf16[2,2,8,3072]{3,2,1,0:T(8,128)(2,1)S(1)} %get-tuple-element.30), channel_id=1, source_target_pairs={{0,16},{16,0},{1,17},{17,1},{2,18},{18,2},{3,19},{19,3},{4,20},{20... | collective-permute-start | bytes 589832 | tf_op jit(solution)/shard_map/ppermute | solution.py:44
  15.2 1.6 %collective-permute-done.1 = bf16[2,8,3200]{2,1,0:T(8,128)(2,1)S(1)} collective-permute-done((bf16[2,8,3200]{2,1,0:T(8,128)(2,1)S(1)}, bf16[2,8,3200]{2,1,0:T(8,128)(2,1)S(1)}, u32[]{:S(2)}, u32[]{:S(2)}) %collective-permute-start.1) | collective-permute-done | bytes 102432 | tf_op jit(solution)/shard_map/ppermute | solution.py:44
  16.8 1.5 %collective-permute-start.2 = (bf16[2,2,8,3200]{3,2,1,0:T(8,128)(2,1)S(1)}, bf16[2,2,8,3200]{3,2,1,0:T(8,128)(2,1)S(1)}, u32[]{:S(2)}, u32[]{:S(2)}) collective-permute-start(bf16[2,2,8,3200]{3,2,1,0:T(8,128)(2,1)S(1)} %get-tuple-element.28), channel_id=1, source_target_pairs={{0,2},{1,3},{2,0},{3,1},{4,6},{5,7},{6,4},{7,5},{8,10},{9,11},{10,... | collective-permute-start | bytes 614408 | tf_op jit(solution)/shard_map/ppermute | solution.py:44
  18.3 1.1 %collective-permute-done.7 = bf16[2,2,8,3072]{3,2,1,0:T(8,128)(2,1)S(1)} collective-permute-done((bf16[2,2,8,3072]{3,2,1,0:T(8,128)(2,1)S(1)}, bf16[2,2,8,3072]{3,2,1,0:T(8,128)(2,1)S(1)}, u32[]{:S(2)}, u32[]{:S(2)}) %collective-permute-start.7) | collective-permute-done | bytes 196640 | tf_op jit(solution)/shard_map/ppermute | solution.py:44
  19.4 1.6 %collective-permute-start.8 = (bf16[2,2,2,8,3072]{4,3,2,1,0:T(8,128)(2,1)S(1)}, bf16[2,2,2,8,3072]{4,3,2,1,0:T(8,128)(2,1)S(1)}, u32[]{:S(2)}, u32[]{:S(2)}) collective-permute-start(bf16[2,2,2,8,3072]{4,3,2,1,0:T(8,128)(2,1)S(1)} %get-tuple-element.26), channel_id=1, source_target_pairs={{0,2},{1,3},{2,0},{3,1},{4,6},{5,7},{6,4},{7,5},{8,10},{9,11},{10,... | collective-permute-start | bytes 1179656 | tf_op jit(solution)/shard_map/ppermute | solution.py:44
  21.0 3.8 %collective-permute-done.2 = bf16[2,2,8,3200]{3,2,1,0:T(8,128)(2,1)S(1)} collective-permute-done((bf16[2,2,8,3200]{3,2,1,0:T(8,128)(2,1)S(1)}, bf16[2,2,8,3200]{3,2,1,0:T(8,128)(2,1)S(1)}, u32[]{:S(2)}, u32[]{:S(2)}) %collective-permute-start.2) | collective-permute-done | bytes 204832 | tf_op jit(solution)/shard_map/ppermute | solution.py:44
  24.9 1.5 %collective-permute-start.3 = (bf16[2,2,2,8,3200]{4,3,2,1,0:T(8,128)(2,1)S(1)}, bf16[2,2,2,8,3200]{4,3,2,1,0:T(8,128)(2,1)S(1)}, u32[]{:S(2)}, u32[]{:S(2)}) collective-permute-start(bf16[2,2,2,8,3200]{4,3,2,1,0:T(8,128)(2,1)S(1)} %get-tuple-element.24.refs_1_), channel_id=1, source_target_pairs={{0,16},{16,0},{1,17},{17,1},{2,18},{18,2},{3,19},{19,3},{4,20},{20... | collective-permute-start | bytes 1228808 | tf_op jit(solution)/shard_map/ppermute | solution.py:44
  26.4 4.6 %shard_map.73.refs_1_ = bf16[4,2,256,3072]{3,2,1,0:T(8,128)(2,1)S(1)} custom-call(bf16[4,2,256,6144]{3,2,1,0:T(8,128)(2,1)} %refs_2_.1, bf16[2,2,2,8,3200]{4,3,2,1,0:T(8,128)(2,1)S(1)} %get-tuple-element.24.refs_1_), custom_call_target="tpu_custom_call" | custom-call | bytes 25165824 | tf_op jit(solution)/shard_map/pallas_call | solution.py:86
  31.1 1.8 %collective-permute-done.3 = bf16[2,2,2,8,3200]{4,3,2,1,0:T(8,128)(2,1)S(1)} collective-permute-done((bf16[2,2,2,8,3200]{4,3,2,1,0:T(8,128)(2,1)S(1)}, bf16[2,2,2,8,3200]{4,3,2,1,0:T(8,128)(2,1)S(1)}, u32[]{:S(2)}, u32[]{:S(2)}) %collective-permute-start.3) | collective-permute-done | bytes 409632 | tf_op jit(solution)/shard_map/ppermute | solution.py:44
  32.9 0.1 fusion.24
  33.1 0.3 collective-permute-done.9
  33.4 0.1 pad_maximum_fusion.1
  33.6 0.1 copy.15
  33.7 4.7 %shard_map.74 = (f32[256,2048]{1,0:T(8,128)S(1)}, bf16[4,2,256,3072]{3,2,1,0:T(8,128)(2,1)S(1)}) custom-call(bf16[256,3072]{1,0:T(8,128)(2,1)S(1)} %bitcast.94, bf16[4,2,256,3072]{3,2,1,0:T(8,128)(2,1)S(1)} %shard_map.73.refs_1_, bf16[4,2,256,6144]{3,2,1,0:T(8,128)(2,1)} %refs_2_.1), custom_call_target="tpu_custom_call" | custom-call | flops 3221225472 | bytes 14680064 | tf_op jit(solution)/shard_map/pallas_call | solution.py:171
  38.4 0.2 pad_maximum_fusion
  38.6 4.6 %shard_map.75 = (bf16[4,256,256]{2,1,0:T(8,128)(2,1)S(1)}, bf16[4,256,6144]{2,1,0:T(8,128)(2,1)S(1)}) custom-call(bf16[256,3200]{1,0:T(8,128)(2,1)S(1)} %bitcast.93, f32[256,2048]{1,0:T(8,128)S(1)} %get-tuple-element.13.refs_1_, bf16[4,2,256,3072]{3,2,1,0:T(8,128)(2,1)S(1)} %get-tuple-element.14.refs_2_, bf16[4,256,6144]{2,1,0:T(8,128)(2,1)} %refs_3_.1), custom_call_target="tpu_custom_call" | custom-call | flops 3221225472 | bytes 14680064 | tf_op jit(solution)/shard_map/pallas_call | solution.py:171
  43.2 2.0 %shard_map.76 = bf16[256,3072]{1,0:T(8,128)(2,1)S(1)} custom-call(bf16[4,256,256]{2,1,0:T(8,128)(2,1)S(1)} %get-tuple-element.15.refs_0_, bf16[4,256,6144]{2,1,0:T(8,128)(2,1)S(1)} %get-tuple-element.16.refs_1_), custom_call_target="tpu_custom_call" | custom-call | flops 1610612736 | bytes 8388608 | tf_op jit(solution)/shard_map/pallas_call | solution.py:214
  45.3 0.2 collective-permute-start.10
  45.5 2.0 %shard_map.77 = bf16[256,3072]{1,0:T(8,128)(2,1)S(1)} custom-call(bf16[4,256,256]{2,1,0:T(8,128)(2,1)S(1)} %get-tuple-element.15.refs_0_, bf16[4,256,6144]{2,1,0:T(8,128)(2,1)S(1)} %get-tuple-element.16.refs_1_), custom_call_target="tpu_custom_call" | custom-call | flops 1610612736 | bytes 8388608 | tf_op jit(solution)/shard_map/pallas_call | solution.py:214
  47.7 0.4 collective-permute-start.15
  48.1 0.2 fusion
  48.3 1.2 %collective-permute-start.11 = (bf16[2,2,2,8,3072]{4,3,2,1,0:T(8,128)(2,1)S(1)}, bf16[2,2,2,8,3072]{4,3,2,1,0:T(8,128)(2,1)S(1)}, u32[]{:S(2)}, u32[]{:S(2)}) collective-permute-start(bf16[2,2,2,8,3072]{4,3,2,1,0:T(8,128)(2,1)S(1)} %slice_bitcast_fusion.2), channel_id=1, source_target_pairs={{0,16},{16,0},{1,17},{17,1},{2,18},{18,2},{3,19},{19,3},{4,20},{20... | collective-permute-start | bytes 1179656 | tf_op jit(solution)/shard_map/ppermute | solution.py:44
  49.5 0.5 collective-permute-done.15
  50.1 0.2 fusion.1
  50.3 1.6 %collective-permute-start.16 = (bf16[2,2,2,8,3072]{4,3,2,1,0:T(8,128)(2,1)S(1)}, bf16[2,2,2,8,3072]{4,3,2,1,0:T(8,128)(2,1)S(1)}, u32[]{:S(2)}, u32[]{:S(2)}) collective-permute-start(bf16[2,2,2,8,3072]{4,3,2,1,0:T(8,128)(2,1)S(1)} %slice_bitcast_fusion), channel_id=1, source_target_pairs={{0,2},{1,3},{2,0},{3,1},{4,6},{5,7},{6,4},{7,5},{8,10},{9,11},{10,... | collective-permute-start | bytes 1179656 | tf_op jit(solution)/shard_map/ppermute | solution.py:44
  51.8 7.8 %collective-permute-done.11 = bf16[2,2,2,8,3072]{4,3,2,1,0:T(8,128)(2,1)S(1)} collective-permute-done((bf16[2,2,2,8,3072]{4,3,2,1,0:T(8,128)(2,1)S(1)}, bf16[2,2,2,8,3072]{4,3,2,1,0:T(8,128)(2,1)S(1)}, u32[]{:S(2)}, u32[]{:S(2)}) %collective-permute-start.11) | collective-permute-done | bytes 393248 | tf_op jit(solution)/shard_map/ppermute | solution.py:44
  59.7 1.5 %collective-permute-start.12 = (bf16[2,2,8,3072]{3,2,1,0:T(8,128)(2,1)S(1)}, bf16[2,2,8,3072]{3,2,1,0:T(8,128)(2,1)S(1)}, u32[]{:S(2)}, u32[]{:S(2)}) collective-permute-start(bf16[2,2,8,3072]{3,2,1,0:T(8,128)(2,1)S(1)} %slice_bitcast_fusion.6), channel_id=1, source_target_pairs={{0,2},{1,3},{2,0},{3,1},{4,6},{5,7},{6,4},{7,5},{8,10},{9,11},{10,... | collective-permute-start | bytes 589832 | tf_op jit(solution)/shard_map/ppermute | solution.py:44
  61.3 0.4 collective-permute-done.16
  61.8 1.3 %collective-permute-start.17 = (bf16[2,2,8,3072]{3,2,1,0:T(8,128)(2,1)S(1)}, bf16[2,2,8,3072]{3,2,1,0:T(8,128)(2,1)S(1)}, u32[]{:S(2)}, u32[]{:S(2)}) collective-permute-start(bf16[2,2,8,3072]{3,2,1,0:T(8,128)(2,1)S(1)} %slice_bitcast_fusion.4), channel_id=1, source_target_pairs={{0,16},{16,0},{1,17},{17,1},{2,18},{18,2},{3,19},{19,3},{4,20},{20... | collective-permute-start | bytes 589832 | tf_op jit(solution)/shard_map/ppermute | solution.py:44
  63.1 2.8 %collective-permute-done.12 = bf16[2,2,8,3072]{3,2,1,0:T(8,128)(2,1)S(1)} collective-permute-done((bf16[2,2,8,3072]{3,2,1,0:T(8,128)(2,1)S(1)}, bf16[2,2,8,3072]{3,2,1,0:T(8,128)(2,1)S(1)}, u32[]{:S(2)}, u32[]{:S(2)}) %collective-permute-start.12) | collective-permute-done | bytes 196640 | tf_op jit(solution)/shard_map/ppermute | solution.py:44
  66.0 1.6 %collective-permute-start.13 = (bf16[2,8,3072]{2,1,0:T(8,128)(2,1)S(1)}, bf16[2,8,3072]{2,1,0:T(8,128)(2,1)S(1)}, u32[]{:S(2)}, u32[]{:S(2)}) collective-permute-start(bf16[2,8,3072]{2,1,0:T(8,128)(2,1)S(1)} %slice_bitcast_fusion.10), channel_id=1, source_target_pairs={{0,4},{4,0},{8,12},{12,8},{1,5},{5,1},{9,13},{13,9},{2,6},{6,2},{1... | collective-permute-start | bytes 294920 | tf_op jit(solution)/shard_map/ppermute | solution.py:44
  67.7 0.6 collective-permute-done.17
  68.3 1.7 %collective-permute-start.18 = (bf16[2,8,3072]{2,1,0:T(8,128)(2,1)S(1)}, bf16[2,8,3072]{2,1,0:T(8,128)(2,1)S(1)}, u32[]{:S(2)}, u32[]{:S(2)}) collective-permute-start(bf16[2,8,3072]{2,1,0:T(8,128)(2,1)S(1)} %slice_bitcast_fusion.8), channel_id=1, source_target_pairs={{0,4},{4,0},{8,12},{12,8},{1,5},{5,1},{9,13},{13,9},{2,6},{6,2},{1... | collective-permute-start | bytes 294920 | tf_op jit(solution)/shard_map/ppermute | solution.py:44
  70.0 1.7 %collective-permute-done.13 = bf16[2,8,3072]{2,1,0:T(8,128)(2,1)S(1)} collective-permute-done((bf16[2,8,3072]{2,1,0:T(8,128)(2,1)S(1)}, bf16[2,8,3072]{2,1,0:T(8,128)(2,1)S(1)}, u32[]{:S(2)}, u32[]{:S(2)}) %collective-permute-start.13) | collective-permute-done | bytes 98336 | tf_op jit(solution)/shard_map/ppermute | solution.py:44
  71.7 1.6 %collective-permute-start.14 = (bf16[8,3072]{1,0:T(8,128)(2,1)S(1)}, bf16[8,3072]{1,0:T(8,128)(2,1)S(1)}, u32[]{:S(2)}, u32[]{:S(2)}) collective-permute-start(bf16[8,3072]{1,0:T(8,128)(2,1)S(1)} %slice_bitcast_fusion.14), channel_id=1, source_target_pairs={{0,8},{4,12},{8,0},{12,4},{1,9},{5,13},{9,1},{13,5},{2,10},{6,14},... | collective-permute-start | bytes 147464 | tf_op jit(solution)/shard_map/ppermute | solution.py:44
  73.3 0.2 collective-permute-done.18
  73.5 1.6 %collective-permute-start.19 = (bf16[8,3072]{1,0:T(8,128)(2,1)S(1)}, bf16[8,3072]{1,0:T(8,128)(2,1)S(1)}, u32[]{:S(2)}, u32[]{:S(2)}) collective-permute-start(bf16[8,3072]{1,0:T(8,128)(2,1)S(1)} %slice_bitcast_fusion.12), channel_id=1, source_target_pairs={{0,8},{4,12},{8,0},{12,4},{1,9},{5,13},{9,1},{13,5},{2,10},{6,14},... | collective-permute-start | bytes 147464 | tf_op jit(solution)/shard_map/ppermute | solution.py:44
  75.1 2.2 %collective-permute-done.14 = bf16[8,3072]{1,0:T(8,128)(2,1)S(1)} collective-permute-done((bf16[8,3072]{1,0:T(8,128)(2,1)S(1)}, bf16[8,3072]{1,0:T(8,128)(2,1)S(1)}, u32[]{:S(2)}, u32[]{:S(2)}) %collective-permute-start.14) | collective-permute-done | bytes 49184 | tf_op jit(solution)/shard_map/ppermute | solution.py:44
  77.3 1.3 %collective-permute-done.19 = bf16[8,3072]{1,0:T(8,128)(2,1)S(1)} collective-permute-done((bf16[8,3072]{1,0:T(8,128)(2,1)S(1)}, bf16[8,3072]{1,0:T(8,128)(2,1)S(1)}, u32[]{:S(2)}, u32[]{:S(2)}) %collective-permute-start.19) | collective-permute-done | bytes 49184 | tf_op jit(solution)/shard_map/ppermute | solution.py:44
  78.6 0.6 pad_maximum_fusion.10
  (38 shorter events, 1.5 us)
Async XLA Ops:
  0.8 6.7 %collective-permute-start.5 = (bf16[8,3072]{1,0:T(8,128)(2,1)S(1)}, bf16[8,3072]{1,0:T(8,128)(2,1)S(1)}, u32[]{:S(2)}, u32[]{:S(2)}) collective-permute-start(bf16[8,3072]{1,0:T(8,128)(2,1)S(1)} %get-tuple-element.36), channel_id=1, source_target_pairs={{0,8},{4,12},{8,0},{12,4},{1,9},{5,13},{9,1},{13,5},{2,10},{6,14},... | collective-permute-start | bytes 147464 | tf_op jit(solution)/shard_map/ppermute | solution.py:44
  6.7 5.3 %collective-permute-start = (bf16[8,3200]{1,0:T(8,128)(2,1)S(1)}, bf16[8,3200]{1,0:T(8,128)(2,1)S(1)}, u32[]{:S(2)}, u32[]{:S(2)}) collective-permute-start(bf16[8,3200]{1,0:T(8,128)(2,1)S(1)} %get-tuple-element.39), channel_id=1, source_target_pairs={{0,8},{4,12},{8,0},{12,4},{1,9},{5,13},{9,1},{13,5},{2,10},{6,14},... | collective-permute-start | bytes 153608 | tf_op jit(solution)/shard_map/ppermute | solution.py:44
  7.6 6.0 %collective-permute-start.6 = (bf16[2,8,3072]{2,1,0:T(8,128)(2,1)S(1)}, bf16[2,8,3072]{2,1,0:T(8,128)(2,1)S(1)}, u32[]{:S(2)}, u32[]{:S(2)}) collective-permute-start(bf16[2,8,3072]{2,1,0:T(8,128)(2,1)S(1)} %get-tuple-element.34), channel_id=1, source_target_pairs={{0,4},{4,0},{8,12},{12,8},{1,5},{5,1},{9,13},{13,9},{2,6},{6,2},{1... | collective-permute-start | bytes 294920 | tf_op jit(solution)/shard_map/ppermute | solution.py:44
  12.0 4.7 %collective-permute-start.1 = (bf16[2,8,3200]{2,1,0:T(8,128)(2,1)S(1)}, bf16[2,8,3200]{2,1,0:T(8,128)(2,1)S(1)}, u32[]{:S(2)}, u32[]{:S(2)}) collective-permute-start(bf16[2,8,3200]{2,1,0:T(8,128)(2,1)S(1)} %get-tuple-element.32), channel_id=1, source_target_pairs={{0,4},{4,0},{8,12},{12,8},{1,5},{5,1},{9,13},{13,9},{2,6},{6,2},{1... | collective-permute-start | bytes 307208 | tf_op jit(solution)/shard_map/ppermute | solution.py:44
  13.6 5.7 %collective-permute-start.7 = (bf16[2,2,8,3072]{3,2,1,0:T(8,128)(2,1)S(1)}, bf16[2,2,8,3072]{3,2,1,0:T(8,128)(2,1)S(1)}, u32[]{:S(2)}, u32[]{:S(2)}) collective-permute-start(bf16[2,2,8,3072]{3,2,1,0:T(8,128)(2,1)S(1)} %get-tuple-element.30), channel_id=1, source_target_pairs={{0,16},{16,0},{1,17},{17,1},{2,18},{18,2},{3,19},{19,3},{4,20},{20... | collective-permute-start | bytes 589832 | tf_op jit(solution)/shard_map/ppermute | solution.py:44
  16.8 8.0 %collective-permute-start.2 = (bf16[2,2,8,3200]{3,2,1,0:T(8,128)(2,1)S(1)}, bf16[2,2,8,3200]{3,2,1,0:T(8,128)(2,1)S(1)}, u32[]{:S(2)}, u32[]{:S(2)}) collective-permute-start(bf16[2,2,8,3200]{3,2,1,0:T(8,128)(2,1)S(1)} %get-tuple-element.28), channel_id=1, source_target_pairs={{0,2},{1,3},{2,0},{3,1},{4,6},{5,7},{6,4},{7,5},{8,10},{9,11},{10,... | collective-permute-start | bytes 614408 | tf_op jit(solution)/shard_map/ppermute | solution.py:44
  19.4 11.6 %collective-permute-start.8 = (bf16[2,2,2,8,3072]{4,3,2,1,0:T(8,128)(2,1)S(1)}, bf16[2,2,2,8,3072]{4,3,2,1,0:T(8,128)(2,1)S(1)}, u32[]{:S(2)}, u32[]{:S(2)}) collective-permute-start(bf16[2,2,2,8,3072]{4,3,2,1,0:T(8,128)(2,1)S(1)} %get-tuple-element.26), channel_id=1, source_target_pairs={{0,2},{1,3},{2,0},{3,1},{4,6},{5,7},{6,4},{7,5},{8,10},{9,11},{10,... | collective-permute-start | bytes 1179656 | tf_op jit(solution)/shard_map/ppermute | solution.py:44
  24.9 8.0 %collective-permute-start.3 = (bf16[2,2,2,8,3200]{4,3,2,1,0:T(8,128)(2,1)S(1)}, bf16[2,2,2,8,3200]{4,3,2,1,0:T(8,128)(2,1)S(1)}, u32[]{:S(2)}, u32[]{:S(2)}) collective-permute-start(bf16[2,2,2,8,3200]{4,3,2,1,0:T(8,128)(2,1)S(1)} %get-tuple-element.24.refs_1_), channel_id=1, source_target_pairs={{0,16},{16,0},{1,17},{17,1},{2,18},{18,2},{3,19},{19,3},{4,20},{20... | collective-permute-start | bytes 1228808 | tf_op jit(solution)/shard_map/ppermute | solution.py:44
  31.1 2.4 %collective-permute-start.9 = (bf16[2,2,2,2,8,3072]{5,4,3,2,0,1:T(8,128)(2,1)S(1)}, bf16[2,2,2,2,8,3072]{5,4,3,2,0,1:T(8,128)(2,1)S(1)}, u32[]{:S(2)}, u32[]{:S(2)}) collective-permute-start(bf16[2,2,2,2,8,3072]{5,4,3,2,0,1:T(8,128)(2,1)S(1)} %pad_maximum_fusion.3), channel_id=1, source_target_pairs={{0,1},{1,0},{2,3},{3,2},{4,5},{5,4},{6,7},{7,6},{8,9},{9,8},{10,11... | collective-permute-start | bytes 2359304 | tf_op jit(solution)/shard_map/ppermute | solution.py:44
  33.0 5.4 %collective-permute-start.4 = (bf16[2,2,2,2,8,3200]{5,4,3,2,1,0:T(8,128)(2,1)S(1)}, bf16[2,2,2,2,8,3200]{5,4,3,2,1,0:T(8,128)(2,1)S(1)}, u32[]{:S(2)}, u32[]{:S(2)}) collective-permute-start(bf16[2,2,2,2,8,3200]{5,4,3,2,1,0:T(8,128)(2,1)S(1)} %get-tuple-element.22), channel_id=1, source_target_pairs={{0,1},{1,0},{2,3},{3,2},{4,5},{5,4},{6,7},{7,6},{8,9},{9,8},{10,11... | collective-permute-start | bytes 2457608 | tf_op jit(solution)/shard_map/ppermute | solution.py:44
  45.3 2.8 %collective-permute-start.10 = (bf16[2,2,2,2,8,3072]{5,4,3,2,1,0:T(8,128)(2,1)S(1)}, bf16[2,2,2,2,8,3072]{5,4,3,2,1,0:T(8,128)(2,1)S(1)}, u32[]{:S(2)}, u32[]{:S(2)}) collective-permute-start(bf16[2,2,2,2,8,3072]{5,4,3,2,1,0:T(8,128)(2,1)S(1)} %bitcast.100), channel_id=1, source_target_pairs={{0,1},{1,0},{2,3},{3,2},{4,5},{5,4},{6,7},{7,6},{8,9},{9,8},{10,11... | collective-permute-start | bytes 2359304 | tf_op jit(solution)/shard_map/ppermute | solution.py:44
  47.7 2.4 %collective-permute-start.15 = (bf16[2,2,2,2,8,3072]{5,4,3,2,0,1:T(8,128)(2,1)S(1)}, bf16[2,2,2,2,8,3072]{5,4,3,2,0,1:T(8,128)(2,1)S(1)}, u32[]{:S(2)}, u32[]{:S(2)}) collective-permute-start(bf16[2,2,2,2,8,3072]{5,4,3,2,0,1:T(8,128)(2,1)S(1)} %copy.16), channel_id=1, source_target_pairs={{0,1},{1,0},{2,3},{3,2},{4,5},{5,4},{6,7},{7,6},{8,9},{9,8},{10,11... | collective-permute-start | bytes 2359304 | tf_op jit(solution)/shard_map/ppermute | solution.py:44
  48.3 11.3 %collective-permute-start.11 = (bf16[2,2,2,8,3072]{4,3,2,1,0:T(8,128)(2,1)S(1)}, bf16[2,2,2,8,3072]{4,3,2,1,0:T(8,128)(2,1)S(1)}, u32[]{:S(2)}, u32[]{:S(2)}) collective-permute-start(bf16[2,2,2,8,3072]{4,3,2,1,0:T(8,128)(2,1)S(1)} %slice_bitcast_fusion.2), channel_id=1, source_target_pairs={{0,16},{16,0},{1,17},{17,1},{2,18},{18,2},{3,19},{19,3},{4,20},{20... | collective-permute-start | bytes 1179656 | tf_op jit(solution)/shard_map/ppermute | solution.py:44
  50.3 11.4 %collective-permute-start.16 = (bf16[2,2,2,8,3072]{4,3,2,1,0:T(8,128)(2,1)S(1)}, bf16[2,2,2,8,3072]{4,3,2,1,0:T(8,128)(2,1)S(1)}, u32[]{:S(2)}, u32[]{:S(2)}) collective-permute-start(bf16[2,2,2,8,3072]{4,3,2,1,0:T(8,128)(2,1)S(1)} %slice_bitcast_fusion), channel_id=1, source_target_pairs={{0,2},{1,3},{2,0},{3,1},{4,6},{5,7},{6,4},{7,5},{8,10},{9,11},{10,... | collective-permute-start | bytes 1179656 | tf_op jit(solution)/shard_map/ppermute | solution.py:44
  59.7 6.2 %collective-permute-start.12 = (bf16[2,2,8,3072]{3,2,1,0:T(8,128)(2,1)S(1)}, bf16[2,2,8,3072]{3,2,1,0:T(8,128)(2,1)S(1)}, u32[]{:S(2)}, u32[]{:S(2)}) collective-permute-start(bf16[2,2,8,3072]{3,2,1,0:T(8,128)(2,1)S(1)} %slice_bitcast_fusion.6), channel_id=1, source_target_pairs={{0,2},{1,3},{2,0},{3,1},{4,6},{5,7},{6,4},{7,5},{8,10},{9,11},{10,... | collective-permute-start | bytes 589832 | tf_op jit(solution)/shard_map/ppermute | solution.py:44
  61.8 6.4 %collective-permute-start.17 = (bf16[2,2,8,3072]{3,2,1,0:T(8,128)(2,1)S(1)}, bf16[2,2,8,3072]{3,2,1,0:T(8,128)(2,1)S(1)}, u32[]{:S(2)}, u32[]{:S(2)}) collective-permute-start(bf16[2,2,8,3072]{3,2,1,0:T(8,128)(2,1)S(1)} %slice_bitcast_fusion.4), channel_id=1, source_target_pairs={{0,16},{16,0},{1,17},{17,1},{2,18},{18,2},{3,19},{19,3},{4,20},{20... | collective-permute-start | bytes 589832 | tf_op jit(solution)/shard_map/ppermute | solution.py:44
  66.0 5.6 %collective-permute-start.13 = (bf16[2,8,3072]{2,1,0:T(8,128)(2,1)S(1)}, bf16[2,8,3072]{2,1,0:T(8,128)(2,1)S(1)}, u32[]{:S(2)}, u32[]{:S(2)}) collective-permute-start(bf16[2,8,3072]{2,1,0:T(8,128)(2,1)S(1)} %slice_bitcast_fusion.10), channel_id=1, source_target_pairs={{0,4},{4,0},{8,12},{12,8},{1,5},{5,1},{9,13},{13,9},{2,6},{6,2},{1... | collective-permute-start | bytes 294920 | tf_op jit(solution)/shard_map/ppermute | solution.py:44
  68.3 5.2 %collective-permute-start.18 = (bf16[2,8,3072]{2,1,0:T(8,128)(2,1)S(1)}, bf16[2,8,3072]{2,1,0:T(8,128)(2,1)S(1)}, u32[]{:S(2)}, u32[]{:S(2)}) collective-permute-start(bf16[2,8,3072]{2,1,0:T(8,128)(2,1)S(1)} %slice_bitcast_fusion.8), channel_id=1, source_target_pairs={{0,4},{4,0},{8,12},{12,8},{1,5},{5,1},{9,13},{13,9},{2,6},{6,2},{1... | collective-permute-start | bytes 294920 | tf_op jit(solution)/shard_map/ppermute | solution.py:44
  71.7 5.6 %collective-permute-start.14 = (bf16[8,3072]{1,0:T(8,128)(2,1)S(1)}, bf16[8,3072]{1,0:T(8,128)(2,1)S(1)}, u32[]{:S(2)}, u32[]{:S(2)}) collective-permute-start(bf16[8,3072]{1,0:T(8,128)(2,1)S(1)} %slice_bitcast_fusion.14), channel_id=1, source_target_pairs={{0,8},{4,12},{8,0},{12,4},{1,9},{5,13},{9,1},{13,5},{2,10},{6,14},... | collective-permute-start | bytes 147464 | tf_op jit(solution)/shard_map/ppermute | solution.py:44
  73.5 5.1 %collective-permute-start.19 = (bf16[8,3072]{1,0:T(8,128)(2,1)S(1)}, bf16[8,3072]{1,0:T(8,128)(2,1)S(1)}, u32[]{:S(2)}, u32[]{:S(2)}) collective-permute-start(bf16[8,3072]{1,0:T(8,128)(2,1)S(1)} %slice_bitcast_fusion.12), channel_id=1, source_target_pairs={{0,8},{4,12},{8,0},{12,4},{1,9},{5,13},{9,1},{13,5},{2,10},{6,14},... | collective-permute-start | bytes 147464 | tf_op jit(solution)/shard_map/ppermute | solution.py:44

commit v10 on v9

--- a/solution.py
+++ b/solution.py
@@ -15,20 +15,53 @@
 DOWN_LIMIT = 8 * 2**20
 
 
-def slot_coefficients(expert_ids, gate_values, old_place, new_place):
-    matches = (new_place[:, None] == old_place[None, :]).astype(jnp.float32)
-    picks = (expert_ids[:, :, None] == jnp.arange(new_place.shape[0], dtype=jnp.int32)).astype(jnp.float32)
-    by_expert = jnp.sum(picks * gate_values[:, :, None], axis=1)
-    return jnp.sum(by_expert[:, :, None] * matches[None, :, :], axis=1)
-
-
-def split_exact(value):
-    pieces = []
-    for _ in range(3):
-        piece = lax.reduce_precision(value, exponent_bits=8, mantissa_bits=7)
-        pieces.append(piece.astype(jnp.bfloat16))
-        value = value - piece
-    return pieces
+def pack_kernel(tokens_ref, ids_ref, gates_ref, old_ref, new_ref, out_ref):
+    rows, width = tokens_ref.shape
+    choices = ids_ref.shape[0]
+    out_ref[:, :width] = tokens_ref[...]
+    square = (rows, rows)
+    diagonal = lax.broadcasted_iota(jnp.int32, square, 0) == lax.broadcasted_iota(
+        jnp.int32, square, 1
+    )
+    lane = lax.broadcasted_iota(jnp.int32, (rows, out_ref.shape[1] - width), 1)
+    extra = jnp.zeros(lane.shape, jnp.float32)
+    old = old_ref[...]
+    index = lax.broadcasted_iota(jnp.int32, old.shape, 1).astype(jnp.float32)
+    for choice in range(choices):
+        ids = ids_ref[choice : choice + 1, :]
+        slot = jnp.zeros(ids.shape, jnp.float32)
+        for expert in range(old_ref.shape[1]):
+            place = new_ref[:, expert : expert + 1]
+            of_expert = jnp.sum(jnp.where(old == place, index, 0.0), axis=1, keepdims=True)
+            slot = jnp.where(ids == expert, of_expert, slot)
+        left = gates_ref[choice : choice + 1, :]
+        values = [slot]
+        for _ in range(3):
+            values.append(left.astype(jnp.bfloat16).astype(jnp.float32))
+            left = left - values[-1]
+        for place, value in enumerate(values):
+            column = jnp.sum(jnp.where(diagonal, value, 0.0), axis=1, keepdims=True)
+            extra = jnp.where(lane == place * choices + choice, column, extra)
+    out_ref[:, width:] = extra.astype(out_ref.dtype)
+
+
+def packed(tokens, width, expert_ids, gate_values, old_place, new_place):
+    rows, choices = expert_ids.shape
+    experts = old_place.shape[0]
+    lanes = -(-4 * choices // LANES) * LANES
+    small = pl.BlockSpec((choices, rows), lambda i: (0, 0))
+    place = pl.BlockSpec((1, experts), lambda i: (0, 0))
+    operands = (tokens, expert_ids.T, gate_values.T, old_place[None, :], new_place[None, :])
+    return pl.pallas_call(
+        pack_kernel,
+        grid=(1,),
+        in_specs=[pl.BlockSpec((rows, width), lambda i: (0, 0)), small, small, place, place],
+        out_specs=pl.BlockSpec((rows, width + lanes), lambda i: (0, 0)),
+        out_shape=jax.ShapeDtypeStruct((rows, width + lanes), tokens.dtype),
+        cost_estimate=pl.CostEstimate(
+            flops=0, bytes_accessed=4 * rows * width, transcendentals=0
+        ),
+    )(*(in_hbm(operand) for operand in operands))
 
 
 class Digit:
@@ -96,7 +129,8 @@
     )(in_hbm(weight), after)
 
 
-def gate_up_kernel(last, take, pieces, row_ref, *refs):
+def gate_up_kernel(choices, take, pieces, row_ref, *refs):
+    last = choices > 0
     if last:
         sum_ref, refs = refs[0], refs[1:]
     w_refs, (next_hbm, out_ref, next_ref, sem) = refs[:pieces], refs[pieces:]
@@ -111,6 +145,11 @@
     if last:
         extra = row_ref[:, half:].astype(jnp.float32)
         lane = lax.broadcasted_iota(jnp.int32, extra.shape, 1)
+        chosen, gates = [], []
+        for choice in range(choices):
+            mine = (lane >= choices) & (lane < 4 * choices) & (lane % choices == choice)
+            chosen.append(jnp.sum(jnp.where(lane == choice, extra, 0.0), axis=1, keepdims=True))
+            gates.append(jnp.sum(jnp.where(mine, extra, 0.0), axis=1, keepdims=True))
     for first in range(0, experts, group):
         columns = slice(first * units, (first + group) * units)
         w_ref, at_slot = w_refs[first // held], first % held
@@ -131,23 +170,25 @@
         for slot in range(first, first + group):
             at = (slot - first) * units
             gate, up = pre[:, at : at + sliver], pre[:, at + sliver : at + units]
-            mine = (lane == slot) | (lane == slot + experts) | (lane == slot + 2 * experts)
-            weigh = jnp.sum(jnp.where(mine, extra, 0.0), axis=1, keepdims=True)
+            weigh = sum(
+                jnp.where(choice == slot, gate_value, 0.0)
+                for choice, gate_value in zip(chosen, gates)
+            )
             hidden = (0.5 * gate) * (1.0 + jnp.tanh(0.5 * gate)) * up * weigh
             out_ref[slot] = hidden.astype(out_ref.dtype)
     pl.when(pl.program_id(0) == 0)(copy.wait)
 
 
-def gate_up_of(row_part, sums, weights, next_weight, take, next_shape):
+def gate_up_of(row_part, others, weights, next_weight, take, next_shape, choices=0):
     held, _, sliver, half = weights[0].shape
     pieces = len(weights)
     experts = held * pieces
     rows = row_part.shape[0]
     row_block = min(ROW_BLOCK, rows)
     whole = rows == row_block
-    last = sums is not None
+    last = choices > 0
     units = experts * 2 * sliver
-    operands = [row_part, sums] if last else [row_part]
+    operands = [row_part] + others
     if whole:
         specs = [pl.BlockSpec(memory_space=pltpu.VMEM)] * len(operands)
         operands = [resident(operand) for operand in operands]
@@ -166,7 +207,7 @@
         out_shape = pltpu.VMEM(out_shape.shape, out_shape.dtype)
 
     def kernel(*refs):
-        gate_up_kernel(last, take, pieces, *refs)
+        gate_up_kernel(choices, take, pieces, *refs)
 
     return pl.pallas_call(
         kernel,
@@ -244,13 +285,8 @@
     dim_order = core_digits + x_digits[::-1] + y_digits[::-1] + z_digits[::-1]
     routes = [z_digits + y_digits + x_digits, z_digits + x_digits + y_digits]
 
-    coefficients = slot_coefficients(expert_ids, gate_values, old_place, new_place)
-    extra = jnp.concatenate(split_exact(coefficients), axis=1)
-    extra = jnp.pad(extra, ((0, 0), (0, -extra.shape[1] % LANES)))
-    parts = [
-        jnp.concatenate([tokens[:, :half], extra], axis=1),
-        tokens[:, half:],
-    ]
+    choices = expert_ids.shape[1]
+    parts = [packed(tokens, half, expert_ids, gate_values, old_place, new_place), tokens[:, half:]]
     half_shape = gate_up_weight.shape[:3] + (half,)
 
     def take_second(ref):
@@ -274,10 +310,16 @@
             held[number].append(digit)
     gathered = [block.reshape(-1, part.shape[1]) for block, part in zip(blocks, parts)]
     sums, next_weights = gate_up_of(
-        gathered[1], None, [first_weights], gate_up_weight, take_first, half_shape
+        gathered[1], [], [first_weights], gate_up_weight, take_first, half_shape
     )
     hidden, down_weight = gate_up_of(
-        gathered[0], sums, [next_weights], down_weight, lambda ref: ref, down_weight.shape
+        gathered[0],
+        [sums],
+        [next_weights],
+        down_weight,
+        lambda ref: ref,
+        down_weight.shape,
+        choices,
     )
     down_weight = resident(down_weight)
     results = []

time: 79.6 us -> 80.5 us (1.011)
  Pallas kernels: 17.8 us -> 19.5 us
  waiting for transfers between devices: 29.3 us -> 30.7 us
  starting transfers between devices: 26.6 us -> 25.5 us
  other arithmetic: 3.74 us -> 2.91 us
    pallas_call x0 -> x1, Pallas kernels: none -> 1.69 us  [packed(): pl.pallas_call(pack_kernel, grid=(1,), in_specs=[pl.BlockSpec((rows, widt...]
    ppermute x20, waiting for transfers between devices: 29.3 us -> 30.7 us  [shift(): return lax.ppermute(value, self.name, pairs)]
    ppermute x20, starting transfers between devices: 26.6 us -> 25.5 us  [shift(): return lax.ppermute(value, self.name, pairs)]
  transfers between devices with their start and end apart: 20 -> 20, of which waited for: 16 -> 16; matrix products, arithmetic and copies ran while one was open for 4% -> 3% of each run, Pallas kernels for 14% -> 16%
where the time goes in v10:
time: 80.5 us; the launch traced here: 80.1 us
  waiting for transfers between devices  30.7 us (38%)
  starting transfers between devices  25.5 us (32%)
  Pallas kernels  19.5 us (24%)
  other arithmetic  2.91 us (4%)
  local copies, waits for them, and re-layouts  1.31 us (2%)
    ppermute x20, waiting for transfers between devices, shift(): return lax.ppermute(value, self.name, pairs)  30.7 us
    ppermute x20, starting transfers between devices, shift(): return lax.ppermute(value, self.name, pairs)  25.5 us
    pallas_call x2, Pallas kernels, gate_up_of(): pl.pallas_call(kernel, grid=(rows // row_block,), in_specs=specs + [pl.Bl...  9.27 us
    pallas_call x1, Pallas kernels, fetched(): pl.pallas_call(kernel, in_specs=[pl.BlockSpec(memory_space=pl.ANY)] * 2,...  4.58 us
    pallas_call x2, Pallas kernels, down_of(): pl.pallas_call(kernel, grid=(rows // row_block,), in_specs=[pl.BlockSpec(...  3.98 us
    pallas_call x1, Pallas kernels, packed(): pl.pallas_call(pack_kernel, grid=(1,), in_specs=[pl.BlockSpec((rows, widt...  1.69 us
  transfers between devices with their start and end apart: 20, of which 16 were waited for; matrix products, arithmetic and copies ran while one was open for 3% of the time, Pallas kernels for 16%

profile of v10, /device:TPU:0, one launch (start us, length us, event | category | flops | bytes accessed | tf_op | source)
XLA Modules:
  0.0 80.1 jit_solution(16953613338250716541)
XLA Ops:
  0.0 0.8 %slice_bitcast_fusion.16 = (bf16[1,8,3072]{2,1,0:T(8,128)(2,1)S(1)}, bf16[8,3072]{1,0:T(8,128)(2,1)S(1)}) fusion(bf16[8,6144]{1,0:T(8,128)(2,1)} %tokens_ref.1), kind=kLoop, calls=%fused_computation.47 | loop fusion | bytes 147456 | tf_op jit(solution)/shard_map/stack | solution.py:80
  0.8 4.0 %collective-permute-start.5 = (bf16[8,3072]{1,0:T(8,128)(2,1)S(1)}, bf16[8,3072]{1,0:T(8,128)(2,1)S(1)}, u32[]{:S(2)}, u32[]{:S(2)}) collective-permute-start(bf16[8,3072]{1,0:T(8,128)(2,1)S(1)} %get-tuple-element.36), channel_id=1, source_target_pairs={{0,8},{4,12},{8,0},{12,4},{1,9},{5,13},{9,1},{13,5},{2,10},{6,14},... | collective-permute-start | bytes 147464 | tf_op jit(solution)/shard_map/ppermute | solution.py:77
  4.8 1.7 %shard_map.73 = bf16[8,3200]{1,0:T(8,128)(2,1)} custom-call(bf16[8,6144]{1,0:T(8,128)(2,1)} %tokens_ref.1, s32[2,8]{1,0:T(2,128)} %bitcast.114, f32[2,8]{1,0:T(2,128)} %bitcast.115, s32[1,4]{1,0:T(1,128)} %bitcast.116, s32[1,4]{1,0:T(1,128)} %bitcast.117), custom_call_target="tpu_custom_call" | custom-call | bytes 98304 | tf_op jit(solution)/shard_map/pallas_call | solution.py:55
  6.5 0.9 %collective-permute-done.5 = bf16[8,3072]{1,0:T(8,128)(2,1)S(1)} collective-permute-done((bf16[8,3072]{1,0:T(8,128)(2,1)S(1)}, bf16[8,3072]{1,0:T(8,128)(2,1)S(1)}, u32[]{:S(2)}, u32[]{:S(2)}) %collective-permute-start.5) | collective-permute-done | bytes 49184 | tf_op jit(solution)/shard_map/ppermute | solution.py:77
  7.5 1.7 %collective-permute-start.6 = (bf16[2,8,3072]{2,1,0:T(8,128)(2,1)S(1)}, bf16[2,8,3072]{2,1,0:T(8,128)(2,1)S(1)}, u32[]{:S(2)}, u32[]{:S(2)}) collective-permute-start(bf16[2,8,3072]{2,1,0:T(8,128)(2,1)S(1)} %get-tuple-element.34), channel_id=1, source_target_pairs={{0,4},{4,0},{8,12},{12,8},{1,5},{5,1},{9,13},{13,9},{2,6},{6,2},{1... | collective-permute-start | bytes 294920 | tf_op jit(solution)/shard_map/ppermute | solution.py:77
  9.2 2.8 %collective-permute-done = bf16[8,3200]{1,0:T(8,128)(2,1)S(1)} collective-permute-done((bf16[8,3200]{1,0:T(8,128)(2,1)}, bf16[8,3200]{1,0:T(8,128)(2,1)S(1)}, u32[]{:S(2)}, u32[]{:S(2)}) %collective-permute-start) | collective-permute-done | bytes 51232 | tf_op jit(solution)/shard_map/ppermute | solution.py:77
  12.0 0.8 %fusion.11 = (bf16[1,2,8,3200]{3,2,1,0:T(8,128)(2,1)S(1)}, bf16[2,8,3200]{2,1,0:T(8,128)(2,1)S(1)}) fusion(bf16[1,8,3200]{2,1,0:T(8,128)(2,1)S(1)} %bitcast.112, bf16[1,8,3200]{2,1,0:T(8,128)(2,1)} %bitcast.108), kind=kLoop, calls=%fused_computation.49 | loop fusion | flops 51200 | bytes 307200 | tf_op jit(solution)/shard_map/stack | solution.py:80
  12.8 1.6 %collective-permute-start.1 = (bf16[2,8,3200]{2,1,0:T(8,128)(2,1)S(1)}, bf16[2,8,3200]{2,1,0:T(8,128)(2,1)S(1)}, u32[]{:S(2)}, u32[]{:S(2)}) collective-permute-start(bf16[2,8,3200]{2,1,0:T(8,128)(2,1)S(1)} %get-tuple-element.32), channel_id=1, source_target_pairs={{0,4},{4,0},{8,12},{12,8},{1,5},{5,1},{9,13},{13,9},{2,6},{6,2},{1... | collective-permute-start | bytes 307208 | tf_op jit(solution)/shard_map/ppermute | solution.py:77
  14.4 1.6 %collective-permute-start.7 = (bf16[2,2,8,3072]{3,2,1,0:T(8,128)(2,1)S(1)}, bf16[2,2,8,3072]{3,2,1,0:T(8,128)(2,1)S(1)}, u32[]{:S(2)}, u32[]{:S(2)}) collective-permute-start(bf16[2,2,8,3072]{3,2,1,0:T(8,128)(2,1)S(1)} %get-tuple-element.30), channel_id=1, source_target_pairs={{0,16},{16,0},{1,17},{17,1},{2,18},{18,2},{3,19},{19,3},{4,20},{20... | collective-permute-start | bytes 589832 | tf_op jit(solution)/shard_map/ppermute | solution.py:77
  16.0 1.6 %collective-permute-done.1 = bf16[2,8,3200]{2,1,0:T(8,128)(2,1)S(1)} collective-permute-done((bf16[2,8,3200]{2,1,0:T(8,128)(2,1)S(1)}, bf16[2,8,3200]{2,1,0:T(8,128)(2,1)S(1)}, u32[]{:S(2)}, u32[]{:S(2)}) %collective-permute-start.1) | collective-permute-done | bytes 102432 | tf_op jit(solution)/shard_map/ppermute | solution.py:77
  17.6 1.6 %collective-permute-start.2 = (bf16[2,2,8,3200]{3,2,1,0:T(8,128)(2,1)S(1)}, bf16[2,2,8,3200]{3,2,1,0:T(8,128)(2,1)S(1)}, u32[]{:S(2)}, u32[]{:S(2)}) collective-permute-start(bf16[2,2,8,3200]{3,2,1,0:T(8,128)(2,1)S(1)} %get-tuple-element.28), channel_id=1, source_target_pairs={{0,2},{1,3},{2,0},{3,1},{4,6},{5,7},{6,4},{7,5},{8,10},{9,11},{10,... | collective-permute-start | bytes 614408 | tf_op jit(solution)/shard_map/ppermute | solution.py:77
  19.2 1.0 %collective-permute-done.7 = bf16[2,2,8,3072]{3,2,1,0:T(8,128)(2,1)S(1)} collective-permute-done((bf16[2,2,8,3072]{3,2,1,0:T(8,128)(2,1)S(1)}, bf16[2,2,8,3072]{3,2,1,0:T(8,128)(2,1)S(1)}, u32[]{:S(2)}, u32[]{:S(2)}) %collective-permute-start.7) | collective-permute-done | bytes 196640 | tf_op jit(solution)/shard_map/ppermute | solution.py:77
  20.2 1.6 %collective-permute-start.8 = (bf16[2,2,2,8,3072]{4,3,2,1,0:T(8,128)(2,1)S(1)}, bf16[2,2,2,8,3072]{4,3,2,1,0:T(8,128)(2,1)S(1)}, u32[]{:S(2)}, u32[]{:S(2)}) collective-permute-start(bf16[2,2,2,8,3072]{4,3,2,1,0:T(8,128)(2,1)S(1)} %get-tuple-element.26), channel_id=1, source_target_pairs={{0,2},{1,3},{2,0},{3,1},{4,6},{5,7},{6,4},{7,5},{8,10},{9,11},{10,... | collective-permute-start | bytes 1179656 | tf_op jit(solution)/shard_map/ppermute | solution.py:77
  21.8 3.8 %collective-permute-done.2 = bf16[2,2,8,3200]{3,2,1,0:T(8,128)(2,1)S(1)} collective-permute-done((bf16[2,2,8,3200]{3,2,1,0:T(8,128)(2,1)S(1)}, bf16[2,2,8,3200]{3,2,1,0:T(8,128)(2,1)S(1)}, u32[]{:S(2)}, u32[]{:S(2)}) %collective-permute-start.2) | collective-permute-done | bytes 204832 | tf_op jit(solution)/shard_map/ppermute | solution.py:77
  25.7 1.6 %collective-permute-start.3 = (bf16[2,2,2,8,3200]{4,3,2,1,0:T(8,128)(2,1)S(1)}, bf16[2,2,2,8,3200]{4,3,2,1,0:T(8,128)(2,1)S(1)}, u32[]{:S(2)}, u32[]{:S(2)}) collective-permute-start(bf16[2,2,2,8,3200]{4,3,2,1,0:T(8,128)(2,1)S(1)} %get-tuple-element.24.refs_1_), channel_id=1, source_target_pairs={{0,16},{16,0},{1,17},{17,1},{2,18},{18,2},{3,19},{19,3},{4,20},{20... | collective-permute-start | bytes 1228808 | tf_op jit(solution)/shard_map/ppermute | solution.py:77
  27.3 4.6 %shard_map.74.refs_1_ = bf16[4,2,256,3072]{3,2,1,0:T(8,128)(2,1)S(1)} custom-call(bf16[4,2,256,6144]{3,2,1,0:T(8,128)(2,1)} %refs_2_.1, bf16[2,2,2,8,3200]{4,3,2,1,0:T(8,128)(2,1)S(1)} %get-tuple-element.24.refs_1_), custom_call_target="tpu_custom_call" | custom-call | bytes 25165824 | tf_op jit(solution)/shard_map/pallas_call | solution.py:119
  32.0 1.7 %collective-permute-done.3 = bf16[2,2,2,8,3200]{4,3,2,1,0:T(8,128)(2,1)S(1)} collective-permute-done((bf16[2,2,2,8,3200]{4,3,2,1,0:T(8,128)(2,1)S(1)}, bf16[2,2,2,8,3200]{4,3,2,1,0:T(8,128)(2,1)S(1)}, u32[]{:S(2)}, u32[]{:S(2)}) %collective-permute-start.3) | collective-permute-done | bytes 409632 | tf_op jit(solution)/shard_map/ppermute | solution.py:77
  33.7 0.1 fusion.16
  33.9 0.4 collective-permute-done.9
  34.3 0.1 pad_maximum_fusion.1
  34.4 0.1 copy.8
  34.6 4.7 %shard_map.75 = (f32[256,2048]{1,0:T(8,128)S(1)}, bf16[4,2,256,3072]{3,2,1,0:T(8,128)(2,1)S(1)}) custom-call(bf16[256,3072]{1,0:T(8,128)(2,1)S(1)} %bitcast.97, bf16[4,2,256,3072]{3,2,1,0:T(8,128)(2,1)S(1)} %shard_map.74.refs_1_, bf16[4,2,256,6144]{3,2,1,0:T(8,128)(2,1)} %refs_2_.1), custom_call_target="tpu_custom_call" | custom-call | flops 3221225472 | bytes 14680064 | tf_op jit(solution)/shard_map/pallas_call | solution.py:212
  39.3 0.2 pad_maximum_fusion
  39.5 4.6 %shard_map.76 = (bf16[4,256,256]{2,1,0:T(8,128)(2,1)S(1)}, bf16[4,256,6144]{2,1,0:T(8,128)(2,1)S(1)}) custom-call(bf16[256,3200]{1,0:T(8,128)(2,1)S(1)} %bitcast.96, f32[256,2048]{1,0:T(8,128)S(1)} %get-tuple-element.13.refs_1_, bf16[4,2,256,3072]{3,2,1,0:T(8,128)(2,1)S(1)} %get-tuple-element.14.refs_2_, bf16[4,256,6144]{2,1,0:T(8,128)(2,1)} %refs_3_.1), custom_call_target="tpu_custom_call" | custom-call | flops 3221225472 | bytes 14680064 | tf_op jit(solution)/shard_map/pallas_call | solution.py:212
  44.1 2.0 %shard_map.77 = bf16[256,3072]{1,0:T(8,128)(2,1)S(1)} custom-call(bf16[4,256,256]{2,1,0:T(8,128)(2,1)S(1)} %get-tuple-element.15.refs_0_, bf16[4,256,6144]{2,1,0:T(8,128)(2,1)S(1)} %get-tuple-element.16.refs_1_), custom_call_target="tpu_custom_call" | custom-call | flops 1610612736 | bytes 8388608 | tf_op jit(solution)/shard_map/pallas_call | solution.py:255
  46.2 0.2 collective-permute-start.10
  46.4 2.0 %shard_map.78 = bf16[256,3072]{1,0:T(8,128)(2,1)S(1)} custom-call(bf16[4,256,256]{2,1,0:T(8,128)(2,1)S(1)} %get-tuple-element.15.refs_0_, bf16[4,256,6144]{2,1,0:T(8,128)(2,1)S(1)} %get-tuple-element.16.refs_1_), custom_call_target="tpu_custom_call" | custom-call | flops 1610612736 | bytes 8388608 | tf_op jit(solution)/shard_map/pallas_call | solution.py:255
  48.5 0.4 collective-permute-start.15
  49.0 0.2 fusion
  49.2 1.2 %collective-permute-start.11 = (bf16[2,2,2,8,3072]{4,3,2,1,0:T(8,128)(2,1)S(1)}, bf16[2,2,2,8,3072]{4,3,2,1,0:T(8,128)(2,1)S(1)}, u32[]{:S(2)}, u32[]{:S(2)}) collective-permute-start(bf16[2,2,2,8,3072]{4,3,2,1,0:T(8,128)(2,1)S(1)} %slice_bitcast_fusion.2), channel_id=1, source_target_pairs={{0,16},{16,0},{1,17},{17,1},{2,18},{18,2},{3,19},{19,3},{4,20},{20... | collective-permute-start | bytes 1179656 | tf_op jit(solution)/shard_map/ppermute | solution.py:77
  50.4 0.5 collective-permute-done.15
  50.9 0.2 fusion.1
  51.1 1.6 %collective-permute-start.16 = (bf16[2,2,2,8,3072]{4,3,2,1,0:T(8,128)(2,1)S(1)}, bf16[2,2,2,8,3072]{4,3,2,1,0:T(8,128)(2,1)S(1)}, u32[]{:S(2)}, u32[]{:S(2)}) collective-permute-start(bf16[2,2,2,8,3072]{4,3,2,1,0:T(8,128)(2,1)S(1)} %slice_bitcast_fusion), channel_id=1, source_target_pairs={{0,2},{1,3},{2,0},{3,1},{4,6},{5,7},{6,4},{7,5},{8,10},{9,11},{10,... | collective-permute-start | bytes 1179656 | tf_op jit(solution)/shard_map/ppermute | solution.py:77
  52.7 7.7 %collective-permute-done.11 = bf16[2,2,2,8,3072]{4,3,2,1,0:T(8,128)(2,1)S(1)} collective-permute-done((bf16[2,2,2,8,3072]{4,3,2,1,0:T(8,128)(2,1)S(1)}, bf16[2,2,2,8,3072]{4,3,2,1,0:T(8,128)(2,1)S(1)}, u32[]{:S(2)}, u32[]{:S(2)}) %collective-permute-start.11) | collective-permute-done | bytes 393248 | tf_op jit(solution)/shard_map/ppermute | solution.py:77
  60.6 1.6 %collective-permute-start.12 = (bf16[2,2,8,3072]{3,2,1,0:T(8,128)(2,1)S(1)}, bf16[2,2,8,3072]{3,2,1,0:T(8,128)(2,1)S(1)}, u32[]{:S(2)}, u32[]{:S(2)}) collective-permute-start(bf16[2,2,8,3072]{3,2,1,0:T(8,128)(2,1)S(1)} %slice_bitcast_fusion.6), channel_id=1, source_target_pairs={{0,2},{1,3},{2,0},{3,1},{4,6},{5,7},{6,4},{7,5},{8,10},{9,11},{10,... | collective-permute-start | bytes 589832 | tf_op jit(solution)/shard_map/ppermute | solution.py:77
  62.1 0.4 collective-permute-done.16
  62.7 1.3 %collective-permute-start.17 = (bf16[2,2,8,3072]{3,2,1,0:T(8,128)(2,1)S(1)}, bf16[2,2,8,3072]{3,2,1,0:T(8,128)(2,1)S(1)}, u32[]{:S(2)}, u32[]{:S(2)}) collective-permute-start(bf16[2,2,8,3072]{3,2,1,0:T(8,128)(2,1)S(1)} %slice_bitcast_fusion.4), channel_id=1, source_target_pairs={{0,16},{16,0},{1,17},{17,1},{2,18},{18,2},{3,19},{19,3},{4,20},{20... | collective-permute-start | bytes 589832 | tf_op jit(solution)/shard_map/ppermute | solution.py:77
  64.0 2.8 %collective-permute-done.12 = bf16[2,2,8,3072]{3,2,1,0:T(8,128)(2,1)S(1)} collective-permute-done((bf16[2,2,8,3072]{3,2,1,0:T(8,128)(2,1)S(1)}, bf16[2,2,8,3072]{3,2,1,0:T(8,128)(2,1)S(1)}, u32[]{:S(2)}, u32[]{:S(2)}) %collective-permute-start.12) | collective-permute-done | bytes 196640 | tf_op jit(solution)/shard_map/ppermute | solution.py:77
  66.9 1.6 %collective-permute-start.13 = (bf16[2,8,3072]{2,1,0:T(8,128)(2,1)S(1)}, bf16[2,8,3072]{2,1,0:T(8,128)(2,1)S(1)}, u32[]{:S(2)}, u32[]{:S(2)}) collective-permute-start(bf16[2,8,3072]{2,1,0:T(8,128)(2,1)S(1)} %slice_bitcast_fusion.10), channel_id=1, source_target_pairs={{0,4},{4,0},{8,12},{12,8},{1,5},{5,1},{9,13},{13,9},{2,6},{6,2},{1... | collective-permute-start | bytes 294920 | tf_op jit(solution)/shard_map/ppermute | solution.py:77
  68.5 0.7 collective-permute-done.17
  69.2 1.6 %collective-permute-start.18 = (bf16[2,8,3072]{2,1,0:T(8,128)(2,1)S(1)}, bf16[2,8,3072]{2,1,0:T(8,128)(2,1)S(1)}, u32[]{:S(2)}, u32[]{:S(2)}) collective-permute-start(bf16[2,8,3072]{2,1,0:T(8,128)(2,1)S(1)} %slice_bitcast_fusion.8), channel_id=1, source_target_pairs={{0,4},{4,0},{8,12},{12,8},{1,5},{5,1},{9,13},{13,9},{2,6},{6,2},{1... | collective-permute-start | bytes 294920 | tf_op jit(solution)/shard_map/ppermute | solution.py:77
  70.8 1.8 %collective-permute-done.13 = bf16[2,8,3072]{2,1,0:T(8,128)(2,1)S(1)} collective-permute-done((bf16[2,8,3072]{2,1,0:T(8,128)(2,1)S(1)}, bf16[2,8,3072]{2,1,0:T(8,128)(2,1)S(1)}, u32[]{:S(2)}, u32[]{:S(2)}) %collective-permute-start.13) | collective-permute-done | bytes 98336 | tf_op jit(solution)/shard_map/ppermute | solution.py:77
  72.6 0.8 collective-permute-start.14
  73.4 1.0 %collective-permute-done.18 = bf16[2,8,3072]{2,1,0:T(8,128)(2,1)S(1)} collective-permute-done((bf16[2,8,3072]{2,1,0:T(8,128)(2,1)S(1)}, bf16[2,8,3072]{2,1,0:T(8,128)(2,1)S(1)}, u32[]{:S(2)}, u32[]{:S(2)}) %collective-permute-start.18) | collective-permute-done | bytes 98336 | tf_op jit(solution)/shard_map/ppermute | solution.py:77
  74.4 1.3 %collective-permute-start.19 = (bf16[8,3072]{1,0:T(8,128)(2,1)S(1)}, bf16[8,3072]{1,0:T(8,128)(2,1)S(1)}, u32[]{:S(2)}, u32[]{:S(2)}) collective-permute-start(bf16[8,3072]{1,0:T(8,128)(2,1)S(1)} %slice_bitcast_fusion.12), channel_id=1, source_target_pairs={{0,8},{4,12},{8,0},{12,4},{1,9},{5,13},{9,1},{13,5},{2,10},{6,14},... | collective-permute-start | bytes 147464 | tf_op jit(solution)/shard_map/ppermute | solution.py:77
  75.7 3.0 %collective-permute-done.14 = bf16[8,3072]{1,0:T(8,128)(2,1)S(1)} collective-permute-done((bf16[8,3072]{1,0:T(8,128)(2,1)S(1)}, bf16[8,3072]{1,0:T(8,128)(2,1)S(1)}, u32[]{:S(2)}, u32[]{:S(2)}) %collective-permute-start.14) | collective-permute-done | bytes 49184 | tf_op jit(solution)/shard_map/ppermute | solution.py:77
  78.7 0.7 collective-permute-done.19
  79.5 0.6 pad_maximum_fusion.10
  (32 shorter events, 1.2 us)
Async XLA Ops:
  0.8 6.6 %collective-permute-start.5 = (bf16[8,3072]{1,0:T(8,128)(2,1)S(1)}, bf16[8,3072]{1,0:T(8,128)(2,1)S(1)}, u32[]{:S(2)}, u32[]{:S(2)}) collective-permute-start(bf16[8,3072]{1,0:T(8,128)(2,1)S(1)} %get-tuple-element.36), channel_id=1, source_target_pairs={{0,8},{4,12},{8,0},{12,4},{1,9},{5,13},{9,1},{13,5},{2,10},{6,14},... | collective-permute-start | bytes 147464 | tf_op jit(solution)/shard_map/ppermute | solution.py:77
  6.5 5.5 %collective-permute-start = (bf16[8,3200]{1,0:T(8,128)(2,1)}, bf16[8,3200]{1,0:T(8,128)(2,1)S(1)}, u32[]{:S(2)}, u32[]{:S(2)}) collective-permute-start(bf16[8,3200]{1,0:T(8,128)(2,1)} %shard_map.73), channel_id=1, source_target_pairs={{0,8},{4,12},{8,0},{12,4},{1,9},{5,13},{9,1},{13,5},{2,10},{6,14},... | collective-permute-start | bytes 153608 | tf_op jit(solution)/shard_map/ppermute | solution.py:77
  7.5 7.0 %collective-permute-start.6 = (bf16[2,8,3072]{2,1,0:T(8,128)(2,1)S(1)}, bf16[2,8,3072]{2,1,0:T(8,128)(2,1)S(1)}, u32[]{:S(2)}, u32[]{:S(2)}) collective-permute-start(bf16[2,8,3072]{2,1,0:T(8,128)(2,1)S(1)} %get-tuple-element.34), channel_id=1, source_target_pairs={{0,4},{4,0},{8,12},{12,8},{1,5},{5,1},{9,13},{13,9},{2,6},{6,2},{1... | collective-permute-start | bytes 294920 | tf_op jit(solution)/shard_map/ppermute | solution.py:77
  12.8 4.7 %collective-permute-start.1 = (bf16[2,8,3200]{2,1,0:T(8,128)(2,1)S(1)}, bf16[2,8,3200]{2,1,0:T(8,128)(2,1)S(1)}, u32[]{:S(2)}, u32[]{:S(2)}) collective-permute-start(bf16[2,8,3200]{2,1,0:T(8,128)(2,1)S(1)} %get-tuple-element.32), channel_id=1, source_target_pairs={{0,4},{4,0},{8,12},{12,8},{1,5},{5,1},{9,13},{13,9},{2,6},{6,2},{1... | collective-permute-start | bytes 307208 | tf_op jit(solution)/shard_map/ppermute | solution.py:77
  14.4 5.7 %collective-permute-start.7 = (bf16[2,2,8,3072]{3,2,1,0:T(8,128)(2,1)S(1)}, bf16[2,2,8,3072]{3,2,1,0:T(8,128)(2,1)S(1)}, u32[]{:S(2)}, u32[]{:S(2)}) collective-permute-start(bf16[2,2,8,3072]{3,2,1,0:T(8,128)(2,1)S(1)} %get-tuple-element.30), channel_id=1, source_target_pairs={{0,16},{16,0},{1,17},{17,1},{2,18},{18,2},{3,19},{19,3},{4,20},{20... | collective-permute-start | bytes 589832 | tf_op jit(solution)/shard_map/ppermute | solution.py:77
  17.6 8.0 %collective-permute-start.2 = (bf16[2,2,8,3200]{3,2,1,0:T(8,128)(2,1)S(1)}, bf16[2,2,8,3200]{3,2,1,0:T(8,128)(2,1)S(1)}, u32[]{:S(2)}, u32[]{:S(2)}) collective-permute-start(bf16[2,2,8,3200]{3,2,1,0:T(8,128)(2,1)S(1)} %get-tuple-element.28), channel_id=1, source_target_pairs={{0,2},{1,3},{2,0},{3,1},{4,6},{5,7},{6,4},{7,5},{8,10},{9,11},{10,... | collective-permute-start | bytes 614408 | tf_op jit(solution)/shard_map/ppermute | solution.py:77
  20.2 11.6 %collective-permute-start.8 = (bf16[2,2,2,8,3072]{4,3,2,1,0:T(8,128)(2,1)S(1)}, bf16[2,2,2,8,3072]{4,3,2,1,0:T(8,128)(2,1)S(1)}, u32[]{:S(2)}, u32[]{:S(2)}) collective-permute-start(bf16[2,2,2,8,3072]{4,3,2,1,0:T(8,128)(2,1)S(1)} %get-tuple-element.26), channel_id=1, source_target_pairs={{0,2},{1,3},{2,0},{3,1},{4,6},{5,7},{6,4},{7,5},{8,10},{9,11},{10,... | collective-permute-start | bytes 1179656 | tf_op jit(solution)/shard_map/ppermute | solution.py:77
  25.7 8.0 %collective-permute-start.3 = (bf16[2,2,2,8,3200]{4,3,2,1,0:T(8,128)(2,1)S(1)}, bf16[2,2,2,8,3200]{4,3,2,1,0:T(8,128)(2,1)S(1)}, u32[]{:S(2)}, u32[]{:S(2)}) collective-permute-start(bf16[2,2,2,8,3200]{4,3,2,1,0:T(8,128)(2,1)S(1)} %get-tuple-element.24.refs_1_), channel_id=1, source_target_pairs={{0,16},{16,0},{1,17},{17,1},{2,18},{18,2},{3,19},{19,3},{4,20},{20... | collective-permute-start | bytes 1228808 | tf_op jit(solution)/shard_map/ppermute | solution.py:77
  31.9 2.4 %collective-permute-start.9 = (bf16[2,2,2,2,8,3072]{5,4,3,2,0,1:T(8,128)(2,1)S(1)}, bf16[2,2,2,2,8,3072]{5,4,3,2,0,1:T(8,128)(2,1)S(1)}, u32[]{:S(2)}, u32[]{:S(2)}) collective-permute-start(bf16[2,2,2,2,8,3072]{5,4,3,2,0,1:T(8,128)(2,1)S(1)} %pad_maximum_fusion.3), channel_id=1, source_target_pairs={{0,1},{1,0},{2,3},{3,2},{4,5},{5,4},{6,7},{7,6},{8,9},{9,8},{10,11... | collective-permute-start | bytes 2359304 | tf_op jit(solution)/shard_map/ppermute | solution.py:77
  33.8 5.4 %collective-permute-start.4 = (bf16[2,2,2,2,8,3200]{5,4,3,2,1,0:T(8,128)(2,1)S(1)}, bf16[2,2,2,2,8,3200]{5,4,3,2,1,0:T(8,128)(2,1)S(1)}, u32[]{:S(2)}, u32[]{:S(2)}) collective-permute-start(bf16[2,2,2,2,8,3200]{5,4,3,2,1,0:T(8,128)(2,1)S(1)} %get-tuple-element.22), channel_id=1, source_target_pairs={{0,1},{1,0},{2,3},{3,2},{4,5},{5,4},{6,7},{7,6},{8,9},{9,8},{10,11... | collective-permute-start | bytes 2457608 | tf_op jit(solution)/shard_map/ppermute | solution.py:77
  46.2 2.8 %collective-permute-start.10 = (bf16[2,2,2,2,8,3072]{5,4,3,2,1,0:T(8,128)(2,1)S(1)}, bf16[2,2,2,2,8,3072]{5,4,3,2,1,0:T(8,128)(2,1)S(1)}, u32[]{:S(2)}, u32[]{:S(2)}) collective-permute-start(bf16[2,2,2,2,8,3072]{5,4,3,2,1,0:T(8,128)(2,1)S(1)} %bitcast.103), channel_id=1, source_target_pairs={{0,1},{1,0},{2,3},{3,2},{4,5},{5,4},{6,7},{7,6},{8,9},{9,8},{10,11... | collective-permute-start | bytes 2359304 | tf_op jit(solution)/shard_map/ppermute | solution.py:77
  48.5 2.4 %collective-permute-start.15 = (bf16[2,2,2,2,8,3072]{5,4,3,2,0,1:T(8,128)(2,1)S(1)}, bf16[2,2,2,2,8,3072]{5,4,3,2,0,1:T(8,128)(2,1)S(1)}, u32[]{:S(2)}, u32[]{:S(2)}) collective-permute-start(bf16[2,2,2,2,8,3072]{5,4,3,2,0,1:T(8,128)(2,1)S(1)} %copy.9), channel_id=1, source_target_pairs={{0,1},{1,0},{2,3},{3,2},{4,5},{5,4},{6,7},{7,6},{8,9},{9,8},{10,11... | collective-permute-start | bytes 2359304 | tf_op jit(solution)/shard_map/ppermute | solution.py:77
  49.2 11.2 %collective-permute-start.11 = (bf16[2,2,2,8,3072]{4,3,2,1,0:T(8,128)(2,1)S(1)}, bf16[2,2,2,8,3072]{4,3,2,1,0:T(8,128)(2,1)S(1)}, u32[]{:S(2)}, u32[]{:S(2)}) collective-permute-start(bf16[2,2,2,8,3072]{4,3,2,1,0:T(8,128)(2,1)S(1)} %slice_bitcast_fusion.2), channel_id=1, source_target_pairs={{0,16},{16,0},{1,17},{17,1},{2,18},{18,2},{3,19},{19,3},{4,20},{20... | collective-permute-start | bytes 1179656 | tf_op jit(solution)/shard_map/ppermute | solution.py:77
  51.1 11.5 %collective-permute-start.16 = (bf16[2,2,2,8,3072]{4,3,2,1,0:T(8,128)(2,1)S(1)}, bf16[2,2,2,8,3072]{4,3,2,1,0:T(8,128)(2,1)S(1)}, u32[]{:S(2)}, u32[]{:S(2)}) collective-permute-start(bf16[2,2,2,8,3072]{4,3,2,1,0:T(8,128)(2,1)S(1)} %slice_bitcast_fusion), channel_id=1, source_target_pairs={{0,2},{1,3},{2,0},{3,1},{4,6},{5,7},{6,4},{7,5},{8,10},{9,11},{10,... | collective-permute-start | bytes 1179656 | tf_op jit(solution)/shard_map/ppermute | solution.py:77
  60.6 6.2 %collective-permute-start.12 = (bf16[2,2,8,3072]{3,2,1,0:T(8,128)(2,1)S(1)}, bf16[2,2,8,3072]{3,2,1,0:T(8,128)(2,1)S(1)}, u32[]{:S(2)}, u32[]{:S(2)}) collective-permute-start(bf16[2,2,8,3072]{3,2,1,0:T(8,128)(2,1)S(1)} %slice_bitcast_fusion.6), channel_id=1, source_target_pairs={{0,2},{1,3},{2,0},{3,1},{4,6},{5,7},{6,4},{7,5},{8,10},{9,11},{10,... | collective-permute-start | bytes 589832 | tf_op jit(solution)/shard_map/ppermute | solution.py:77
  62.7 6.4 %collective-permute-start.17 = (bf16[2,2,8,3072]{3,2,1,0:T(8,128)(2,1)S(1)}, bf16[2,2,8,3072]{3,2,1,0:T(8,128)(2,1)S(1)}, u32[]{:S(2)}, u32[]{:S(2)}) collective-permute-start(bf16[2,2,8,3072]{3,2,1,0:T(8,128)(2,1)S(1)} %slice_bitcast_fusion.4), channel_id=1, source_target_pairs={{0,16},{16,0},{1,17},{17,1},{2,18},{18,2},{3,19},{19,3},{4,20},{20... | collective-permute-start | bytes 589832 | tf_op jit(solution)/shard_map/ppermute | solution.py:77
  66.9 5.7 %collective-permute-start.13 = (bf16[2,8,3072]{2,1,0:T(8,128)(2,1)S(1)}, bf16[2,8,3072]{2,1,0:T(8,128)(2,1)S(1)}, u32[]{:S(2)}, u32[]{:S(2)}) collective-permute-start(bf16[2,8,3072]{2,1,0:T(8,128)(2,1)S(1)} %slice_bitcast_fusion.10), channel_id=1, source_target_pairs={{0,4},{4,0},{8,12},{12,8},{1,5},{5,1},{9,13},{13,9},{2,6},{6,2},{1... | collective-permute-start | bytes 294920 | tf_op jit(solution)/shard_map/ppermute | solution.py:77
  69.2 5.2 %collective-permute-start.18 = (bf16[2,8,3072]{2,1,0:T(8,128)(2,1)S(1)}, bf16[2,8,3072]{2,1,0:T(8,128)(2,1)S(1)}, u32[]{:S(2)}, u32[]{:S(2)}) collective-permute-start(bf16[2,8,3072]{2,1,0:T(8,128)(2,1)S(1)} %slice_bitcast_fusion.8), channel_id=1, source_target_pairs={{0,4},{4,0},{8,12},{12,8},{1,5},{5,1},{9,13},{13,9},{2,6},{6,2},{1... | collective-permute-start | bytes 294920 | tf_op jit(solution)/shard_map/ppermute | solution.py:77
  72.6 6.1 %collective-permute-start.14 = (bf16[8,3072]{1,0:T(8,128)(2,1)S(1)}, bf16[8,3072]{1,0:T(8,128)(2,1)S(1)}, u32[]{:S(2)}, u32[]{:S(2)}) collective-permute-start(bf16[8,3072]{1,0:T(8,128)(2,1)S(1)} %slice_bitcast_fusion.14), channel_id=1, source_target_pairs={{0,8},{4,12},{8,0},{12,4},{1,9},{5,13},{9,1},{13,5},{2,10},{6,14},... | collective-permute-start | bytes 147464 | tf_op jit(solution)/shard_map/ppermute | solution.py:77
  74.4 5.1 %collective-permute-start.19 = (bf16[8,3072]{1,0:T(8,128)(2,1)S(1)}, bf16[8,3072]{1,0:T(8,128)(2,1)S(1)}, u32[]{:S(2)}, u32[]{:S(2)}) collective-permute-start(bf16[8,3072]{1,0:T(8,128)(2,1)S(1)} %slice_bitcast_fusion.12), channel_id=1, source_target_pairs={{0,8},{4,12},{8,0},{12,4},{1,9},{5,13},{9,1},{13,5},{2,10},{6,14},... | collective-permute-start | bytes 147464 | tf_op jit(solution)/shard_map/ppermute | solution.py:77

commit v11 on v9

--- a/solution.py
+++ b/solution.py
@@ -72,11 +72,20 @@
     return pltpu.with_memory_space_constraint(value, pltpu.HBM)
 
 
-def fetch_kernel(take, w_ref, after_ref, out_ref, sem):
+def slot_copies(source, target, sems):
+    return [
+        pltpu.make_async_copy(source.at[slot], target.at[slot], sems.at[slot])
+        for slot in range(target.shape[0])
+    ]
+
+
+def fetch_kernel(take, w_ref, after_ref, out_ref, sems):
     del after_ref
-    copy = pltpu.make_async_copy(take(w_ref), out_ref, sem)
-    copy.start()
-    copy.wait()
+    copies = slot_copies(take(w_ref), out_ref, sems)
+    for copy in copies:
+        copy.start()
+    for copy in copies:
+        copy.wait()
 
 
 def fetched(weight, take, shape, after):
@@ -88,7 +97,7 @@
         in_specs=[pl.BlockSpec(memory_space=pl.ANY)] * 2,
         out_specs=pl.BlockSpec(memory_space=pltpu.VMEM),
         out_shape=pltpu.VMEM(shape, weight.dtype),
-        scratch_shapes=[pltpu.SemaphoreType.DMA],
+        scratch_shapes=[pltpu.SemaphoreType.DMA((shape[0],))],
         compiler_params=pltpu.CompilerParams(vmem_limit_bytes=FETCH_LIMIT),
         cost_estimate=pl.CostEstimate(
             flops=0, bytes_accessed=4 * math.prod(shape), transcendentals=0
@@ -99,15 +108,16 @@
 def gate_up_kernel(last, take, pieces, row_ref, *refs):
     if last:
         sum_ref, refs = refs[0], refs[1:]
-    w_refs, (next_hbm, out_ref, next_ref, sem) = refs[:pieces], refs[pieces:]
+    w_refs, (next_hbm, out_ref, next_ref, sems) = refs[:pieces], refs[pieces:]
     held, _, sliver, half = w_refs[0].shape
     experts = held * pieces
     group = experts // 2 if experts % 2 == 0 else experts
     units = 2 * sliver
     depths = 2 if last else 1
     depth = half // depths
-    copy = pltpu.make_async_copy(take(next_hbm), next_ref, sem)
-    pl.when(pl.program_id(0) == 0)(copy.start)
+    copies = slot_copies(take(next_hbm), next_ref, sems)
+    for copy in copies:
+        pl.when(pl.program_id(0) == 0)(copy.start)
     if last:
         extra = row_ref[:, half:].astype(jnp.float32)
         lane = lax.broadcasted_iota(jnp.int32, extra.shape, 1)
@@ -135,7 +145,8 @@
             weigh = jnp.sum(jnp.where(mine, extra, 0.0), axis=1, keepdims=True)
             hidden = (0.5 * gate) * (1.0 + jnp.tanh(0.5 * gate)) * up * weigh
             out_ref[slot] = hidden.astype(out_ref.dtype)
-    pl.when(pl.program_id(0) == 0)(copy.wait)
+    for copy in copies:
+        pl.when(pl.program_id(0) == 0)(copy.wait)
 
 
 def gate_up_of(row_part, sums, weights, next_weight, take, next_shape):
@@ -176,7 +187,7 @@
         + [pl.BlockSpec(memory_space=pl.ANY)],
         out_specs=[out_spec, pl.BlockSpec(memory_space=pltpu.VMEM)],
         out_shape=[out_shape, pltpu.VMEM(next_shape, next_weight.dtype)],
-        scratch_shapes=[pltpu.SemaphoreType.DMA],
+        scratch_shapes=[pltpu.SemaphoreType.DMA((next_shape[0],))],
         compiler_params=pltpu.CompilerParams(vmem_limit_bytes=GATE_UP_LIMIT),
         cost_estimate=pl.CostEstimate(
             flops=4 * rows * experts * sliver * half,

time: 79.6 us -> 79.7 us (level)
  no operation moved by 1% of the time
where the time goes in v11:
time: 79.7 us; the launch traced here: 79.5 us
  waiting for transfers between devices  29.8 us (37%)
  starting transfers between devices  26.2 us (33%)
  Pallas kernels  18.1 us (23%)
  other arithmetic  3.74 us (5%)
  local copies, waits for them, and re-layouts  1.43 us (2%)
    ppermute x20, waiting for transfers between devices, shift(): return lax.ppermute(value, self.name, pairs)  29.8 us
    ppermute x20, starting transfers between devices, shift(): return lax.ppermute(value, self.name, pairs)  26.2 us
    pallas_call x2, Pallas kernels, gate_up_of(): pl.pallas_call(kernel, grid=(rows // row_block,), in_specs=specs + [pl.Bl...  9.42 us
    pallas_call x1, Pallas kernels, fetched(): pl.pallas_call(kernel, in_specs=[pl.BlockSpec(memory_space=pl.ANY)] * 2,...  4.68 us
    pallas_call x2, Pallas kernels, down_of(): pl.pallas_call(kernel, grid=(rows // row_block,), in_specs=[pl.BlockSpec(...  3.98 us
  transfers between devices with their start and end apart: 20, of which 16 were waited for; matrix products, arithmetic and copies ran while one was open for 4% of the time, Pallas kernels for 14%

profile of v11, /device:TPU:0, one launch (start us, length us, event | category | flops | bytes accessed | tf_op | source)
XLA Modules:
  0.0 79.5 jit_solution(14487147641422818637)
XLA Ops:
  0.0 0.8 %slice_bitcast_fusion.16 = (bf16[1,8,3072]{2,1,0:T(8,128)(2,1)S(1)}, bf16[8,3072]{1,0:T(8,128)(2,1)S(1)}, bf16[8,3072]{1,0:T(8,128)(2,1)S(1)}) fusion(bf16[8,6144]{1,0:T(8,128)(2,1)} %param.8), kind=kLoop, calls=%fused_computation.64 | loop fusion | bytes 245760 | tf_op jit(solution)/shard_map/stack | solution.py:47
  0.8 4.1 %collective-permute-start.5 = (bf16[8,3072]{1,0:T(8,128)(2,1)S(1)}, bf16[8,3072]{1,0:T(8,128)(2,1)S(1)}, u32[]{:S(2)}, u32[]{:S(2)}) collective-permute-start(bf16[8,3072]{1,0:T(8,128)(2,1)S(1)} %get-tuple-element.36), channel_id=1, source_target_pairs={{0,8},{4,12},{8,0},{12,4},{1,9},{5,13},{9,1},{13,5},{2,10},{6,14},... | collective-permute-start | bytes 147464 | tf_op jit(solution)/shard_map/ppermute | solution.py:44
  4.9 0.7 compare_convert_fusion
  5.7 0.7 select_reduce_fusion
  6.7 0.8 collective-permute-done.5
  7.6 1.9 %collective-permute-start.6 = (bf16[2,8,3072]{2,1,0:T(8,128)(2,1)S(1)}, bf16[2,8,3072]{2,1,0:T(8,128)(2,1)S(1)}, u32[]{:S(2)}, u32[]{:S(2)}) collective-permute-start(bf16[2,8,3072]{2,1,0:T(8,128)(2,1)S(1)} %get-tuple-element.34), channel_id=1, source_target_pairs={{0,4},{4,0},{8,12},{12,8},{1,5},{5,1},{9,13},{13,9},{2,6},{6,2},{1... | collective-permute-start | bytes 294920 | tf_op jit(solution)/shard_map/ppermute | solution.py:44
  9.4 2.6 %collective-permute-done = bf16[8,3200]{1,0:T(8,128)(2,1)S(1)} collective-permute-done((bf16[8,3200]{1,0:T(8,128)(2,1)S(1)}, bf16[8,3200]{1,0:T(8,128)(2,1)S(1)}, u32[]{:S(2)}, u32[]{:S(2)}) %collective-permute-start) | collective-permute-done | bytes 51232 | tf_op jit(solution)/shard_map/ppermute | solution.py:44
  12.0 1.6 %collective-permute-start.1 = (bf16[2,8,3200]{2,1,0:T(8,128)(2,1)S(1)}, bf16[2,8,3200]{2,1,0:T(8,128)(2,1)S(1)}, u32[]{:S(2)}, u32[]{:S(2)}) collective-permute-start(bf16[2,8,3200]{2,1,0:T(8,128)(2,1)S(1)} %get-tuple-element.32), channel_id=1, source_target_pairs={{0,4},{4,0},{8,12},{12,8},{1,5},{5,1},{9,13},{13,9},{2,6},{6,2},{1... | collective-permute-start | bytes 307208 | tf_op jit(solution)/shard_map/ppermute | solution.py:44
  13.6 1.6 %collective-permute-start.7 = (bf16[2,2,8,3072]{3,2,1,0:T(8,128)(2,1)S(1)}, bf16[2,2,8,3072]{3,2,1,0:T(8,128)(2,1)S(1)}, u32[]{:S(2)}, u32[]{:S(2)}) collective-permute-start(bf16[2,2,8,3072]{3,2,1,0:T(8,128)(2,1)S(1)} %get-tuple-element.30), channel_id=1, source_target_pairs={{0,16},{16,0},{1,17},{17,1},{2,18},{18,2},{3,19},{19,3},{4,20},{20... | collective-permute-start | bytes 589832 | tf_op jit(solution)/shard_map/ppermute | solution.py:44
  15.2 1.6 %collective-permute-done.1 = bf16[2,8,3200]{2,1,0:T(8,128)(2,1)S(1)} collective-permute-done((bf16[2,8,3200]{2,1,0:T(8,128)(2,1)S(1)}, bf16[2,8,3200]{2,1,0:T(8,128)(2,1)S(1)}, u32[]{:S(2)}, u32[]{:S(2)}) %collective-permute-start.1) | collective-permute-done | bytes 102432 | tf_op jit(solution)/shard_map/ppermute | solution.py:44
  16.8 1.5 %collective-permute-start.2 = (bf16[2,2,8,3200]{3,2,1,0:T(8,128)(2,1)S(1)}, bf16[2,2,8,3200]{3,2,1,0:T(8,128)(2,1)S(1)}, u32[]{:S(2)}, u32[]{:S(2)}) collective-permute-start(bf16[2,2,8,3200]{3,2,1,0:T(8,128)(2,1)S(1)} %get-tuple-element.28), channel_id=1, source_target_pairs={{0,2},{1,3},{2,0},{3,1},{4,6},{5,7},{6,4},{7,5},{8,10},{9,11},{10,... | collective-permute-start | bytes 614408 | tf_op jit(solution)/shard_map/ppermute | solution.py:44
  18.3 1.1 %collective-permute-done.7 = bf16[2,2,8,3072]{3,2,1,0:T(8,128)(2,1)S(1)} collective-permute-done((bf16[2,2,8,3072]{3,2,1,0:T(8,128)(2,1)S(1)}, bf16[2,2,8,3072]{3,2,1,0:T(8,128)(2,1)S(1)}, u32[]{:S(2)}, u32[]{:S(2)}) %collective-permute-start.7) | collective-permute-done | bytes 196640 | tf_op jit(solution)/shard_map/ppermute | solution.py:44
  19.4 1.6 %collective-permute-start.8 = (bf16[2,2,2,8,3072]{4,3,2,1,0:T(8,128)(2,1)S(1)}, bf16[2,2,2,8,3072]{4,3,2,1,0:T(8,128)(2,1)S(1)}, u32[]{:S(2)}, u32[]{:S(2)}) collective-permute-start(bf16[2,2,2,8,3072]{4,3,2,1,0:T(8,128)(2,1)S(1)} %get-tuple-element.26), channel_id=1, source_target_pairs={{0,2},{1,3},{2,0},{3,1},{4,6},{5,7},{6,4},{7,5},{8,10},{9,11},{10,... | collective-permute-start | bytes 1179656 | tf_op jit(solution)/shard_map/ppermute | solution.py:44
  21.0 3.8 %collective-permute-done.2 = bf16[2,2,8,3200]{3,2,1,0:T(8,128)(2,1)S(1)} collective-permute-done((bf16[2,2,8,3200]{3,2,1,0:T(8,128)(2,1)S(1)}, bf16[2,2,8,3200]{3,2,1,0:T(8,128)(2,1)S(1)}, u32[]{:S(2)}, u32[]{:S(2)}) %collective-permute-start.2) | collective-permute-done | bytes 204832 | tf_op jit(solution)/shard_map/ppermute | solution.py:44
  24.9 1.5 %collective-permute-start.3 = (bf16[2,2,2,8,3200]{4,3,2,1,0:T(8,128)(2,1)S(1)}, bf16[2,2,2,8,3200]{4,3,2,1,0:T(8,128)(2,1)S(1)}, u32[]{:S(2)}, u32[]{:S(2)}) collective-permute-start(bf16[2,2,2,8,3200]{4,3,2,1,0:T(8,128)(2,1)S(1)} %get-tuple-element.24.refs_1_), channel_id=1, source_target_pairs={{0,16},{16,0},{1,17},{17,1},{2,18},{18,2},{3,19},{19,3},{4,20},{20... | collective-permute-start | bytes 1228808 | tf_op jit(solution)/shard_map/ppermute | solution.py:44
  26.4 4.7 %shard_map.73.refs_1_ = bf16[4,2,256,3072]{3,2,1,0:T(8,128)(2,1)S(1)} custom-call(bf16[4,2,256,6144]{3,2,1,0:T(8,128)(2,1)} %refs_2_.1, bf16[2,2,2,8,3200]{4,3,2,1,0:T(8,128)(2,1)S(1)} %get-tuple-element.24.refs_1_), custom_call_target="tpu_custom_call" | custom-call | bytes 25165824 | tf_op jit(solution)/shard_map/pallas_call | solution.py:95
  31.2 1.7 %collective-permute-done.3 = bf16[2,2,2,8,3200]{4,3,2,1,0:T(8,128)(2,1)S(1)} collective-permute-done((bf16[2,2,2,8,3200]{4,3,2,1,0:T(8,128)(2,1)S(1)}, bf16[2,2,2,8,3200]{4,3,2,1,0:T(8,128)(2,1)S(1)}, u32[]{:S(2)}, u32[]{:S(2)}) %collective-permute-start.3) | collective-permute-done | bytes 409632 | tf_op jit(solution)/shard_map/ppermute | solution.py:44
  32.9 0.1 fusion.24
  33.1 0.4 collective-permute-done.9
  33.5 0.1 pad_maximum_fusion.1
  33.7 0.1 copy.15
  33.8 4.7 %shard_map.74 = (f32[256,2048]{1,0:T(8,128)S(1)}, bf16[4,2,256,3072]{3,2,1,0:T(8,128)(2,1)S(1)}) custom-call(bf16[256,3072]{1,0:T(8,128)(2,1)S(1)} %bitcast.94, bf16[4,2,256,3072]{3,2,1,0:T(8,128)(2,1)S(1)} %shard_map.73.refs_1_, bf16[4,2,256,6144]{3,2,1,0:T(8,128)(2,1)} %refs_2_.1), custom_call_target="tpu_custom_call" | custom-call | flops 3221225472 | bytes 14680064 | tf_op jit(solution)/shard_map/pallas_call | solution.py:182
  38.5 0.2 pad_maximum_fusion
  38.7 4.7 %shard_map.75 = (bf16[4,256,256]{2,1,0:T(8,128)(2,1)S(1)}, bf16[4,256,6144]{2,1,0:T(8,128)(2,1)S(1)}) custom-call(bf16[256,3200]{1,0:T(8,128)(2,1)S(1)} %bitcast.93, f32[256,2048]{1,0:T(8,128)S(1)} %get-tuple-element.13.refs_1_, bf16[4,2,256,3072]{3,2,1,0:T(8,128)(2,1)S(1)} %get-tuple-element.14.refs_2_, bf16[4,256,6144]{2,1,0:T(8,128)(2,1)} %refs_3_.1), custom_call_target="tpu_custom_call" | custom-call | flops 3221225472 | bytes 14680064 | tf_op jit(solution)/shard_map/pallas_call | solution.py:182
  43.4 2.0 %shard_map.76 = bf16[256,3072]{1,0:T(8,128)(2,1)S(1)} custom-call(bf16[4,256,256]{2,1,0:T(8,128)(2,1)S(1)} %get-tuple-element.15.refs_0_, bf16[4,256,6144]{2,1,0:T(8,128)(2,1)S(1)} %get-tuple-element.16.refs_1_), custom_call_target="tpu_custom_call" | custom-call | flops 1610612736 | bytes 8388608 | tf_op jit(solution)/shard_map/pallas_call | solution.py:225
  45.5 0.2 collective-permute-start.10
  45.7 2.0 %shard_map.77 = bf16[256,3072]{1,0:T(8,128)(2,1)S(1)} custom-call(bf16[4,256,256]{2,1,0:T(8,128)(2,1)S(1)} %get-tuple-element.15.refs_0_, bf16[4,256,6144]{2,1,0:T(8,128)(2,1)S(1)} %get-tuple-element.16.refs_1_), custom_call_target="tpu_custom_call" | custom-call | flops 1610612736 | bytes 8388608 | tf_op jit(solution)/shard_map/pallas_call | solution.py:225
  47.9 0.4 collective-permute-start.15
  48.4 0.2 fusion
  48.6 1.1 %collective-permute-start.11 = (bf16[2,2,2,8,3072]{4,3,2,1,0:T(8,128)(2,1)S(1)}, bf16[2,2,2,8,3072]{4,3,2,1,0:T(8,128)(2,1)S(1)}, u32[]{:S(2)}, u32[]{:S(2)}) collective-permute-start(bf16[2,2,2,8,3072]{4,3,2,1,0:T(8,128)(2,1)S(1)} %slice_bitcast_fusion.2), channel_id=1, source_target_pairs={{0,16},{16,0},{1,17},{17,1},{2,18},{18,2},{3,19},{19,3},{4,20},{20... | collective-permute-start | bytes 1179656 | tf_op jit(solution)/shard_map/ppermute | solution.py:44
  49.7 0.6 collective-permute-done.15
  50.3 0.2 fusion.1
  50.5 1.6 %collective-permute-start.16 = (bf16[2,2,2,8,3072]{4,3,2,1,0:T(8,128)(2,1)S(1)}, bf16[2,2,2,8,3072]{4,3,2,1,0:T(8,128)(2,1)S(1)}, u32[]{:S(2)}, u32[]{:S(2)}) collective-permute-start(bf16[2,2,2,8,3072]{4,3,2,1,0:T(8,128)(2,1)S(1)} %slice_bitcast_fusion), channel_id=1, source_target_pairs={{0,2},{1,3},{2,0},{3,1},{4,6},{5,7},{6,4},{7,5},{8,10},{9,11},{10,... | collective-permute-start | bytes 1179656 | tf_op jit(solution)/shard_map/ppermute | solution.py:44
  52.1 7.7 %collective-permute-done.11 = bf16[2,2,2,8,3072]{4,3,2,1,0:T(8,128)(2,1)S(1)} collective-permute-done((bf16[2,2,2,8,3072]{4,3,2,1,0:T(8,128)(2,1)S(1)}, bf16[2,2,2,8,3072]{4,3,2,1,0:T(8,128)(2,1)S(1)}, u32[]{:S(2)}, u32[]{:S(2)}) %collective-permute-start.11) | collective-permute-done | bytes 393248 | tf_op jit(solution)/shard_map/ppermute | solution.py:44
  59.9 1.6 %collective-permute-start.12 = (bf16[2,2,8,3072]{3,2,1,0:T(8,128)(2,1)S(1)}, bf16[2,2,8,3072]{3,2,1,0:T(8,128)(2,1)S(1)}, u32[]{:S(2)}, u32[]{:S(2)}) collective-permute-start(bf16[2,2,8,3072]{3,2,1,0:T(8,128)(2,1)S(1)} %slice_bitcast_fusion.6), channel_id=1, source_target_pairs={{0,2},{1,3},{2,0},{3,1},{4,6},{5,7},{6,4},{7,5},{8,10},{9,11},{10,... | collective-permute-start | bytes 589832 | tf_op jit(solution)/shard_map/ppermute | solution.py:44
  61.5 0.4 collective-permute-done.16
  62.1 1.2 %collective-permute-start.17 = (bf16[2,2,8,3072]{3,2,1,0:T(8,128)(2,1)S(1)}, bf16[2,2,8,3072]{3,2,1,0:T(8,128)(2,1)S(1)}, u32[]{:S(2)}, u32[]{:S(2)}) collective-permute-start(bf16[2,2,8,3072]{3,2,1,0:T(8,128)(2,1)S(1)} %slice_bitcast_fusion.4), channel_id=1, source_target_pairs={{0,16},{16,0},{1,17},{17,1},{2,18},{18,2},{3,19},{19,3},{4,20},{20... | collective-permute-start | bytes 589832 | tf_op jit(solution)/shard_map/ppermute | solution.py:44
  63.3 2.9 %collective-permute-done.12 = bf16[2,2,8,3072]{3,2,1,0:T(8,128)(2,1)S(1)} collective-permute-done((bf16[2,2,8,3072]{3,2,1,0:T(8,128)(2,1)S(1)}, bf16[2,2,8,3072]{3,2,1,0:T(8,128)(2,1)S(1)}, u32[]{:S(2)}, u32[]{:S(2)}) %collective-permute-start.12) | collective-permute-done | bytes 196640 | tf_op jit(solution)/shard_map/ppermute | solution.py:44
  66.2 1.7 %collective-permute-start.13 = (bf16[2,8,3072]{2,1,0:T(8,128)(2,1)S(1)}, bf16[2,8,3072]{2,1,0:T(8,128)(2,1)S(1)}, u32[]{:S(2)}, u32[]{:S(2)}) collective-permute-start(bf16[2,8,3072]{2,1,0:T(8,128)(2,1)S(1)} %slice_bitcast_fusion.10), channel_id=1, source_target_pairs={{0,4},{4,0},{8,12},{12,8},{1,5},{5,1},{9,13},{13,9},{2,6},{6,2},{1... | collective-permute-start | bytes 294920 | tf_op jit(solution)/shard_map/ppermute | solution.py:44
  67.9 0.6 collective-permute-done.17
  68.6 1.7 %collective-permute-start.18 = (bf16[2,8,3072]{2,1,0:T(8,128)(2,1)S(1)}, bf16[2,8,3072]{2,1,0:T(8,128)(2,1)S(1)}, u32[]{:S(2)}, u32[]{:S(2)}) collective-permute-start(bf16[2,8,3072]{2,1,0:T(8,128)(2,1)S(1)} %slice_bitcast_fusion.8), channel_id=1, source_target_pairs={{0,4},{4,0},{8,12},{12,8},{1,5},{5,1},{9,13},{13,9},{2,6},{6,2},{1... | collective-permute-start | bytes 294920 | tf_op jit(solution)/shard_map/ppermute | solution.py:44
  70.2 1.7 %collective-permute-done.13 = bf16[2,8,3072]{2,1,0:T(8,128)(2,1)S(1)} collective-permute-done((bf16[2,8,3072]{2,1,0:T(8,128)(2,1)S(1)}, bf16[2,8,3072]{2,1,0:T(8,128)(2,1)S(1)}, u32[]{:S(2)}, u32[]{:S(2)}) %collective-permute-start.13) | collective-permute-done | bytes 98336 | tf_op jit(solution)/shard_map/ppermute | solution.py:44
  72.0 1.4 %collective-permute-start.14 = (bf16[8,3072]{1,0:T(8,128)(2,1)S(1)}, bf16[8,3072]{1,0:T(8,128)(2,1)S(1)}, u32[]{:S(2)}, u32[]{:S(2)}) collective-permute-start(bf16[8,3072]{1,0:T(8,128)(2,1)S(1)} %slice_bitcast_fusion.14), channel_id=1, source_target_pairs={{0,8},{4,12},{8,0},{12,4},{1,9},{5,13},{9,1},{13,5},{2,10},{6,14},... | collective-permute-start | bytes 147464 | tf_op jit(solution)/shard_map/ppermute | solution.py:44
  73.4 0.3 collective-permute-done.18
  73.8 1.4 %collective-permute-start.19 = (bf16[8,3072]{1,0:T(8,128)(2,1)S(1)}, bf16[8,3072]{1,0:T(8,128)(2,1)S(1)}, u32[]{:S(2)}, u32[]{:S(2)}) collective-permute-start(bf16[8,3072]{1,0:T(8,128)(2,1)S(1)} %slice_bitcast_fusion.12), channel_id=1, source_target_pairs={{0,8},{4,12},{8,0},{12,4},{1,9},{5,13},{9,1},{13,5},{2,10},{6,14},... | collective-permute-start | bytes 147464 | tf_op jit(solution)/shard_map/ppermute | solution.py:44
  75.2 2.9 %collective-permute-done.14 = bf16[8,3072]{1,0:T(8,128)(2,1)S(1)} collective-permute-done((bf16[8,3072]{1,0:T(8,128)(2,1)S(1)}, bf16[8,3072]{1,0:T(8,128)(2,1)S(1)}, u32[]{:S(2)}, u32[]{:S(2)}) %collective-permute-start.14) | collective-permute-done | bytes 49184 | tf_op jit(solution)/shard_map/ppermute | solution.py:44
  78.1 0.7 collective-permute-done.19
  78.9 0.6 pad_maximum_fusion.10
  (38 shorter events, 1.5 us)
Async XLA Ops:
  0.8 6.7 %collective-permute-start.5 = (bf16[8,3072]{1,0:T(8,128)(2,1)S(1)}, bf16[8,3072]{1,0:T(8,128)(2,1)S(1)}, u32[]{:S(2)}, u32[]{:S(2)}) collective-permute-start(bf16[8,3072]{1,0:T(8,128)(2,1)S(1)} %get-tuple-element.36), channel_id=1, source_target_pairs={{0,8},{4,12},{8,0},{12,4},{1,9},{5,13},{9,1},{13,5},{2,10},{6,14},... | collective-permute-start | bytes 147464 | tf_op jit(solution)/shard_map/ppermute | solution.py:44
  6.7 5.3 %collective-permute-start = (bf16[8,3200]{1,0:T(8,128)(2,1)S(1)}, bf16[8,3200]{1,0:T(8,128)(2,1)S(1)}, u32[]{:S(2)}, u32[]{:S(2)}) collective-permute-start(bf16[8,3200]{1,0:T(8,128)(2,1)S(1)} %get-tuple-element.39), channel_id=1, source_target_pairs={{0,8},{4,12},{8,0},{12,4},{1,9},{5,13},{9,1},{13,5},{2,10},{6,14},... | collective-permute-start | bytes 153608 | tf_op jit(solution)/shard_map/ppermute | solution.py:44
  7.6 6.0 %collective-permute-start.6 = (bf16[2,8,3072]{2,1,0:T(8,128)(2,1)S(1)}, bf16[2,8,3072]{2,1,0:T(8,128)(2,1)S(1)}, u32[]{:S(2)}, u32[]{:S(2)}) collective-permute-start(bf16[2,8,3072]{2,1,0:T(8,128)(2,1)S(1)} %get-tuple-element.34), channel_id=1, source_target_pairs={{0,4},{4,0},{8,12},{12,8},{1,5},{5,1},{9,13},{13,9},{2,6},{6,2},{1... | collective-permute-start | bytes 294920 | tf_op jit(solution)/shard_map/ppermute | solution.py:44
  12.0 4.7 %collective-permute-start.1 = (bf16[2,8,3200]{2,1,0:T(8,128)(2,1)S(1)}, bf16[2,8,3200]{2,1,0:T(8,128)(2,1)S(1)}, u32[]{:S(2)}, u32[]{:S(2)}) collective-permute-start(bf16[2,8,3200]{2,1,0:T(8,128)(2,1)S(1)} %get-tuple-element.32), channel_id=1, source_target_pairs={{0,4},{4,0},{8,12},{12,8},{1,5},{5,1},{9,13},{13,9},{2,6},{6,2},{1... | collective-permute-start | bytes 307208 | tf_op jit(solution)/shard_map/ppermute | solution.py:44
  13.6 5.7 %collective-permute-start.7 = (bf16[2,2,8,3072]{3,2,1,0:T(8,128)(2,1)S(1)}, bf16[2,2,8,3072]{3,2,1,0:T(8,128)(2,1)S(1)}, u32[]{:S(2)}, u32[]{:S(2)}) collective-permute-start(bf16[2,2,8,3072]{3,2,1,0:T(8,128)(2,1)S(1)} %get-tuple-element.30), channel_id=1, source_target_pairs={{0,16},{16,0},{1,17},{17,1},{2,18},{18,2},{3,19},{19,3},{4,20},{20... | collective-permute-start | bytes 589832 | tf_op jit(solution)/shard_map/ppermute | solution.py:44
  16.8 8.0 %collective-permute-start.2 = (bf16[2,2,8,3200]{3,2,1,0:T(8,128)(2,1)S(1)}, bf16[2,2,8,3200]{3,2,1,0:T(8,128)(2,1)S(1)}, u32[]{:S(2)}, u32[]{:S(2)}) collective-permute-start(bf16[2,2,8,3200]{3,2,1,0:T(8,128)(2,1)S(1)} %get-tuple-element.28), channel_id=1, source_target_pairs={{0,2},{1,3},{2,0},{3,1},{4,6},{5,7},{6,4},{7,5},{8,10},{9,11},{10,... | collective-permute-start | bytes 614408 | tf_op jit(solution)/shard_map/ppermute | solution.py:44
  19.4 11.7 %collective-permute-start.8 = (bf16[2,2,2,8,3072]{4,3,2,1,0:T(8,128)(2,1)S(1)}, bf16[2,2,2,8,3072]{4,3,2,1,0:T(8,128)(2,1)S(1)}, u32[]{:S(2)}, u32[]{:S(2)}) collective-permute-start(bf16[2,2,2,8,3072]{4,3,2,1,0:T(8,128)(2,1)S(1)} %get-tuple-element.26), channel_id=1, source_target_pairs={{0,2},{1,3},{2,0},{3,1},{4,6},{5,7},{6,4},{7,5},{8,10},{9,11},{10,... | collective-permute-start | bytes 1179656 | tf_op jit(solution)/shard_map/ppermute | solution.py:44
  24.9 8.0 %collective-permute-start.3 = (bf16[2,2,2,8,3200]{4,3,2,1,0:T(8,128)(2,1)S(1)}, bf16[2,2,2,8,3200]{4,3,2,1,0:T(8,128)(2,1)S(1)}, u32[]{:S(2)}, u32[]{:S(2)}) collective-permute-start(bf16[2,2,2,8,3200]{4,3,2,1,0:T(8,128)(2,1)S(1)} %get-tuple-element.24.refs_1_), channel_id=1, source_target_pairs={{0,16},{16,0},{1,17},{17,1},{2,18},{18,2},{3,19},{19,3},{4,20},{20... | collective-permute-start | bytes 1228808 | tf_op jit(solution)/shard_map/ppermute | solution.py:44
  31.2 2.4 %collective-permute-start.9 = (bf16[2,2,2,2,8,3072]{5,4,3,2,0,1:T(8,128)(2,1)S(1)}, bf16[2,2,2,2,8,3072]{5,4,3,2,0,1:T(8,128)(2,1)S(1)}, u32[]{:S(2)}, u32[]{:S(2)}) collective-permute-start(bf16[2,2,2,2,8,3072]{5,4,3,2,0,1:T(8,128)(2,1)S(1)} %pad_maximum_fusion.3), channel_id=1, source_target_pairs={{0,1},{1,0},{2,3},{3,2},{4,5},{5,4},{6,7},{7,6},{8,9},{9,8},{10,11... | collective-permute-start | bytes 2359304 | tf_op jit(solution)/shard_map/ppermute | solution.py:44
  33.0 5.5 %collective-permute-start.4 = (bf16[2,2,2,2,8,3200]{5,4,3,2,1,0:T(8,128)(2,1)S(1)}, bf16[2,2,2,2,8,3200]{5,4,3,2,1,0:T(8,128)(2,1)S(1)}, u32[]{:S(2)}, u32[]{:S(2)}) collective-permute-start(bf16[2,2,2,2,8,3200]{5,4,3,2,1,0:T(8,128)(2,1)S(1)} %get-tuple-element.22), channel_id=1, source_target_pairs={{0,1},{1,0},{2,3},{3,2},{4,5},{5,4},{6,7},{7,6},{8,9},{9,8},{10,11... | collective-permute-start | bytes 2457608 | tf_op jit(solution)/shard_map/ppermute | solution.py:44
  45.5 2.8 %collective-permute-start.10 = (bf16[2,2,2,2,8,3072]{5,4,3,2,1,0:T(8,128)(2,1)S(1)}, bf16[2,2,2,2,8,3072]{5,4,3,2,1,0:T(8,128)(2,1)S(1)}, u32[]{:S(2)}, u32[]{:S(2)}) collective-permute-start(bf16[2,2,2,2,8,3072]{5,4,3,2,1,0:T(8,128)(2,1)S(1)} %bitcast.100), channel_id=1, source_target_pairs={{0,1},{1,0},{2,3},{3,2},{4,5},{5,4},{6,7},{7,6},{8,9},{9,8},{10,11... | collective-permute-start | bytes 2359304 | tf_op jit(solution)/shard_map/ppermute | solution.py:44
  47.9 2.4 %collective-permute-start.15 = (bf16[2,2,2,2,8,3072]{5,4,3,2,0,1:T(8,128)(2,1)S(1)}, bf16[2,2,2,2,8,3072]{5,4,3,2,0,1:T(8,128)(2,1)S(1)}, u32[]{:S(2)}, u32[]{:S(2)}) collective-permute-start(bf16[2,2,2,2,8,3072]{5,4,3,2,0,1:T(8,128)(2,1)S(1)} %copy.16), channel_id=1, source_target_pairs={{0,1},{1,0},{2,3},{3,2},{4,5},{5,4},{6,7},{7,6},{8,9},{9,8},{10,11... | collective-permute-start | bytes 2359304 | tf_op jit(solution)/shard_map/ppermute | solution.py:44
  48.6 11.2 %collective-permute-start.11 = (bf16[2,2,2,8,3072]{4,3,2,1,0:T(8,128)(2,1)S(1)}, bf16[2,2,2,8,3072]{4,3,2,1,0:T(8,128)(2,1)S(1)}, u32[]{:S(2)}, u32[]{:S(2)}) collective-permute-start(bf16[2,2,2,8,3072]{4,3,2,1,0:T(8,128)(2,1)S(1)} %slice_bitcast_fusion.2), channel_id=1, source_target_pairs={{0,16},{16,0},{1,17},{17,1},{2,18},{18,2},{3,19},{19,3},{4,20},{20... | collective-permute-start | bytes 1179656 | tf_op jit(solution)/shard_map/ppermute | solution.py:44
  50.5 11.5 %collective-permute-start.16 = (bf16[2,2,2,8,3072]{4,3,2,1,0:T(8,128)(2,1)S(1)}, bf16[2,2,2,8,3072]{4,3,2,1,0:T(8,128)(2,1)S(1)}, u32[]{:S(2)}, u32[]{:S(2)}) collective-permute-start(bf16[2,2,2,8,3072]{4,3,2,1,0:T(8,128)(2,1)S(1)} %slice_bitcast_fusion), channel_id=1, source_target_pairs={{0,2},{1,3},{2,0},{3,1},{4,6},{5,7},{6,4},{7,5},{8,10},{9,11},{10,... | collective-permute-start | bytes 1179656 | tf_op jit(solution)/shard_map/ppermute | solution.py:44
  59.9 6.2 %collective-permute-start.12 = (bf16[2,2,8,3072]{3,2,1,0:T(8,128)(2,1)S(1)}, bf16[2,2,8,3072]{3,2,1,0:T(8,128)(2,1)S(1)}, u32[]{:S(2)}, u32[]{:S(2)}) collective-permute-start(bf16[2,2,8,3072]{3,2,1,0:T(8,128)(2,1)S(1)} %slice_bitcast_fusion.6), channel_id=1, source_target_pairs={{0,2},{1,3},{2,0},{3,1},{4,6},{5,7},{6,4},{7,5},{8,10},{9,11},{10,... | collective-permute-start | bytes 589832 | tf_op jit(solution)/shard_map/ppermute | solution.py:44
  62.1 6.4 %collective-permute-start.17 = (bf16[2,2,8,3072]{3,2,1,0:T(8,128)(2,1)S(1)}, bf16[2,2,8,3072]{3,2,1,0:T(8,128)(2,1)S(1)}, u32[]{:S(2)}, u32[]{:S(2)}) collective-permute-start(bf16[2,2,8,3072]{3,2,1,0:T(8,128)(2,1)S(1)} %slice_bitcast_fusion.4), channel_id=1, source_target_pairs={{0,16},{16,0},{1,17},{17,1},{2,18},{18,2},{3,19},{19,3},{4,20},{20... | collective-permute-start | bytes 589832 | tf_op jit(solution)/shard_map/ppermute | solution.py:44
  66.2 5.7 %collective-permute-start.13 = (bf16[2,8,3072]{2,1,0:T(8,128)(2,1)S(1)}, bf16[2,8,3072]{2,1,0:T(8,128)(2,1)S(1)}, u32[]{:S(2)}, u32[]{:S(2)}) collective-permute-start(bf16[2,8,3072]{2,1,0:T(8,128)(2,1)S(1)} %slice_bitcast_fusion.10), channel_id=1, source_target_pairs={{0,4},{4,0},{8,12},{12,8},{1,5},{5,1},{9,13},{13,9},{2,6},{6,2},{1... | collective-permute-start | bytes 294920 | tf_op jit(solution)/shard_map/ppermute | solution.py:44
  68.6 5.2 %collective-permute-start.18 = (bf16[2,8,3072]{2,1,0:T(8,128)(2,1)S(1)}, bf16[2,8,3072]{2,1,0:T(8,128)(2,1)S(1)}, u32[]{:S(2)}, u32[]{:S(2)}) collective-permute-start(bf16[2,8,3072]{2,1,0:T(8,128)(2,1)S(1)} %slice_bitcast_fusion.8), channel_id=1, source_target_pairs={{0,4},{4,0},{8,12},{12,8},{1,5},{5,1},{9,13},{13,9},{2,6},{6,2},{1... | collective-permute-start | bytes 294920 | tf_op jit(solution)/shard_map/ppermute | solution.py:44
  72.0 6.1 %collective-permute-start.14 = (bf16[8,3072]{1,0:T(8,128)(2,1)S(1)}, bf16[8,3072]{1,0:T(8,128)(2,1)S(1)}, u32[]{:S(2)}, u32[]{:S(2)}) collective-permute-start(bf16[8,3072]{1,0:T(8,128)(2,1)S(1)} %slice_bitcast_fusion.14), channel_id=1, source_target_pairs={{0,8},{4,12},{8,0},{12,4},{1,9},{5,13},{9,1},{13,5},{2,10},{6,14},... | collective-permute-start | bytes 147464 | tf_op jit(solution)/shard_map/ppermute | solution.py:44
  73.8 5.1 %collective-permute-start.19 = (bf16[8,3072]{1,0:T(8,128)(2,1)S(1)}, bf16[8,3072]{1,0:T(8,128)(2,1)S(1)}, u32[]{:S(2)}, u32[]{:S(2)}) collective-permute-start(bf16[8,3072]{1,0:T(8,128)(2,1)S(1)} %slice_bitcast_fusion.12), channel_id=1, source_target_pairs={{0,8},{4,12},{8,0},{12,4},{1,9},{5,13},{9,1},{13,5},{2,10},{6,14},... | collective-permute-start | bytes 147464 | tf_op jit(solution)/shard_map/ppermute | solution.py:44

commit v12 on v9

--- a/solution.py
+++ b/solution.py
@@ -9,10 +9,12 @@
 
 AXES = ("dp", "expert", "shard")
 LANES = 128
+MATRIX = 256
 ROW_BLOCK = 256
 FETCH_LIMIT = 1 * 2**20
 GATE_UP_LIMIT = 8 * 2**20
-DOWN_LIMIT = 8 * 2**20
+DOWN_LIMIT = 12 * 2**20
+REORDER_LIMIT = 48 * 2**20
 
 
 def slot_coefficients(expert_ids, gate_values, old_place, new_place):
@@ -104,8 +106,7 @@
     experts = held * pieces
     group = experts // 2 if experts % 2 == 0 else experts
     units = 2 * sliver
-    depths = 2 if last else 1
-    depth = half // depths
+    middle = -(-half // (2 * MATRIX)) * MATRIX if last else half
     copy = pltpu.make_async_copy(take(next_hbm), next_ref, sem)
     pl.when(pl.program_id(0) == 0)(copy.start)
     if last:
@@ -115,12 +116,10 @@
         columns = slice(first * units, (first + group) * units)
         w_ref, at_slot = w_refs[first // held], first % held
         pre = sum_ref[:, columns] if last else None
-        for at in range(0, half, depth):
+        for at, end in ((0, middle), (middle, half))[: 1 + (middle < half)]:
             product = lax.dot_general(
-                row_ref[:, at : at + depth],
-                w_ref[at_slot : at_slot + group, :, :, at : at + depth].reshape(
-                    group * units, depth
-                ),
+                row_ref[:, at:end],
+                w_ref[at_slot : at_slot + group, :, :, at:end].reshape(group * units, end - at),
                 (((1,), (1,)), ((), ())),
                 preferred_element_type=jnp.float32,
             )
@@ -186,30 +185,22 @@
     )(*operands, *(resident(weight) for weight in weights), in_hbm(next_weight))
 
 
-def down_kernel(part, hidden_ref, w_ref, out_ref):
+def down_kernel(start, hidden_ref, w_ref, out_ref):
     experts, _, sliver = hidden_ref.shape
     columns = out_ref.shape[1]
-    block = next(size for size in (1536, 1024, 512, 384, 256, 128, columns) if columns % size == 0)
-
-    def one_block(step, carry):
-        at = pl.multiple_of(step * block, block)
-        taken = pl.ds(pl.multiple_of(part * columns + step * block, block), block)
-        hidden = jnp.concatenate([hidden_ref[slot] for slot in range(experts)], axis=1)
-        weights = w_ref[:, :, taken].reshape(experts * sliver, block)
-        out_ref[:, pl.ds(at, block)] = jnp.dot(
-            hidden, weights, preferred_element_type=jnp.float32
-        ).astype(out_ref.dtype)
-        return carry
-
-    lax.fori_loop(0, columns // block, one_block, 0)
-
-
-def down_of(hidden, down_weight, part, columns):
+    hidden = jnp.concatenate([hidden_ref[slot] for slot in range(experts)], axis=1)
+    weights = w_ref[:, :, start : start + columns].reshape(experts * sliver, columns)
+    out_ref[...] = jnp.dot(hidden, weights, preferred_element_type=jnp.float32).astype(
+        out_ref.dtype
+    )
+
+
+def down_of(hidden, down_weight, start, columns):
     experts, rows, sliver = hidden.shape
     row_block = min(ROW_BLOCK, rows)
 
     def kernel(*refs):
-        down_kernel(part, *refs)
+        down_kernel(start, *refs)
 
     return pl.pallas_call(
         kernel,
@@ -229,12 +220,50 @@
     )(hidden, down_weight)
 
 
+def reorder_kernel(order_ref, rows_ref, out_ref):
+    for place in range(out_ref.shape[0]):
+        out_ref[place] = rows_ref[order_ref[place]]
+
+
+def reordered(order, blocks):
+    return pl.pallas_call(
+        reorder_kernel,
+        in_specs=[pl.BlockSpec(memory_space=pltpu.SMEM), pl.BlockSpec(memory_space=pltpu.VMEM)],
+        out_specs=pl.BlockSpec(memory_space=pltpu.VMEM),
+        out_shape=jax.ShapeDtypeStruct(blocks.shape, blocks.dtype),
+        compiler_params=pltpu.CompilerParams(vmem_limit_bytes=REORDER_LIMIT),
+        cost_estimate=pl.CostEstimate(
+            flops=0, bytes_accessed=4 * blocks.size, transcendentals=0
+        ),
+    )(order, blocks)
+
+
+def row_orders(ways, dim_order):
+    devices = math.prod(ways.values())
+    number = jnp.arange(devices, dtype=jnp.int32)
+    mine = {name: lax.axis_index(name) for name in AXES}
+    weight, left = {}, 1
+    for name in AXES[::-1]:
+        weight[name] = left
+        left *= ways[name]
+    owner, block, stride = jnp.zeros_like(number), jnp.zeros_like(number), 1
+    for digit in dim_order[::-1]:
+        me = mine[digit.name] // digit.stride % digit.size
+        slot = number // stride % digit.size
+        owner += (me + digit.size - slot) % digit.size * digit.stride * weight[digit.name]
+        other = number // weight[digit.name] % ways[digit.name] // digit.stride % digit.size
+        block += (me + digit.size - other) % digit.size * stride
+        stride *= digit.size
+    return owner, block
+
+
 def local(
     tokens, gate_up_weight, down_weight, expert_ids, slot_ids, gate_values, old_place, new_place
 ):
     model_width = tokens.shape[1]
     rows = tokens.shape[0]
-    half = model_width // 2
+    large = -(-model_width * 5 // (12 * MATRIX)) * MATRIX
+    middle = 2 * large
     ways = {name: lax.axis_size(name) for name in AXES}
     cores = 2 if ways["shard"] % 2 == 0 else 1
     x_digits = digits_of("dp", ways["dp"])
@@ -248,16 +277,22 @@
     extra = jnp.concatenate(split_exact(coefficients), axis=1)
     extra = jnp.pad(extra, ((0, 0), (0, -extra.shape[1] % LANES)))
     parts = [
-        jnp.concatenate([tokens[:, :half], extra], axis=1),
-        tokens[:, half:],
+        jnp.concatenate([tokens[:, :large], extra], axis=1),
+        tokens[:, large:middle],
     ]
-    half_shape = gate_up_weight.shape[:3] + (half,)
+    outer_shape = gate_up_weight.shape[:3]
+    first_shape = outer_shape + (large,)
+    second_shape = outer_shape + (model_width - large,)
 
     def take_second(ref):
-        return ref.at[:, :, :, pl.ds(half, half)]
+        return ref.at[:, :, :, pl.ds(large, model_width - large)]
 
     def take_first(ref):
-        return ref.at[:, :, :, pl.ds(0, half)]
+        return ref.at[:, :, :, pl.ds(0, large)]
+
+    rest = lax.all_gather(tokens[:, middle:], AXES, axis=0, tiled=False)
+    owner, block_of = row_orders(ways, dim_order)
+    parts[0], owner, block_of = lax.optimization_barrier((parts[0], owner, block_of))
 
     blocks, held = list(parts), [[], []]
     last = len(routes[0]) - 1
@@ -265,7 +300,7 @@
         if step == last:
             before_last = blocks[0]
         if step == last + 1:
-            first_weights = fetched(gate_up_weight, take_second, half_shape, before_last)
+            first_weights = fetched(gate_up_weight, take_second, second_shape, before_last)
             blocks[1], first_weights = lax.optimization_barrier((blocks[1], first_weights))
         for number in (1, 0):
             digit = (routes[number] + core_digits)[step]
@@ -273,22 +308,28 @@
             blocks[number] = digit.gather(blocks[number], dim)
             held[number].append(digit)
     gathered = [block.reshape(-1, part.shape[1]) for block, part in zip(blocks, parts)]
+    rest = reordered(owner, rest).reshape(-1, model_width - middle)
+    gathered[1] = jnp.concatenate([gathered[1], rest], axis=1)
     sums, next_weights = gate_up_of(
-        gathered[1], None, [first_weights], gate_up_weight, take_first, half_shape
+        gathered[1], None, [first_weights], gate_up_weight, take_first, first_shape
     )
     hidden, down_weight = gate_up_of(
         gathered[0], sums, [next_weights], down_weight, lambda ref: ref, down_weight.shape
     )
     down_weight = resident(down_weight)
+    rest = down_of(hidden, down_weight, middle, model_width - middle)
+    rest = reordered(block_of, rest.reshape(-1, rows, model_width - middle))
+    rest = lax.psum_scatter(rest, AXES, scatter_dimension=0, tiled=False)
     results = []
     for number, route in enumerate(routes):
-        block = down_of(hidden, down_weight, number, half)
-        block = block.reshape([digit.size for digit in dim_order] + [rows, half])
+        block = down_of(hidden, down_weight, number * large, large)
+        block = block.reshape([digit.size for digit in dim_order] + [rows, large])
         held = list(dim_order)
         for digit in core_digits + route[::-1]:
             block = digit.reduce(block, held.index(digit))
             held.remove(digit)
         results.append(block)
+    results.append(rest)
     return jnp.concatenate(results, axis=1)
 
 

time: 79.6 us -> 237 us (2.98)
  waiting for transfers between devices: 29.3 us -> 136 us
  blocking collectives: 0 us -> 40.3 us
  between operations: 0.28 us -> 13.7 us
  starting transfers between devices: 26.6 us -> 16.6 us
  other arithmetic: 3.74 us -> 9.64 us
    reduce_scatter x0 -> x1, waiting for transfers between devices: none -> 101 us  [local(): rest = lax.psum_scatter(rest, AXES, scatter_dimension=0, tiled=False)]
    all_gather x0 -> x1, blocking collectives: none -> 40.3 us  [local(): rest = lax.all_gather(tokens[:, middle:], AXES, axis=0, tiled=False)]
    ppermute x20, starting transfers between devices: 26.6 us -> 16.6 us  [shift(): return lax.ppermute(value, self.name, pairs)]
    ppermute x20, waiting for transfers between devices: 29.3 us -> 34.6 us  [shift(): return lax.ppermute(value, self.name, pairs)]
    another operation x11 -> x10, other arithmetic: 0.72 us -> 3.69 us  [gather(): jnp.stack([block] + [self.shift(block, s) for s in range(1, self.size)],...]
  transfers between devices with their start and end apart: 20 -> 21, of which waited for: 16 -> 14; matrix products, arithmetic and copies ran while one was open for 4% -> 4% of each run, Pallas kernels for 14% -> 5%
where the time goes in v12:
time: 237 us
  waiting for transfers between devices  136 us (57%)
  blocking collectives  40.3 us (17%)
  Pallas kernels  19.5 us (8%)
  starting transfers between devices  16.6 us (7%)
  between operations  13.7 us (6%)
  other arithmetic  9.64 us (4%)
    reduce_scatter x1, waiting for transfers between devices, local(): rest = lax.psum_scatter(rest, AXES, scatter_dimension=0, tiled=False)  101 us
    all_gather x1, blocking collectives, local(): rest = lax.all_gather(tokens[:, middle:], AXES, axis=0, tiled=False)  40.3 us
    ppermute x20, waiting for transfers between devices, shift(): return lax.ppermute(value, self.name, pairs)  34.6 us
    ppermute x20, starting transfers between devices, shift(): return lax.ppermute(value, self.name, pairs)  16.6 us
    pallas_call x2, Pallas kernels, gate_up_of(): pl.pallas_call(kernel, grid=(rows // row_block,), in_specs=specs + [pl.Bl...  8.61 us
    pallas_call x1, Pallas kernels, fetched(): pl.pallas_call(kernel, in_specs=[pl.BlockSpec(memory_space=pl.ANY)] * 2,...  5.18 us
  transfers between devices with their start and end apart: 21, of which 14 were waited for; matrix products, arithmetic and copies ran while one was open for 4% of the time, Pallas kernels for 5%

profile of v12, /device:TPU:0, one launch (start us, length us, event | category | flops | bytes accessed | tf_op | source)
XLA Modules:
  0.0 236.9 jit_solution(14094635007132516575)
XLA Ops:
  6.5 0.8 slice_bitcast_fusion.16
  7.3 4.1 %collective-permute-start.5 = (bf16[8,2560]{1,0:T(8,128)(2,1)S(1)}, bf16[8,2560]{1,0:T(8,128)(2,1)S(1)}, u32[]{:S(2)}, u32[]{:S(2)}) collective-permute-start(bf16[8,2560]{1,0:T(8,128)(2,1)S(1)} %get-tuple-element.39), channel_id=1, source_target_pairs={{0,8},{4,12},{8,0},{12,4},{1,9},{5,13},{9,1},{13,5},{2,10},{6,14},... | collective-permute-start | bytes 122888 | tf_op jit(solution)/shard_map/ppermute | solution.py:46
  11.4 0.7 compare_convert_fusion
  12.2 0.7 select_reduce_fusion
  13.2 0.2 collective-permute-start
  13.4 0.5 collective-permute-done.5
  13.9 1.5 collective-permute-start.6
  15.4 2.9 %collective-permute-done = bf16[8,2688]{1,0:T(8,128)(2,1)S(1)} collective-permute-done((bf16[8,2688]{1,0:T(8,128)(2,1)S(1)}, bf16[8,2688]{1,0:T(8,128)(2,1)S(1)}, u32[]{:S(2)}, u32[]{:S(2)}) %collective-permute-start) | collective-permute-done | bytes 43040 | tf_op jit(solution)/shard_map/ppermute | solution.py:46
  18.4 1.5 collective-permute-start.1
  19.9 1.6 collective-permute-start.7
  21.4 1.5 collective-permute-done.1
  23.0 1.6 collective-permute-start.2
  24.5 0.7 collective-permute-done.7
  25.3 1.6 collective-permute-start.8
  26.9 3.4 %collective-permute-done.2 = bf16[2,2,8,2688]{3,2,1,0:T(8,128)(2,1)S(1)} collective-permute-done((bf16[2,2,8,2688]{3,2,1,0:T(8,128)(2,1)S(1)}, bf16[2,2,8,2688]{3,2,1,0:T(8,128)(2,1)S(1)}, u32[]{:S(2)}, u32[]{:S(2)}) %collective-permute-start.2) | collective-permute-done | bytes 172064 | tf_op jit(solution)/shard_map/ppermute | solution.py:46
  30.4 1.6 collective-permute-start.3
  31.9 5.2 %shard_map.73.refs_1_ = bf16[4,2,256,3584]{3,2,1,0:T(8,128)(2,1)S(1)} custom-call(bf16[4,2,256,6144]{3,2,1,0:T(8,128)(2,1)} %refs_2_.1, bf16[2,2,2,8,2688]{4,3,2,1,0:T(8,128)(2,1)S(1)} %get-tuple-element.30.refs_1_), custom_call_target="tpu_custom_call" | custom-call | bytes 29360128 | tf_op jit(solution)/shard_map/pallas_call | solution.py:88
  37.1 0.9 pad_maximum_fusion.4
  38.0 40.3 %all-gather = bf16[256,1024]{1,0:T(8,128)(2,1)S(1)} all-gather(bf16[8,1024]{1,0:T(8,128)(2,1)S(1)} %slice-done), channel_id=2, replica_groups=mesh['dp'=2,'expert'=4,'shard'=4] {'dp','expert','shard'}, dimensions={0}, use_global_device_ids=true | all-gather | bytes 540672 | tf_op jit(solution)/shard_map/all_gather | solution.py:293
  78.3 0.6 shard_map.74
  78.9 1.1 fusion.65
  80.0 0.4 collective-permute-start.4
  80.4 1.4 pad_maximum_fusion.2
  81.8 0.1 copy.15
  81.9 0.1 pad_maximum_fusion.refs_0_
  82.1 4.0 %shard_map.75 = (f32[256,2048]{1,0:T(8,128)S(1)}, bf16[4,2,256,2560]{3,2,1,0:T(8,128)(2,1)S(1)}) custom-call(bf16[256,3584]{1,0:T(8,128)(2,1)S(1)} %pad_maximum_fusion.refs_0_, bf16[4,2,256,3584]{3,2,1,0:T(8,128)(2,1)S(1)} %shard_map.73.refs_1_, bf16[4,2,256,6144]{3,2,1,0:T(8,128)(2,1)} %refs_2_.1), custom_call_target="tpu_custom_call" | custom-call | flops 3758096384 | bytes 12582912 | tf_op jit(solution)/shard_map/pallas_call | solution.py:170
  86.1 0.1 pad_maximum_fusion.1
  86.3 4.6 %shard_map.76 = (bf16[4,256,256]{2,1,0:T(8,128)(2,1)S(1)}, bf16[4,256,6144]{2,1,0:T(8,128)(2,1)S(1)}) custom-call(bf16[256,2688]{1,0:T(8,128)(2,1)S(1)} %bitcast.96, f32[256,2048]{1,0:T(8,128)S(1)} %get-tuple-element.18.refs_1_, bf16[4,2,256,2560]{3,2,1,0:T(8,128)(2,1)S(1)} %get-tuple-element.19.refs_2_, bf16[4,256,6144]{2,1,0:T(8,128)(2,1)} %refs_3_.1), custom_call_target="tpu_custom_call" | custom-call | flops 2684354560 | bytes 14680064 | tf_op jit(solution)/shard_map/pallas_call | solution.py:170
  90.8 1.5 shard_map.77
  92.4 1.5 shard_map.78
  93.9 0.1 fusion.66
  94.0 0.2 collective-permute-start.10
  94.4 0.4 collective-permute-start.15
  94.8 0.7 shard_map.79
  95.5 1.4 shard_map.80
  96.9 1.2 fusion
  98.2 1.5 collective-permute-start.11
  99.7 1.2 fusion.1
  101.0 7.0 %collective-permute-done.11 = bf16[2,2,2,8,2560]{4,3,2,1,0:T(8,128)(2,1)S(1)} collective-permute-done((bf16[2,2,2,8,2560]{4,3,2,1,0:T(8,128)(2,1)S(1)}, bf16[2,2,2,8,2560]{4,3,2,1,0:T(8,128)(2,1)S(1)}, u32[]{:S(2)}, u32[]{:S(2)}) %collective-permute-start.11) | collective-permute-done | bytes 327712 | tf_op jit(solution)/shard_map/ppermute | solution.py:46
  108.2 3.3 %collective-permute-done.16 = bf16[2,2,2,8,2560]{4,3,2,1,0:T(8,128)(2,1)S(1)} collective-permute-done((bf16[2,2,2,8,2560]{4,3,2,1,0:T(8,128)(2,1)S(1)}, bf16[2,2,2,8,2560]{4,3,2,1,0:T(8,128)(2,1)S(1)}, u32[]{:S(2)}, u32[]{:S(2)}) %collective-permute-start.16) | collective-permute-done | bytes 327712 | tf_op jit(solution)/shard_map/ppermute | solution.py:46
  111.7 3.0 %collective-permute-done.12 = bf16[2,2,8,2560]{3,2,1,0:T(8,128)(2,1)S(1)} collective-permute-done((bf16[2,2,8,2560]{3,2,1,0:T(8,128)(2,1)S(1)}, bf16[2,2,8,2560]{3,2,1,0:T(8,128)(2,1)S(1)}, u32[]{:S(2)}, u32[]{:S(2)}) %collective-permute-start.12) | collective-permute-done | bytes 163872 | tf_op jit(solution)/shard_map/ppermute | solution.py:46
  114.8 2.2 collective-permute-done.17
  117.1 2.1 collective-permute-done.13
  119.3 3.1 %collective-permute-done.18 = bf16[2,8,2560]{2,1,0:T(8,128)(2,1)S(1)} collective-permute-done((bf16[2,8,2560]{2,1,0:T(8,128)(2,1)S(1)}, bf16[2,8,2560]{2,1,0:T(8,128)(2,1)S(1)}, u32[]{:S(2)}, u32[]{:S(2)}) %collective-permute-start.18) | collective-permute-done | bytes 81952 | tf_op jit(solution)/shard_map/ppermute | solution.py:46
  122.5 2.1 collective-permute-done.14
  124.7 2.7 %collective-permute-done.19 = bf16[8,2560]{1,0:T(8,128)(2,1)S(1)} collective-permute-done((bf16[8,2560]{1,0:T(8,128)(2,1)S(1)}, bf16[8,2560]{1,0:T(8,128)(2,1)S(1)}, u32[]{:S(2)}, u32[]{:S(2)}) %collective-permute-start.19) | collective-permute-done | bytes 40992 | tf_op jit(solution)/shard_map/ppermute | solution.py:46
  127.4 101.2 %reduce-scatter.2.cloned.1.call-done = bf16[1,8,1024]{2,1,0:T(8,128)(2,1)} async-done(((bf16[32,8,1024]{2,1,0:T(8,128)(2,1)}), bf16[1,8,1024]{2,1,0:T(8,128)(2,1)}) %reduce-scatter.2.cloned.1.call-update) | async-done | bytes 16400 | tf_op jit(solution)/shard_map/reduce_scatter | solution.py:322
  228.7 1.4 pad_maximum_fusion.9
  (49 shorter events, 1.6 us)
Async XLA Ops:
  6.5 222.2 %reduce-scatter.2.cloned.1.call-start = ((), (), s32[]{:S(2)}) async-start(), calls=%async_computation.1 | async-start | bytes 540672 | tf_op jit(solution)/shard_map/reduce_scatter | solution.py:322
  7.3 6.5 %collective-permute-start.5 = (bf16[8,2560]{1,0:T(8,128)(2,1)S(1)}, bf16[8,2560]{1,0:T(8,128)(2,1)S(1)}, u32[]{:S(2)}, u32[]{:S(2)}) collective-permute-start(bf16[8,2560]{1,0:T(8,128)(2,1)S(1)} %get-tuple-element.39), channel_id=1, source_target_pairs={{0,8},{4,12},{8,0},{12,4},{1,9},{5,13},{9,1},{13,5},{2,10},{6,14},... | collective-permute-start | bytes 122888 | tf_op jit(solution)/shard_map/ppermute | solution.py:46
  13.2 5.2 %collective-permute-start = (bf16[8,2688]{1,0:T(8,128)(2,1)S(1)}, bf16[8,2688]{1,0:T(8,128)(2,1)S(1)}, u32[]{:S(2)}, u32[]{:S(2)}) collective-permute-start(bf16[8,2688]{1,0:T(8,128)(2,1)S(1)} %pad_maximum_fusion.12), channel_id=1, source_target_pairs={{0,8},{4,12},{8,0},{12,4},{1,9},{5,13},{9,1},{13,5},{2,10},{6,14},... | collective-permute-start | bytes 129032 | tf_op jit(solution)/shard_map/ppermute | solution.py:46
  13.9 6.0 %collective-permute-start.6 = (bf16[2,8,2560]{2,1,0:T(8,128)(2,1)S(1)}, bf16[2,8,2560]{2,1,0:T(8,128)(2,1)S(1)}, u32[]{:S(2)}, u32[]{:S(2)}) collective-permute-start(bf16[2,8,2560]{2,1,0:T(8,128)(2,1)S(1)} %get-tuple-element.43), channel_id=1, source_target_pairs={{0,4},{4,0},{8,12},{12,8},{1,5},{5,1},{9,13},{13,9},{2,6},{6,2},{1... | collective-permute-start | bytes 245768 | tf_op jit(solution)/shard_map/ppermute | solution.py:46
  18.4 4.6 %collective-permute-start.1 = (bf16[2,8,2688]{2,1,0:T(8,128)(2,1)S(1)}, bf16[2,8,2688]{2,1,0:T(8,128)(2,1)S(1)}, u32[]{:S(2)}, u32[]{:S(2)}) collective-permute-start(bf16[2,8,2688]{2,1,0:T(8,128)(2,1)S(1)} %get-tuple-element.41), channel_id=1, source_target_pairs={{0,4},{4,0},{8,12},{12,8},{1,5},{5,1},{9,13},{13,9},{2,6},{6,2},{1... | collective-permute-start | bytes 258056 | tf_op jit(solution)/shard_map/ppermute | solution.py:46
  19.9 5.4 %collective-permute-start.7 = (bf16[2,2,8,2560]{3,2,1,0:T(8,128)(2,1)S(1)}, bf16[2,2,8,2560]{3,2,1,0:T(8,128)(2,1)S(1)}, u32[]{:S(2)}, u32[]{:S(2)}) collective-permute-start(bf16[2,2,8,2560]{3,2,1,0:T(8,128)(2,1)S(1)} %get-tuple-element.36), channel_id=1, source_target_pairs={{0,16},{16,0},{1,17},{17,1},{2,18},{18,2},{3,19},{19,3},{4,20},{20... | collective-permute-start | bytes 491528 | tf_op jit(solution)/shard_map/ppermute | solution.py:46
  23.0 7.4 %collective-permute-start.2 = (bf16[2,2,8,2688]{3,2,1,0:T(8,128)(2,1)S(1)}, bf16[2,2,8,2688]{3,2,1,0:T(8,128)(2,1)S(1)}, u32[]{:S(2)}, u32[]{:S(2)}) collective-permute-start(bf16[2,2,8,2688]{3,2,1,0:T(8,128)(2,1)S(1)} %get-tuple-element.34), channel_id=1, source_target_pairs={{0,2},{1,3},{2,0},{3,1},{4,6},{5,7},{6,4},{7,5},{8,10},{9,11},{10,... | collective-permute-start | bytes 516104 | tf_op jit(solution)/shard_map/ppermute | solution.py:46
  25.3 11.8 %collective-permute-start.8 = (bf16[2,2,2,8,2560]{4,3,2,1,0:T(8,128)(2,1)S(1)}, bf16[2,2,2,8,2560]{4,3,2,1,0:T(8,128)(2,1)S(1)}, u32[]{:S(2)}, u32[]{:S(2)}) collective-permute-start(bf16[2,2,2,8,2560]{4,3,2,1,0:T(8,128)(2,1)S(1)} %get-tuple-element.32), channel_id=1, source_target_pairs={{0,2},{1,3},{2,0},{3,1},{4,6},{5,7},{6,4},{7,5},{8,10},{9,11},{10,... | collective-permute-start | bytes 983048 | tf_op jit(solution)/shard_map/ppermute | solution.py:46
  30.4 48.5 %collective-permute-start.3 = (bf16[2,2,2,8,2688]{4,3,2,1,0:T(8,128)(2,1)S(1)}, bf16[2,2,2,8,2688]{4,3,2,1,0:T(8,128)(2,1)}, u32[]{:S(2)}, u32[]{:S(2)}) collective-permute-start(bf16[2,2,2,8,2688]{4,3,2,1,0:T(8,128)(2,1)S(1)} %get-tuple-element.30.refs_1_), channel_id=1, source_target_pairs={{0,16},{16,0},{1,17},{17,1},{2,18},{18,2},{3,19},{19,3},{4,20},{20... | collective-permute-start | bytes 1032200 | tf_op jit(solution)/shard_map/ppermute | solution.py:46
  37.1 0.9 slice-start
  38.0 42.4 %collective-permute-start.9 = (bf16[2,2,2,2,8,2560]{5,4,3,2,0,1:T(8,128)(2,1)}, bf16[2,2,2,2,8,2560]{5,4,3,2,0,1:T(8,128)(2,1)}, u32[]{:S(2)}, u32[]{:S(2)}) collective-permute-start(bf16[2,2,2,2,8,2560]{5,4,3,2,0,1:T(8,128)(2,1)} %pad_maximum_fusion.4), channel_id=1, source_target_pairs={{0,1},{1,0},{2,3},{3,2},{4,5},{5,4},{6,7},{7,6},{8,9},{9,8},{10,11... | collective-permute-start | bytes 1966088 | tf_op jit(solution)/shard_map/ppermute | solution.py:46
  80.0 6.1 %collective-permute-start.4 = (bf16[2,2,2,2,8,2688]{5,4,3,2,1,0:T(8,128)(2,1)S(1)}, bf16[2,2,2,2,8,2688]{5,4,3,2,1,0:T(8,128)(2,1)S(1)}, u32[]{:S(2)}, u32[]{:S(2)}) collective-permute-start(bf16[2,2,2,2,8,2688]{5,4,3,2,1,0:T(8,128)(2,1)S(1)} %get-tuple-element.28), channel_id=1, source_target_pairs={{0,1},{1,0},{2,3},{3,2},{4,5},{5,4},{6,7},{7,6},{8,9},{9,8},{10,11... | collective-permute-start | bytes 2064392 | tf_op jit(solution)/shard_map/ppermute | solution.py:46
  94.0 2.9 %collective-permute-start.10 = (bf16[2,2,2,2,8,2560]{5,4,3,2,1,0:T(8,128)(2,1)S(1)}, bf16[2,2,2,2,8,2560]{5,4,3,2,1,0:T(8,128)(2,1)}, u32[]{:S(2)}, u32[]{:S(2)}) collective-permute-start(bf16[2,2,2,2,8,2560]{5,4,3,2,1,0:T(8,128)(2,1)S(1)} %bitcast.105), channel_id=1, source_target_pairs={{0,1},{1,0},{2,3},{3,2},{4,5},{5,4},{6,7},{7,6},{8,9},{9,8},{10,11... | collective-permute-start | bytes 1966088 | tf_op jit(solution)/shard_map/ppermute | solution.py:46
  94.4 5.3 %collective-permute-start.15 = (bf16[2,2,2,2,8,2560]{5,4,3,2,0,1:T(8,128)(2,1)S(1)}, bf16[2,2,2,2,8,2560]{5,4,3,2,0,1:T(8,128)(2,1)}, u32[]{:S(2)}, u32[]{:S(2)}) collective-permute-start(bf16[2,2,2,2,8,2560]{5,4,3,2,0,1:T(8,128)(2,1)S(1)} %copy.16), channel_id=1, source_target_pairs={{0,1},{1,0},{2,3},{3,2},{4,5},{5,4},{6,7},{7,6},{8,9},{9,8},{10,11... | collective-permute-start | bytes 1966088 | tf_op jit(solution)/shard_map/ppermute | solution.py:46
  98.2 9.8 %collective-permute-start.11 = (bf16[2,2,2,8,2560]{4,3,2,1,0:T(8,128)(2,1)S(1)}, bf16[2,2,2,8,2560]{4,3,2,1,0:T(8,128)(2,1)S(1)}, u32[]{:S(2)}, u32[]{:S(2)}) collective-permute-start(bf16[2,2,2,8,2560]{4,3,2,1,0:T(8,128)(2,1)S(1)} %slice_bitcast_fusion.2), channel_id=1, source_target_pairs={{0,16},{16,0},{1,17},{17,1},{2,18},{18,2},{3,19},{19,3},{4,20},{20... | collective-permute-start | bytes 983048 | tf_op jit(solution)/shard_map/ppermute | solution.py:46
  101.0 10.5 %collective-permute-start.16 = (bf16[2,2,2,8,2560]{4,3,2,1,0:T(8,128)(2,1)S(1)}, bf16[2,2,2,8,2560]{4,3,2,1,0:T(8,128)(2,1)S(1)}, u32[]{:S(2)}, u32[]{:S(2)}) collective-permute-start(bf16[2,2,2,8,2560]{4,3,2,1,0:T(8,128)(2,1)S(1)} %slice_bitcast_fusion), channel_id=1, source_target_pairs={{0,2},{1,3},{2,0},{3,1},{4,6},{5,7},{6,4},{7,5},{8,10},{9,11},{10,... | collective-permute-start | bytes 983048 | tf_op jit(solution)/shard_map/ppermute | solution.py:46
  108.1 6.5 %collective-permute-start.12 = (bf16[2,2,8,2560]{3,2,1,0:T(8,128)(2,1)S(1)}, bf16[2,2,8,2560]{3,2,1,0:T(8,128)(2,1)S(1)}, u32[]{:S(2)}, u32[]{:S(2)}) collective-permute-start(bf16[2,2,8,2560]{3,2,1,0:T(8,128)(2,1)S(1)} %slice_bitcast_fusion.6), channel_id=1, source_target_pairs={{0,2},{1,3},{2,0},{3,1},{4,6},{5,7},{6,4},{7,5},{8,10},{9,11},{10,... | collective-permute-start | bytes 491528 | tf_op jit(solution)/shard_map/ppermute | solution.py:46
  111.6 5.4 %collective-permute-start.17 = (bf16[2,2,8,2560]{3,2,1,0:T(8,128)(2,1)S(1)}, bf16[2,2,8,2560]{3,2,1,0:T(8,128)(2,1)S(1)}, u32[]{:S(2)}, u32[]{:S(2)}) collective-permute-start(bf16[2,2,8,2560]{3,2,1,0:T(8,128)(2,1)S(1)} %slice_bitcast_fusion.4), channel_id=1, source_target_pairs={{0,16},{16,0},{1,17},{17,1},{2,18},{18,2},{3,19},{19,3},{4,20},{20... | collective-permute-start | bytes 491528 | tf_op jit(solution)/shard_map/ppermute | solution.py:46
  114.7 4.5 %collective-permute-start.13 = (bf16[2,8,2560]{2,1,0:T(8,128)(2,1)S(1)}, bf16[2,8,2560]{2,1,0:T(8,128)(2,1)S(1)}, u32[]{:S(2)}, u32[]{:S(2)}) collective-permute-start(bf16[2,8,2560]{2,1,0:T(8,128)(2,1)S(1)} %slice_bitcast_fusion.10), channel_id=1, source_target_pairs={{0,4},{4,0},{8,12},{12,8},{1,5},{5,1},{9,13},{13,9},{2,6},{6,2},{1... | collective-permute-start | bytes 245768 | tf_op jit(solution)/shard_map/ppermute | solution.py:46
  117.0 5.4 %collective-permute-start.18 = (bf16[2,8,2560]{2,1,0:T(8,128)(2,1)S(1)}, bf16[2,8,2560]{2,1,0:T(8,128)(2,1)S(1)}, u32[]{:S(2)}, u32[]{:S(2)}) collective-permute-start(bf16[2,8,2560]{2,1,0:T(8,128)(2,1)S(1)} %slice_bitcast_fusion.8), channel_id=1, source_target_pairs={{0,4},{4,0},{8,12},{12,8},{1,5},{5,1},{9,13},{13,9},{2,6},{6,2},{1... | collective-permute-start | bytes 245768 | tf_op jit(solution)/shard_map/ppermute | solution.py:46
  119.3 5.4 %collective-permute-start.14 = (bf16[8,2560]{1,0:T(8,128)(2,1)S(1)}, bf16[8,2560]{1,0:T(8,128)(2,1)S(1)}, u32[]{:S(2)}, u32[]{:S(2)}) collective-permute-start(bf16[8,2560]{1,0:T(8,128)(2,1)S(1)} %slice_bitcast_fusion.14), channel_id=1, source_target_pairs={{0,8},{4,12},{8,0},{12,4},{1,9},{5,13},{9,1},{13,5},{2,10},{6,14},... | collective-permute-start | bytes 122888 | tf_op jit(solution)/shard_map/ppermute | solution.py:46
  122.5 5.0 %collective-permute-start.19 = (bf16[8,2560]{1,0:T(8,128)(2,1)S(1)}, bf16[8,2560]{1,0:T(8,128)(2,1)S(1)}, u32[]{:S(2)}, u32[]{:S(2)}) collective-permute-start(bf16[8,2560]{1,0:T(8,128)(2,1)S(1)} %slice_bitcast_fusion.12), channel_id=1, source_target_pairs={{0,8},{4,12},{8,0},{12,4},{1,9},{5,13},{9,1},{13,5},{2,10},{6,14},... | collective-permute-start | bytes 122888 | tf_op jit(solution)/shard_map/ppermute | solution.py:46
Sparse Core Ops, SparseCore 0:
  97.0 131.6 reduce-scatter.1

commit v13 on v10

--- a/solution.py
+++ b/solution.py
@@ -15,10 +15,11 @@
 DOWN_LIMIT = 8 * 2**20
 
 
-def pack_kernel(tokens_ref, ids_ref, gates_ref, old_ref, new_ref, out_ref):
-    rows, width = tokens_ref.shape
+def pack_kernel(tokens_ref, ids_ref, gates_ref, old_ref, new_ref, out_ref, other_ref):
+    rows, width = tokens_ref.shape[0], tokens_ref.shape[1] - other_ref.shape[1]
+    other_ref[...] = tokens_ref[:, width:]
     choices = ids_ref.shape[0]
-    out_ref[:, :width] = tokens_ref[...]
+    out_ref[:, :width] = tokens_ref[:, :width]
     square = (rows, rows)
     diagonal = lax.broadcasted_iota(jnp.int32, square, 0) == lax.broadcasted_iota(
         jnp.int32, square, 1
@@ -52,15 +53,18 @@
     small = pl.BlockSpec((choices, rows), lambda i: (0, 0))
     place = pl.BlockSpec((1, experts), lambda i: (0, 0))
     operands = (tokens, expert_ids.T, gate_values.T, old_place[None, :], new_place[None, :])
+    model_width = tokens.shape[1]
     return pl.pallas_call(
         pack_kernel,
         grid=(1,),
-        in_specs=[pl.BlockSpec((rows, width), lambda i: (0, 0)), small, small, place, place],
-        out_specs=pl.BlockSpec((rows, width + lanes), lambda i: (0, 0)),
-        out_shape=jax.ShapeDtypeStruct((rows, width + lanes), tokens.dtype),
-        cost_estimate=pl.CostEstimate(
-            flops=0, bytes_accessed=4 * rows * width, transcendentals=0
-        ),
+        in_specs=[pl.BlockSpec(tokens.shape, lambda i: (0, 0)), small, small, place, place],
+        out_specs=[pl.BlockSpec(memory_space=pltpu.VMEM)] * 2,
+        out_shape=[
+            pltpu.VMEM((rows, width + lanes), tokens.dtype),
+            pltpu.VMEM((rows, model_width - width), tokens.dtype),
+        ],
+        compiler_params=pltpu.CompilerParams(vmem_limit_bytes=FETCH_LIMIT),
+        cost_estimate=pl.CostEstimate(flops=0, bytes_accessed=4 * tokens.size, transcendentals=0),
     )(*(in_hbm(operand) for operand in operands))
 
 
@@ -286,7 +290,7 @@
     routes = [z_digits + y_digits + x_digits, z_digits + x_digits + y_digits]
 
     choices = expert_ids.shape[1]
-    parts = [packed(tokens, half, expert_ids, gate_values, old_place, new_place), tokens[:, half:]]
+    parts = packed(tokens, half, expert_ids, gate_values, old_place, new_place)
     half_shape = gate_up_weight.shape[:3] + (half,)
 
     def take_second(ref):

time: 80.5 us -> 80.1 us (level)
  starting transfers between devices: 25.5 us -> 31 us
  waiting for transfers between devices: 30.7 us -> 27 us
  other arithmetic: 2.91 us -> 2.1 us
    ppermute x20, starting transfers between devices: 25.5 us -> 31 us  [shift(): return lax.ppermute(value, self.name, pairs)]
    ppermute x20, waiting for transfers between devices: 30.7 us -> 27 us  [shift(): return lax.ppermute(value, self.name, pairs)]
  transfers between devices with their start and end apart: 20 -> 20, of which waited for: 16 -> 15; matrix products, arithmetic and copies ran while one was open for 3% -> 2% of each run, Pallas kernels for 16% -> 14%
where the time goes in v13:
time: 80.1 us; the launch traced here: 79.9 us
  starting transfers between devices  31 us (39%)
  waiting for transfers between devices  27 us (34%)
  Pallas kernels  19 us (24%)
  other arithmetic  2.1 us (3%)
    ppermute x20, starting transfers between devices, shift(): return lax.ppermute(value, self.name, pairs)  31 us
    ppermute x20, waiting for transfers between devices, shift(): return lax.ppermute(value, self.name, pairs)  27 us
    pallas_call x2, Pallas kernels, gate_up_of(): pl.pallas_call(kernel, grid=(rows // row_block,), in_specs=specs + [pl.Bl...  9.27 us
    pallas_call x1, Pallas kernels, fetched(): pl.pallas_call(kernel, in_specs=[pl.BlockSpec(memory_space=pl.ANY)] * 2,...  4.58 us
    pallas_call x2, Pallas kernels, down_of(): pl.pallas_call(kernel, grid=(rows // row_block,), in_specs=[pl.BlockSpec(...  3.98 us
  transfers between devices with their start and end apart: 20, of which 15 were waited for; matrix products, arithmetic and copies ran while one was open for 2% of the time, Pallas kernels for 14%

profile of v13, /device:TPU:0, one launch (start us, length us, event | category | flops | bytes accessed | tf_op | source)
XLA Modules:
  0.0 79.9 jit_solution(13531937384132782312)
XLA Ops:
  0.0 1.2 %shard_map.73 = (bf16[8,3200]{1,0:T(8,128)(2,1)S(1)}, bf16[8,3072]{1,0:T(8,128)(2,1)S(1)}) custom-call(bf16[8,6144]{1,0:T(8,128)(2,1)} %tokens_ref.1, s32[2,8]{1,0:T(2,128)} %bitcast.114, f32[2,8]{1,0:T(2,128)} %bitcast.115, s32[1,4]{1,0:T(1,128)} %bitcast.116, s32[1,4]{1,0:T(1,128)} %bitcast.117), custom_call_target="tpu_custom_call" | custom-call | bytes 196608 | tf_op jit(solution)/shard_map/pallas_call | solution.py:57
  1.2 4.1 %collective-permute-start.5 = (bf16[8,3072]{1,0:T(8,128)(2,1)S(1)}, bf16[8,3072]{1,0:T(8,128)(2,1)S(1)}, u32[]{:S(2)}, u32[]{:S(2)}) collective-permute-start(bf16[8,3072]{1,0:T(8,128)(2,1)S(1)} %get-tuple-element.14), channel_id=1, source_target_pairs={{0,8},{4,12},{8,0},{12,4},{1,9},{5,13},{9,1},{13,5},{2,10},{6,14},... | collective-permute-start | bytes 147464 | tf_op jit(solution)/shard_map/ppermute | solution.py:81
  5.3 2.5 %collective-permute-done.5 = bf16[8,3072]{1,0:T(8,128)(2,1)S(1)} collective-permute-done((bf16[8,3072]{1,0:T(8,128)(2,1)S(1)}, bf16[8,3072]{1,0:T(8,128)(2,1)S(1)}, u32[]{:S(2)}, u32[]{:S(2)}) %collective-permute-start.5) | collective-permute-done | bytes 49184 | tf_op jit(solution)/shard_map/ppermute | solution.py:81
  7.8 2.2 %collective-permute-start.6 = (bf16[2,8,3072]{2,1,0:T(8,128)(2,1)S(1)}, bf16[2,8,3072]{2,1,0:T(8,128)(2,1)S(1)}, u32[]{:S(2)}, u32[]{:S(2)}) collective-permute-start(bf16[2,8,3072]{2,1,0:T(8,128)(2,1)S(1)} %get-tuple-element.38), channel_id=1, source_target_pairs={{0,4},{4,0},{8,12},{12,8},{1,5},{5,1},{9,13},{13,9},{2,6},{6,2},{1... | collective-permute-start | bytes 294920 | tf_op jit(solution)/shard_map/ppermute | solution.py:81
  10.0 0.4 collective-permute-done
  10.4 1.5 %collective-permute-start.1 = (bf16[2,8,3200]{2,1,0:T(8,128)(2,1)S(1)}, bf16[2,8,3200]{2,1,0:T(8,128)(2,1)S(1)}, u32[]{:S(2)}, u32[]{:S(2)}) collective-permute-start(bf16[2,8,3200]{2,1,0:T(8,128)(2,1)S(1)} %get-tuple-element.36), channel_id=1, source_target_pairs={{0,4},{4,0},{8,12},{12,8},{1,5},{5,1},{9,13},{13,9},{2,6},{6,2},{1... | collective-permute-start | bytes 307208 | tf_op jit(solution)/shard_map/ppermute | solution.py:81
  11.9 1.6 %collective-permute-done.6 = bf16[2,8,3072]{2,1,0:T(8,128)(2,1)S(1)} collective-permute-done((bf16[2,8,3072]{2,1,0:T(8,128)(2,1)S(1)}, bf16[2,8,3072]{2,1,0:T(8,128)(2,1)S(1)}, u32[]{:S(2)}, u32[]{:S(2)}) %collective-permute-start.6) | collective-permute-done | bytes 98336 | tf_op jit(solution)/shard_map/ppermute | solution.py:81
  13.5 1.6 %collective-permute-start.7 = (bf16[2,2,8,3072]{3,2,1,0:T(8,128)(2,1)S(1)}, bf16[2,2,8,3072]{3,2,1,0:T(8,128)(2,1)S(1)}, u32[]{:S(2)}, u32[]{:S(2)}) collective-permute-start(bf16[2,2,8,3072]{3,2,1,0:T(8,128)(2,1)S(1)} %get-tuple-element.34), channel_id=1, source_target_pairs={{0,16},{16,0},{1,17},{17,1},{2,18},{18,2},{3,19},{19,3},{4,20},{20... | collective-permute-start | bytes 589832 | tf_op jit(solution)/shard_map/ppermute | solution.py:81
  15.2 1.6 %collective-permute-start.2 = (bf16[2,2,8,3200]{3,2,1,0:T(8,128)(2,1)S(1)}, bf16[2,2,8,3200]{3,2,1,0:T(8,128)(2,1)S(1)}, u32[]{:S(2)}, u32[]{:S(2)}) collective-permute-start(bf16[2,2,8,3200]{3,2,1,0:T(8,128)(2,1)S(1)} %get-tuple-element.32), channel_id=1, source_target_pairs={{0,2},{1,3},{2,0},{3,1},{4,6},{5,7},{6,4},{7,5},{8,10},{9,11},{10,... | collective-permute-start | bytes 614408 | tf_op jit(solution)/shard_map/ppermute | solution.py:81
  16.7 2.5 %collective-permute-done.7 = bf16[2,2,8,3072]{3,2,1,0:T(8,128)(2,1)S(1)} collective-permute-done((bf16[2,2,8,3072]{3,2,1,0:T(8,128)(2,1)S(1)}, bf16[2,2,8,3072]{3,2,1,0:T(8,128)(2,1)S(1)}, u32[]{:S(2)}, u32[]{:S(2)}) %collective-permute-start.7) | collective-permute-done | bytes 196640 | tf_op jit(solution)/shard_map/ppermute | solution.py:81
  19.3 1.6 %collective-permute-start.8 = (bf16[2,2,2,8,3072]{4,3,2,1,0:T(8,128)(2,1)S(1)}, bf16[2,2,2,8,3072]{4,3,2,1,0:T(8,128)(2,1)S(1)}, u32[]{:S(2)}, u32[]{:S(2)}) collective-permute-start(bf16[2,2,2,8,3072]{4,3,2,1,0:T(8,128)(2,1)S(1)} %get-tuple-element.30), channel_id=1, source_target_pairs={{0,2},{1,3},{2,0},{3,1},{4,6},{5,7},{6,4},{7,5},{8,10},{9,11},{10,... | collective-permute-start | bytes 1179656 | tf_op jit(solution)/shard_map/ppermute | solution.py:81
  20.9 1.5 %collective-permute-done.2 = bf16[2,2,8,3200]{3,2,1,0:T(8,128)(2,1)S(1)} collective-permute-done((bf16[2,2,8,3200]{3,2,1,0:T(8,128)(2,1)S(1)}, bf16[2,2,8,3200]{3,2,1,0:T(8,128)(2,1)S(1)}, u32[]{:S(2)}, u32[]{:S(2)}) %collective-permute-start.2) | collective-permute-done | bytes 204832 | tf_op jit(solution)/shard_map/ppermute | solution.py:81
  22.4 1.7 %collective-permute-start.3 = (bf16[2,2,2,8,3200]{4,3,2,1,0:T(8,128)(2,1)S(1)}, bf16[2,2,2,8,3200]{4,3,2,1,0:T(8,128)(2,1)S(1)}, u32[]{:S(2)}, u32[]{:S(2)}) collective-permute-start(bf16[2,2,2,8,3200]{4,3,2,1,0:T(8,128)(2,1)S(1)} %get-tuple-element.28.refs_1_), channel_id=1, source_target_pairs={{0,16},{16,0},{1,17},{17,1},{2,18},{18,2},{3,19},{19,3},{4,20},{20... | collective-permute-start | bytes 1228808 | tf_op jit(solution)/shard_map/ppermute | solution.py:81
  24.2 4.6 %shard_map.74.refs_1_ = bf16[4,2,256,3072]{3,2,1,0:T(8,128)(2,1)S(1)} custom-call(bf16[4,2,256,6144]{3,2,1,0:T(8,128)(2,1)} %refs_2_.1, bf16[2,2,2,8,3200]{4,3,2,1,0:T(8,128)(2,1)S(1)} %get-tuple-element.28.refs_1_), custom_call_target="tpu_custom_call" | custom-call | bytes 25165824 | tf_op jit(solution)/shard_map/pallas_call | solution.py:123
  28.7 0.7 collective-permute-done.8
  29.6 0.9 %collective-permute-done.3 = bf16[2,2,2,8,3200]{4,3,2,1,0:T(8,128)(2,1)S(1)} collective-permute-done((bf16[2,2,2,8,3200]{4,3,2,1,0:T(8,128)(2,1)S(1)}, bf16[2,2,2,8,3200]{4,3,2,1,0:T(8,128)(2,1)S(1)}, u32[]{:S(2)}, u32[]{:S(2)}) %collective-permute-start.3) | collective-permute-done | bytes 409632 | tf_op jit(solution)/shard_map/ppermute | solution.py:81
  30.5 0.1 fusion.16
  30.7 1.2 %collective-permute-done.9 = bf16[2,2,2,2,8,3072]{5,4,3,2,0,1:T(8,128)(2,1)S(1)} collective-permute-done((bf16[2,2,2,2,8,3072]{5,4,3,2,0,1:T(8,128)(2,1)S(1)}, bf16[2,2,2,2,8,3072]{5,4,3,2,0,1:T(8,128)(2,1)S(1)}, u32[]{:S(2)}, u32[]{:S(2)}) %collective-permute-start.9) | collective-permute-done | bytes 786464 | tf_op jit(solution)/shard_map/ppermute | solution.py:81
  31.8 0.1 pad_maximum_fusion.1
  32.0 0.1 copy.8
  32.1 4.7 %shard_map.75 = (f32[256,2048]{1,0:T(8,128)S(1)}, bf16[4,2,256,3072]{3,2,1,0:T(8,128)(2,1)S(1)}) custom-call(bf16[256,3072]{1,0:T(8,128)(2,1)S(1)} %bitcast.96, bf16[4,2,256,3072]{3,2,1,0:T(8,128)(2,1)S(1)} %shard_map.74.refs_1_, bf16[4,2,256,6144]{3,2,1,0:T(8,128)(2,1)} %refs_2_.1), custom_call_target="tpu_custom_call" | custom-call | flops 3221225472 | bytes 14680064 | tf_op jit(solution)/shard_map/pallas_call | solution.py:216
  36.8 0.2 pad_maximum_fusion
  37.0 4.6 %shard_map.76 = (bf16[4,256,256]{2,1,0:T(8,128)(2,1)S(1)}, bf16[4,256,6144]{2,1,0:T(8,128)(2,1)S(1)}) custom-call(bf16[256,3200]{1,0:T(8,128)(2,1)S(1)} %bitcast.95, f32[256,2048]{1,0:T(8,128)S(1)} %get-tuple-element.17.refs_1_, bf16[4,2,256,3072]{3,2,1,0:T(8,128)(2,1)S(1)} %get-tuple-element.18.refs_2_, bf16[4,256,6144]{2,1,0:T(8,128)(2,1)} %refs_3_.1), custom_call_target="tpu_custom_call" | custom-call | flops 3221225472 | bytes 14680064 | tf_op jit(solution)/shard_map/pallas_call | solution.py:216
  41.6 2.0 %shard_map.77 = bf16[256,3072]{1,0:T(8,128)(2,1)S(1)} custom-call(bf16[4,256,256]{2,1,0:T(8,128)(2,1)S(1)} %get-tuple-element.19.refs_0_, bf16[4,256,6144]{2,1,0:T(8,128)(2,1)S(1)} %get-tuple-element.20.refs_1_), custom_call_target="tpu_custom_call" | custom-call | flops 1610612736 | bytes 8388608 | tf_op jit(solution)/shard_map/pallas_call | solution.py:259
  43.6 0.1 fusion.17
  43.7 0.2 collective-permute-start.10
  43.9 2.0 %shard_map.78 = bf16[256,3072]{1,0:T(8,128)(2,1)S(1)} custom-call(bf16[4,256,256]{2,1,0:T(8,128)(2,1)S(1)} %get-tuple-element.19.refs_0_, bf16[4,256,6144]{2,1,0:T(8,128)(2,1)S(1)} %get-tuple-element.20.refs_1_), custom_call_target="tpu_custom_call" | custom-call | flops 1610612736 | bytes 8388608 | tf_op jit(solution)/shard_map/pallas_call | solution.py:259
  45.9 0.1 fusion.18
  46.1 0.4 collective-permute-start.15
  46.5 0.2 fusion
  46.8 1.6 %collective-permute-start.11 = (bf16[2,2,2,8,3072]{4,3,2,1,0:T(8,128)(2,1)S(1)}, bf16[2,2,2,8,3072]{4,3,2,1,0:T(8,128)(2,1)S(1)}, u32[]{:S(2)}, u32[]{:S(2)}) collective-permute-start(bf16[2,2,2,8,3072]{4,3,2,1,0:T(8,128)(2,1)S(1)} %slice_bitcast_fusion.2), channel_id=1, source_target_pairs={{0,16},{16,0},{1,17},{17,1},{2,18},{18,2},{3,19},{19,3},{4,20},{20... | collective-permute-start | bytes 1179656 | tf_op jit(solution)/shard_map/ppermute | solution.py:81
  48.3 0.1 collective-permute-done.15
  48.4 0.2 fusion.1
  48.7 1.6 %collective-permute-start.16 = (bf16[2,2,2,8,3072]{4,3,2,1,0:T(8,128)(2,1)S(1)}, bf16[2,2,2,8,3072]{4,3,2,1,0:T(8,128)(2,1)S(1)}, u32[]{:S(2)}, u32[]{:S(2)}) collective-permute-start(bf16[2,2,2,8,3072]{4,3,2,1,0:T(8,128)(2,1)S(1)} %slice_bitcast_fusion), channel_id=1, source_target_pairs={{0,2},{1,3},{2,0},{3,1},{4,6},{5,7},{6,4},{7,5},{8,10},{9,11},{10,... | collective-permute-start | bytes 1179656 | tf_op jit(solution)/shard_map/ppermute | solution.py:81
  50.3 7.7 %collective-permute-done.11 = bf16[2,2,2,8,3072]{4,3,2,1,0:T(8,128)(2,1)S(1)} collective-permute-done((bf16[2,2,2,8,3072]{4,3,2,1,0:T(8,128)(2,1)S(1)}, bf16[2,2,2,8,3072]{4,3,2,1,0:T(8,128)(2,1)S(1)}, u32[]{:S(2)}, u32[]{:S(2)}) %collective-permute-start.11) | collective-permute-done | bytes 393248 | tf_op jit(solution)/shard_map/ppermute | solution.py:81
  58.1 1.6 %collective-permute-start.12 = (bf16[2,2,8,3072]{3,2,1,0:T(8,128)(2,1)S(1)}, bf16[2,2,8,3072]{3,2,1,0:T(8,128)(2,1)S(1)}, u32[]{:S(2)}, u32[]{:S(2)}) collective-permute-start(bf16[2,2,8,3072]{3,2,1,0:T(8,128)(2,1)S(1)} %slice_bitcast_fusion.6), channel_id=1, source_target_pairs={{0,2},{1,3},{2,0},{3,1},{4,6},{5,7},{6,4},{7,5},{8,10},{9,11},{10,... | collective-permute-start | bytes 589832 | tf_op jit(solution)/shard_map/ppermute | solution.py:81
  59.7 0.4 collective-permute-done.16
  60.1 0.1 fusion.2
  60.3 1.6 %collective-permute-start.17 = (bf16[2,2,8,3072]{3,2,1,0:T(8,128)(2,1)S(1)}, bf16[2,2,8,3072]{3,2,1,0:T(8,128)(2,1)S(1)}, u32[]{:S(2)}, u32[]{:S(2)}) collective-permute-start(bf16[2,2,8,3072]{3,2,1,0:T(8,128)(2,1)S(1)} %slice_bitcast_fusion.4), channel_id=1, source_target_pairs={{0,16},{16,0},{1,17},{17,1},{2,18},{18,2},{3,19},{19,3},{4,20},{20... | collective-permute-start | bytes 589832 | tf_op jit(solution)/shard_map/ppermute | solution.py:81
  61.8 2.5 %collective-permute-done.12 = bf16[2,2,8,3072]{3,2,1,0:T(8,128)(2,1)S(1)} collective-permute-done((bf16[2,2,8,3072]{3,2,1,0:T(8,128)(2,1)S(1)}, bf16[2,2,8,3072]{3,2,1,0:T(8,128)(2,1)S(1)}, u32[]{:S(2)}, u32[]{:S(2)}) %collective-permute-start.12) | collective-permute-done | bytes 196640 | tf_op jit(solution)/shard_map/ppermute | solution.py:81
  64.4 2.3 %collective-permute-start.13 = (bf16[2,8,3072]{2,1,0:T(8,128)(2,1)S(1)}, bf16[2,8,3072]{2,1,0:T(8,128)(2,1)S(1)}, u32[]{:S(2)}, u32[]{:S(2)}) collective-permute-start(bf16[2,8,3072]{2,1,0:T(8,128)(2,1)S(1)} %slice_bitcast_fusion.10), channel_id=1, source_target_pairs={{0,4},{4,0},{8,12},{12,8},{1,5},{5,1},{9,13},{13,9},{2,6},{6,2},{1... | collective-permute-start | bytes 294920 | tf_op jit(solution)/shard_map/ppermute | solution.py:81
  66.8 2.0 %collective-permute-start.18 = (bf16[2,8,3072]{2,1,0:T(8,128)(2,1)S(1)}, bf16[2,8,3072]{2,1,0:T(8,128)(2,1)S(1)}, u32[]{:S(2)}, u32[]{:S(2)}) collective-permute-start(bf16[2,8,3072]{2,1,0:T(8,128)(2,1)S(1)} %slice_bitcast_fusion.8), channel_id=1, source_target_pairs={{0,4},{4,0},{8,12},{12,8},{1,5},{5,1},{9,13},{13,9},{2,6},{6,2},{1... | collective-permute-start | bytes 294920 | tf_op jit(solution)/shard_map/ppermute | solution.py:81
  68.8 1.5 %collective-permute-done.13 = bf16[2,8,3072]{2,1,0:T(8,128)(2,1)S(1)} collective-permute-done((bf16[2,8,3072]{2,1,0:T(8,128)(2,1)S(1)}, bf16[2,8,3072]{2,1,0:T(8,128)(2,1)S(1)}, u32[]{:S(2)}, u32[]{:S(2)}) %collective-permute-start.13) | collective-permute-done | bytes 98336 | tf_op jit(solution)/shard_map/ppermute | solution.py:81
  70.3 3.8 %collective-permute-start.14 = (bf16[8,3072]{1,0:T(8,128)(2,1)S(1)}, bf16[8,3072]{1,0:T(8,128)(2,1)S(1)}, u32[]{:S(2)}, u32[]{:S(2)}) collective-permute-start(bf16[8,3072]{1,0:T(8,128)(2,1)S(1)} %slice_bitcast_fusion.14), channel_id=1, source_target_pairs={{0,8},{4,12},{8,0},{12,4},{1,9},{5,13},{9,1},{13,5},{2,10},{6,14},... | collective-permute-start | bytes 147464 | tf_op jit(solution)/shard_map/ppermute | solution.py:81
  74.2 1.5 %collective-permute-start.19 = (bf16[8,3072]{1,0:T(8,128)(2,1)S(1)}, bf16[8,3072]{1,0:T(8,128)(2,1)S(1)}, u32[]{:S(2)}, u32[]{:S(2)}) collective-permute-start(bf16[8,3072]{1,0:T(8,128)(2,1)S(1)} %slice_bitcast_fusion.12), channel_id=1, source_target_pairs={{0,8},{4,12},{8,0},{12,4},{1,9},{5,13},{9,1},{13,5},{2,10},{6,14},... | collective-permute-start | bytes 147464 | tf_op jit(solution)/shard_map/ppermute | solution.py:81
  75.7 1.5 %collective-permute-done.14 = bf16[8,3072]{1,0:T(8,128)(2,1)S(1)} collective-permute-done((bf16[8,3072]{1,0:T(8,128)(2,1)S(1)}, bf16[8,3072]{1,0:T(8,128)(2,1)S(1)}, u32[]{:S(2)}, u32[]{:S(2)}) %collective-permute-start.14) | collective-permute-done | bytes 49184 | tf_op jit(solution)/shard_map/ppermute | solution.py:81
  77.2 2.0 %collective-permute-done.19 = bf16[8,3072]{1,0:T(8,128)(2,1)S(1)} collective-permute-done((bf16[8,3072]{1,0:T(8,128)(2,1)S(1)}, bf16[8,3072]{1,0:T(8,128)(2,1)S(1)}, u32[]{:S(2)}, u32[]{:S(2)}) %collective-permute-start.19) | collective-permute-done | bytes 49184 | tf_op jit(solution)/shard_map/ppermute | solution.py:81
  79.2 0.6 pad_maximum_fusion.10
  (31 shorter events, 1.0 us)
Async XLA Ops:
  1.2 6.7 %collective-permute-start.5 = (bf16[8,3072]{1,0:T(8,128)(2,1)S(1)}, bf16[8,3072]{1,0:T(8,128)(2,1)S(1)}, u32[]{:S(2)}, u32[]{:S(2)}) collective-permute-start(bf16[8,3072]{1,0:T(8,128)(2,1)S(1)} %get-tuple-element.14), channel_id=1, source_target_pairs={{0,8},{4,12},{8,0},{12,4},{1,9},{5,13},{9,1},{13,5},{2,10},{6,14},... | collective-permute-start | bytes 147464 | tf_op jit(solution)/shard_map/ppermute | solution.py:81
  5.2 5.2 %collective-permute-start = (bf16[8,3200]{1,0:T(8,128)(2,1)S(1)}, bf16[8,3200]{1,0:T(8,128)(2,1)S(1)}, u32[]{:S(2)}, u32[]{:S(2)}) collective-permute-start(bf16[8,3200]{1,0:T(8,128)(2,1)S(1)} %get-tuple-element.13), channel_id=1, source_target_pairs={{0,8},{4,12},{8,0},{12,4},{1,9},{5,13},{9,1},{13,5},{2,10},{6,14},... | collective-permute-start | bytes 153608 | tf_op jit(solution)/shard_map/ppermute | solution.py:81
  7.8 5.6 %collective-permute-start.6 = (bf16[2,8,3072]{2,1,0:T(8,128)(2,1)S(1)}, bf16[2,8,3072]{2,1,0:T(8,128)(2,1)S(1)}, u32[]{:S(2)}, u32[]{:S(2)}) collective-permute-start(bf16[2,8,3072]{2,1,0:T(8,128)(2,1)S(1)} %get-tuple-element.38), channel_id=1, source_target_pairs={{0,4},{4,0},{8,12},{12,8},{1,5},{5,1},{9,13},{13,9},{2,6},{6,2},{1... | collective-permute-start | bytes 294920 | tf_op jit(solution)/shard_map/ppermute | solution.py:81
  10.4 4.7 %collective-permute-start.1 = (bf16[2,8,3200]{2,1,0:T(8,128)(2,1)S(1)}, bf16[2,8,3200]{2,1,0:T(8,128)(2,1)S(1)}, u32[]{:S(2)}, u32[]{:S(2)}) collective-permute-start(bf16[2,8,3200]{2,1,0:T(8,128)(2,1)S(1)} %get-tuple-element.36), channel_id=1, source_target_pairs={{0,4},{4,0},{8,12},{12,8},{1,5},{5,1},{9,13},{13,9},{2,6},{6,2},{1... | collective-permute-start | bytes 307208 | tf_op jit(solution)/shard_map/ppermute | solution.py:81
  13.5 5.7 %collective-permute-start.7 = (bf16[2,2,8,3072]{3,2,1,0:T(8,128)(2,1)S(1)}, bf16[2,2,8,3072]{3,2,1,0:T(8,128)(2,1)S(1)}, u32[]{:S(2)}, u32[]{:S(2)}) collective-permute-start(bf16[2,2,8,3072]{3,2,1,0:T(8,128)(2,1)S(1)} %get-tuple-element.34), channel_id=1, source_target_pairs={{0,16},{16,0},{1,17},{17,1},{2,18},{18,2},{3,19},{19,3},{4,20},{20... | collective-permute-start | bytes 589832 | tf_op jit(solution)/shard_map/ppermute | solution.py:81
  15.2 7.2 %collective-permute-start.2 = (bf16[2,2,8,3200]{3,2,1,0:T(8,128)(2,1)S(1)}, bf16[2,2,8,3200]{3,2,1,0:T(8,128)(2,1)S(1)}, u32[]{:S(2)}, u32[]{:S(2)}) collective-permute-start(bf16[2,2,8,3200]{3,2,1,0:T(8,128)(2,1)S(1)} %get-tuple-element.32), channel_id=1, source_target_pairs={{0,2},{1,3},{2,0},{3,1},{4,6},{5,7},{6,4},{7,5},{8,10},{9,11},{10,... | collective-permute-start | bytes 614408 | tf_op jit(solution)/shard_map/ppermute | solution.py:81
  19.3 10.1 %collective-permute-start.8 = (bf16[2,2,2,8,3072]{4,3,2,1,0:T(8,128)(2,1)S(1)}, bf16[2,2,2,8,3072]{4,3,2,1,0:T(8,128)(2,1)S(1)}, u32[]{:S(2)}, u32[]{:S(2)}) collective-permute-start(bf16[2,2,2,8,3072]{4,3,2,1,0:T(8,128)(2,1)S(1)} %get-tuple-element.30), channel_id=1, source_target_pairs={{0,2},{1,3},{2,0},{3,1},{4,6},{5,7},{6,4},{7,5},{8,10},{9,11},{10,... | collective-permute-start | bytes 1179656 | tf_op jit(solution)/shard_map/ppermute | solution.py:81
  22.4 8.0 %collective-permute-start.3 = (bf16[2,2,2,8,3200]{4,3,2,1,0:T(8,128)(2,1)S(1)}, bf16[2,2,2,8,3200]{4,3,2,1,0:T(8,128)(2,1)S(1)}, u32[]{:S(2)}, u32[]{:S(2)}) collective-permute-start(bf16[2,2,2,8,3200]{4,3,2,1,0:T(8,128)(2,1)S(1)} %get-tuple-element.28.refs_1_), channel_id=1, source_target_pairs={{0,16},{16,0},{1,17},{17,1},{2,18},{18,2},{3,19},{19,3},{4,20},{20... | collective-permute-start | bytes 1228808 | tf_op jit(solution)/shard_map/ppermute | solution.py:81
  29.5 2.4 %collective-permute-start.9 = (bf16[2,2,2,2,8,3072]{5,4,3,2,0,1:T(8,128)(2,1)S(1)}, bf16[2,2,2,2,8,3072]{5,4,3,2,0,1:T(8,128)(2,1)S(1)}, u32[]{:S(2)}, u32[]{:S(2)}) collective-permute-start(bf16[2,2,2,2,8,3072]{5,4,3,2,0,1:T(8,128)(2,1)S(1)} %pad_maximum_fusion.3), channel_id=1, source_target_pairs={{0,1},{1,0},{2,3},{3,2},{4,5},{5,4},{6,7},{7,6},{8,9},{9,8},{10,11... | collective-permute-start | bytes 2359304 | tf_op jit(solution)/shard_map/ppermute | solution.py:81
  30.6 6.2 %collective-permute-start.4 = (bf16[2,2,2,2,8,3200]{5,4,3,2,1,0:T(8,128)(2,1)S(1)}, bf16[2,2,2,2,8,3200]{5,4,3,2,1,0:T(8,128)(2,1)S(1)}, u32[]{:S(2)}, u32[]{:S(2)}) collective-permute-start(bf16[2,2,2,2,8,3200]{5,4,3,2,1,0:T(8,128)(2,1)S(1)} %get-tuple-element.26), channel_id=1, source_target_pairs={{0,1},{1,0},{2,3},{3,2},{4,5},{5,4},{6,7},{7,6},{8,9},{9,8},{10,11... | collective-permute-start | bytes 2457608 | tf_op jit(solution)/shard_map/ppermute | solution.py:81
  43.7 2.8 %collective-permute-start.10 = (bf16[2,2,2,2,8,3072]{5,4,3,2,1,0:T(8,128)(2,1)S(1)}, bf16[2,2,2,2,8,3072]{5,4,3,2,1,0:T(8,128)(2,1)S(1)}, u32[]{:S(2)}, u32[]{:S(2)}) collective-permute-start(bf16[2,2,2,2,8,3072]{5,4,3,2,1,0:T(8,128)(2,1)S(1)} %bitcast.104), channel_id=1, source_target_pairs={{0,1},{1,0},{2,3},{3,2},{4,5},{5,4},{6,7},{7,6},{8,9},{9,8},{10,11... | collective-permute-start | bytes 2359304 | tf_op jit(solution)/shard_map/ppermute | solution.py:81
  46.1 2.4 %collective-permute-start.15 = (bf16[2,2,2,2,8,3072]{5,4,3,2,0,1:T(8,128)(2,1)S(1)}, bf16[2,2,2,2,8,3072]{5,4,3,2,0,1:T(8,128)(2,1)S(1)}, u32[]{:S(2)}, u32[]{:S(2)}) collective-permute-start(bf16[2,2,2,2,8,3072]{5,4,3,2,0,1:T(8,128)(2,1)S(1)} %copy.9), channel_id=1, source_target_pairs={{0,1},{1,0},{2,3},{3,2},{4,5},{5,4},{6,7},{7,6},{8,9},{9,8},{10,11... | collective-permute-start | bytes 2359304 | tf_op jit(solution)/shard_map/ppermute | solution.py:81
  46.8 11.2 %collective-permute-start.11 = (bf16[2,2,2,8,3072]{4,3,2,1,0:T(8,128)(2,1)S(1)}, bf16[2,2,2,8,3072]{4,3,2,1,0:T(8,128)(2,1)S(1)}, u32[]{:S(2)}, u32[]{:S(2)}) collective-permute-start(bf16[2,2,2,8,3072]{4,3,2,1,0:T(8,128)(2,1)S(1)} %slice_bitcast_fusion.2), channel_id=1, source_target_pairs={{0,16},{16,0},{1,17},{17,1},{2,18},{18,2},{3,19},{19,3},{4,20},{20... | collective-permute-start | bytes 1179656 | tf_op jit(solution)/shard_map/ppermute | solution.py:81
  48.7 11.5 %collective-permute-start.16 = (bf16[2,2,2,8,3072]{4,3,2,1,0:T(8,128)(2,1)S(1)}, bf16[2,2,2,8,3072]{4,3,2,1,0:T(8,128)(2,1)S(1)}, u32[]{:S(2)}, u32[]{:S(2)}) collective-permute-start(bf16[2,2,2,8,3072]{4,3,2,1,0:T(8,128)(2,1)S(1)} %slice_bitcast_fusion), channel_id=1, source_target_pairs={{0,2},{1,3},{2,0},{3,1},{4,6},{5,7},{6,4},{7,5},{8,10},{9,11},{10,... | collective-permute-start | bytes 1179656 | tf_op jit(solution)/shard_map/ppermute | solution.py:81
  58.1 6.2 %collective-permute-start.12 = (bf16[2,2,8,3072]{3,2,1,0:T(8,128)(2,1)S(1)}, bf16[2,2,8,3072]{3,2,1,0:T(8,128)(2,1)S(1)}, u32[]{:S(2)}, u32[]{:S(2)}) collective-permute-start(bf16[2,2,8,3072]{3,2,1,0:T(8,128)(2,1)S(1)} %slice_bitcast_fusion.6), channel_id=1, source_target_pairs={{0,2},{1,3},{2,0},{3,1},{4,6},{5,7},{6,4},{7,5},{8,10},{9,11},{10,... | collective-permute-start | bytes 589832 | tf_op jit(solution)/shard_map/ppermute | solution.py:81
  60.3 6.4 %collective-permute-start.17 = (bf16[2,2,8,3072]{3,2,1,0:T(8,128)(2,1)S(1)}, bf16[2,2,8,3072]{3,2,1,0:T(8,128)(2,1)S(1)}, u32[]{:S(2)}, u32[]{:S(2)}) collective-permute-start(bf16[2,2,8,3072]{3,2,1,0:T(8,128)(2,1)S(1)} %slice_bitcast_fusion.4), channel_id=1, source_target_pairs={{0,16},{16,0},{1,17},{17,1},{2,18},{18,2},{3,19},{19,3},{4,20},{20... | collective-permute-start | bytes 589832 | tf_op jit(solution)/shard_map/ppermute | solution.py:81
  64.4 5.9 %collective-permute-start.13 = (bf16[2,8,3072]{2,1,0:T(8,128)(2,1)S(1)}, bf16[2,8,3072]{2,1,0:T(8,128)(2,1)S(1)}, u32[]{:S(2)}, u32[]{:S(2)}) collective-permute-start(bf16[2,8,3072]{2,1,0:T(8,128)(2,1)S(1)} %slice_bitcast_fusion.10), channel_id=1, source_target_pairs={{0,4},{4,0},{8,12},{12,8},{1,5},{5,1},{9,13},{13,9},{2,6},{6,2},{1... | collective-permute-start | bytes 294920 | tf_op jit(solution)/shard_map/ppermute | solution.py:81
  66.8 7.4 %collective-permute-start.18 = (bf16[2,8,3072]{2,1,0:T(8,128)(2,1)S(1)}, bf16[2,8,3072]{2,1,0:T(8,128)(2,1)S(1)}, u32[]{:S(2)}, u32[]{:S(2)}) collective-permute-start(bf16[2,8,3072]{2,1,0:T(8,128)(2,1)S(1)} %slice_bitcast_fusion.8), channel_id=1, source_target_pairs={{0,4},{4,0},{8,12},{12,8},{1,5},{5,1},{9,13},{13,9},{2,6},{6,2},{1... | collective-permute-start | bytes 294920 | tf_op jit(solution)/shard_map/ppermute | solution.py:81
  70.3 6.9 %collective-permute-start.14 = (bf16[8,3072]{1,0:T(8,128)(2,1)S(1)}, bf16[8,3072]{1,0:T(8,128)(2,1)S(1)}, u32[]{:S(2)}, u32[]{:S(2)}) collective-permute-start(bf16[8,3072]{1,0:T(8,128)(2,1)S(1)} %slice_bitcast_fusion.14), channel_id=1, source_target_pairs={{0,8},{4,12},{8,0},{12,4},{1,9},{5,13},{9,1},{13,5},{2,10},{6,14},... | collective-permute-start | bytes 147464 | tf_op jit(solution)/shard_map/ppermute | solution.py:81
  74.2 5.1 %collective-permute-start.19 = (bf16[8,3072]{1,0:T(8,128)(2,1)S(1)}, bf16[8,3072]{1,0:T(8,128)(2,1)S(1)}, u32[]{:S(2)}, u32[]{:S(2)}) collective-permute-start(bf16[8,3072]{1,0:T(8,128)(2,1)S(1)} %slice_bitcast_fusion.12), channel_id=1, source_target_pairs={{0,8},{4,12},{8,0},{12,4},{1,9},{5,13},{9,1},{13,5},{2,10},{6,14},... | collective-permute-start | bytes 147464 | tf_op jit(solution)/shard_map/ppermute | solution.py:81

commit v14 on v13

--- a/solution.py
+++ b/solution.py
@@ -287,7 +287,7 @@
     y_digits = digits_of("shard", ways["shard"], cores)
     core_digits = [Digit("shard", ways["shard"], 1, cores)]
     dim_order = core_digits + x_digits[::-1] + y_digits[::-1] + z_digits[::-1]
-    routes = [z_digits + y_digits + x_digits, z_digits + x_digits + y_digits]
+    routes = [z_digits + y_digits + x_digits, z_digits[::-1] + x_digits + y_digits]
 
     choices = expert_ids.shape[1]
     parts = packed(tokens, half, expert_ids, gate_values, old_place, new_place)

time: 80.1 us -> 79.5 us (level)
  starting transfers between devices: 31 us -> 29.6 us
    ppermute x20, starting transfers between devices: 31 us -> 29.6 us  [shift(): return lax.ppermute(value, self.name, pairs)]
  transfers between devices with their start and end apart: 20 -> 20, of which waited for: 15 -> 16; matrix products, arithmetic and copies ran while one was open for 2% -> 2% of each run, Pallas kernels for 14% -> 14%
where the time goes in v14:
time: 79.5 us; the launch traced here: 79.2 us
  starting transfers between devices  29.6 us (37%)
  waiting for transfers between devices  27.7 us (35%)
  Pallas kernels  19 us (24%)
  other arithmetic  2.1 us (3%)
    ppermute x20, starting transfers between devices, shift(): return lax.ppermute(value, self.name, pairs)  29.6 us
    ppermute x20, waiting for transfers between devices, shift(): return lax.ppermute(value, self.name, pairs)  27.7 us
    pallas_call x2, Pallas kernels, gate_up_of(): pl.pallas_call(kernel, grid=(rows // row_block,), in_specs=specs + [pl.Bl...  9.27 us
    pallas_call x1, Pallas kernels, fetched(): pl.pallas_call(kernel, in_specs=[pl.BlockSpec(memory_space=pl.ANY)] * 2,...  4.58 us
    pallas_call x2, Pallas kernels, down_of(): pl.pallas_call(kernel, grid=(rows // row_block,), in_specs=[pl.BlockSpec(...  3.99 us
  transfers between devices with their start and end apart: 20, of which 16 were waited for; matrix products, arithmetic and copies ran while one was open for 2% of the time, Pallas kernels for 14%

profile of v14, /device:TPU:0, one launch (start us, length us, event | category | flops | bytes accessed | tf_op | source)
XLA Modules:
  0.0 79.2 jit_solution(18398400707489392747)
XLA Ops:
  0.0 1.2 %shard_map.73 = (bf16[8,3200]{1,0:T(8,128)(2,1)S(1)}, bf16[8,3072]{1,0:T(8,128)(2,1)S(1)}) custom-call(bf16[8,6144]{1,0:T(8,128)(2,1)} %tokens_ref.1, s32[2,8]{1,0:T(2,128)} %bitcast.114, f32[2,8]{1,0:T(2,128)} %bitcast.115, s32[1,4]{1,0:T(1,128)} %bitcast.116, s32[1,4]{1,0:T(1,128)} %bitcast.117), custom_call_target="tpu_custom_call" | custom-call | bytes 196608 | tf_op jit(solution)/shard_map/pallas_call | solution.py:57
  1.2 3.0 %collective-permute-start.5 = (bf16[8,3072]{1,0:T(8,128)(2,1)S(1)}, bf16[8,3072]{1,0:T(8,128)(2,1)S(1)}, u32[]{:S(2)}, u32[]{:S(2)}) collective-permute-start(bf16[8,3072]{1,0:T(8,128)(2,1)S(1)} %get-tuple-element.14), channel_id=1, source_target_pairs={{0,4},{4,0},{8,12},{12,8},{1,5},{5,1},{9,13},{13,9},{2,6},{6,2},{1... | collective-permute-start | bytes 147464 | tf_op jit(solution)/shard_map/ppermute | solution.py:81
  4.2 2.6 %collective-permute-start = (bf16[8,3200]{1,0:T(8,128)(2,1)S(1)}, bf16[8,3200]{1,0:T(8,128)(2,1)S(1)}, u32[]{:S(2)}, u32[]{:S(2)}) collective-permute-start(bf16[8,3200]{1,0:T(8,128)(2,1)S(1)} %get-tuple-element.13), channel_id=1, source_target_pairs={{0,8},{4,12},{8,0},{12,4},{1,9},{5,13},{9,1},{13,5},{2,10},{6,14},... | collective-permute-start | bytes 153608 | tf_op jit(solution)/shard_map/ppermute | solution.py:81
  6.8 2.6 %collective-permute-start.6 = (bf16[2,8,3072]{2,1,0:T(8,128)(2,1)S(1)}, bf16[2,8,3072]{2,1,0:T(8,128)(2,1)S(1)}, u32[]{:S(2)}, u32[]{:S(2)}) collective-permute-start(bf16[2,8,3072]{2,1,0:T(8,128)(2,1)S(1)} %get-tuple-element.38), channel_id=1, source_target_pairs={{0,8},{4,12},{8,0},{12,4},{1,9},{5,13},{9,1},{13,5},{2,10},{6,14},... | collective-permute-start | bytes 294920 | tf_op jit(solution)/shard_map/ppermute | solution.py:81
  9.4 0.5 collective-permute-done
  9.9 1.6 %collective-permute-start.1 = (bf16[2,8,3200]{2,1,0:T(8,128)(2,1)S(1)}, bf16[2,8,3200]{2,1,0:T(8,128)(2,1)S(1)}, u32[]{:S(2)}, u32[]{:S(2)}) collective-permute-start(bf16[2,8,3200]{2,1,0:T(8,128)(2,1)S(1)} %get-tuple-element.36), channel_id=1, source_target_pairs={{0,4},{4,0},{8,12},{12,8},{1,5},{5,1},{9,13},{13,9},{2,6},{6,2},{1... | collective-permute-start | bytes 307208 | tf_op jit(solution)/shard_map/ppermute | solution.py:81
  11.5 2.0 %collective-permute-done.6 = bf16[2,8,3072]{2,1,0:T(8,128)(2,1)S(1)} collective-permute-done((bf16[2,8,3072]{2,1,0:T(8,128)(2,1)S(1)}, bf16[2,8,3072]{2,1,0:T(8,128)(2,1)S(1)}, u32[]{:S(2)}, u32[]{:S(2)}) %collective-permute-start.6) | collective-permute-done | bytes 98336 | tf_op jit(solution)/shard_map/ppermute | solution.py:81
  13.5 1.6 %collective-permute-start.7 = (bf16[2,2,8,3072]{3,2,0,1:T(8,128)(2,1)S(1)}, bf16[2,2,8,3072]{3,2,0,1:T(8,128)(2,1)S(1)}, u32[]{:S(2)}, u32[]{:S(2)}) collective-permute-start(bf16[2,2,8,3072]{3,2,0,1:T(8,128)(2,1)S(1)} %get-tuple-element.34), channel_id=1, source_target_pairs={{0,16},{16,0},{1,17},{17,1},{2,18},{18,2},{3,19},{19,3},{4,20},{20... | collective-permute-start | bytes 589832 | tf_op jit(solution)/shard_map/ppermute | solution.py:81
  15.1 1.6 %collective-permute-start.2 = (bf16[2,2,8,3200]{3,2,1,0:T(8,128)(2,1)S(1)}, bf16[2,2,8,3200]{3,2,1,0:T(8,128)(2,1)S(1)}, u32[]{:S(2)}, u32[]{:S(2)}) collective-permute-start(bf16[2,2,8,3200]{3,2,1,0:T(8,128)(2,1)S(1)} %get-tuple-element.32), channel_id=1, source_target_pairs={{0,2},{1,3},{2,0},{3,1},{4,6},{5,7},{6,4},{7,5},{8,10},{9,11},{10,... | collective-permute-start | bytes 614408 | tf_op jit(solution)/shard_map/ppermute | solution.py:81
  16.7 2.7 %collective-permute-done.7 = bf16[2,2,8,3072]{3,2,0,1:T(8,128)(2,1)S(1)} collective-permute-done((bf16[2,2,8,3072]{3,2,0,1:T(8,128)(2,1)S(1)}, bf16[2,2,8,3072]{3,2,0,1:T(8,128)(2,1)S(1)}, u32[]{:S(2)}, u32[]{:S(2)}) %collective-permute-start.7) | collective-permute-done | bytes 196640 | tf_op jit(solution)/shard_map/ppermute | solution.py:81
  19.5 1.6 %collective-permute-start.8 = (bf16[2,2,2,8,3072]{4,3,1,2,0:T(8,128)(2,1)S(1)}, bf16[2,2,2,8,3072]{4,3,1,2,0:T(8,128)(2,1)S(1)}, u32[]{:S(2)}, u32[]{:S(2)}) collective-permute-start(bf16[2,2,2,8,3072]{4,3,1,2,0:T(8,128)(2,1)S(1)} %get-tuple-element.30), channel_id=1, source_target_pairs={{0,2},{1,3},{2,0},{3,1},{4,6},{5,7},{6,4},{7,5},{8,10},{9,11},{10,... | collective-permute-start | bytes 1179656 | tf_op jit(solution)/shard_map/ppermute | solution.py:81
  21.0 0.8 %collective-permute-done.2 = bf16[2,2,8,3200]{3,2,1,0:T(8,128)(2,1)S(1)} collective-permute-done((bf16[2,2,8,3200]{3,2,1,0:T(8,128)(2,1)S(1)}, bf16[2,2,8,3200]{3,2,1,0:T(8,128)(2,1)S(1)}, u32[]{:S(2)}, u32[]{:S(2)}) %collective-permute-start.2) | collective-permute-done | bytes 204832 | tf_op jit(solution)/shard_map/ppermute | solution.py:81
  21.9 1.5 %collective-permute-start.3 = (bf16[2,2,2,8,3200]{4,3,2,1,0:T(8,128)(2,1)S(1)}, bf16[2,2,2,8,3200]{4,3,2,1,0:T(8,128)(2,1)S(1)}, u32[]{:S(2)}, u32[]{:S(2)}) collective-permute-start(bf16[2,2,2,8,3200]{4,3,2,1,0:T(8,128)(2,1)S(1)} %get-tuple-element.28.refs_1_), channel_id=1, source_target_pairs={{0,16},{16,0},{1,17},{17,1},{2,18},{18,2},{3,19},{19,3},{4,20},{20... | collective-permute-start | bytes 1228808 | tf_op jit(solution)/shard_map/ppermute | solution.py:81
  23.5 4.6 %shard_map.74.refs_1_ = bf16[4,2,256,3072]{3,2,1,0:T(8,128)(2,1)S(1)} custom-call(bf16[4,2,256,6144]{3,2,1,0:T(8,128)(2,1)} %refs_2_.1, bf16[2,2,2,8,3200]{4,3,2,1,0:T(8,128)(2,1)S(1)} %get-tuple-element.28.refs_1_), custom_call_target="tpu_custom_call" | custom-call | bytes 25165824 | tf_op jit(solution)/shard_map/pallas_call | solution.py:123
  28.0 1.4 %collective-permute-done.8 = bf16[2,2,2,8,3072]{4,3,1,2,0:T(8,128)(2,1)S(1)} collective-permute-done((bf16[2,2,2,8,3072]{4,3,1,2,0:T(8,128)(2,1)S(1)}, bf16[2,2,2,8,3072]{4,3,1,2,0:T(8,128)(2,1)S(1)}, u32[]{:S(2)}, u32[]{:S(2)}) %collective-permute-start.8) | collective-permute-done | bytes 393248 | tf_op jit(solution)/shard_map/ppermute | solution.py:81
  29.6 0.9 %collective-permute-done.3 = bf16[2,2,2,8,3200]{4,3,2,1,0:T(8,128)(2,1)S(1)} collective-permute-done((bf16[2,2,2,8,3200]{4,3,2,1,0:T(8,128)(2,1)S(1)}, bf16[2,2,2,8,3200]{4,3,2,1,0:T(8,128)(2,1)S(1)}, u32[]{:S(2)}, u32[]{:S(2)}) %collective-permute-start.3) | collective-permute-done | bytes 409632 | tf_op jit(solution)/shard_map/ppermute | solution.py:81
  30.5 0.1 fusion.16
  30.7 1.2 %collective-permute-done.9 = bf16[2,2,2,2,8,3072]{5,4,2,3,0,1:T(8,128)(2,1)S(1)} collective-permute-done((bf16[2,2,2,2,8,3072]{5,4,2,3,0,1:T(8,128)(2,1)S(1)}, bf16[2,2,2,2,8,3072]{5,4,2,3,0,1:T(8,128)(2,1)S(1)}, u32[]{:S(2)}, u32[]{:S(2)}) %collective-permute-start.9) | collective-permute-done | bytes 786464 | tf_op jit(solution)/shard_map/ppermute | solution.py:81
  31.9 0.1 pad_maximum_fusion.1
  32.0 0.1 copy.8
  32.2 4.7 %shard_map.75 = (f32[256,2048]{1,0:T(8,128)S(1)}, bf16[4,2,256,3072]{3,2,1,0:T(8,128)(2,1)S(1)}) custom-call(bf16[256,3072]{1,0:T(8,128)(2,1)S(1)} %bitcast.96, bf16[4,2,256,3072]{3,2,1,0:T(8,128)(2,1)S(1)} %shard_map.74.refs_1_, bf16[4,2,256,6144]{3,2,1,0:T(8,128)(2,1)} %refs_2_.1), custom_call_target="tpu_custom_call" | custom-call | flops 3221225472 | bytes 14680064 | tf_op jit(solution)/shard_map/pallas_call | solution.py:216
  36.9 0.2 pad_maximum_fusion
  37.1 4.6 %shard_map.76 = (bf16[4,256,256]{2,1,0:T(8,128)(2,1)S(1)}, bf16[4,256,6144]{2,1,0:T(8,128)(2,1)S(1)}) custom-call(bf16[256,3200]{1,0:T(8,128)(2,1)S(1)} %bitcast.95, f32[256,2048]{1,0:T(8,128)S(1)} %get-tuple-element.17.refs_1_, bf16[4,2,256,3072]{3,2,1,0:T(8,128)(2,1)S(1)} %get-tuple-element.18.refs_2_, bf16[4,256,6144]{2,1,0:T(8,128)(2,1)} %refs_3_.1), custom_call_target="tpu_custom_call" | custom-call | flops 3221225472 | bytes 14680064 | tf_op jit(solution)/shard_map/pallas_call | solution.py:216
  41.7 2.0 %shard_map.77 = bf16[256,3072]{1,0:T(8,128)(2,1)S(1)} custom-call(bf16[4,256,256]{2,1,0:T(8,128)(2,1)S(1)} %get-tuple-element.19.refs_0_, bf16[4,256,6144]{2,1,0:T(8,128)(2,1)S(1)} %get-tuple-element.20.refs_1_), custom_call_target="tpu_custom_call" | custom-call | flops 1610612736 | bytes 8388608 | tf_op jit(solution)/shard_map/pallas_call | solution.py:259
  43.7 0.1 fusion.17
  43.8 0.2 collective-permute-start.10
  44.0 2.0 %shard_map.78 = bf16[256,3072]{1,0:T(8,128)(2,1)S(1)} custom-call(bf16[4,256,256]{2,1,0:T(8,128)(2,1)S(1)} %get-tuple-element.19.refs_0_, bf16[4,256,6144]{2,1,0:T(8,128)(2,1)S(1)} %get-tuple-element.20.refs_1_), custom_call_target="tpu_custom_call" | custom-call | flops 1610612736 | bytes 8388608 | tf_op jit(solution)/shard_map/pallas_call | solution.py:259
  46.1 0.5 collective-permute-start.15
  46.6 0.2 fusion
  46.8 1.5 %collective-permute-start.11 = (bf16[2,2,2,8,3072]{4,3,2,1,0:T(8,128)(2,1)S(1)}, bf16[2,2,2,8,3072]{4,3,2,1,0:T(8,128)(2,1)S(1)}, u32[]{:S(2)}, u32[]{:S(2)}) collective-permute-start(bf16[2,2,2,8,3072]{4,3,2,1,0:T(8,128)(2,1)S(1)} %slice_bitcast_fusion.2), channel_id=1, source_target_pairs={{0,16},{16,0},{1,17},{17,1},{2,18},{18,2},{3,19},{19,3},{4,20},{20... | collective-permute-start | bytes 1179656 | tf_op jit(solution)/shard_map/ppermute | solution.py:81
  48.4 0.1 collective-permute-done.15
  48.5 0.2 fusion.1
  48.7 1.6 %collective-permute-start.16 = (bf16[2,2,2,8,3072]{4,3,1,2,0:T(8,128)(2,1)S(1)}, bf16[2,2,2,8,3072]{4,3,1,2,0:T(8,128)(2,1)S(1)}, u32[]{:S(2)}, u32[]{:S(2)}) collective-permute-start(bf16[2,2,2,8,3072]{4,3,1,2,0:T(8,128)(2,1)S(1)} %slice_bitcast_fusion), channel_id=1, source_target_pairs={{0,2},{1,3},{2,0},{3,1},{4,6},{5,7},{6,4},{7,5},{8,10},{9,11},{10,... | collective-permute-start | bytes 1179656 | tf_op jit(solution)/shard_map/ppermute | solution.py:81
  50.3 7.7 %collective-permute-done.11 = bf16[2,2,2,8,3072]{4,3,2,1,0:T(8,128)(2,1)S(1)} collective-permute-done((bf16[2,2,2,8,3072]{4,3,2,1,0:T(8,128)(2,1)S(1)}, bf16[2,2,2,8,3072]{4,3,2,1,0:T(8,128)(2,1)S(1)}, u32[]{:S(2)}, u32[]{:S(2)}) %collective-permute-start.11) | collective-permute-done | bytes 393248 | tf_op jit(solution)/shard_map/ppermute | solution.py:81
  58.2 1.6 %collective-permute-start.12 = (bf16[2,2,8,3072]{3,2,1,0:T(8,128)(2,1)S(1)}, bf16[2,2,8,3072]{3,2,1,0:T(8,128)(2,1)S(1)}, u32[]{:S(2)}, u32[]{:S(2)}) collective-permute-start(bf16[2,2,8,3072]{3,2,1,0:T(8,128)(2,1)S(1)} %slice_bitcast_fusion.6), channel_id=1, source_target_pairs={{0,2},{1,3},{2,0},{3,1},{4,6},{5,7},{6,4},{7,5},{8,10},{9,11},{10,... | collective-permute-start | bytes 589832 | tf_op jit(solution)/shard_map/ppermute | solution.py:81
  59.7 0.5 collective-permute-done.16
  60.3 1.5 %collective-permute-start.17 = (bf16[2,2,8,3072]{3,2,0,1:T(8,128)(2,1)S(1)}, bf16[2,2,8,3072]{3,2,0,1:T(8,128)(2,1)S(1)}, u32[]{:S(2)}, u32[]{:S(2)}) collective-permute-start(bf16[2,2,8,3072]{3,2,0,1:T(8,128)(2,1)S(1)} %slice_bitcast_fusion.4), channel_id=1, source_target_pairs={{0,16},{16,0},{1,17},{17,1},{2,18},{18,2},{3,19},{19,3},{4,20},{20... | collective-permute-start | bytes 589832 | tf_op jit(solution)/shard_map/ppermute | solution.py:81
  61.9 2.5 %collective-permute-done.12 = bf16[2,2,8,3072]{3,2,1,0:T(8,128)(2,1)S(1)} collective-permute-done((bf16[2,2,8,3072]{3,2,1,0:T(8,128)(2,1)S(1)}, bf16[2,2,8,3072]{3,2,1,0:T(8,128)(2,1)S(1)}, u32[]{:S(2)}, u32[]{:S(2)}) %collective-permute-start.12) | collective-permute-done | bytes 196640 | tf_op jit(solution)/shard_map/ppermute | solution.py:81
  64.5 1.8 %collective-permute-start.13 = (bf16[2,8,3072]{2,1,0:T(8,128)(2,1)S(1)}, bf16[2,8,3072]{2,1,0:T(8,128)(2,1)S(1)}, u32[]{:S(2)}, u32[]{:S(2)}) collective-permute-start(bf16[2,8,3072]{2,1,0:T(8,128)(2,1)S(1)} %slice_bitcast_fusion.10), channel_id=1, source_target_pairs={{0,4},{4,0},{8,12},{12,8},{1,5},{5,1},{9,13},{13,9},{2,6},{6,2},{1... | collective-permute-start | bytes 294920 | tf_op jit(solution)/shard_map/ppermute | solution.py:81
  66.3 0.5 collective-permute-done.17
  66.8 2.1 %collective-permute-start.18 = (bf16[2,8,3072]{2,1,0:T(8,128)(2,1)S(1)}, bf16[2,8,3072]{2,1,0:T(8,128)(2,1)S(1)}, u32[]{:S(2)}, u32[]{:S(2)}) collective-permute-start(bf16[2,8,3072]{2,1,0:T(8,128)(2,1)S(1)} %slice_bitcast_fusion.8), channel_id=1, source_target_pairs={{0,8},{4,12},{8,0},{12,4},{1,9},{5,13},{9,1},{13,5},{2,10},{6,14},... | collective-permute-start | bytes 294920 | tf_op jit(solution)/shard_map/ppermute | solution.py:81
  68.9 0.6 collective-permute-done.13
  69.5 2.4 %collective-permute-start.14 = (bf16[8,3072]{1,0:T(8,128)(2,1)S(1)}, bf16[8,3072]{1,0:T(8,128)(2,1)S(1)}, u32[]{:S(2)}, u32[]{:S(2)}) collective-permute-start(bf16[8,3072]{1,0:T(8,128)(2,1)S(1)} %slice_bitcast_fusion.14), channel_id=1, source_target_pairs={{0,8},{4,12},{8,0},{12,4},{1,9},{5,13},{9,1},{13,5},{2,10},{6,14},... | collective-permute-start | bytes 147464 | tf_op jit(solution)/shard_map/ppermute | solution.py:81
  71.9 2.4 %collective-permute-done.18 = bf16[2,8,3072]{2,1,0:T(8,128)(2,1)S(1)} collective-permute-done((bf16[2,8,3072]{2,1,0:T(8,128)(2,1)S(1)}, bf16[2,8,3072]{2,1,0:T(8,128)(2,1)S(1)}, u32[]{:S(2)}, u32[]{:S(2)}) %collective-permute-start.18) | collective-permute-done | bytes 98336 | tf_op jit(solution)/shard_map/ppermute | solution.py:81
  74.4 0.2 collective-permute-start.19
  74.6 0.3 collective-permute-done.14
  74.9 3.6 %collective-permute-done.19 = bf16[8,3072]{1,0:T(8,128)(2,1)S(1)} collective-permute-done((bf16[8,3072]{1,0:T(8,128)(2,1)S(1)}, bf16[8,3072]{1,0:T(8,128)(2,1)S(1)}, u32[]{:S(2)}, u32[]{:S(2)}) %collective-permute-start.19) | collective-permute-done | bytes 49184 | tf_op jit(solution)/shard_map/ppermute | solution.py:81
  78.6 0.6 pad_maximum_fusion.10
  (31 shorter events, 1.1 us)
Async XLA Ops:
  1.2 5.6 %collective-permute-start.5 = (bf16[8,3072]{1,0:T(8,128)(2,1)S(1)}, bf16[8,3072]{1,0:T(8,128)(2,1)S(1)}, u32[]{:S(2)}, u32[]{:S(2)}) collective-permute-start(bf16[8,3072]{1,0:T(8,128)(2,1)S(1)} %get-tuple-element.14), channel_id=1, source_target_pairs={{0,4},{4,0},{8,12},{12,8},{1,5},{5,1},{9,13},{13,9},{2,6},{6,2},{1... | collective-permute-start | bytes 147464 | tf_op jit(solution)/shard_map/ppermute | solution.py:81
  4.2 5.7 %collective-permute-start = (bf16[8,3200]{1,0:T(8,128)(2,1)S(1)}, bf16[8,3200]{1,0:T(8,128)(2,1)S(1)}, u32[]{:S(2)}, u32[]{:S(2)}) collective-permute-start(bf16[8,3200]{1,0:T(8,128)(2,1)S(1)} %get-tuple-element.13), channel_id=1, source_target_pairs={{0,8},{4,12},{8,0},{12,4},{1,9},{5,13},{9,1},{13,5},{2,10},{6,14},... | collective-permute-start | bytes 153608 | tf_op jit(solution)/shard_map/ppermute | solution.py:81
  6.8 6.7 %collective-permute-start.6 = (bf16[2,8,3072]{2,1,0:T(8,128)(2,1)S(1)}, bf16[2,8,3072]{2,1,0:T(8,128)(2,1)S(1)}, u32[]{:S(2)}, u32[]{:S(2)}) collective-permute-start(bf16[2,8,3072]{2,1,0:T(8,128)(2,1)S(1)} %get-tuple-element.38), channel_id=1, source_target_pairs={{0,8},{4,12},{8,0},{12,4},{1,9},{5,13},{9,1},{13,5},{2,10},{6,14},... | collective-permute-start | bytes 294920 | tf_op jit(solution)/shard_map/ppermute | solution.py:81
  9.9 5.2 %collective-permute-start.1 = (bf16[2,8,3200]{2,1,0:T(8,128)(2,1)S(1)}, bf16[2,8,3200]{2,1,0:T(8,128)(2,1)S(1)}, u32[]{:S(2)}, u32[]{:S(2)}) collective-permute-start(bf16[2,8,3200]{2,1,0:T(8,128)(2,1)S(1)} %get-tuple-element.36), channel_id=1, source_target_pairs={{0,4},{4,0},{8,12},{12,8},{1,5},{5,1},{9,13},{13,9},{2,6},{6,2},{1... | collective-permute-start | bytes 307208 | tf_op jit(solution)/shard_map/ppermute | solution.py:81
  13.5 5.9 %collective-permute-start.7 = (bf16[2,2,8,3072]{3,2,0,1:T(8,128)(2,1)S(1)}, bf16[2,2,8,3072]{3,2,0,1:T(8,128)(2,1)S(1)}, u32[]{:S(2)}, u32[]{:S(2)}) collective-permute-start(bf16[2,2,8,3072]{3,2,0,1:T(8,128)(2,1)S(1)} %get-tuple-element.34), channel_id=1, source_target_pairs={{0,16},{16,0},{1,17},{17,1},{2,18},{18,2},{3,19},{19,3},{4,20},{20... | collective-permute-start | bytes 589832 | tf_op jit(solution)/shard_map/ppermute | solution.py:81
  15.1 6.7 %collective-permute-start.2 = (bf16[2,2,8,3200]{3,2,1,0:T(8,128)(2,1)S(1)}, bf16[2,2,8,3200]{3,2,1,0:T(8,128)(2,1)S(1)}, u32[]{:S(2)}, u32[]{:S(2)}) collective-permute-start(bf16[2,2,8,3200]{3,2,1,0:T(8,128)(2,1)S(1)} %get-tuple-element.32), channel_id=1, source_target_pairs={{0,2},{1,3},{2,0},{3,1},{4,6},{5,7},{6,4},{7,5},{8,10},{9,11},{10,... | collective-permute-start | bytes 614408 | tf_op jit(solution)/shard_map/ppermute | solution.py:81
  19.5 10.0 %collective-permute-start.8 = (bf16[2,2,2,8,3072]{4,3,1,2,0:T(8,128)(2,1)S(1)}, bf16[2,2,2,8,3072]{4,3,1,2,0:T(8,128)(2,1)S(1)}, u32[]{:S(2)}, u32[]{:S(2)}) collective-permute-start(bf16[2,2,2,8,3072]{4,3,1,2,0:T(8,128)(2,1)S(1)} %get-tuple-element.30), channel_id=1, source_target_pairs={{0,2},{1,3},{2,0},{3,1},{4,6},{5,7},{6,4},{7,5},{8,10},{9,11},{10,... | collective-permute-start | bytes 1179656 | tf_op jit(solution)/shard_map/ppermute | solution.py:81
  21.9 8.6 %collective-permute-start.3 = (bf16[2,2,2,8,3200]{4,3,2,1,0:T(8,128)(2,1)S(1)}, bf16[2,2,2,8,3200]{4,3,2,1,0:T(8,128)(2,1)S(1)}, u32[]{:S(2)}, u32[]{:S(2)}) collective-permute-start(bf16[2,2,2,8,3200]{4,3,2,1,0:T(8,128)(2,1)S(1)} %get-tuple-element.28.refs_1_), channel_id=1, source_target_pairs={{0,16},{16,0},{1,17},{17,1},{2,18},{18,2},{3,19},{19,3},{4,20},{20... | collective-permute-start | bytes 1228808 | tf_op jit(solution)/shard_map/ppermute | solution.py:81
  29.5 2.4 %collective-permute-start.9 = (bf16[2,2,2,2,8,3072]{5,4,2,3,0,1:T(8,128)(2,1)S(1)}, bf16[2,2,2,2,8,3072]{5,4,2,3,0,1:T(8,128)(2,1)S(1)}, u32[]{:S(2)}, u32[]{:S(2)}) collective-permute-start(bf16[2,2,2,2,8,3072]{5,4,2,3,0,1:T(8,128)(2,1)S(1)} %pad_maximum_fusion.3), channel_id=1, source_target_pairs={{0,1},{1,0},{2,3},{3,2},{4,5},{5,4},{6,7},{7,6},{8,9},{9,8},{10,11... | collective-permute-start | bytes 2359304 | tf_op jit(solution)/shard_map/ppermute | solution.py:81
  30.6 6.3 %collective-permute-start.4 = (bf16[2,2,2,2,8,3200]{5,4,3,2,1,0:T(8,128)(2,1)S(1)}, bf16[2,2,2,2,8,3200]{5,4,3,2,1,0:T(8,128)(2,1)S(1)}, u32[]{:S(2)}, u32[]{:S(2)}) collective-permute-start(bf16[2,2,2,2,8,3200]{5,4,3,2,1,0:T(8,128)(2,1)S(1)} %get-tuple-element.26), channel_id=1, source_target_pairs={{0,1},{1,0},{2,3},{3,2},{4,5},{5,4},{6,7},{7,6},{8,9},{9,8},{10,11... | collective-permute-start | bytes 2457608 | tf_op jit(solution)/shard_map/ppermute | solution.py:81
  43.8 2.8 %collective-permute-start.10 = (bf16[2,2,2,2,8,3072]{5,4,3,2,1,0:T(8,128)(2,1)S(1)}, bf16[2,2,2,2,8,3072]{5,4,3,2,1,0:T(8,128)(2,1)S(1)}, u32[]{:S(2)}, u32[]{:S(2)}) collective-permute-start(bf16[2,2,2,2,8,3072]{5,4,3,2,1,0:T(8,128)(2,1)S(1)} %bitcast.104), channel_id=1, source_target_pairs={{0,1},{1,0},{2,3},{3,2},{4,5},{5,4},{6,7},{7,6},{8,9},{9,8},{10,11... | collective-permute-start | bytes 2359304 | tf_op jit(solution)/shard_map/ppermute | solution.py:81
  46.1 2.4 %collective-permute-start.15 = (bf16[2,2,2,2,8,3072]{5,4,2,3,0,1:T(8,128)(2,1)S(1)}, bf16[2,2,2,2,8,3072]{5,4,2,3,0,1:T(8,128)(2,1)S(1)}, u32[]{:S(2)}, u32[]{:S(2)}) collective-permute-start(bf16[2,2,2,2,8,3072]{5,4,2,3,0,1:T(8,128)(2,1)S(1)} %copy.9), channel_id=1, source_target_pairs={{0,1},{1,0},{2,3},{3,2},{4,5},{5,4},{6,7},{7,6},{8,9},{9,8},{10,11... | collective-permute-start | bytes 2359304 | tf_op jit(solution)/shard_map/ppermute | solution.py:81
  46.8 11.2 %collective-permute-start.11 = (bf16[2,2,2,8,3072]{4,3,2,1,0:T(8,128)(2,1)S(1)}, bf16[2,2,2,8,3072]{4,3,2,1,0:T(8,128)(2,1)S(1)}, u32[]{:S(2)}, u32[]{:S(2)}) collective-permute-start(bf16[2,2,2,8,3072]{4,3,2,1,0:T(8,128)(2,1)S(1)} %slice_bitcast_fusion.2), channel_id=1, source_target_pairs={{0,16},{16,0},{1,17},{17,1},{2,18},{18,2},{3,19},{19,3},{4,20},{20... | collective-permute-start | bytes 1179656 | tf_op jit(solution)/shard_map/ppermute | solution.py:81
  48.7 11.5 %collective-permute-start.16 = (bf16[2,2,2,8,3072]{4,3,1,2,0:T(8,128)(2,1)S(1)}, bf16[2,2,2,8,3072]{4,3,1,2,0:T(8,128)(2,1)S(1)}, u32[]{:S(2)}, u32[]{:S(2)}) collective-permute-start(bf16[2,2,2,8,3072]{4,3,1,2,0:T(8,128)(2,1)S(1)} %slice_bitcast_fusion), channel_id=1, source_target_pairs={{0,2},{1,3},{2,0},{3,1},{4,6},{5,7},{6,4},{7,5},{8,10},{9,11},{10,... | collective-permute-start | bytes 1179656 | tf_op jit(solution)/shard_map/ppermute | solution.py:81
  58.2 6.2 %collective-permute-start.12 = (bf16[2,2,8,3072]{3,2,1,0:T(8,128)(2,1)S(1)}, bf16[2,2,8,3072]{3,2,1,0:T(8,128)(2,1)S(1)}, u32[]{:S(2)}, u32[]{:S(2)}) collective-permute-start(bf16[2,2,8,3072]{3,2,1,0:T(8,128)(2,1)S(1)} %slice_bitcast_fusion.6), channel_id=1, source_target_pairs={{0,2},{1,3},{2,0},{3,1},{4,6},{5,7},{6,4},{7,5},{8,10},{9,11},{10,... | collective-permute-start | bytes 589832 | tf_op jit(solution)/shard_map/ppermute | solution.py:81
  60.3 6.4 %collective-permute-start.17 = (bf16[2,2,8,3072]{3,2,0,1:T(8,128)(2,1)S(1)}, bf16[2,2,8,3072]{3,2,0,1:T(8,128)(2,1)S(1)}, u32[]{:S(2)}, u32[]{:S(2)}) collective-permute-start(bf16[2,2,8,3072]{3,2,0,1:T(8,128)(2,1)S(1)} %slice_bitcast_fusion.4), channel_id=1, source_target_pairs={{0,16},{16,0},{1,17},{17,1},{2,18},{18,2},{3,19},{19,3},{4,20},{20... | collective-permute-start | bytes 589832 | tf_op jit(solution)/shard_map/ppermute | solution.py:81
  64.5 5.0 %collective-permute-start.13 = (bf16[2,8,3072]{2,1,0:T(8,128)(2,1)S(1)}, bf16[2,8,3072]{2,1,0:T(8,128)(2,1)S(1)}, u32[]{:S(2)}, u32[]{:S(2)}) collective-permute-start(bf16[2,8,3072]{2,1,0:T(8,128)(2,1)S(1)} %slice_bitcast_fusion.10), channel_id=1, source_target_pairs={{0,4},{4,0},{8,12},{12,8},{1,5},{5,1},{9,13},{13,9},{2,6},{6,2},{1... | collective-permute-start | bytes 294920 | tf_op jit(solution)/shard_map/ppermute | solution.py:81
  66.8 7.5 %collective-permute-start.18 = (bf16[2,8,3072]{2,1,0:T(8,128)(2,1)S(1)}, bf16[2,8,3072]{2,1,0:T(8,128)(2,1)S(1)}, u32[]{:S(2)}, u32[]{:S(2)}) collective-permute-start(bf16[2,8,3072]{2,1,0:T(8,128)(2,1)S(1)} %slice_bitcast_fusion.8), channel_id=1, source_target_pairs={{0,8},{4,12},{8,0},{12,4},{1,9},{5,13},{9,1},{13,5},{2,10},{6,14},... | collective-permute-start | bytes 294920 | tf_op jit(solution)/shard_map/ppermute | solution.py:81
  69.5 5.4 %collective-permute-start.14 = (bf16[8,3072]{1,0:T(8,128)(2,1)S(1)}, bf16[8,3072]{1,0:T(8,128)(2,1)S(1)}, u32[]{:S(2)}, u32[]{:S(2)}) collective-permute-start(bf16[8,3072]{1,0:T(8,128)(2,1)S(1)} %slice_bitcast_fusion.14), channel_id=1, source_target_pairs={{0,8},{4,12},{8,0},{12,4},{1,9},{5,13},{9,1},{13,5},{2,10},{6,14},... | collective-permute-start | bytes 147464 | tf_op jit(solution)/shard_map/ppermute | solution.py:81
  74.4 4.2 %collective-permute-start.19 = (bf16[8,3072]{1,0:T(8,128)(2,1)S(1)}, bf16[8,3072]{1,0:T(8,128)(2,1)S(1)}, u32[]{:S(2)}, u32[]{:S(2)}) collective-permute-start(bf16[8,3072]{1,0:T(8,128)(2,1)S(1)} %slice_bitcast_fusion.12), channel_id=1, source_target_pairs={{0,4},{4,0},{8,12},{12,8},{1,5},{5,1},{9,13},{13,9},{2,6},{6,2},{1... | collective-permute-start | bytes 147464 | tf_op jit(solution)/shard_map/ppermute | solution.py:81

commit v15 on v9

--- a/solution.py
+++ b/solution.py
@@ -242,7 +242,7 @@
     y_digits = digits_of("shard", ways["shard"], cores)
     core_digits = [Digit("shard", ways["shard"], 1, cores)]
     dim_order = core_digits + x_digits[::-1] + y_digits[::-1] + z_digits[::-1]
-    routes = [z_digits + y_digits + x_digits, z_digits + x_digits + y_digits]
+    routes = [z_digits + y_digits + x_digits, z_digits[::-1] + x_digits + y_digits]
 
     coefficients = slot_coefficients(expert_ids, gate_values, old_place, new_place)
     extra = jnp.concatenate(split_exact(coefficients), axis=1)

time: 79.6 us -> 82.3 us (1.034)
  waiting for transfers between devices: 29.3 us -> 31.5 us
    ppermute x20, waiting for transfers between devices: 29.3 us -> 31.5 us  [shift(): return lax.ppermute(value, self.name, pairs)]
where the time goes in v15:
time: 82.3 us; the launch traced here: 82 us
  waiting for transfers between devices  31.5 us (38%)
  starting transfers between devices  27.2 us (33%)
  Pallas kernels  17.8 us (22%)
  other arithmetic  3.74 us (5%)
  local copies, waits for them, and re-layouts  1.42 us (2%)
    ppermute x20, waiting for transfers between devices, shift(): return lax.ppermute(value, self.name, pairs)  31.5 us
    ppermute x20, starting transfers between devices, shift(): return lax.ppermute(value, self.name, pairs)  27.2 us
    pallas_call x2, Pallas kernels, gate_up_of(): pl.pallas_call(kernel, grid=(rows // row_block,), in_specs=specs + [pl.Bl...  9.27 us
    pallas_call x1, Pallas kernels, fetched(): pl.pallas_call(kernel, in_specs=[pl.BlockSpec(memory_space=pl.ANY)] * 2,...  4.58 us
    pallas_call x2, Pallas kernels, down_of(): pl.pallas_call(kernel, grid=(rows // row_block,), in_specs=[pl.BlockSpec(...  3.98 us
  transfers between devices with their start and end apart: 20, of which 16 were waited for; matrix products, arithmetic and copies ran while one was open for 4% of the time, Pallas kernels for 14%

profile of v15, /device:TPU:0, one launch (start us, length us, event | category | flops | bytes accessed | tf_op | source)
XLA Modules:
  0.0 82.0 jit_solution(2794196124636859730)
XLA Ops:
  0.0 0.8 %slice_bitcast_fusion.16 = (bf16[1,8,3072]{2,1,0:T(8,128)(2,1)S(1)}, bf16[8,3072]{1,0:T(8,128)(2,1)S(1)}, bf16[8,3072]{1,0:T(8,128)(2,1)S(1)}) fusion(bf16[8,6144]{1,0:T(8,128)(2,1)} %param.8), kind=kLoop, calls=%fused_computation.64 | loop fusion | bytes 245760 | tf_op jit(solution)/shard_map/stack | solution.py:47
  0.8 3.1 %collective-permute-start.5 = (bf16[8,3072]{1,0:T(8,128)(2,1)S(1)}, bf16[8,3072]{1,0:T(8,128)(2,1)S(1)}, u32[]{:S(2)}, u32[]{:S(2)}) collective-permute-start(bf16[8,3072]{1,0:T(8,128)(2,1)S(1)} %get-tuple-element.36), channel_id=1, source_target_pairs={{0,4},{4,0},{8,12},{12,8},{1,5},{5,1},{9,13},{13,9},{2,6},{6,2},{1... | collective-permute-start | bytes 147464 | tf_op jit(solution)/shard_map/ppermute | solution.py:44
  3.9 0.7 compare_convert_fusion
  4.7 0.7 select_reduce_fusion
  5.6 2.7 %collective-permute-start = (bf16[8,3200]{1,0:T(8,128)(2,1)S(1)}, bf16[8,3200]{1,0:T(8,128)(2,1)S(1)}, u32[]{:S(2)}, u32[]{:S(2)}) collective-permute-start(bf16[8,3200]{1,0:T(8,128)(2,1)S(1)} %get-tuple-element.39), channel_id=1, source_target_pairs={{0,8},{4,12},{8,0},{12,4},{1,9},{5,13},{9,1},{13,5},{2,10},{6,14},... | collective-permute-start | bytes 153608 | tf_op jit(solution)/shard_map/ppermute | solution.py:44
  8.3 0.8 collective-permute-start.6
  9.1 1.7 %collective-permute-done = bf16[8,3200]{1,0:T(8,128)(2,1)S(1)} collective-permute-done((bf16[8,3200]{1,0:T(8,128)(2,1)S(1)}, bf16[8,3200]{1,0:T(8,128)(2,1)S(1)}, u32[]{:S(2)}, u32[]{:S(2)}) %collective-permute-start) | collective-permute-done | bytes 51232 | tf_op jit(solution)/shard_map/ppermute | solution.py:44
  10.8 2.3 %collective-permute-start.1 = (bf16[2,8,3200]{2,1,0:T(8,128)(2,1)S(1)}, bf16[2,8,3200]{2,1,0:T(8,128)(2,1)S(1)}, u32[]{:S(2)}, u32[]{:S(2)}) collective-permute-start(bf16[2,8,3200]{2,1,0:T(8,128)(2,1)S(1)} %get-tuple-element.32), channel_id=1, source_target_pairs={{0,4},{4,0},{8,12},{12,8},{1,5},{5,1},{9,13},{13,9},{2,6},{6,2},{1... | collective-permute-start | bytes 307208 | tf_op jit(solution)/shard_map/ppermute | solution.py:44
  13.2 2.2 %collective-permute-done.6 = bf16[2,8,3072]{2,1,0:T(8,128)(2,1)S(1)} collective-permute-done((bf16[2,8,3072]{2,1,0:T(8,128)(2,1)S(1)}, bf16[2,8,3072]{2,1,0:T(8,128)(2,1)S(1)}, u32[]{:S(2)}, u32[]{:S(2)}) %collective-permute-start.6) | collective-permute-done | bytes 98336 | tf_op jit(solution)/shard_map/ppermute | solution.py:44
  15.4 1.6 %collective-permute-start.7 = (bf16[2,2,8,3072]{3,2,0,1:T(8,128)(2,1)S(1)}, bf16[2,2,8,3072]{3,2,0,1:T(8,128)(2,1)S(1)}, u32[]{:S(2)}, u32[]{:S(2)}) collective-permute-start(bf16[2,2,8,3072]{3,2,0,1:T(8,128)(2,1)S(1)} %get-tuple-element.30), channel_id=1, source_target_pairs={{0,16},{16,0},{1,17},{17,1},{2,18},{18,2},{3,19},{19,3},{4,20},{20... | collective-permute-start | bytes 589832 | tf_op jit(solution)/shard_map/ppermute | solution.py:44
  17.0 1.7 %collective-permute-start.2 = (bf16[2,2,8,3200]{3,2,1,0:T(8,128)(2,1)S(1)}, bf16[2,2,8,3200]{3,2,1,0:T(8,128)(2,1)S(1)}, u32[]{:S(2)}, u32[]{:S(2)}) collective-permute-start(bf16[2,2,8,3200]{3,2,1,0:T(8,128)(2,1)S(1)} %get-tuple-element.28), channel_id=1, source_target_pairs={{0,2},{1,3},{2,0},{3,1},{4,6},{5,7},{6,4},{7,5},{8,10},{9,11},{10,... | collective-permute-start | bytes 614408 | tf_op jit(solution)/shard_map/ppermute | solution.py:44
  18.7 2.8 %collective-permute-done.7 = bf16[2,2,8,3072]{3,2,0,1:T(8,128)(2,1)S(1)} collective-permute-done((bf16[2,2,8,3072]{3,2,0,1:T(8,128)(2,1)S(1)}, bf16[2,2,8,3072]{3,2,0,1:T(8,128)(2,1)S(1)}, u32[]{:S(2)}, u32[]{:S(2)}) %collective-permute-start.7) | collective-permute-done | bytes 196640 | tf_op jit(solution)/shard_map/ppermute | solution.py:44
  21.5 1.8 %collective-permute-start.8 = (bf16[2,2,2,8,3072]{4,3,1,2,0:T(8,128)(2,1)S(1)}, bf16[2,2,2,8,3072]{4,3,1,2,0:T(8,128)(2,1)S(1)}, u32[]{:S(2)}, u32[]{:S(2)}) collective-permute-start(bf16[2,2,2,8,3072]{4,3,1,2,0:T(8,128)(2,1)S(1)} %get-tuple-element.26), channel_id=1, source_target_pairs={{0,2},{1,3},{2,0},{3,1},{4,6},{5,7},{6,4},{7,5},{8,10},{9,11},{10,... | collective-permute-start | bytes 1179656 | tf_op jit(solution)/shard_map/ppermute | solution.py:44
  23.3 0.3 collective-permute-done.2
  23.7 1.2 %collective-permute-start.3 = (bf16[2,2,2,8,3200]{4,3,2,1,0:T(8,128)(2,1)S(1)}, bf16[2,2,2,8,3200]{4,3,2,1,0:T(8,128)(2,1)S(1)}, u32[]{:S(2)}, u32[]{:S(2)}) collective-permute-start(bf16[2,2,2,8,3200]{4,3,2,1,0:T(8,128)(2,1)S(1)} %get-tuple-element.24.refs_1_), channel_id=1, source_target_pairs={{0,16},{16,0},{1,17},{17,1},{2,18},{18,2},{3,19},{19,3},{4,20},{20... | collective-permute-start | bytes 1228808 | tf_op jit(solution)/shard_map/ppermute | solution.py:44
  25.0 4.6 %shard_map.73.refs_1_ = bf16[4,2,256,3072]{3,2,1,0:T(8,128)(2,1)S(1)} custom-call(bf16[4,2,256,6144]{3,2,1,0:T(8,128)(2,1)} %refs_2_.1, bf16[2,2,2,8,3200]{4,3,2,1,0:T(8,128)(2,1)S(1)} %get-tuple-element.24.refs_1_), custom_call_target="tpu_custom_call" | custom-call | bytes 25165824 | tf_op jit(solution)/shard_map/pallas_call | solution.py:86
  29.6 2.1 %collective-permute-done.8 = bf16[2,2,2,8,3072]{4,3,1,2,0:T(8,128)(2,1)S(1)} collective-permute-done((bf16[2,2,2,8,3072]{4,3,1,2,0:T(8,128)(2,1)S(1)}, bf16[2,2,2,8,3072]{4,3,1,2,0:T(8,128)(2,1)S(1)}, u32[]{:S(2)}, u32[]{:S(2)}) %collective-permute-start.8) | collective-permute-done | bytes 393248 | tf_op jit(solution)/shard_map/ppermute | solution.py:44
  31.8 1.2 %collective-permute-done.3 = bf16[2,2,2,8,3200]{4,3,2,1,0:T(8,128)(2,1)S(1)} collective-permute-done((bf16[2,2,2,8,3200]{4,3,2,1,0:T(8,128)(2,1)S(1)}, bf16[2,2,2,8,3200]{4,3,2,1,0:T(8,128)(2,1)S(1)}, u32[]{:S(2)}, u32[]{:S(2)}) %collective-permute-start.3) | collective-permute-done | bytes 409632 | tf_op jit(solution)/shard_map/ppermute | solution.py:44
  33.0 0.1 fusion.24
  33.2 0.8 %collective-permute-done.9 = bf16[2,2,2,2,8,3072]{5,4,2,3,0,1:T(8,128)(2,1)S(1)} collective-permute-done((bf16[2,2,2,2,8,3072]{5,4,2,3,0,1:T(8,128)(2,1)S(1)}, bf16[2,2,2,2,8,3072]{5,4,2,3,0,1:T(8,128)(2,1)S(1)}, u32[]{:S(2)}, u32[]{:S(2)}) %collective-permute-start.9) | collective-permute-done | bytes 786464 | tf_op jit(solution)/shard_map/ppermute | solution.py:44
  34.0 0.1 pad_maximum_fusion.1
  34.2 0.1 copy.15
  34.3 4.7 %shard_map.74 = (f32[256,2048]{1,0:T(8,128)S(1)}, bf16[4,2,256,3072]{3,2,1,0:T(8,128)(2,1)S(1)}) custom-call(bf16[256,3072]{1,0:T(8,128)(2,1)S(1)} %bitcast.94, bf16[4,2,256,3072]{3,2,1,0:T(8,128)(2,1)S(1)} %shard_map.73.refs_1_, bf16[4,2,256,6144]{3,2,1,0:T(8,128)(2,1)} %refs_2_.1), custom_call_target="tpu_custom_call" | custom-call | flops 3221225472 | bytes 14680064 | tf_op jit(solution)/shard_map/pallas_call | solution.py:171
  39.0 0.2 pad_maximum_fusion
  39.2 4.6 %shard_map.75 = (bf16[4,256,256]{2,1,0:T(8,128)(2,1)S(1)}, bf16[4,256,6144]{2,1,0:T(8,128)(2,1)S(1)}) custom-call(bf16[256,3200]{1,0:T(8,128)(2,1)S(1)} %bitcast.93, f32[256,2048]{1,0:T(8,128)S(1)} %get-tuple-element.13.refs_1_, bf16[4,2,256,3072]{3,2,1,0:T(8,128)(2,1)S(1)} %get-tuple-element.14.refs_2_, bf16[4,256,6144]{2,1,0:T(8,128)(2,1)} %refs_3_.1), custom_call_target="tpu_custom_call" | custom-call | flops 3221225472 | bytes 14680064 | tf_op jit(solution)/shard_map/pallas_call | solution.py:171
  43.8 2.0 %shard_map.76 = bf16[256,3072]{1,0:T(8,128)(2,1)S(1)} custom-call(bf16[4,256,256]{2,1,0:T(8,128)(2,1)S(1)} %get-tuple-element.15.refs_0_, bf16[4,256,6144]{2,1,0:T(8,128)(2,1)S(1)} %get-tuple-element.16.refs_1_), custom_call_target="tpu_custom_call" | custom-call | flops 1610612736 | bytes 8388608 | tf_op jit(solution)/shard_map/pallas_call | solution.py:214
  45.9 0.2 collective-permute-start.10
  46.1 2.0 %shard_map.77 = bf16[256,3072]{1,0:T(8,128)(2,1)S(1)} custom-call(bf16[4,256,256]{2,1,0:T(8,128)(2,1)S(1)} %get-tuple-element.15.refs_0_, bf16[4,256,6144]{2,1,0:T(8,128)(2,1)S(1)} %get-tuple-element.16.refs_1_), custom_call_target="tpu_custom_call" | custom-call | flops 1610612736 | bytes 8388608 | tf_op jit(solution)/shard_map/pallas_call | solution.py:214
  48.3 0.4 collective-permute-start.15
  48.7 0.2 fusion
  49.0 1.3 %collective-permute-start.11 = (bf16[2,2,2,8,3072]{4,3,2,1,0:T(8,128)(2,1)S(1)}, bf16[2,2,2,8,3072]{4,3,2,1,0:T(8,128)(2,1)S(1)}, u32[]{:S(2)}, u32[]{:S(2)}) collective-permute-start(bf16[2,2,2,8,3072]{4,3,2,1,0:T(8,128)(2,1)S(1)} %slice_bitcast_fusion.2), channel_id=1, source_target_pairs={{0,16},{16,0},{1,17},{17,1},{2,18},{18,2},{3,19},{19,3},{4,20},{20... | collective-permute-start | bytes 1179656 | tf_op jit(solution)/shard_map/ppermute | solution.py:44
  50.3 0.4 collective-permute-done.15
  50.6 0.2 fusion.1
  50.9 1.6 %collective-permute-start.16 = (bf16[2,2,2,8,3072]{4,3,1,2,0:T(8,128)(2,1)S(1)}, bf16[2,2,2,8,3072]{4,3,1,2,0:T(8,128)(2,1)S(1)}, u32[]{:S(2)}, u32[]{:S(2)}) collective-permute-start(bf16[2,2,2,8,3072]{4,3,1,2,0:T(8,128)(2,1)S(1)} %slice_bitcast_fusion), channel_id=1, source_target_pairs={{0,2},{1,3},{2,0},{3,1},{4,6},{5,7},{6,4},{7,5},{8,10},{9,11},{10,... | collective-permute-start | bytes 1179656 | tf_op jit(solution)/shard_map/ppermute | solution.py:44
  52.5 7.7 %collective-permute-done.11 = bf16[2,2,2,8,3072]{4,3,2,1,0:T(8,128)(2,1)S(1)} collective-permute-done((bf16[2,2,2,8,3072]{4,3,2,1,0:T(8,128)(2,1)S(1)}, bf16[2,2,2,8,3072]{4,3,2,1,0:T(8,128)(2,1)S(1)}, u32[]{:S(2)}, u32[]{:S(2)}) %collective-permute-start.11) | collective-permute-done | bytes 393248 | tf_op jit(solution)/shard_map/ppermute | solution.py:44
  60.3 1.6 %collective-permute-start.12 = (bf16[2,2,8,3072]{3,2,1,0:T(8,128)(2,1)S(1)}, bf16[2,2,8,3072]{3,2,1,0:T(8,128)(2,1)S(1)}, u32[]{:S(2)}, u32[]{:S(2)}) collective-permute-start(bf16[2,2,8,3072]{3,2,1,0:T(8,128)(2,1)S(1)} %slice_bitcast_fusion.6), channel_id=1, source_target_pairs={{0,2},{1,3},{2,0},{3,1},{4,6},{5,7},{6,4},{7,5},{8,10},{9,11},{10,... | collective-permute-start | bytes 589832 | tf_op jit(solution)/shard_map/ppermute | solution.py:44
  61.9 0.4 collective-permute-done.16
  62.5 1.3 %collective-permute-start.17 = (bf16[2,2,8,3072]{3,2,0,1:T(8,128)(2,1)S(1)}, bf16[2,2,8,3072]{3,2,0,1:T(8,128)(2,1)S(1)}, u32[]{:S(2)}, u32[]{:S(2)}) collective-permute-start(bf16[2,2,8,3072]{3,2,0,1:T(8,128)(2,1)S(1)} %slice_bitcast_fusion.4), channel_id=1, source_target_pairs={{0,16},{16,0},{1,17},{17,1},{2,18},{18,2},{3,19},{19,3},{4,20},{20... | collective-permute-start | bytes 589832 | tf_op jit(solution)/shard_map/ppermute | solution.py:44
  63.8 2.8 %collective-permute-done.12 = bf16[2,2,8,3072]{3,2,1,0:T(8,128)(2,1)S(1)} collective-permute-done((bf16[2,2,8,3072]{3,2,1,0:T(8,128)(2,1)S(1)}, bf16[2,2,8,3072]{3,2,1,0:T(8,128)(2,1)S(1)}, u32[]{:S(2)}, u32[]{:S(2)}) %collective-permute-start.12) | collective-permute-done | bytes 196640 | tf_op jit(solution)/shard_map/ppermute | solution.py:44
  66.6 0.6 collective-permute-start.13
  67.2 1.7 %collective-permute-done.17 = bf16[2,2,8,3072]{3,2,0,1:T(8,128)(2,1)S(1)} collective-permute-done((bf16[2,2,8,3072]{3,2,0,1:T(8,128)(2,1)S(1)}, bf16[2,2,8,3072]{3,2,0,1:T(8,128)(2,1)S(1)}, u32[]{:S(2)}, u32[]{:S(2)}) %collective-permute-start.17) | collective-permute-done | bytes 196640 | tf_op jit(solution)/shard_map/ppermute | solution.py:44
  69.0 2.5 %collective-permute-start.18 = (bf16[2,8,3072]{2,1,0:T(8,128)(2,1)S(1)}, bf16[2,8,3072]{2,1,0:T(8,128)(2,1)S(1)}, u32[]{:S(2)}, u32[]{:S(2)}) collective-permute-start(bf16[2,8,3072]{2,1,0:T(8,128)(2,1)S(1)} %slice_bitcast_fusion.8), channel_id=1, source_target_pairs={{0,8},{4,12},{8,0},{12,4},{1,9},{5,13},{9,1},{13,5},{2,10},{6,14},... | collective-permute-start | bytes 294920 | tf_op jit(solution)/shard_map/ppermute | solution.py:44
  71.5 0.9 %collective-permute-done.13 = bf16[2,8,3072]{2,1,0:T(8,128)(2,1)S(1)} collective-permute-done((bf16[2,8,3072]{2,1,0:T(8,128)(2,1)S(1)}, bf16[2,8,3072]{2,1,0:T(8,128)(2,1)S(1)}, u32[]{:S(2)}, u32[]{:S(2)}) %collective-permute-start.13) | collective-permute-done | bytes 98336 | tf_op jit(solution)/shard_map/ppermute | solution.py:44
  72.4 2.3 %collective-permute-start.14 = (bf16[8,3072]{1,0:T(8,128)(2,1)S(1)}, bf16[8,3072]{1,0:T(8,128)(2,1)S(1)}, u32[]{:S(2)}, u32[]{:S(2)}) collective-permute-start(bf16[8,3072]{1,0:T(8,128)(2,1)S(1)} %slice_bitcast_fusion.14), channel_id=1, source_target_pairs={{0,8},{4,12},{8,0},{12,4},{1,9},{5,13},{9,1},{13,5},{2,10},{6,14},... | collective-permute-start | bytes 147464 | tf_op jit(solution)/shard_map/ppermute | solution.py:44
  74.7 2.4 %collective-permute-done.18 = bf16[2,8,3072]{2,1,0:T(8,128)(2,1)S(1)} collective-permute-done((bf16[2,8,3072]{2,1,0:T(8,128)(2,1)S(1)}, bf16[2,8,3072]{2,1,0:T(8,128)(2,1)S(1)}, u32[]{:S(2)}, u32[]{:S(2)}) %collective-permute-start.18) | collective-permute-done | bytes 98336 | tf_op jit(solution)/shard_map/ppermute | solution.py:44
  77.3 0.9 %collective-permute-done.14 = bf16[8,3072]{1,0:T(8,128)(2,1)S(1)} collective-permute-done((bf16[8,3072]{1,0:T(8,128)(2,1)S(1)}, bf16[8,3072]{1,0:T(8,128)(2,1)S(1)}, u32[]{:S(2)}, u32[]{:S(2)}) %collective-permute-start.14) | collective-permute-done | bytes 49184 | tf_op jit(solution)/shard_map/ppermute | solution.py:44
  78.2 3.2 %collective-permute-done.19 = bf16[8,3072]{1,0:T(8,128)(2,1)S(1)} collective-permute-done((bf16[8,3072]{1,0:T(8,128)(2,1)S(1)}, bf16[8,3072]{1,0:T(8,128)(2,1)S(1)}, u32[]{:S(2)}, u32[]{:S(2)}) %collective-permute-start.19) | collective-permute-done | bytes 49184 | tf_op jit(solution)/shard_map/ppermute | solution.py:44
  81.4 0.6 pad_maximum_fusion.10
  (38 shorter events, 1.5 us)
Async XLA Ops:
  0.8 7.5 %collective-permute-start.5 = (bf16[8,3072]{1,0:T(8,128)(2,1)S(1)}, bf16[8,3072]{1,0:T(8,128)(2,1)S(1)}, u32[]{:S(2)}, u32[]{:S(2)}) collective-permute-start(bf16[8,3072]{1,0:T(8,128)(2,1)S(1)} %get-tuple-element.36), channel_id=1, source_target_pairs={{0,4},{4,0},{8,12},{12,8},{1,5},{5,1},{9,13},{13,9},{2,6},{6,2},{1... | collective-permute-start | bytes 147464 | tf_op jit(solution)/shard_map/ppermute | solution.py:44
  5.6 5.2 %collective-permute-start = (bf16[8,3200]{1,0:T(8,128)(2,1)S(1)}, bf16[8,3200]{1,0:T(8,128)(2,1)S(1)}, u32[]{:S(2)}, u32[]{:S(2)}) collective-permute-start(bf16[8,3200]{1,0:T(8,128)(2,1)S(1)} %get-tuple-element.39), channel_id=1, source_target_pairs={{0,8},{4,12},{8,0},{12,4},{1,9},{5,13},{9,1},{13,5},{2,10},{6,14},... | collective-permute-start | bytes 153608 | tf_op jit(solution)/shard_map/ppermute | solution.py:44
  8.3 7.0 %collective-permute-start.6 = (bf16[2,8,3072]{2,1,0:T(8,128)(2,1)S(1)}, bf16[2,8,3072]{2,1,0:T(8,128)(2,1)S(1)}, u32[]{:S(2)}, u32[]{:S(2)}) collective-permute-start(bf16[2,8,3072]{2,1,0:T(8,128)(2,1)S(1)} %get-tuple-element.34), channel_id=1, source_target_pairs={{0,8},{4,12},{8,0},{12,4},{1,9},{5,13},{9,1},{13,5},{2,10},{6,14},... | collective-permute-start | bytes 294920 | tf_op jit(solution)/shard_map/ppermute | solution.py:44
  10.8 6.2 %collective-permute-start.1 = (bf16[2,8,3200]{2,1,0:T(8,128)(2,1)S(1)}, bf16[2,8,3200]{2,1,0:T(8,128)(2,1)S(1)}, u32[]{:S(2)}, u32[]{:S(2)}) collective-permute-start(bf16[2,8,3200]{2,1,0:T(8,128)(2,1)S(1)} %get-tuple-element.32), channel_id=1, source_target_pairs={{0,4},{4,0},{8,12},{12,8},{1,5},{5,1},{9,13},{13,9},{2,6},{6,2},{1... | collective-permute-start | bytes 307208 | tf_op jit(solution)/shard_map/ppermute | solution.py:44
  15.4 6.1 %collective-permute-start.7 = (bf16[2,2,8,3072]{3,2,0,1:T(8,128)(2,1)S(1)}, bf16[2,2,8,3072]{3,2,0,1:T(8,128)(2,1)S(1)}, u32[]{:S(2)}, u32[]{:S(2)}) collective-permute-start(bf16[2,2,8,3072]{3,2,0,1:T(8,128)(2,1)S(1)} %get-tuple-element.30), channel_id=1, source_target_pairs={{0,16},{16,0},{1,17},{17,1},{2,18},{18,2},{3,19},{19,3},{4,20},{20... | collective-permute-start | bytes 589832 | tf_op jit(solution)/shard_map/ppermute | solution.py:44
  17.0 6.6 %collective-permute-start.2 = (bf16[2,2,8,3200]{3,2,1,0:T(8,128)(2,1)S(1)}, bf16[2,2,8,3200]{3,2,1,0:T(8,128)(2,1)S(1)}, u32[]{:S(2)}, u32[]{:S(2)}) collective-permute-start(bf16[2,2,8,3200]{3,2,1,0:T(8,128)(2,1)S(1)} %get-tuple-element.28), channel_id=1, source_target_pairs={{0,2},{1,3},{2,0},{3,1},{4,6},{5,7},{6,4},{7,5},{8,10},{9,11},{10,... | collective-permute-start | bytes 614408 | tf_op jit(solution)/shard_map/ppermute | solution.py:44
  21.5 10.1 %collective-permute-start.8 = (bf16[2,2,2,8,3072]{4,3,1,2,0:T(8,128)(2,1)S(1)}, bf16[2,2,2,8,3072]{4,3,1,2,0:T(8,128)(2,1)S(1)}, u32[]{:S(2)}, u32[]{:S(2)}) collective-permute-start(bf16[2,2,2,8,3072]{4,3,1,2,0:T(8,128)(2,1)S(1)} %get-tuple-element.26), channel_id=1, source_target_pairs={{0,2},{1,3},{2,0},{3,1},{4,6},{5,7},{6,4},{7,5},{8,10},{9,11},{10,... | collective-permute-start | bytes 1179656 | tf_op jit(solution)/shard_map/ppermute | solution.py:44
  23.7 9.3 %collective-permute-start.3 = (bf16[2,2,2,8,3200]{4,3,2,1,0:T(8,128)(2,1)S(1)}, bf16[2,2,2,8,3200]{4,3,2,1,0:T(8,128)(2,1)S(1)}, u32[]{:S(2)}, u32[]{:S(2)}) collective-permute-start(bf16[2,2,2,8,3200]{4,3,2,1,0:T(8,128)(2,1)S(1)} %get-tuple-element.24.refs_1_), channel_id=1, source_target_pairs={{0,16},{16,0},{1,17},{17,1},{2,18},{18,2},{3,19},{19,3},{4,20},{20... | collective-permute-start | bytes 1228808 | tf_op jit(solution)/shard_map/ppermute | solution.py:44
  31.7 2.4 %collective-permute-start.9 = (bf16[2,2,2,2,8,3072]{5,4,2,3,0,1:T(8,128)(2,1)S(1)}, bf16[2,2,2,2,8,3072]{5,4,2,3,0,1:T(8,128)(2,1)S(1)}, u32[]{:S(2)}, u32[]{:S(2)}) collective-permute-start(bf16[2,2,2,2,8,3072]{5,4,2,3,0,1:T(8,128)(2,1)S(1)} %pad_maximum_fusion.3), channel_id=1, source_target_pairs={{0,1},{1,0},{2,3},{3,2},{4,5},{5,4},{6,7},{7,6},{8,9},{9,8},{10,11... | collective-permute-start | bytes 2359304 | tf_op jit(solution)/shard_map/ppermute | solution.py:44
  33.1 5.9 %collective-permute-start.4 = (bf16[2,2,2,2,8,3200]{5,4,3,2,1,0:T(8,128)(2,1)S(1)}, bf16[2,2,2,2,8,3200]{5,4,3,2,1,0:T(8,128)(2,1)S(1)}, u32[]{:S(2)}, u32[]{:S(2)}) collective-permute-start(bf16[2,2,2,2,8,3200]{5,4,3,2,1,0:T(8,128)(2,1)S(1)} %get-tuple-element.22), channel_id=1, source_target_pairs={{0,1},{1,0},{2,3},{3,2},{4,5},{5,4},{6,7},{7,6},{8,9},{9,8},{10,11... | collective-permute-start | bytes 2457608 | tf_op jit(solution)/shard_map/ppermute | solution.py:44
  45.9 2.8 %collective-permute-start.10 = (bf16[2,2,2,2,8,3072]{5,4,3,2,1,0:T(8,128)(2,1)S(1)}, bf16[2,2,2,2,8,3072]{5,4,3,2,1,0:T(8,128)(2,1)S(1)}, u32[]{:S(2)}, u32[]{:S(2)}) collective-permute-start(bf16[2,2,2,2,8,3072]{5,4,3,2,1,0:T(8,128)(2,1)S(1)} %bitcast.100), channel_id=1, source_target_pairs={{0,1},{1,0},{2,3},{3,2},{4,5},{5,4},{6,7},{7,6},{8,9},{9,8},{10,11... | collective-permute-start | bytes 2359304 | tf_op jit(solution)/shard_map/ppermute | solution.py:44
  48.3 2.4 %collective-permute-start.15 = (bf16[2,2,2,2,8,3072]{5,4,2,3,0,1:T(8,128)(2,1)S(1)}, bf16[2,2,2,2,8,3072]{5,4,2,3,0,1:T(8,128)(2,1)S(1)}, u32[]{:S(2)}, u32[]{:S(2)}) collective-permute-start(bf16[2,2,2,2,8,3072]{5,4,2,3,0,1:T(8,128)(2,1)S(1)} %copy.16), channel_id=1, source_target_pairs={{0,1},{1,0},{2,3},{3,2},{4,5},{5,4},{6,7},{7,6},{8,9},{9,8},{10,11... | collective-permute-start | bytes 2359304 | tf_op jit(solution)/shard_map/ppermute | solution.py:44
  49.0 11.2 %collective-permute-start.11 = (bf16[2,2,2,8,3072]{4,3,2,1,0:T(8,128)(2,1)S(1)}, bf16[2,2,2,8,3072]{4,3,2,1,0:T(8,128)(2,1)S(1)}, u32[]{:S(2)}, u32[]{:S(2)}) collective-permute-start(bf16[2,2,2,8,3072]{4,3,2,1,0:T(8,128)(2,1)S(1)} %slice_bitcast_fusion.2), channel_id=1, source_target_pairs={{0,16},{16,0},{1,17},{17,1},{2,18},{18,2},{3,19},{19,3},{4,20},{20... | collective-permute-start | bytes 1179656 | tf_op jit(solution)/shard_map/ppermute | solution.py:44
  50.9 11.5 %collective-permute-start.16 = (bf16[2,2,2,8,3072]{4,3,1,2,0:T(8,128)(2,1)S(1)}, bf16[2,2,2,8,3072]{4,3,1,2,0:T(8,128)(2,1)S(1)}, u32[]{:S(2)}, u32[]{:S(2)}) collective-permute-start(bf16[2,2,2,8,3072]{4,3,1,2,0:T(8,128)(2,1)S(1)} %slice_bitcast_fusion), channel_id=1, source_target_pairs={{0,2},{1,3},{2,0},{3,1},{4,6},{5,7},{6,4},{7,5},{8,10},{9,11},{10,... | collective-permute-start | bytes 1179656 | tf_op jit(solution)/shard_map/ppermute | solution.py:44
  60.3 6.2 %collective-permute-start.12 = (bf16[2,2,8,3072]{3,2,1,0:T(8,128)(2,1)S(1)}, bf16[2,2,8,3072]{3,2,1,0:T(8,128)(2,1)S(1)}, u32[]{:S(2)}, u32[]{:S(2)}) collective-permute-start(bf16[2,2,8,3072]{3,2,1,0:T(8,128)(2,1)S(1)} %slice_bitcast_fusion.6), channel_id=1, source_target_pairs={{0,2},{1,3},{2,0},{3,1},{4,6},{5,7},{6,4},{7,5},{8,10},{9,11},{10,... | collective-permute-start | bytes 589832 | tf_op jit(solution)/shard_map/ppermute | solution.py:44
  62.5 6.4 %collective-permute-start.17 = (bf16[2,2,8,3072]{3,2,0,1:T(8,128)(2,1)S(1)}, bf16[2,2,8,3072]{3,2,0,1:T(8,128)(2,1)S(1)}, u32[]{:S(2)}, u32[]{:S(2)}) collective-permute-start(bf16[2,2,8,3072]{3,2,0,1:T(8,128)(2,1)S(1)} %slice_bitcast_fusion.4), channel_id=1, source_target_pairs={{0,16},{16,0},{1,17},{17,1},{2,18},{18,2},{3,19},{19,3},{4,20},{20... | collective-permute-start | bytes 589832 | tf_op jit(solution)/shard_map/ppermute | solution.py:44
  66.6 5.7 %collective-permute-start.13 = (bf16[2,8,3072]{2,1,0:T(8,128)(2,1)S(1)}, bf16[2,8,3072]{2,1,0:T(8,128)(2,1)S(1)}, u32[]{:S(2)}, u32[]{:S(2)}) collective-permute-start(bf16[2,8,3072]{2,1,0:T(8,128)(2,1)S(1)} %slice_bitcast_fusion.10), channel_id=1, source_target_pairs={{0,4},{4,0},{8,12},{12,8},{1,5},{5,1},{9,13},{13,9},{2,6},{6,2},{1... | collective-permute-start | bytes 294920 | tf_op jit(solution)/shard_map/ppermute | solution.py:44
  69.0 8.2 %collective-permute-start.18 = (bf16[2,8,3072]{2,1,0:T(8,128)(2,1)S(1)}, bf16[2,8,3072]{2,1,0:T(8,128)(2,1)S(1)}, u32[]{:S(2)}, u32[]{:S(2)}) collective-permute-start(bf16[2,8,3072]{2,1,0:T(8,128)(2,1)S(1)} %slice_bitcast_fusion.8), channel_id=1, source_target_pairs={{0,8},{4,12},{8,0},{12,4},{1,9},{5,13},{9,1},{13,5},{2,10},{6,14},... | collective-permute-start | bytes 294920 | tf_op jit(solution)/shard_map/ppermute | solution.py:44
  72.4 5.7 %collective-permute-start.14 = (bf16[8,3072]{1,0:T(8,128)(2,1)S(1)}, bf16[8,3072]{1,0:T(8,128)(2,1)S(1)}, u32[]{:S(2)}, u32[]{:S(2)}) collective-permute-start(bf16[8,3072]{1,0:T(8,128)(2,1)S(1)} %slice_bitcast_fusion.14), channel_id=1, source_target_pairs={{0,8},{4,12},{8,0},{12,4},{1,9},{5,13},{9,1},{13,5},{2,10},{6,14},... | collective-permute-start | bytes 147464 | tf_op jit(solution)/shard_map/ppermute | solution.py:44
  77.2 4.2 %collective-permute-start.19 = (bf16[8,3072]{1,0:T(8,128)(2,1)S(1)}, bf16[8,3072]{1,0:T(8,128)(2,1)S(1)}, u32[]{:S(2)}, u32[]{:S(2)}) collective-permute-start(bf16[8,3072]{1,0:T(8,128)(2,1)S(1)} %slice_bitcast_fusion.12), channel_id=1, source_target_pairs={{0,4},{4,0},{8,12},{12,8},{1,5},{5,1},{9,13},{13,9},{2,6},{6,2},{1... | collective-permute-start | bytes 147464 | tf_op jit(solution)/shard_map/ppermute | solution.py:44

commit v16 on v14

--- a/solution.py
+++ b/solution.py
@@ -331,7 +331,8 @@
         block = down_of(hidden, down_weight, number, half)
         block = block.reshape([digit.size for digit in dim_order] + [rows, half])
         held = list(dim_order)
-        for digit in core_digits + route[::-1]:
+        along_z = routes[1 - number][: len(z_digits)][::-1]
+        for digit in core_digits + route[len(z_digits) :][::-1] + along_z:
             block = digit.reduce(block, held.index(digit))
             held.remove(digit)
         results.append(block)

time: 79.5 us -> 78.1 us (0.982)
  waiting for transfers between devices: 27.7 us -> 24.6 us
  starting transfers between devices: 29.6 us -> 31.3 us
    ppermute x20, waiting for transfers between devices: 27.7 us -> 24.6 us  [shift(): return lax.ppermute(value, self.name, pairs)]
    ppermute x20, starting transfers between devices: 29.6 us -> 31.3 us  [shift(): return lax.ppermute(value, self.name, pairs)]
  transfers between devices with their start and end apart: 20 -> 20, of which waited for: 16 -> 15; matrix products, arithmetic and copies ran while one was open for 2% -> 2% of each run, Pallas kernels for 14% -> 14%
where the time goes in v16:
time: 78.1 us; the launch traced here: 77.8 us
  starting transfers between devices  31.3 us (40%)
  waiting for transfers between devices  24.6 us (31%)
  Pallas kernels  19 us (24%)
  other arithmetic  2.1 us (3%)
    ppermute x20, starting transfers between devices, shift(): return lax.ppermute(value, self.name, pairs)  31.3 us
    ppermute x20, waiting for transfers between devices, shift(): return lax.ppermute(value, self.name, pairs)  24.6 us
    pallas_call x2, Pallas kernels, gate_up_of(): pl.pallas_call(kernel, grid=(rows // row_block,), in_specs=specs + [pl.Bl...  9.27 us
    pallas_call x1, Pallas kernels, fetched(): pl.pallas_call(kernel, in_specs=[pl.BlockSpec(memory_space=pl.ANY)] * 2,...  4.58 us
    pallas_call x2, Pallas kernels, down_of(): pl.pallas_call(kernel, grid=(rows // row_block,), in_specs=[pl.BlockSpec(...  3.99 us
  transfers between devices with their start and end apart: 20, of which 15 were waited for; matrix products, arithmetic and copies ran while one was open for 2% of the time, Pallas kernels for 14%

profile of v16, /device:TPU:0, one launch (start us, length us, event | category | flops | bytes accessed | tf_op | source)
XLA Modules:
  0.0 77.8 jit_solution(9243371575798657298)
XLA Ops:
  0.0 1.2 %shard_map.73 = (bf16[8,3200]{1,0:T(8,128)(2,1)S(1)}, bf16[8,3072]{1,0:T(8,128)(2,1)S(1)}) custom-call(bf16[8,6144]{1,0:T(8,128)(2,1)} %tokens_ref.1, s32[2,8]{1,0:T(2,128)} %bitcast.114, f32[2,8]{1,0:T(2,128)} %bitcast.115, s32[1,4]{1,0:T(1,128)} %bitcast.116, s32[1,4]{1,0:T(1,128)} %bitcast.117), custom_call_target="tpu_custom_call" | custom-call | bytes 196608 | tf_op jit(solution)/shard_map/pallas_call | solution.py:57
  1.2 3.0 %collective-permute-start.5 = (bf16[8,3072]{1,0:T(8,128)(2,1)S(1)}, bf16[8,3072]{1,0:T(8,128)(2,1)S(1)}, u32[]{:S(2)}, u32[]{:S(2)}) collective-permute-start(bf16[8,3072]{1,0:T(8,128)(2,1)S(1)} %get-tuple-element.14), channel_id=1, source_target_pairs={{0,4},{4,0},{8,12},{12,8},{1,5},{5,1},{9,13},{13,9},{2,6},{6,2},{1... | collective-permute-start | bytes 147464 | tf_op jit(solution)/shard_map/ppermute | solution.py:81
  4.2 2.6 %collective-permute-start = (bf16[8,3200]{1,0:T(8,128)(2,1)S(1)}, bf16[8,3200]{1,0:T(8,128)(2,1)S(1)}, u32[]{:S(2)}, u32[]{:S(2)}) collective-permute-start(bf16[8,3200]{1,0:T(8,128)(2,1)S(1)} %get-tuple-element.13), channel_id=1, source_target_pairs={{0,8},{4,12},{8,0},{12,4},{1,9},{5,13},{9,1},{13,5},{2,10},{6,14},... | collective-permute-start | bytes 153608 | tf_op jit(solution)/shard_map/ppermute | solution.py:81
  6.8 2.6 %collective-permute-start.6 = (bf16[2,8,3072]{2,1,0:T(8,128)(2,1)S(1)}, bf16[2,8,3072]{2,1,0:T(8,128)(2,1)S(1)}, u32[]{:S(2)}, u32[]{:S(2)}) collective-permute-start(bf16[2,8,3072]{2,1,0:T(8,128)(2,1)S(1)} %get-tuple-element.38), channel_id=1, source_target_pairs={{0,8},{4,12},{8,0},{12,4},{1,9},{5,13},{9,1},{13,5},{2,10},{6,14},... | collective-permute-start | bytes 294920 | tf_op jit(solution)/shard_map/ppermute | solution.py:81
  9.4 0.5 collective-permute-done
  9.9 1.6 %collective-permute-start.1 = (bf16[2,8,3200]{2,1,0:T(8,128)(2,1)S(1)}, bf16[2,8,3200]{2,1,0:T(8,128)(2,1)S(1)}, u32[]{:S(2)}, u32[]{:S(2)}) collective-permute-start(bf16[2,8,3200]{2,1,0:T(8,128)(2,1)S(1)} %get-tuple-element.36), channel_id=1, source_target_pairs={{0,4},{4,0},{8,12},{12,8},{1,5},{5,1},{9,13},{13,9},{2,6},{6,2},{1... | collective-permute-start | bytes 307208 | tf_op jit(solution)/shard_map/ppermute | solution.py:81
  11.5 2.0 %collective-permute-done.6 = bf16[2,8,3072]{2,1,0:T(8,128)(2,1)S(1)} collective-permute-done((bf16[2,8,3072]{2,1,0:T(8,128)(2,1)S(1)}, bf16[2,8,3072]{2,1,0:T(8,128)(2,1)S(1)}, u32[]{:S(2)}, u32[]{:S(2)}) %collective-permute-start.6) | collective-permute-done | bytes 98336 | tf_op jit(solution)/shard_map/ppermute | solution.py:81
  13.5 1.6 %collective-permute-start.7 = (bf16[2,2,8,3072]{3,2,0,1:T(8,128)(2,1)S(1)}, bf16[2,2,8,3072]{3,2,0,1:T(8,128)(2,1)S(1)}, u32[]{:S(2)}, u32[]{:S(2)}) collective-permute-start(bf16[2,2,8,3072]{3,2,0,1:T(8,128)(2,1)S(1)} %get-tuple-element.34), channel_id=1, source_target_pairs={{0,16},{16,0},{1,17},{17,1},{2,18},{18,2},{3,19},{19,3},{4,20},{20... | collective-permute-start | bytes 589832 | tf_op jit(solution)/shard_map/ppermute | solution.py:81
  15.1 1.6 %collective-permute-start.2 = (bf16[2,2,8,3200]{3,2,1,0:T(8,128)(2,1)S(1)}, bf16[2,2,8,3200]{3,2,1,0:T(8,128)(2,1)S(1)}, u32[]{:S(2)}, u32[]{:S(2)}) collective-permute-start(bf16[2,2,8,3200]{3,2,1,0:T(8,128)(2,1)S(1)} %get-tuple-element.32), channel_id=1, source_target_pairs={{0,2},{1,3},{2,0},{3,1},{4,6},{5,7},{6,4},{7,5},{8,10},{9,11},{10,... | collective-permute-start | bytes 614408 | tf_op jit(solution)/shard_map/ppermute | solution.py:81
  16.7 2.7 %collective-permute-done.7 = bf16[2,2,8,3072]{3,2,0,1:T(8,128)(2,1)S(1)} collective-permute-done((bf16[2,2,8,3072]{3,2,0,1:T(8,128)(2,1)S(1)}, bf16[2,2,8,3072]{3,2,0,1:T(8,128)(2,1)S(1)}, u32[]{:S(2)}, u32[]{:S(2)}) %collective-permute-start.7) | collective-permute-done | bytes 196640 | tf_op jit(solution)/shard_map/ppermute | solution.py:81
  19.5 1.6 %collective-permute-start.8 = (bf16[2,2,2,8,3072]{4,3,1,2,0:T(8,128)(2,1)S(1)}, bf16[2,2,2,8,3072]{4,3,1,2,0:T(8,128)(2,1)S(1)}, u32[]{:S(2)}, u32[]{:S(2)}) collective-permute-start(bf16[2,2,2,8,3072]{4,3,1,2,0:T(8,128)(2,1)S(1)} %get-tuple-element.30), channel_id=1, source_target_pairs={{0,2},{1,3},{2,0},{3,1},{4,6},{5,7},{6,4},{7,5},{8,10},{9,11},{10,... | collective-permute-start | bytes 1179656 | tf_op jit(solution)/shard_map/ppermute | solution.py:81
  21.0 0.8 %collective-permute-done.2 = bf16[2,2,8,3200]{3,2,1,0:T(8,128)(2,1)S(1)} collective-permute-done((bf16[2,2,8,3200]{3,2,1,0:T(8,128)(2,1)S(1)}, bf16[2,2,8,3200]{3,2,1,0:T(8,128)(2,1)S(1)}, u32[]{:S(2)}, u32[]{:S(2)}) %collective-permute-start.2) | collective-permute-done | bytes 204832 | tf_op jit(solution)/shard_map/ppermute | solution.py:81
  21.9 1.5 %collective-permute-start.3 = (bf16[2,2,2,8,3200]{4,3,2,1,0:T(8,128)(2,1)S(1)}, bf16[2,2,2,8,3200]{4,3,2,1,0:T(8,128)(2,1)S(1)}, u32[]{:S(2)}, u32[]{:S(2)}) collective-permute-start(bf16[2,2,2,8,3200]{4,3,2,1,0:T(8,128)(2,1)S(1)} %get-tuple-element.28.refs_1_), channel_id=1, source_target_pairs={{0,16},{16,0},{1,17},{17,1},{2,18},{18,2},{3,19},{19,3},{4,20},{20... | collective-permute-start | bytes 1228808 | tf_op jit(solution)/shard_map/ppermute | solution.py:81
  23.5 4.6 %shard_map.74.refs_1_ = bf16[4,2,256,3072]{3,2,1,0:T(8,128)(2,1)S(1)} custom-call(bf16[4,2,256,6144]{3,2,1,0:T(8,128)(2,1)} %refs_2_.1, bf16[2,2,2,8,3200]{4,3,2,1,0:T(8,128)(2,1)S(1)} %get-tuple-element.28.refs_1_), custom_call_target="tpu_custom_call" | custom-call | bytes 25165824 | tf_op jit(solution)/shard_map/pallas_call | solution.py:123
  28.0 1.4 %collective-permute-done.8 = bf16[2,2,2,8,3072]{4,3,1,2,0:T(8,128)(2,1)S(1)} collective-permute-done((bf16[2,2,2,8,3072]{4,3,1,2,0:T(8,128)(2,1)S(1)}, bf16[2,2,2,8,3072]{4,3,1,2,0:T(8,128)(2,1)S(1)}, u32[]{:S(2)}, u32[]{:S(2)}) %collective-permute-start.8) | collective-permute-done | bytes 393248 | tf_op jit(solution)/shard_map/ppermute | solution.py:81
  29.6 0.9 %collective-permute-done.3 = bf16[2,2,2,8,3200]{4,3,2,1,0:T(8,128)(2,1)S(1)} collective-permute-done((bf16[2,2,2,8,3200]{4,3,2,1,0:T(8,128)(2,1)S(1)}, bf16[2,2,2,8,3200]{4,3,2,1,0:T(8,128)(2,1)S(1)}, u32[]{:S(2)}, u32[]{:S(2)}) %collective-permute-start.3) | collective-permute-done | bytes 409632 | tf_op jit(solution)/shard_map/ppermute | solution.py:81
  30.5 0.1 fusion.16
  30.7 1.2 %collective-permute-done.9 = bf16[2,2,2,2,8,3072]{5,4,2,3,0,1:T(8,128)(2,1)S(1)} collective-permute-done((bf16[2,2,2,2,8,3072]{5,4,2,3,0,1:T(8,128)(2,1)S(1)}, bf16[2,2,2,2,8,3072]{5,4,2,3,0,1:T(8,128)(2,1)S(1)}, u32[]{:S(2)}, u32[]{:S(2)}) %collective-permute-start.9) | collective-permute-done | bytes 786464 | tf_op jit(solution)/shard_map/ppermute | solution.py:81
  31.9 0.1 pad_maximum_fusion.1
  32.0 0.1 copy.8
  32.2 4.7 %shard_map.75 = (f32[256,2048]{1,0:T(8,128)S(1)}, bf16[4,2,256,3072]{3,2,1,0:T(8,128)(2,1)S(1)}) custom-call(bf16[256,3072]{1,0:T(8,128)(2,1)S(1)} %bitcast.96, bf16[4,2,256,3072]{3,2,1,0:T(8,128)(2,1)S(1)} %shard_map.74.refs_1_, bf16[4,2,256,6144]{3,2,1,0:T(8,128)(2,1)} %refs_2_.1), custom_call_target="tpu_custom_call" | custom-call | flops 3221225472 | bytes 14680064 | tf_op jit(solution)/shard_map/pallas_call | solution.py:216
  36.9 0.2 pad_maximum_fusion
  37.1 4.6 %shard_map.76 = (bf16[4,256,256]{2,1,0:T(8,128)(2,1)S(1)}, bf16[4,256,6144]{2,1,0:T(8,128)(2,1)S(1)}) custom-call(bf16[256,3200]{1,0:T(8,128)(2,1)S(1)} %bitcast.95, f32[256,2048]{1,0:T(8,128)S(1)} %get-tuple-element.17.refs_1_, bf16[4,2,256,3072]{3,2,1,0:T(8,128)(2,1)S(1)} %get-tuple-element.18.refs_2_, bf16[4,256,6144]{2,1,0:T(8,128)(2,1)} %refs_3_.1), custom_call_target="tpu_custom_call" | custom-call | flops 3221225472 | bytes 14680064 | tf_op jit(solution)/shard_map/pallas_call | solution.py:216
  41.7 2.0 %shard_map.77 = bf16[256,3072]{1,0:T(8,128)(2,1)S(1)} custom-call(bf16[4,256,256]{2,1,0:T(8,128)(2,1)S(1)} %get-tuple-element.19.refs_0_, bf16[4,256,6144]{2,1,0:T(8,128)(2,1)S(1)} %get-tuple-element.20.refs_1_), custom_call_target="tpu_custom_call" | custom-call | flops 1610612736 | bytes 8388608 | tf_op jit(solution)/shard_map/pallas_call | solution.py:259
  43.7 0.1 fusion.17
  43.8 0.2 collective-permute-start.10
  44.0 2.0 %shard_map.78 = bf16[256,3072]{1,0:T(8,128)(2,1)S(1)} custom-call(bf16[4,256,256]{2,1,0:T(8,128)(2,1)S(1)} %get-tuple-element.19.refs_0_, bf16[4,256,6144]{2,1,0:T(8,128)(2,1)S(1)} %get-tuple-element.20.refs_1_), custom_call_target="tpu_custom_call" | custom-call | flops 1610612736 | bytes 8388608 | tf_op jit(solution)/shard_map/pallas_call | solution.py:259
  46.0 0.1 fusion.18
  46.2 0.5 collective-permute-start.15
  46.7 0.2 fusion.1
  46.9 1.5 %collective-permute-start.11 = (bf16[2,2,2,8,3072]{4,3,1,2,0:T(8,128)(2,1)S(1)}, bf16[2,2,2,8,3072]{4,3,1,2,0:T(8,128)(2,1)S(1)}, u32[]{:S(2)}, u32[]{:S(2)}) collective-permute-start(bf16[2,2,2,8,3072]{4,3,1,2,0:T(8,128)(2,1)S(1)} %slice_bitcast_fusion.2), channel_id=1, source_target_pairs={{0,16},{16,0},{1,17},{17,1},{2,18},{18,2},{3,19},{19,3},{4,20},{20... | collective-permute-start | bytes 1179656 | tf_op jit(solution)/shard_map/ppermute | solution.py:81
  48.5 0.1 collective-permute-done.15
  48.6 0.2 fusion
  48.8 1.6 %collective-permute-start.16 = (bf16[2,2,2,8,3072]{4,3,2,1,0:T(8,128)(2,1)S(1)}, bf16[2,2,2,8,3072]{4,3,2,1,0:T(8,128)(2,1)S(1)}, u32[]{:S(2)}, u32[]{:S(2)}) collective-permute-start(bf16[2,2,2,8,3072]{4,3,2,1,0:T(8,128)(2,1)S(1)} %slice_bitcast_fusion), channel_id=1, source_target_pairs={{0,2},{1,3},{2,0},{3,1},{4,6},{5,7},{6,4},{7,5},{8,10},{9,11},{10,... | collective-permute-start | bytes 1179656 | tf_op jit(solution)/shard_map/ppermute | solution.py:81
  50.4 7.7 %collective-permute-done.11 = bf16[2,2,2,8,3072]{4,3,1,2,0:T(8,128)(2,1)S(1)} collective-permute-done((bf16[2,2,2,8,3072]{4,3,1,2,0:T(8,128)(2,1)S(1)}, bf16[2,2,2,8,3072]{4,3,1,2,0:T(8,128)(2,1)S(1)}, u32[]{:S(2)}, u32[]{:S(2)}) %collective-permute-start.11) | collective-permute-done | bytes 393248 | tf_op jit(solution)/shard_map/ppermute | solution.py:81
  58.2 1.6 %collective-permute-start.12 = (bf16[2,2,8,3072]{3,2,0,1:T(8,128)(2,1)S(1)}, bf16[2,2,8,3072]{3,2,0,1:T(8,128)(2,1)S(1)}, u32[]{:S(2)}, u32[]{:S(2)}) collective-permute-start(bf16[2,2,8,3072]{3,2,0,1:T(8,128)(2,1)S(1)} %slice_bitcast_fusion.6), channel_id=1, source_target_pairs={{0,2},{1,3},{2,0},{3,1},{4,6},{5,7},{6,4},{7,5},{8,10},{9,11},{10,... | collective-permute-start | bytes 589832 | tf_op jit(solution)/shard_map/ppermute | solution.py:81
  59.8 0.5 collective-permute-done.16
  60.4 1.5 %collective-permute-start.17 = (bf16[2,2,8,3072]{3,2,1,0:T(8,128)(2,1)S(1)}, bf16[2,2,8,3072]{3,2,1,0:T(8,128)(2,1)S(1)}, u32[]{:S(2)}, u32[]{:S(2)}) collective-permute-start(bf16[2,2,8,3072]{3,2,1,0:T(8,128)(2,1)S(1)} %slice_bitcast_fusion.4), channel_id=1, source_target_pairs={{0,16},{16,0},{1,17},{17,1},{2,18},{18,2},{3,19},{19,3},{4,20},{20... | collective-permute-start | bytes 589832 | tf_op jit(solution)/shard_map/ppermute | solution.py:81
  61.9 2.5 %collective-permute-done.12 = bf16[2,2,8,3072]{3,2,0,1:T(8,128)(2,1)S(1)} collective-permute-done((bf16[2,2,8,3072]{3,2,0,1:T(8,128)(2,1)S(1)}, bf16[2,2,8,3072]{3,2,0,1:T(8,128)(2,1)S(1)}, u32[]{:S(2)}, u32[]{:S(2)}) %collective-permute-start.12) | collective-permute-done | bytes 196640 | tf_op jit(solution)/shard_map/ppermute | solution.py:81
  64.6 1.6 %collective-permute-start.13 = (bf16[2,8,3072]{2,1,0:T(8,128)(2,1)S(1)}, bf16[2,8,3072]{2,1,0:T(8,128)(2,1)S(1)}, u32[]{:S(2)}, u32[]{:S(2)}) collective-permute-start(bf16[2,8,3072]{2,1,0:T(8,128)(2,1)S(1)} %slice_bitcast_fusion.10), channel_id=1, source_target_pairs={{0,8},{4,12},{8,0},{12,4},{1,9},{5,13},{9,1},{13,5},{2,10},{6,14},... | collective-permute-start | bytes 294920 | tf_op jit(solution)/shard_map/ppermute | solution.py:81
  66.2 0.7 collective-permute-done.17
  66.9 2.1 %collective-permute-start.18 = (bf16[2,8,3072]{2,1,0:T(8,128)(2,1)S(1)}, bf16[2,8,3072]{2,1,0:T(8,128)(2,1)S(1)}, u32[]{:S(2)}, u32[]{:S(2)}) collective-permute-start(bf16[2,8,3072]{2,1,0:T(8,128)(2,1)S(1)} %slice_bitcast_fusion.8), channel_id=1, source_target_pairs={{0,4},{4,0},{8,12},{12,8},{1,5},{5,1},{9,13},{13,9},{2,6},{6,2},{1... | collective-permute-start | bytes 294920 | tf_op jit(solution)/shard_map/ppermute | solution.py:81
  69.0 1.3 %collective-permute-done.13 = bf16[2,8,3072]{2,1,0:T(8,128)(2,1)S(1)} collective-permute-done((bf16[2,8,3072]{2,1,0:T(8,128)(2,1)S(1)}, bf16[2,8,3072]{2,1,0:T(8,128)(2,1)S(1)}, u32[]{:S(2)}, u32[]{:S(2)}) %collective-permute-start.13) | collective-permute-done | bytes 98336 | tf_op jit(solution)/shard_map/ppermute | solution.py:81
  70.3 1.7 %collective-permute-start.14 = (bf16[8,3072]{1,0:T(8,128)(2,1)S(1)}, bf16[8,3072]{1,0:T(8,128)(2,1)S(1)}, u32[]{:S(2)}, u32[]{:S(2)}) collective-permute-start(bf16[8,3072]{1,0:T(8,128)(2,1)S(1)} %slice_bitcast_fusion.14), channel_id=1, source_target_pairs={{0,4},{4,0},{8,12},{12,8},{1,5},{5,1},{9,13},{13,9},{2,6},{6,2},{1... | collective-permute-start | bytes 147464 | tf_op jit(solution)/shard_map/ppermute | solution.py:81
  72.0 0.1 collective-permute-done.18
  72.1 2.8 %collective-permute-start.19 = (bf16[8,3072]{1,0:T(8,128)(2,1)S(1)}, bf16[8,3072]{1,0:T(8,128)(2,1)S(1)}, u32[]{:S(2)}, u32[]{:S(2)}) collective-permute-start(bf16[8,3072]{1,0:T(8,128)(2,1)S(1)} %slice_bitcast_fusion.12), channel_id=1, source_target_pairs={{0,8},{4,12},{8,0},{12,4},{1,9},{5,13},{9,1},{13,5},{2,10},{6,14},... | collective-permute-start | bytes 147464 | tf_op jit(solution)/shard_map/ppermute | solution.py:81
  75.0 2.2 %collective-permute-done.19 = bf16[8,3072]{1,0:T(8,128)(2,1)S(1)} collective-permute-done((bf16[8,3072]{1,0:T(8,128)(2,1)S(1)}, bf16[8,3072]{1,0:T(8,128)(2,1)S(1)}, u32[]{:S(2)}, u32[]{:S(2)}) %collective-permute-start.19) | collective-permute-done | bytes 49184 | tf_op jit(solution)/shard_map/ppermute | solution.py:81
  77.2 0.6 pad_maximum_fusion.10
  (32 shorter events, 1.0 us)
Async XLA Ops:
  1.2 5.6 %collective-permute-start.5 = (bf16[8,3072]{1,0:T(8,128)(2,1)S(1)}, bf16[8,3072]{1,0:T(8,128)(2,1)S(1)}, u32[]{:S(2)}, u32[]{:S(2)}) collective-permute-start(bf16[8,3072]{1,0:T(8,128)(2,1)S(1)} %get-tuple-element.14), channel_id=1, source_target_pairs={{0,4},{4,0},{8,12},{12,8},{1,5},{5,1},{9,13},{13,9},{2,6},{6,2},{1... | collective-permute-start | bytes 147464 | tf_op jit(solution)/shard_map/ppermute | solution.py:81
  4.2 5.7 %collective-permute-start = (bf16[8,3200]{1,0:T(8,128)(2,1)S(1)}, bf16[8,3200]{1,0:T(8,128)(2,1)S(1)}, u32[]{:S(2)}, u32[]{:S(2)}) collective-permute-start(bf16[8,3200]{1,0:T(8,128)(2,1)S(1)} %get-tuple-element.13), channel_id=1, source_target_pairs={{0,8},{4,12},{8,0},{12,4},{1,9},{5,13},{9,1},{13,5},{2,10},{6,14},... | collective-permute-start | bytes 153608 | tf_op jit(solution)/shard_map/ppermute | solution.py:81
  6.8 6.7 %collective-permute-start.6 = (bf16[2,8,3072]{2,1,0:T(8,128)(2,1)S(1)}, bf16[2,8,3072]{2,1,0:T(8,128)(2,1)S(1)}, u32[]{:S(2)}, u32[]{:S(2)}) collective-permute-start(bf16[2,8,3072]{2,1,0:T(8,128)(2,1)S(1)} %get-tuple-element.38), channel_id=1, source_target_pairs={{0,8},{4,12},{8,0},{12,4},{1,9},{5,13},{9,1},{13,5},{2,10},{6,14},... | collective-permute-start | bytes 294920 | tf_op jit(solution)/shard_map/ppermute | solution.py:81
  9.9 5.2 %collective-permute-start.1 = (bf16[2,8,3200]{2,1,0:T(8,128)(2,1)S(1)}, bf16[2,8,3200]{2,1,0:T(8,128)(2,1)S(1)}, u32[]{:S(2)}, u32[]{:S(2)}) collective-permute-start(bf16[2,8,3200]{2,1,0:T(8,128)(2,1)S(1)} %get-tuple-element.36), channel_id=1, source_target_pairs={{0,4},{4,0},{8,12},{12,8},{1,5},{5,1},{9,13},{13,9},{2,6},{6,2},{1... | collective-permute-start | bytes 307208 | tf_op jit(solution)/shard_map/ppermute | solution.py:81
  13.5 5.9 %collective-permute-start.7 = (bf16[2,2,8,3072]{3,2,0,1:T(8,128)(2,1)S(1)}, bf16[2,2,8,3072]{3,2,0,1:T(8,128)(2,1)S(1)}, u32[]{:S(2)}, u32[]{:S(2)}) collective-permute-start(bf16[2,2,8,3072]{3,2,0,1:T(8,128)(2,1)S(1)} %get-tuple-element.34), channel_id=1, source_target_pairs={{0,16},{16,0},{1,17},{17,1},{2,18},{18,2},{3,19},{19,3},{4,20},{20... | collective-permute-start | bytes 589832 | tf_op jit(solution)/shard_map/ppermute | solution.py:81
  15.1 6.7 %collective-permute-start.2 = (bf16[2,2,8,3200]{3,2,1,0:T(8,128)(2,1)S(1)}, bf16[2,2,8,3200]{3,2,1,0:T(8,128)(2,1)S(1)}, u32[]{:S(2)}, u32[]{:S(2)}) collective-permute-start(bf16[2,2,8,3200]{3,2,1,0:T(8,128)(2,1)S(1)} %get-tuple-element.32), channel_id=1, source_target_pairs={{0,2},{1,3},{2,0},{3,1},{4,6},{5,7},{6,4},{7,5},{8,10},{9,11},{10,... | collective-permute-start | bytes 614408 | tf_op jit(solution)/shard_map/ppermute | solution.py:81
  19.5 10.0 %collective-permute-start.8 = (bf16[2,2,2,8,3072]{4,3,1,2,0:T(8,128)(2,1)S(1)}, bf16[2,2,2,8,3072]{4,3,1,2,0:T(8,128)(2,1)S(1)}, u32[]{:S(2)}, u32[]{:S(2)}) collective-permute-start(bf16[2,2,2,8,3072]{4,3,1,2,0:T(8,128)(2,1)S(1)} %get-tuple-element.30), channel_id=1, source_target_pairs={{0,2},{1,3},{2,0},{3,1},{4,6},{5,7},{6,4},{7,5},{8,10},{9,11},{10,... | collective-permute-start | bytes 1179656 | tf_op jit(solution)/shard_map/ppermute | solution.py:81
  21.9 8.6 %collective-permute-start.3 = (bf16[2,2,2,8,3200]{4,3,2,1,0:T(8,128)(2,1)S(1)}, bf16[2,2,2,8,3200]{4,3,2,1,0:T(8,128)(2,1)S(1)}, u32[]{:S(2)}, u32[]{:S(2)}) collective-permute-start(bf16[2,2,2,8,3200]{4,3,2,1,0:T(8,128)(2,1)S(1)} %get-tuple-element.28.refs_1_), channel_id=1, source_target_pairs={{0,16},{16,0},{1,17},{17,1},{2,18},{18,2},{3,19},{19,3},{4,20},{20... | collective-permute-start | bytes 1228808 | tf_op jit(solution)/shard_map/ppermute | solution.py:81
  29.5 2.4 %collective-permute-start.9 = (bf16[2,2,2,2,8,3072]{5,4,2,3,0,1:T(8,128)(2,1)S(1)}, bf16[2,2,2,2,8,3072]{5,4,2,3,0,1:T(8,128)(2,1)S(1)}, u32[]{:S(2)}, u32[]{:S(2)}) collective-permute-start(bf16[2,2,2,2,8,3072]{5,4,2,3,0,1:T(8,128)(2,1)S(1)} %pad_maximum_fusion.3), channel_id=1, source_target_pairs={{0,1},{1,0},{2,3},{3,2},{4,5},{5,4},{6,7},{7,6},{8,9},{9,8},{10,11... | collective-permute-start | bytes 2359304 | tf_op jit(solution)/shard_map/ppermute | solution.py:81
  30.6 6.3 %collective-permute-start.4 = (bf16[2,2,2,2,8,3200]{5,4,3,2,1,0:T(8,128)(2,1)S(1)}, bf16[2,2,2,2,8,3200]{5,4,3,2,1,0:T(8,128)(2,1)S(1)}, u32[]{:S(2)}, u32[]{:S(2)}) collective-permute-start(bf16[2,2,2,2,8,3200]{5,4,3,2,1,0:T(8,128)(2,1)S(1)} %get-tuple-element.26), channel_id=1, source_target_pairs={{0,1},{1,0},{2,3},{3,2},{4,5},{5,4},{6,7},{7,6},{8,9},{9,8},{10,11... | collective-permute-start | bytes 2457608 | tf_op jit(solution)/shard_map/ppermute | solution.py:81
  43.8 2.8 %collective-permute-start.10 = (bf16[2,2,2,2,8,3072]{5,4,2,3,1,0:T(8,128)(2,1)S(1)}, bf16[2,2,2,2,8,3072]{5,4,2,3,1,0:T(8,128)(2,1)S(1)}, u32[]{:S(2)}, u32[]{:S(2)}) collective-permute-start(bf16[2,2,2,2,8,3072]{5,4,2,3,1,0:T(8,128)(2,1)S(1)} %copy.9), channel_id=1, source_target_pairs={{0,1},{1,0},{2,3},{3,2},{4,5},{5,4},{6,7},{7,6},{8,9},{9,8},{10,11... | collective-permute-start | bytes 2359304 | tf_op jit(solution)/shard_map/ppermute | solution.py:81
  46.2 2.4 %collective-permute-start.15 = (bf16[2,2,2,2,8,3072]{5,4,3,2,0,1:T(8,128)(2,1)S(1)}, bf16[2,2,2,2,8,3072]{5,4,3,2,0,1:T(8,128)(2,1)S(1)}, u32[]{:S(2)}, u32[]{:S(2)}) collective-permute-start(bf16[2,2,2,2,8,3072]{5,4,3,2,0,1:T(8,128)(2,1)S(1)} %copy.11), channel_id=1, source_target_pairs={{0,1},{1,0},{2,3},{3,2},{4,5},{5,4},{6,7},{7,6},{8,9},{9,8},{10,11... | collective-permute-start | bytes 2359304 | tf_op jit(solution)/shard_map/ppermute | solution.py:81
  46.9 11.2 %collective-permute-start.11 = (bf16[2,2,2,8,3072]{4,3,1,2,0:T(8,128)(2,1)S(1)}, bf16[2,2,2,8,3072]{4,3,1,2,0:T(8,128)(2,1)S(1)}, u32[]{:S(2)}, u32[]{:S(2)}) collective-permute-start(bf16[2,2,2,8,3072]{4,3,1,2,0:T(8,128)(2,1)S(1)} %slice_bitcast_fusion.2), channel_id=1, source_target_pairs={{0,16},{16,0},{1,17},{17,1},{2,18},{18,2},{3,19},{19,3},{4,20},{20... | collective-permute-start | bytes 1179656 | tf_op jit(solution)/shard_map/ppermute | solution.py:81
  48.8 11.5 %collective-permute-start.16 = (bf16[2,2,2,8,3072]{4,3,2,1,0:T(8,128)(2,1)S(1)}, bf16[2,2,2,8,3072]{4,3,2,1,0:T(8,128)(2,1)S(1)}, u32[]{:S(2)}, u32[]{:S(2)}) collective-permute-start(bf16[2,2,2,8,3072]{4,3,2,1,0:T(8,128)(2,1)S(1)} %slice_bitcast_fusion), channel_id=1, source_target_pairs={{0,2},{1,3},{2,0},{3,1},{4,6},{5,7},{6,4},{7,5},{8,10},{9,11},{10,... | collective-permute-start | bytes 1179656 | tf_op jit(solution)/shard_map/ppermute | solution.py:81
  58.2 6.2 %collective-permute-start.12 = (bf16[2,2,8,3072]{3,2,0,1:T(8,128)(2,1)S(1)}, bf16[2,2,8,3072]{3,2,0,1:T(8,128)(2,1)S(1)}, u32[]{:S(2)}, u32[]{:S(2)}) collective-permute-start(bf16[2,2,8,3072]{3,2,0,1:T(8,128)(2,1)S(1)} %slice_bitcast_fusion.6), channel_id=1, source_target_pairs={{0,2},{1,3},{2,0},{3,1},{4,6},{5,7},{6,4},{7,5},{8,10},{9,11},{10,... | collective-permute-start | bytes 589832 | tf_op jit(solution)/shard_map/ppermute | solution.py:81
  60.4 6.4 %collective-permute-start.17 = (bf16[2,2,8,3072]{3,2,1,0:T(8,128)(2,1)S(1)}, bf16[2,2,8,3072]{3,2,1,0:T(8,128)(2,1)S(1)}, u32[]{:S(2)}, u32[]{:S(2)}) collective-permute-start(bf16[2,2,8,3072]{3,2,1,0:T(8,128)(2,1)S(1)} %slice_bitcast_fusion.4), channel_id=1, source_target_pairs={{0,16},{16,0},{1,17},{17,1},{2,18},{18,2},{3,19},{19,3},{4,20},{20... | collective-permute-start | bytes 589832 | tf_op jit(solution)/shard_map/ppermute | solution.py:81
  64.6 5.7 %collective-permute-start.13 = (bf16[2,8,3072]{2,1,0:T(8,128)(2,1)S(1)}, bf16[2,8,3072]{2,1,0:T(8,128)(2,1)S(1)}, u32[]{:S(2)}, u32[]{:S(2)}) collective-permute-start(bf16[2,8,3072]{2,1,0:T(8,128)(2,1)S(1)} %slice_bitcast_fusion.10), channel_id=1, source_target_pairs={{0,8},{4,12},{8,0},{12,4},{1,9},{5,13},{9,1},{13,5},{2,10},{6,14},... | collective-permute-start | bytes 294920 | tf_op jit(solution)/shard_map/ppermute | solution.py:81
  66.9 5.2 %collective-permute-start.18 = (bf16[2,8,3072]{2,1,0:T(8,128)(2,1)S(1)}, bf16[2,8,3072]{2,1,0:T(8,128)(2,1)S(1)}, u32[]{:S(2)}, u32[]{:S(2)}) collective-permute-start(bf16[2,8,3072]{2,1,0:T(8,128)(2,1)S(1)} %slice_bitcast_fusion.8), channel_id=1, source_target_pairs={{0,4},{4,0},{8,12},{12,8},{1,5},{5,1},{9,13},{13,9},{2,6},{6,2},{1... | collective-permute-start | bytes 294920 | tf_op jit(solution)/shard_map/ppermute | solution.py:81
  70.3 4.7 %collective-permute-start.14 = (bf16[8,3072]{1,0:T(8,128)(2,1)S(1)}, bf16[8,3072]{1,0:T(8,128)(2,1)S(1)}, u32[]{:S(2)}, u32[]{:S(2)}) collective-permute-start(bf16[8,3072]{1,0:T(8,128)(2,1)S(1)} %slice_bitcast_fusion.14), channel_id=1, source_target_pairs={{0,4},{4,0},{8,12},{12,8},{1,5},{5,1},{9,13},{13,9},{2,6},{6,2},{1... | collective-permute-start | bytes 147464 | tf_op jit(solution)/shard_map/ppermute | solution.py:81
  72.1 5.1 %collective-permute-start.19 = (bf16[8,3072]{1,0:T(8,128)(2,1)S(1)}, bf16[8,3072]{1,0:T(8,128)(2,1)S(1)}, u32[]{:S(2)}, u32[]{:S(2)}) collective-permute-start(bf16[8,3072]{1,0:T(8,128)(2,1)S(1)} %slice_bitcast_fusion.12), channel_id=1, source_target_pairs={{0,8},{4,12},{8,0},{12,4},{1,9},{5,13},{9,1},{13,5},{2,10},{6,14},... | collective-permute-start | bytes 147464 | tf_op jit(solution)/shard_map/ppermute | solution.py:81
